TPU v7x, 32 devices: a whole 2x2x4 slice. The times are simulated.
32 devices in a mesh: grp: 2 (over y), kpt: 4 (over z), pw: 2 (over x), band: 2 (over core).
Axes of the slice: x: 2, y: 2, z: 4, core: 2. Of those that a mesh axis runs over, the one named last changes fastest.
Arguments:
- conduction: bfloat16 [4, 32, 64, 4000], P('grp', 'kpt', 'band', 'pw'), parts along dimension 0, may hold values from -6 to 6
- conduction_head: bfloat16 [4, 32, 64], P('grp', 'kpt', 'band'), parts along dimension 0, may hold values from -6 to 6
- valence: bfloat16 [4, 32, 64, 4000], P('grp', 'kpt', None, 'pw'), parts along dimension 0, may hold values from -6 to 6
- valence_head: bfloat16 [4, 32, 64], P('grp', 'kpt'), parts along dimension 0, may hold values from -6 to 6
- screened: bfloat16 [4, 4000, 4000], P('grp', 'kpt', 'pw'), parts along dimension 0, may hold values from -0.0014648438 to 0.0014648438
- wing_column: bfloat16 [4, 4000], P('grp'), parts along dimension 0, may hold values from -0.09375 to 0.09375
- wing_row: bfloat16 [4, 4000], P('grp', 'pw'), parts along dimension 0, may hold values from -0.09375 to 0.09375
- head_value: float32 [4], P('grp'), parts along dimension 0, may hold values from -4 to 4
- partner: int32 [64], P('grp'), parts along dimension 0, may hold values from 0 to 31, as said below
- pair_select: int32 [64], replicated, may hold values from 0 to 63, each once
- neighbors: int32 [64, 4], replicated, may hold values from 0 to 31
- weights: float32 [64, 4], replicated, may hold values from 0.2 to 1
- counts: int32 [64], replicated, may hold values from 1 to 4
Outputs:
- fine_kernel: float32 [4, 64, 4096], P('grp', 'kpt', 'band'), parts along dimension 0
There are 2 independent parts, one for each index of `grp`. A program takes and returns all parts, laid end to end along the dimension named above; an argument that names none is the same for every part. Nothing has to cross between parts.
Inputs may be any that keep to these rules, and one draw needn't show every extreme that they name: partner is a permutation of the 32 rows; the 8 points of one kpt index find their rows on any one kpt index at most 2 times, and some pair of indices reaches 2.
All inputs are finite; a program needn't handle non-finite values.
Results may differ from a plain program's by a relative error of at most 0.0032.
Values may be sent and summed in bfloat16 or wider, within the bound.
No kernel may reach another device: no remote copies, remote signals or barrier semaphores. Data moves between devices by JAX's collectives and lax.ppermute only.
A program may use at most 192 MiB of HBM per device.

v0:
```python
import jax
import jax.numpy as jnp
from jax import lax
from jax.sharding import PartitionSpec as P

highest = lax.Precision.HIGHEST


def expanded_left(conduction_all, row_count):
    planes = conduction_all.shape[3]
    real_part = conduction_all[0].reshape(row_count, planes)
    imag_part = conduction_all[1].reshape(row_count, planes)
    upper = jnp.stack([real_part, imag_part], axis=1)
    lower = jnp.stack([-imag_part, real_part], axis=1)
    return jnp.concatenate([upper, lower], axis=0)


def pair_contract(screened_rows, valence_rows):

    def multiply(first, second):
        return jnp.einsum("kcg,kvg->kcv", first, second, preferred_element_type=jnp.float32)

    real_part = multiply(screened_rows[0], valence_rows[0]) - multiply(
        screened_rows[1], valence_rows[1]
    )
    imag_part = multiply(screened_rows[0], valence_rows[1]) + multiply(
        screened_rows[1], valence_rows[0]
    )
    return jnp.stack([real_part, imag_part])


def row_folder(left, piece):
    doubled = left.shape[0]
    span = piece.shape[1]
    columns = left.reshape(doubled, 2 * span)
    stacked = piece.reshape(2 * span, piece.shape[2])
    return jnp.dot(columns, stacked, preferred_element_type=jnp.float32)


def stencil_matrix(near, live, span):
    point_ids = jnp.arange(span)
    match = near[:, :, None] == point_ids[None, None, :]
    return jnp.sum(jnp.where(match, live[:, :, None], jnp.float32(0.0)), axis=1)


def on_device(
    conduction,
    conduction_head,
    valence,
    valence_head,
    screened,
    wing_column,
    wing_row,
    head_value,
    partner,
    pair_select,
    neighbors,
    weights,
    counts,
):
    points = conduction.shape[1]
    pair_half = conduction.shape[2]
    valence_pairs = valence.shape[2]
    kpt_count = lax.axis_size("kpt")
    position = lax.axis_index("kpt")
    capacity = -(-points // kpt_count)
    table = partner.reshape(kpt_count, points)
    source = table // points
    within = table % points
    earlier = jnp.tril(jnp.ones((points, points), jnp.int32), -1)
    same_source = (source[:, :, None] == source[:, None, :]).astype(jnp.int32)
    rank = jnp.sum(same_source * earlier[None, :, :], axis=2)
    from_here = source == position
    slot_ids = jnp.arange(capacity)
    chosen = from_here[:, :, None] & (rank[:, :, None] == slot_ids[None, None, :])
    picked = jnp.sum(jnp.where(chosen, within[:, :, None], 0), axis=1).reshape(-1)
    outgoing = jnp.take(valence, picked, axis=1)
    outgoing_head = jnp.take(valence_head, picked, axis=1)
    arrived, arrived_head = (
        lax.all_to_all(outgoing, "kpt", split_axis=1, concat_axis=1, tiled=True),
        lax.all_to_all(outgoing_head, "kpt", split_axis=1, concat_axis=1, tiled=True),
    )
    my_source = lax.dynamic_index_in_dim(source, position, 0, keepdims=False)
    my_rank = lax.dynamic_index_in_dim(rank, position, 0, keepdims=False)
    lookup = my_source * capacity + my_rank
    partner_rows = jnp.take(arrived, lookup, axis=1)
    partner_head = jnp.take(arrived_head, lookup, axis=1)
    conduction_all = lax.all_gather(conduction, "pw", axis=3, tiled=True)

    def column_sum(first, second):
        return jnp.einsum("kcg,g->kc", first, second, preferred_element_type=jnp.float32)

    side_real = column_sum(conduction_all[0], wing_column[0]) + column_sum(
        conduction_all[1], wing_column[1]
    )
    side_imag = column_sum(conduction_all[0], wing_column[1]) - column_sum(
        conduction_all[1], wing_column[0]
    )

    def row_sum(first, second):
        return jnp.einsum("g,kvg->kv", first, second, preferred_element_type=jnp.float32)

    wing_real = row_sum(wing_row[0], partner_rows[0]) - row_sum(wing_row[1], partner_rows[1])
    wing_imag = row_sum(wing_row[0], partner_rows[1]) + row_sum(wing_row[1], partner_rows[0])
    valence_wing = jnp.stack([wing_real, wing_imag])
    column_count = screened.shape[2]
    band_count = lax.axis_size("band")
    conduction_pairs = lax.all_gather(conduction_all, "band", axis=2, tiled=True)
    width = column_count // band_count
    lower = lax.axis_index("band") * width
    screen_part = lax.dynamic_slice_in_dim(screened, lower, width, 2)
    valence_part = lax.dynamic_slice_in_dim(partner_rows, lower, width, 3)
    all_pairs = conduction_pairs.shape[2]
    left = expanded_left(conduction_pairs, points * all_pairs)
    folded = row_folder(left, lax.all_gather(screen_part, "kpt", axis=1, tiled=True))
    screened_rows = folded.astype(jnp.bfloat16).reshape(2, points, all_pairs, width)
    block = pair_contract(screened_rows, valence_part)
    block = lax.psum_scatter(block, "band", scatter_dimension=2, tiled=True)
    block, valence_wing = lax.psum((block, valence_wing), "pw")
    conj_real = conduction_head[0].astype(jnp.float32)
    conj_imag = -conduction_head[1].astype(jnp.float32)
    head_real = partner_head[0].astype(jnp.float32)
    head_imag = partner_head[1].astype(jnp.float32)
    first_real = (
        conj_real[:, :, None] * valence_wing[0][:, None, :]
        - conj_imag[:, :, None] * valence_wing[1][:, None, :]
    )
    first_imag = (
        conj_real[:, :, None] * valence_wing[1][:, None, :]
        + conj_imag[:, :, None] * valence_wing[0][:, None, :]
    )
    scaled_real = side_real + conj_real * head_value[0] - conj_imag * head_value[1]
    scaled_imag = side_imag + conj_real * head_value[1] + conj_imag * head_value[0]
    second_real = (
        scaled_real[:, :, None] * head_real[:, None, :]
        - scaled_imag[:, :, None] * head_imag[:, None, :]
    )
    second_imag = (
        scaled_real[:, :, None] * head_imag[:, None, :]
        + scaled_imag[:, :, None] * head_real[:, None, :]
    )
    kernel = block + jnp.stack([first_real + second_real, first_imag + second_imag])
    selector = (jnp.arange(valence_pairs)[:, None] == pair_select[None, :]).astype(jnp.float32)
    kernel = jnp.einsum("xkcw,wv->xkcv", kernel, selector, precision=highest)
    coarse = kernel.astype(jnp.bfloat16).reshape(2, points, pair_half * valence_pairs)
    fine_points = neighbors.shape[0] // kpt_count
    stencil_slots = neighbors.shape[1]
    every_live = jnp.where(
        jnp.arange(stencil_slots)[None, :] < counts[:, None], weights, jnp.float32(0.0)
    )
    my_near = lax.dynamic_slice_in_dim(neighbors, position * fine_points, fine_points, 0)
    my_live = lax.dynamic_slice_in_dim(every_live, position * fine_points, fine_points, 0)
    piece = lax.all_gather(coarse, "kpt", axis=1, tiled=True)
    stencil = stencil_matrix(my_near, my_live, piece.shape[1])
    return jnp.einsum("fr,xrq->xfq", stencil, piece.astype(jnp.float32), precision=highest)


def solution(mesh):
    return jax.shard_map(
        on_device,
        mesh=mesh,
        in_specs=(
            P("grp", "kpt", "band", "pw"),
            P("grp", "kpt", "band"),
            P("grp", "kpt", None, "pw"),
            P("grp", "kpt", None),
            P("grp", "kpt", "pw"),
            P("grp", None),
            P("grp", "pw"),
            P("grp"),
            P("grp"),
            P(),
            P(),
            P(),
            P(),
        ),
        out_specs=P("grp", "kpt", "band"),
        check_vma=False,
    )
```

profile of v0, /device:TPU:0, one launch (start us, length us, event | category | flops | bytes accessed | tf_op | source)
XLA Modules:
  0.0 716.1 jit_solution(5080052032103388098)
XLA Ops:
  6.5 10.0 %copy.79 = bf16[2,8,32,2000]{2,1,0,3:T(8,128)(2,1)} copy(bf16[2,8,32,2000]{3,2,1,0:T(8,128)(2,1)} %param.17) | data formatting | bytes 4096000 | tf_op args[0]
  16.6 197.2 %all-gather.4.cloned.1.call-done = bf16[2,8,32,4000]{2,1,0,3:T(8,128)(2,1)} async-done(((bf16[2,8,32,2000]{2,1,0,3:T(8,128)(2,1)}), bf16[2,8,32,4000]{2,1,0,3:T(8,128)(2,1)}) %all-gather.4.cloned.1.call-update) | async-done | bytes 4096016 | tf_op jit(solution)/shard_map/all_gather | solution.py:88
  213.8 19.7 %copy.80 = bf16[2,8,32,4000]{3,1,0,2:T(8,128)(2,1)} copy(bf16[2,8,32,4000]{2,1,0,3:T(8,128)(2,1)} %all-gather.4.cloned.1.call-done) | data formatting | bytes 8192000 | tf_op jit(solution)/shard_map/all_gather | solution.py:88
  233.6 4.5 constant_dynamic-slice_fusion.4
  238.2 6.4 copy.106
  246.7 4.6 all-to-all-start.1
  251.3 5.0 gather_fusion
  256.3 4.7 select_bitcast_fusion
  261.0 5.2 all-to-all-start
  268.1 12.0 %slice_bitcast_fusion = (bf16[8,32,4000]{1,0,2:T(8,128)(2,1)}, bf16[8,32,4000]{1,0,2:T(8,128)(2,1)}) fusion(bf16[2,8,32,4000]{2,1,0,3:T(8,128)(2,1)} %all-gather.4.cloned.1.call-done), kind=kLoop, calls=%fused_computation.13 | loop fusion | bytes 8192000 | tf_op jit(solution)/shard_map/squeeze | solution.py:94
  280.1 8.2 %copy.99 = bf16[8,32,4000]{2,1,0:T(8,128)(2,1)S(1)} copy(bf16[8,32,4000]{1,0,2:T(8,128)(2,1)} %get-tuple-element.12) | data formatting | bytes 4096000 | tf_op jit(solution)/shard_map/squeeze | solution.py:93
  288.4 9.3 %copy.101 = bf16[8,32,4000]{2,1,0:T(8,128)(2,1)} copy(bf16[8,32,4000]{1,0,2:T(8,128)(2,1)} %get-tuple-element.11) | data formatting | bytes 4096000 | tf_op jit(solution)/shard_map/squeeze | solution.py:94
  304.9 176.5 %all-to-all-done = bf16[2,8,64,2000]{3,2,0,1:T(8,128)(2,1)} async-done(((bf16[2,8,64,2000]{3,2,0,1:T(8,128)(2,1)}), bf16[2,8,64,2000]{3,2,0,1:T(8,128)(2,1)}, u32[]{:S(2)}, u32[]{:S(2)}) %all-to-all-start) | async-done | bytes 4096032 | tf_op jit(solution)/shard_map/all_to_all | solution.py:80
  481.4 4.7 copy.91
  486.1 5.0 gather_fusion.1
  497.5 5.2 fusion.61
  506.9 6.5 copy.84
  513.4 5.1 neg.20
  522.8 6.5 copy.83
  529.2 94.0 %all-gather.8.cloned.1.call-done = bf16[2,4000,1000]{2,0,1:T(2,128)(2,1)} async-done(((bf16[2,1000,1000]{2,0,1:T(2,128)(2,1)}), bf16[2,4000,1000]{2,0,1:T(2,128)(2,1)}) %all-gather.8.cloned.1.call-update) | async-done | bytes 16000016 | tf_op jit(solution)/shard_map/all_gather | solution.py:115
  623.2 27.7 %bitcast_convert_fusion = bf16[1024,1000]{0,1:T(8,128)(2,1)S(1)} fusion(bf16[2,4000,1000]{2,0,1:T(2,128)(2,1)} %all-gather.8.cloned.1.call-done, bf16[512,1,4000]{0,2,1:T(8,128)(2,1)} %copy.83, bf16[512,1,4000]{0,2,1:T(8,128)(2,1)} %neg.20, bf16[512,1,4000]{0,2,1:T(8,128)(2,1)} %copy.84), kind=kOutput, calls=%fused_computation.18 | convolution fusion | flops 16450560000 | bytes 30336000 | tf_op jit(solution)/shard_map/dot_general | solution.py:37
  660.5 5.0 psum.15
  666.9 26.4 %all-reduce.2.cloned.1.call-done = f32[2,8,32,64]{3,2,1,0:T(8,128)} async-done(((f32[2,8,32,64]{3,2,1,0:T(8,128)}), f32[2,8,32,64]{3,2,1,0:T(8,128)}) %all-reduce.2.cloned.1.call-update) | async-done | bytes 131088 | tf_op jit(solution)/shard_map/psum | solution.py:119
  694.7 13.9 %all_gather.15 = bf16[2,32,2048]{2,1,0:T(8,128)(2,1)S(1)} all-gather(bf16[2,8,2048]{2,1,0:T(8,128)(2,1)S(1)} %reshape.222), channel_id=1, replica_groups=mesh['grp'=2,'kpt'=4,'pw'=2,'band'=2] {'kpt'}, dimensions={1}, use_global_device_ids=true | all-gather | bytes 327680 | tf_op jit(solution)/shard_map/all_gather | solution.py:153
  (97 shorter events, 39.5 us)
Async XLA Ops:
  6.5 238.9 %copy-start = (bf16[2,8,64]{2,1,0:T(8,128)(2,1)S(1)}, bf16[2,8,64]{2,1,0:T(8,128)(2,1)}, u32[]{:S(2)}) copy-start(bf16[2,8,64]{2,1,0:T(8,128)(2,1)} %param.20) | copy-start | bytes 6148
  6.5 207.3 %all-gather.4.cloned.1.call-start = ((), (), s32[]{:S(2)}) async-start(), calls=%async_computation.3 | async-start | bytes 24576000 | tf_op jit(solution)/shard_map/all_gather | solution.py:88
  16.5 481.0 %all-gather.6.cloned.1.call-start = ((), (), s32[]{:S(2)}) async-start(), calls=%async_computation.4 | async-start | bytes 12582912 | tf_op jit(solution)/shard_map/all_gather | solution.py:108
  233.6 389.7 %all-gather.8.cloned.1.call-start = ((), (), s32[]{:S(2)}) async-start(), calls=%async_computation.5 | async-start | bytes 20480000 | tf_op jit(solution)/shard_map/all_gather | solution.py:115
  238.2 6.5 copy-start.10
  246.7 14.3 %all-to-all-start.1 = ((bf16[4,2,128]{2,1,0:T(2,128)(2,1)}), bf16[4,2,128]{2,1,0:T(2,128)(2,1)S(1)}, u32[]{:S(2)}, u32[]{:S(2)}) async-start(bf16[4,2,128]{2,1,0:T(2,128)(2,1)} %reshape.297), calls=%async_computation.2 | async-start | bytes 4096 | tf_op jit(solution)/shard_map/all_to_all | solution.py:81
  261.0 5.4 copy-start.7
  261.0 5.4 copy-start.11
  261.0 5.5 copy-start.8
  261.0 5.6 copy-start.9
  261.0 6.4 copy-start.6
  261.0 220.4 %all-to-all-start = ((bf16[2,8,64,2000]{3,2,0,1:T(8,128)(2,1)}), bf16[2,8,64,2000]{3,2,0,1:T(8,128)(2,1)}, u32[]{:S(2)}, u32[]{:S(2)}) async-start(bf16[2,8,64,2000]{3,2,0,1:T(8,128)(2,1)} %select_bitcast_fusion), calls=%async_computation | async-start | bytes 8388608 | tf_op jit(solution)/shard_map/all_to_all | solution.py:80
  266.2 400.4 %reduce-scatter.2.cloned.1.call-start = ((), (), s32[]{:S(2)}) async-start(), calls=%async_computation.6 | async-start | bytes 786432 | tf_op jit(solution)/shard_map/reduce_scatter | solution.py:118
  288.4 9.3 %copy-start.5 = (bf16[2,4000]{1,0:T(2,128)(2,1)S(1)}, bf16[2,4000]{1,0:T(2,128)(2,1)}, u32[]{:S(2)}) copy-start(bf16[2,4000]{1,0:T(2,128)(2,1)} %param.22) | copy-start | bytes 48004
  297.7 2.9 copy-start.2
  491.1 2.7 copy-start.13
  493.8 2.8 copy-start.3
  513.4 5.1 copy-start.4
  655.8 37.5 %copy-start.12 = (s32[64]{0:T(128)S(1)}, s32[64]{0:T(128)}, u32[]{:S(2)}) copy-start(s32[64]{0:T(128)} %param.26) | copy-start | bytes 772
  655.8 53.8 %copy-start.1 = (bf16[2,8,64]{2,1,0:T(8,128)(2,1)S(1)}, bf16[2,8,64]{2,1,0:T(8,128)(2,1)}, u32[]{:S(2)}) copy-start(bf16[2,8,64]{2,1,0:T(8,128)(2,1)} %param.20) | copy-start | bytes 6148
  660.4 32.8 %all-reduce.2.cloned.1.call-start = ((), (), s32[]{:S(2)}) async-start(), calls=%async_computation.7 | async-start | bytes 524288 | tf_op jit(solution)/shard_map/psum | solution.py:119
Sparse Core Ops, SparseCore 0:
  16.6 197.1 all-gather.3
  233.7 19.8 all-gather.5
  255.2 368.0 all-gather.7
  660.5 6.0 reduce-scatter.1
  668.9 24.3 all-reduce.1
where the time goes:
time: 718 us; the launch traced here: 716 us
  waiting for transfers between devices  495 us (69%)
  local copies, waits for them, and re-layouts  116 us (16%)
  matrix products  46.7 us (7%)
  blocking collectives  19 us (3%)
  other arithmetic  15.7 us (2%)
  between operations  13.5 us (2%)
  starting transfers between devices  10.1 us (1%)
    all_gather x1, waiting for transfers between devices, on_device(): conduction_all = lax.all_gather(conduction, 'pw', axis=3, tiled=True)  197 us
    all_to_all x1, waiting for transfers between devices, on_device(): lax.all_to_all(outgoing, 'kpt', split_axis=1, concat_axis=1, tiled=True)  176 us
    all_gather x1, waiting for transfers between devices, on_device(): lax.all_gather(screen_part, 'kpt', axis=1, tiled=True)  94 us
    dot_general x1, matrix products, row_folder(): return jnp.dot(columns, stacked, preferred_element_type=jnp.float32)  27.7 us
    psum x1, waiting for transfers between devices, on_device(): block, valence_wing = lax.psum((block, valence_wing), 'pw')  26.4 us
    squeeze x2, local copies, waits for them, and re-layouts, on_device(): conduction_all[1]  21.3 us
    all_gather x1, local copies, waits for them, and re-layouts, on_device(): conduction_all = lax.all_gather(conduction, 'pw', axis=3, tiled=True)  19.7 us
    unnamed x32, local copies, waits for them, and re-layouts  17.2 us
  transfers between devices with their start and end apart: 7, of which 5 were waited for; matrix products, arithmetic and copies ran while one was open for 15% of the time, Pallas kernels for 0%

commit v1 on v0

v1 whole, which is shorter than its diff:
```python
import jax
import jax.numpy as jnp
from jax import lax
from jax.experimental import pallas as pl
from jax.experimental.pallas import tpu as pltpu
from jax.sharding import PartitionSpec as P

highest = lax.Precision.HIGHEST
f32 = jnp.float32
bf16 = jnp.bfloat16
HEAD_PARTS = 3
VMEM_BYTES = 48 * 1024 * 1024


def round_up(value, step):
    return -(-value // step) * step


def shifted(x, name, shift):
    count = lax.axis_size(name)
    pairs = [(source, (source + shift) % count) for source in range(count)]
    return lax.ppermute(x, name, pairs)


def share(x, name):
    return [x] + [shifted(x, name, shift) for shift in range(1, lax.axis_size(name))]


def deal(x, name):
    count = lax.axis_size(name)
    me = lax.axis_index(name)
    pieces = []
    for shift in range(count):
        piece = lax.dynamic_index_in_dim(x, (me + shift) % count, 0, keepdims=False)
        pieces.append(shifted(piece, name, shift) if shift else piece)
    return pieces


def valence_columns(valence, valence_head, selector, core, width, last):
    parts, points, pairs, columns = valence.shape
    head_at = columns - last * width

    def kernel(core_ref, valence_ref, head_ref, selector_ref, out_ref):
        column = lax.broadcasted_iota(jnp.int32, (pairs, width), 1)
        at_last = core_ref[0] == last
        limit = jnp.where(at_last, head_at, width)
        head_column = jnp.where(at_last, head_at, width)
        for point in range(points):
            rows = valence_ref[0, point].astype(f32)
            head = jnp.broadcast_to(head_ref[0, point].astype(f32), (pairs, width))
            rows = jnp.where(column < limit, rows, 0.0)
            rows = jnp.where(column == head_column, head, rows)
            moved = jnp.dot(selector_ref[...], rows.astype(bf16), preferred_element_type=f32)
            out_ref[0, point] = moved.astype(bf16)

    return pl.pallas_call(
        kernel,
        out_shape=jax.ShapeDtypeStruct((parts, points, pairs, width), bf16),
        grid_spec=pltpu.PrefetchScalarGridSpec(
            num_scalar_prefetch=1,
            grid=(parts,),
            in_specs=[
                pl.BlockSpec((1, points, pairs, width), lambda x, core: (x, 0, 0, core[0])),
                pl.BlockSpec((1, points, pairs, 1), lambda x, core: (x, 0, 0, 0)),
                pl.BlockSpec((pairs, pairs), lambda x, core: (0, 0)),
            ],
            out_specs=pl.BlockSpec((1, points, pairs, width), lambda x, core: (x, 0, 0, 0)),
        ),
        compiler_params=pltpu.CompilerParams(vmem_limit_bytes=VMEM_BYTES),
        name="valence_columns",
    )(core.reshape(1), valence, valence_head[..., None], selector)


def screen_product(places, pieces, right, per_index, half):
    _, deep, width = right.shape
    planes = deep // 2
    rows = per_index * half
    count = len(pieces)
    bands = 2
    pw_count = count // bands
    points = pw_count * per_index
    tile = min(256, width)

    def kernel(place_ref, *refs):
        piece_refs, right_ref, out_ref, left_ref = refs[:count], refs[count], refs[count + 1], refs[count + 2]

        @pl.when((pl.program_id(0) == 0) & (pl.program_id(1) == 0))
        def _():
            for index in range(count):
                start = pl.multiple_of(place_ref[index] * rows, rows)
                left_ref[pl.ds(start, rows), 0:planes] = piece_refs[index][0]
                left_ref[pl.ds(start, rows), planes:deep] = piece_refs[index][1]

        total = jnp.dot(left_ref[...], right_ref[0], preferred_element_type=f32).astype(bf16)
        for pw in range(pw_count):
            for band in range(bands):
                for point in range(per_index):
                    start = (pw * bands + band) * rows + point * half
                    out_ref[pw * per_index + point, band, 0] = total[start : start + half]

    whole = pl.BlockSpec((2, rows, planes), lambda x, n, place: (0, 0, 0))
    return pl.pallas_call(
        kernel,
        out_shape=jax.ShapeDtypeStruct((points, bands, 2, half, width), bf16),
        grid_spec=pltpu.PrefetchScalarGridSpec(
            num_scalar_prefetch=1,
            grid=(2, width // tile),
            in_specs=[whole] * count + [pl.BlockSpec((1, deep, tile), lambda x, n, place: (x, 0, n))],
            out_specs=pl.BlockSpec((points, bands, 1, half, tile), lambda x, n, place: (0, 0, x, 0, n)),
            scratch_shapes=[pltpu.VMEM((count * rows, deep), bf16)],
        ),
        compiler_params=pltpu.CompilerParams(vmem_limit_bytes=VMEM_BYTES),
        cost_estimate=pl.CostEstimate(
            flops=2 * count * rows * deep * width * 2,
            bytes_accessed=2 * (2 * deep * width + 2 * points * bands * half * width),
            transcendentals=0,
        ),
        name="screen_product",
    )(places, *pieces, right)


def contract(rows, product, gathered):
    points, bands, _, half, width = product.shape
    _, _, stored, pairs, _ = gathered.shape
    group = 4 if points % 4 == 0 else 1

    def kernel(row_ref, product_ref, *refs):
        out_ref = refs[group]
        lane = lax.broadcasted_iota(jnp.int32, (half, 2 * pairs), 1)
        for index in range(group):
            left = product_ref[index].reshape(bands * 2 * half, width)
            right = refs[index][0, :, 0].reshape(2 * pairs, width)
            square = lax.dot_general(left, right, (((1,), (1,)), ((), ())), preferred_element_type=f32)
            for band in range(bands):
                first = square[2 * band * half : (2 * band + 1) * half]
                second = square[(2 * band + 1) * half : (2 * band + 2) * half]
                turned = pltpu.roll(second, pairs, 1)
                total = first + jnp.where(lane < pairs, -turned, turned)
                out_ref[index, band * half : (band + 1) * half, :] = total

    def valence_spec(index):
        return pl.BlockSpec(
            (1, 2, 1, pairs, width),
            lambda step, row: (row[step * group + index] // stored, 0, row[step * group + index] % stored, 0, 0),
        )

    return pl.pallas_call(
        kernel,
        out_shape=jax.ShapeDtypeStruct((points, bands * half, 2 * pairs), f32),
        grid_spec=pltpu.PrefetchScalarGridSpec(
            num_scalar_prefetch=1,
            grid=(points // group,),
            in_specs=[pl.BlockSpec((group, bands, 2, half, width), lambda step, row: (step, 0, 0, 0, 0))]
            + [valence_spec(index) for index in range(group)],
            out_specs=pl.BlockSpec((group, bands * half, 2 * pairs), lambda step, row: (step, 0, 0)),
        ),
        compiler_params=pltpu.CompilerParams(vmem_limit_bytes=VMEM_BYTES),
        cost_estimate=pl.CostEstimate(
            flops=2 * points * bands * 2 * half * 2 * pairs * width,
            bytes_accessed=2 * points * width * (bands * 2 * half + 2 * pairs),
            transcendentals=0,
        ),
        name="contract",
    )(rows, product, *([gathered] * group))


def on_device(
    conduction,
    conduction_head,
    valence,
    valence_head,
    screened,
    wing_column,
    wing_row,
    head_value,
    partner,
    pair_select,
    neighbors,
    weights,
    counts,
):
    points = conduction.shape[1]
    half = conduction.shape[2]
    pairs = valence.shape[2]
    block, columns = screened.shape[1], screened.shape[2]
    kpt_count, pw_count, band_count = lax.axis_size("kpt"), lax.axis_size("pw"), lax.axis_size("band")
    kpt, pw, band = lax.axis_index("kpt"), lax.axis_index("pw"), lax.axis_index("band")
    per_index = points // pw_count
    rows = per_index * half
    blocks_here = columns // block
    deep = round_up(block + HEAD_PARTS, 128)
    width = round_up(-(-(columns + 1) // band_count), 128)
    last = band_count - 1
    head_at = columns - last * width

    selector = (pair_select[:, None] == jnp.arange(pairs)[None, :]).astype(bf16)
    own_valence = valence_columns(valence, valence_head, selector, band, width, last)
    gathered = lax.all_gather(own_valence, "kpt", axis=0)

    plane = jnp.arange(deep)
    is_head = (plane >= block) & (plane < block + HEAD_PARTS)
    cut = []
    for index in range(blocks_here):
        padded = jnp.pad(
            conduction[..., index * block : (index + 1) * block], ((0, 0), (0, 0), (0, 0), (0, deep - block))
        )
        cut.append(jnp.where(is_head, conduction_head[..., None], padded))
    cut = jnp.stack(cut).reshape(blocks_here, 2, pw_count, rows, deep)
    dealt = jnp.stack(deal(jnp.moveaxis(cut, 2, 0), "pw"))

    def block_for(target):
        owner = target // blocks_here
        return lax.dynamic_index_in_dim(
            lax.dynamic_index_in_dim(dealt, (pw - owner) % pw_count, 0, keepdims=False),
            target % blocks_here,
            0,
            keepdims=False,
        )

    screen = jnp.pad(screened, ((0, 0), (0, deep - block), (0, band_count * width - columns)))
    screen = lax.dynamic_slice_in_dim(screen, band * width, width, 2)
    row_part = jnp.pad(wing_row, ((0, 0), (0, band_count * width - columns)))
    row_part = lax.dynamic_slice_in_dim(row_part, band * width, width, 1)
    first_kpt = kpt == 0
    row_part = jnp.where(first_kpt, row_part, 0)
    corner = []
    rest = head_value
    for _ in range(HEAD_PARTS):
        part = lax.reduce_precision(rest, 8, 7)
        corner.append(jnp.where(first_kpt, part, 0.0))
        rest = rest - part
    corner = jnp.stack(corner, axis=1).astype(bf16)
    column_part = jnp.concatenate(
        [lax.dynamic_slice_in_dim(wing_column, kpt * block, block, 1), corner], axis=1
    )
    column_part = jnp.pad(column_part, ((0, 0), (0, deep - block - HEAD_PARTS)))
    has_column = (pw == 0) & (band == last)
    screen = jnp.where(plane[None, :, None] == block, row_part[:, None, :], screen)
    screen = jnp.where(
        (jnp.arange(width)[None, None, :] == head_at) & has_column, column_part[:, :, None], screen
    )
    right = jnp.stack(
        [
            jnp.concatenate([screen[0], screen[1]], axis=0),
            jnp.concatenate([screen[1], -screen[0]], axis=0),
        ]
    )

    places = jnp.stack(
        [
            ((pw - pw_shift) % pw_count) * band_count + (band - band_shift) % band_count
            for pw_shift in range(pw_count)
            for band_shift in range(band_count)
        ]
    ).astype(jnp.int32)

    live = jnp.where(jnp.arange(neighbors.shape[1])[None, :] < counts[:, None], weights, 0.0)
    all_points = kpt_count * points
    match = neighbors[:, :, None] == jnp.arange(all_points)[None, None, :]
    stencil = jnp.sum(jnp.where(match, live[:, :, None], 0.0), axis=1)

    products = []
    for shift in range(kpt_count):
        piece = block_for((kpt + shift) % kpt_count)
        if shift:
            piece = shifted(piece, "kpt", shift)
        pieces = [own for across in share(piece, "pw") for own in share(across, "band")]
        products.append(screen_product(places, pieces, right, per_index, half))

    totals = []
    stencils = []
    for shift in range(kpt_count):
        source = (kpt - shift) % kpt_count
        row_ids = lax.dynamic_slice_in_dim(partner, source * points, points, 0)
        totals.append(contract(row_ids, products[shift], gathered))
        stencils.append(lax.dynamic_slice_in_dim(stencil, source * points, points, 1))
    body = jnp.concatenate(totals, axis=0)
    stencil = jnp.concatenate(stencils, axis=1)

    lanes = 2 * pairs
    body = body.reshape(all_points, band_count, half, lanes)
    body = sum(deal(jnp.moveaxis(body, 1, 0), "band"))
    kept = half // pw_count
    body = body.reshape(all_points, pw_count, kept, lanes)
    body = sum(deal(jnp.moveaxis(body, 1, 0), "pw"))
    fine = jnp.dot(stencil, body.reshape(all_points, kept * lanes), precision=highest)
    fine_here = neighbors.shape[0] // kpt_count
    fine = fine.astype(bf16).reshape(kpt_count, fine_here, kept, lanes)
    fine = sum(piece.astype(f32) for piece in deal(fine, "kpt"))
    fine = lax.all_gather(fine, "pw", axis=0)
    fine = fine.reshape(pw_count, fine_here, kept, 2, pairs)
    return jnp.transpose(fine, (3, 1, 0, 2, 4)).reshape(2, fine_here, half * pairs)


def solution(mesh):
    return jax.shard_map(
        on_device,
        mesh=mesh,
        in_specs=(
            P("grp", "kpt", "band", "pw"),
            P("grp", "kpt", "band"),
            P("grp", "kpt", None, "pw"),
            P("grp", "kpt", None),
            P("grp", "kpt", "pw"),
            P("grp", None),
            P("grp", "pw"),
            P("grp"),
            P("grp"),
            P(),
            P(),
            P(),
            P(),
        ),
        out_specs=P("grp", "kpt", "band"),
        check_vma=False,
    )
```

time: 718 us -> 255 us (0.36)
  waiting for transfers between devices: 495 us -> 125 us
  local copies, waits for them, and re-layouts: 116 us -> 12.8 us
  Pallas kernels: 0 us -> 55 us
  matrix products: 46.7 us -> 0.63 us
  blocking collectives: 19 us -> 5.64 us
  starting transfers between devices: 10.1 us -> 21.2 us
    all_gather x3 -> x1, waiting for transfers between devices: 291 us -> 40.4 us  [on_device(): gathered = lax.all_gather(own_valence, 'kpt', axis=0)]
    all_to_all x2 -> x0, waiting for transfers between devices: 176 us -> none  [the longest x1 176 us: on_device(): lax.all_to_all(outgoing, 'kpt', split_axis=1, concat_axis=1, tiled=True)]
    ppermute x0 -> x21, waiting for transfers between devices: none -> 85 us  [shifted(): return lax.ppermute(x, name, pairs)]
    pallas_call x0 -> x9, Pallas kernels: none -> 55 us  [the longest x4 39.4 us: screen_product(): pl.pallas_call(kernel, out_shape=jax.ShapeDtypeStruct((points, bands, 2,...]
    dot_general x15 -> x1, matrix products: 46.7 us -> 0.63 us  [on_device(): jnp.dot(stencil, body.reshape(all_points, kept * lanes), precision=highest)]
    squeeze x3 -> x4, local copies, waits for them, and re-layouts: 29.6 us -> 0.54 us  [the longest x1 0.44 us: on_device(): screen[0]]
    psum x1 -> x0, waiting for transfers between devices: 26.4 us -> none  [on_device(): block, valence_wing = lax.psum((block, valence_wing), 'pw')]
    ppermute x0 -> x21, starting transfers between devices: none -> 21.2 us  [shifted(): return lax.ppermute(x, name, pairs)]
  transfers between devices with their start and end apart: 7 -> 22, of which waited for: 5 -> 8; matrix products, arithmetic and copies ran while one was open for 15% -> 8% of each run, Pallas kernels for 0% -> 16%
where the time goes in v1:
time: 255 us; the launch traced here: 254 us
  waiting for transfers between devices  125 us (49%)
  Pallas kernels  55 us (22%)
  starting transfers between devices  21.2 us (8%)
  other arithmetic  19.6 us (8%)
  between operations  13.9 us (5%)
  local copies, waits for them, and re-layouts  12.8 us (5%)
  blocking collectives  5.64 us (2%)
    ppermute x21, waiting for transfers between devices, shifted(): return lax.ppermute(x, name, pairs)  85 us
    all_gather x1, waiting for transfers between devices, on_device(): gathered = lax.all_gather(own_valence, 'kpt', axis=0)  40.4 us
    pallas_call x4, Pallas kernels, screen_product(): pl.pallas_call(kernel, out_shape=jax.ShapeDtypeStruct((points, bands, 2,...  39.4 us
    ppermute x21, starting transfers between devices, shifted(): return lax.ppermute(x, name, pairs)  21.2 us
    pallas_call x4, Pallas kernels, contract(): pl.pallas_call(kernel, out_shape=jax.ShapeDtypeStruct((points, bands * ha...  12.2 us
    another operation x2, other arithmetic, on_device(): jnp.stack([jnp.concatenate([screen[0], screen[1]], axis=0), jnp.concatena...  11.5 us
    unnamed x47, local copies, waits for them, and re-layouts  8.87 us
    all_gather x1, blocking collectives, on_device(): fine = lax.all_gather(fine, 'pw', axis=0)  5.64 us
  transfers between devices with their start and end apart: 22, of which 8 were waited for; matrix products, arithmetic and copies ran while one was open for 8% of the time, Pallas kernels for 16%

profile of v1, /device:TPU:0, one launch (start us, length us, event | category | flops | bytes accessed | tf_op | source)
XLA Modules:
  0.0 254.2 jit_solution(8703417348773515017)
XLA Ops:
  8.2 3.4 %valence_columns.1 = bf16[2,8,64,1024]{3,2,1,0:T(8,128)(2,1)} custom-call(s32[1]{0:T(128)} %bitcast.17.core_ref, bf16[2,8,64,2000]{3,2,1,0:T(8,128)(2,1)} %valence_ref.1, bf16[2,8,64,1]{3,2,1,0:T(8,128)(2,1)S(1)} %copy.37.head_ref, bf16[64,64]{1,0:T(8,128)(2,1)S(1)} %fusion.19.selector_ref), custom_call_target="tpu_custom_call" | custom-call | tf_op jit(solution)/shard_map/valence_columns/pallas_call | solution.py:56
  13.1 3.0 %collective-permute-start = (bf16[2,2,128,1024]{3,2,1,0:T(8,128)(2,1)S(1)}, bf16[2,2,128,1024]{3,2,1,0:T(8,128)(2,1)}, u32[]{:S(2)}, u32[]{:S(2)}) collective-permute-start(bf16[2,2,128,1024]{3,2,1,0:T(8,128)(2,1)S(1)} %get-tuple-element.13), channel_id=1, source_target_pairs={{0,2},{2,0},{1,3},{3,1},{4,6},{6,4},{5,7},{7,5},{8,10},{10,8},{9,1... | collective-permute-start | bytes 3145736 | tf_op jit(solution)/shard_map/ppermute | solution.py:22
  16.7 3.3 %fusion.1 = bf16[2,1024,1024]{2,1,0:T(8,128)(2,1)S(1)} fusion(s32[]{:T(128)S(6)} %select_n.299, bf16[2,1000,2000]{2,1,0:T(8,128)(2,1)} %param.17, pred[1024]{0:T(1024)(128)(4,1)S(1)} %get-tuple-element.31, pred[1024]{0:T(1024)(128)(4,1)S(1)} %get-tuple-element.32, bf16[2,1024]{1,0:T(2,128)(2,1)S(1)} %broadcast_select_fusion, bf16[2,1024]{1,0:T(2,128)(2,1)S(1)} %fusion.33), kind=kLoop, calls=%fused_computation.3 | loop fusion | flops 4194304 | bytes 12204548 | tf_op jit(solution)/shard_map/jit(_where)/select_n | solution.py:239
  20.0 19.4 %collective-permute-done = bf16[2,2,128,1024]{3,2,1,0:T(8,128)(2,1)} collective-permute-done((bf16[2,2,128,1024]{3,2,1,0:T(8,128)(2,1)S(1)}, bf16[2,2,128,1024]{3,2,1,0:T(8,128)(2,1)}, u32[]{:S(2)}, u32[]{:S(2)}) %collective-permute-start) | collective-permute-done | bytes 1048608 | tf_op jit(solution)/shard_map/ppermute | solution.py:22
  39.4 2.8 %fusion.10 = (bf16[2,128,1024]{2,1,0:T(8,128)(2,1)S(1)}, bf16[2,128,1024]{2,1,0:T(8,128)(2,1)S(1)}, bf16[2,128,1024]{2,1,0:T(8,128)(2,1)}, bf16[2,128,1024]{2,1,0:T(8,128)(2,1)S(1)}) fusion(s32[]{:T(128)S(6)} %select_n.289, s32[]{:T(128)S(6)} %select_n.292, bf16[1,2,2,128,1024]{4,3,2,1,0:T(8,128)(2,1)S(1)} %get-tuple-element.14, ...), kind=kLoop, calls=%fused_computation.32 | loop fusion | flops 1048576 | bytes 4194336 | tf_op jit(solution)/shard_map/jit(dynamic_index_in_dim)/squeeze | solution.py:213
  46.0 2.6 %collective-permute-start.8 = (bf16[2,128,1024]{2,1,0:T(8,128)(2,1)}, bf16[2,128,1024]{2,1,0:T(8,128)(2,1)}, u32[]{:S(2)}, u32[]{:S(2)}) collective-permute-start(bf16[2,128,1024]{2,1,0:T(8,128)(2,1)} %get-tuple-element.9), channel_id=1, source_target_pairs={{0,8},{4,12},{8,0},{12,4},{1,9},{5,13},{9,1},{13,5},{2,10},{6,14},... | collective-permute-start | bytes 1572872 | tf_op jit(solution)/shard_map/ppermute | solution.py:22
  50.4 19.6 %collective-permute-done.4.refs_0_ = bf16[2,128,1024]{2,1,0:T(8,128)(2,1)S(1)} collective-permute-done((bf16[2,128,1024]{2,1,0:T(8,128)(2,1)S(1)}, bf16[2,128,1024]{2,1,0:T(8,128)(2,1)S(1)}, u32[]{:S(2)}, u32[]{:S(2)}) %collective-permute-start.4) | collective-permute-done | bytes 524320 | tf_op jit(solution)/shard_map/ppermute | solution.py:22
  71.7 3.9 %maximum_bitcast_fusion = (bf16[1,2048,1024]{2,1,0:T(8,128)(2,1)}, bf16[1,2048,1024]{2,1,0:T(8,128)(2,1)}) fusion(bf16[1024,1024]{1,0:T(8,128)(2,1)S(1)} %get-tuple-element.6, bf16[1024,1024]{1,0:T(8,128)(2,1)S(1)} %get-tuple-element.5, bf16[1024,1024]{1,0:T(8,128)(2,1)S(1)} %fusion.43), kind=kLoop, calls=%fused_computation.4 | loop fusion | flops 16777216 | bytes 14680064 | tf_op jit(solution)/shard_map/stack | solution.py:242
  75.7 33.2 %collective-permute-done.8.refs_0_ = bf16[2,128,1024]{2,1,0:T(8,128)(2,1)} collective-permute-done((bf16[2,128,1024]{2,1,0:T(8,128)(2,1)}, bf16[2,128,1024]{2,1,0:T(8,128)(2,1)}, u32[]{:S(2)}, u32[]{:S(2)}) %collective-permute-start.8) | collective-permute-done | bytes 524320 | tf_op jit(solution)/shard_map/ppermute | solution.py:22
  109.7 7.5 %pad_maximum_fusion.refs_4_ = bf16[2,2048,1024]{2,1,0:T(8,128)(2,1)} fusion(bf16[1,2048,1024]{2,1,0:T(8,128)(2,1)} %get-tuple-element.12, bf16[1,2048,1024]{2,1,0:T(8,128)(2,1)} %get-tuple-element.11), kind=kLoop, calls=%fused_computation | loop fusion | flops 4194304 | bytes 16777216 | tf_op jit(solution)/shard_map/stack | solution.py:242
  124.2 9.5 %screen_product.4.product_ref = bf16[8,2,2,32,1024]{4,3,2,1,0:T(8,128)(2,1)S(1)} custom-call(s32[4]{0:T(128)S(1)} %pad_add_fusion.place_ref, bf16[2,128,1024]{2,1,0:T(8,128)(2,1)S(1)} %get-tuple-element.7.refs_0_, bf16[2,128,1024]{2,1,0:T(8,128)(2,1)S(1)} %copy-done.11, bf16[2,128,1024]{2,1,0:T(8,128)(2,1)S(1)} %copy-done.9, ...), custom_call_target="tpu_custom_call" | custom-call | flops 4294967296 | bytes 10485760 | tf_op jit(solution)/shard_map/screen_product/pallas_call | solution.py:102
  134.3 10.1 %screen_product.5.product_ref = bf16[8,2,2,32,1024]{4,3,2,1,0:T(8,128)(2,1)S(1)} custom-call(s32[4]{0:T(128)S(1)} %pad_add_fusion.place_ref, bf16[2,128,1024]{2,1,0:T(8,128)(2,1)S(1)} %collective-permute-done.4.refs_0_, bf16[2,128,1024]{2,1,0:T(8,128)(2,1)} %collective-permute-done.5.refs_1_, bf16[2,128,1024]{2,1,0:T(8,128)(2,1)} %collective-permute-done.6.refs_2_, ...), custom_call_target="tpu_custom_call" | custom-call | flops 4294967296 | bytes 10485760 | tf_op jit(solution)/shard_map/screen_product/pallas_call | solution.py:102
  145.7 9.9 %screen_product.6.product_ref = bf16[8,2,2,32,1024]{4,3,2,1,0:T(8,128)(2,1)S(1)} custom-call(s32[4]{0:T(128)S(1)} %pad_add_fusion.place_ref, bf16[2,128,1024]{2,1,0:T(8,128)(2,1)} %collective-permute-done.8.refs_0_, bf16[2,128,1024]{2,1,0:T(8,128)(2,1)S(1)} %collective-permute-done.9.refs_1_, bf16[2,128,1024]{2,1,0:T(8,128)(2,1)} %collective-permute-done.10.refs_2_, ...), custom_call_target="tpu_custom_call" | custom-call | flops 4294967296 | bytes 10485760 | tf_op jit(solution)/shard_map/screen_product/pallas_call | solution.py:102
  157.0 9.9 %screen_product.7.product_ref = bf16[8,2,2,32,1024]{4,3,2,1,0:T(8,128)(2,1)S(1)} custom-call(s32[4]{0:T(128)S(1)} %pad_add_fusion.place_ref, bf16[2,128,1024]{2,1,0:T(8,128)(2,1)} %collective-permute-done.12.refs_0_, bf16[2,128,1024]{2,1,0:T(8,128)(2,1)S(1)} %collective-permute-done.13.refs_1_, bf16[2,128,1024]{2,1,0:T(8,128)(2,1)} %collective-permute-done.14.refs_2_, ...), custom_call_target="tpu_custom_call" | custom-call | flops 4294967296 | bytes 10485760 | tf_op jit(solution)/shard_map/screen_product/pallas_call | solution.py:102
  168.3 40.4 %all-gather.4.cloned.1.call-done = bf16[8,8,64,1024]{3,2,1,0:T(8,128)(2,1)} async-done(((bf16[2,8,64,1024]{3,2,1,0:T(8,128)(2,1)}), bf16[8,8,64,1024]{3,2,1,0:T(8,128)(2,1)}) %all-gather.4.cloned.1.call-update) | async-done | bytes 8388624 | tf_op jit(solution)/shard_map/all_gather | solution.py:198
  208.7 3.0 %contract.4 = f32[8,64,128]{2,1,0:T(8,128)S(1)} custom-call(s32[8]{0:T(128)S(1)} %get-tuple-element.24.row_ref, bf16[8,2,2,32,1024]{4,3,2,1,0:T(8,128)(2,1)S(1)} %screen_product.4.product_ref, bf16[4,2,8,64,1024]{4,3,2,1,0:T(8,128)(2,1)} %bitcast.68, bf16[4,2,8,64,1024]{4,3,2,1,0:T(8,128)(2,1)} %bitcast.69, bf16[4,2,8,64,1024]{4,3,2,1,0:T(8,128)(2,1)} %bitcast.70, ...), custom_call_target="tpu_custom_call" | custom-call | flops 268435456 | bytes 4194304 | tf_op jit(solution)/shard_map/contract/pallas_call | solution.py:147
  211.8 3.0 %contract.5 = f32[8,64,128]{2,1,0:T(8,128)S(1)} custom-call(s32[8]{0:T(128)S(1)} %get-tuple-element.25.row_ref, bf16[8,2,2,32,1024]{4,3,2,1,0:T(8,128)(2,1)S(1)} %copy-done.3, bf16[4,2,8,64,1024]{4,3,2,1,0:T(8,128)(2,1)} %bitcast.72, bf16[4,2,8,64,1024]{4,3,2,1,0:T(8,128)(2,1)} %bitcast.73, bf16[4,2,8,64,1024]{4,3,2,1,0:T(8,128)(2,1)} %bitcast.74, ...), custom_call_target="tpu_custom_call" | custom-call | flops 268435456 | bytes 4194304 | tf_op jit(solution)/shard_map/contract/pallas_call | solution.py:147
  214.8 3.1 %contract.6 = f32[8,64,128]{2,1,0:T(8,128)S(1)} custom-call(s32[8]{0:T(128)S(1)} %get-tuple-element.27.row_ref, bf16[8,2,2,32,1024]{4,3,2,1,0:T(8,128)(2,1)S(1)} %copy-done.5, bf16[4,2,8,64,1024]{4,3,2,1,0:T(8,128)(2,1)} %bitcast.76, bf16[4,2,8,64,1024]{4,3,2,1,0:T(8,128)(2,1)} %bitcast.77, bf16[4,2,8,64,1024]{4,3,2,1,0:T(8,128)(2,1)} %bitcast.78, ...), custom_call_target="tpu_custom_call" | custom-call | flops 268435456 | bytes 4194304 | tf_op jit(solution)/shard_map/contract/pallas_call | solution.py:147
  217.9 3.0 %contract.7 = f32[8,64,128]{2,1,0:T(8,128)S(1)} custom-call(s32[8]{0:T(128)S(1)} %get-tuple-element.26.row_ref, bf16[8,2,2,32,1024]{4,3,2,1,0:T(8,128)(2,1)S(1)} %copy-done.7, bf16[4,2,8,64,1024]{4,3,2,1,0:T(8,128)(2,1)} %bitcast.80, bf16[4,2,8,64,1024]{4,3,2,1,0:T(8,128)(2,1)} %bitcast.81, bf16[4,2,8,64,1024]{4,3,2,1,0:T(8,128)(2,1)} %bitcast.82, ...), custom_call_target="tpu_custom_call" | custom-call | flops 268435456 | bytes 4194304 | tf_op jit(solution)/shard_map/contract/pallas_call | solution.py:147
  224.9 6.8 %collective-permute-done.17 = f32[32,16,128]{2,1,0:T(8,128)S(1)} collective-permute-done((f32[32,16,128]{2,1,0:T(8,128)S(1)}, f32[32,16,128]{2,1,0:T(8,128)S(1)}, u32[]{:S(2)}, u32[]{:S(2)}) %collective-permute-start.17) | collective-permute-done | bytes 262176 | tf_op jit(solution)/shard_map/ppermute | solution.py:22
  232.5 1.9 collective-permute-start.19
  234.4 1.9 collective-permute-start.20
  236.3 2.7 %collective-permute-done.18 = bf16[16,16,128]{2,1,0:T(8,128)(2,1)S(1)} collective-permute-done((bf16[16,16,128]{2,1,0:T(8,128)(2,1)S(1)}, bf16[16,16,128]{2,1,0:T(8,128)(2,1)S(1)}, u32[]{:S(2)}, u32[]{:S(2)}) %collective-permute-start.18) | collective-permute-done | bytes 65568 | tf_op jit(solution)/shard_map/ppermute | solution.py:22
  240.4 5.6 %all-gather.1 = f32[32,16,128]{2,1,0:T(8,128)S(1)} all-gather(f32[16,16,128]{2,1,0:T(8,128)S(1)} %fusion.18), channel_id=3, replica_groups=mesh['grp'=2,'kpt'=4,'pw'=2,'band'=2] {'pw'}, dimensions={0}, use_global_device_ids=true | all-gather | bytes 393216 | tf_op jit(solution)/shard_map/all_gather | solution.py:290
  (114 shorter events, 30.4 us)
Async XLA Ops:
  6.5 202.2 %all-gather.4.cloned.1.call-start = ((), (), s32[]{:S(2)}) async-start(), calls=%async_computation | async-start | bytes 10485760 | tf_op jit(solution)/shard_map/all_gather | solution.py:198
  13.1 26.3 %collective-permute-start = (bf16[2,2,128,1024]{3,2,1,0:T(8,128)(2,1)S(1)}, bf16[2,2,128,1024]{3,2,1,0:T(8,128)(2,1)}, u32[]{:S(2)}, u32[]{:S(2)}) collective-permute-start(bf16[2,2,128,1024]{3,2,1,0:T(8,128)(2,1)S(1)} %get-tuple-element.13), channel_id=1, source_target_pairs={{0,2},{2,0},{1,3},{3,1},{4,6},{6,4},{5,7},{7,5},{8,10},{10,8},{9,1... | collective-permute-start | bytes 3145736 | tf_op jit(solution)/shard_map/ppermute | solution.py:22
  42.2 27.8 %collective-permute-start.4 = (bf16[2,128,1024]{2,1,0:T(8,128)(2,1)S(1)}, bf16[2,128,1024]{2,1,0:T(8,128)(2,1)S(1)}, u32[]{:S(2)}, u32[]{:S(2)}) collective-permute-start(bf16[2,128,1024]{2,1,0:T(8,128)(2,1)S(1)} %get-tuple-element.8), channel_id=1, source_target_pairs={{0,4},{4,8},{8,12},{12,0},{1,5},{5,9},{9,13},{13,1},{2,6},{6,10},{... | collective-permute-start | bytes 1572872 | tf_op jit(solution)/shard_map/ppermute | solution.py:22
  44.5 31.2 %collective-permute-start.2 = (bf16[2,128,1024]{2,1,0:T(8,128)(2,1)S(1)}, bf16[2,128,1024]{2,1,0:T(8,128)(2,1)S(1)}, u32[]{:S(2)}, u32[]{:S(2)}) collective-permute-start(bf16[2,128,1024]{2,1,0:T(8,128)(2,1)S(1)} %get-tuple-element.7.refs_0_), channel_id=1, source_target_pairs={{0,2},{2,0},{1,3},{3,1},{4,6},{6,4},{5,7},{7,5},{8,10},{10,8},{9,1... | collective-permute-start | bytes 1572872 | tf_op jit(solution)/shard_map/ppermute | solution.py:22
  46.0 62.9 %collective-permute-start.8 = (bf16[2,128,1024]{2,1,0:T(8,128)(2,1)}, bf16[2,128,1024]{2,1,0:T(8,128)(2,1)}, u32[]{:S(2)}, u32[]{:S(2)}) collective-permute-start(bf16[2,128,1024]{2,1,0:T(8,128)(2,1)} %get-tuple-element.9), channel_id=1, source_target_pairs={{0,8},{4,12},{8,0},{12,4},{1,9},{5,13},{9,1},{13,5},{2,10},{6,14},... | collective-permute-start | bytes 1572872 | tf_op jit(solution)/shard_map/ppermute | solution.py:22
  48.8 68.4 %collective-permute-start.1 = (bf16[2,128,1024]{2,1,0:T(8,128)(2,1)S(1)}, bf16[2,128,1024]{2,1,0:T(8,128)(2,1)S(1)}, u32[]{:S(2)}, u32[]{:S(2)}) collective-permute-start(bf16[2,128,1024]{2,1,0:T(8,128)(2,1)S(1)} %get-tuple-element.7.refs_0_), channel_id=1, source_target_pairs={{0,1},{1,0},{2,3},{3,2},{4,5},{5,4},{6,7},{7,6},{8,9},{9,8},{10,11... | collective-permute-start | bytes 1572872 | tf_op jit(solution)/shard_map/ppermute | solution.py:22
  48.9 69.1 %collective-permute-start.12 = (bf16[2,128,1024]{2,1,0:T(8,128)(2,1)S(1)}, bf16[2,128,1024]{2,1,0:T(8,128)(2,1)}, u32[]{:S(2)}, u32[]{:S(2)}) collective-permute-start(bf16[2,128,1024]{2,1,0:T(8,128)(2,1)S(1)} %get-tuple-element.10), channel_id=1, source_target_pairs={{0,12},{4,0},{8,4},{12,8},{1,13},{5,1},{9,5},{13,9},{2,14},{6,2},{... | collective-permute-start | bytes 1572872 | tf_op jit(solution)/shard_map/ppermute | solution.py:22
  70.0 49.3 %collective-permute-start.6 = (bf16[2,128,1024]{2,1,0:T(8,128)(2,1)S(1)}, bf16[2,128,1024]{2,1,0:T(8,128)(2,1)}, u32[]{:S(2)}, u32[]{:S(2)}) collective-permute-start(bf16[2,128,1024]{2,1,0:T(8,128)(2,1)S(1)} %collective-permute-done.4.refs_0_), channel_id=1, source_target_pairs={{0,2},{2,0},{1,3},{3,1},{4,6},{6,4},{5,7},{7,5},{8,10},{10,8},{9,1... | collective-permute-start | bytes 1572872 | tf_op jit(solution)/shard_map/ppermute | solution.py:22
  75.7 41.5 %copy-start.8 = (bf16[2,128,1024]{2,1,0:T(8,128)(2,1)}, bf16[2,128,1024]{2,1,0:T(8,128)(2,1)S(1)}, u32[]{:S(2)}) copy-start(bf16[2,128,1024]{2,1,0:T(8,128)(2,1)S(1)} %collective-permute-done.2.refs_2_) | copy-start | bytes 1572868
  75.7 44.0 %collective-permute-start.3 = (bf16[2,128,1024]{2,1,0:T(8,128)(2,1)S(1)}, bf16[2,128,1024]{2,1,0:T(8,128)(2,1)S(1)}, u32[]{:S(2)}, u32[]{:S(2)}) collective-permute-start(bf16[2,128,1024]{2,1,0:T(8,128)(2,1)S(1)} %collective-permute-done.2.refs_2_), channel_id=1, source_target_pairs={{0,1},{1,0},{2,3},{3,2},{4,5},{5,4},{6,7},{7,6},{8,9},{9,8},{10,11... | collective-permute-start | bytes 1572872 | tf_op jit(solution)/shard_map/ppermute | solution.py:22
  108.9 11.9 %collective-permute-start.10 = (bf16[2,128,1024]{2,1,0:T(8,128)(2,1)}, bf16[2,128,1024]{2,1,0:T(8,128)(2,1)}, u32[]{:S(2)}, u32[]{:S(2)}) collective-permute-start(bf16[2,128,1024]{2,1,0:T(8,128)(2,1)} %collective-permute-done.8.refs_0_), channel_id=1, source_target_pairs={{0,2},{2,0},{1,3},{3,1},{4,6},{6,4},{5,7},{7,5},{8,10},{10,8},{9,1... | collective-permute-start | bytes 1572872 | tf_op jit(solution)/shard_map/ppermute | solution.py:22
  118.0 15.7 %collective-permute-start.5 = (bf16[2,128,1024]{2,1,0:T(8,128)(2,1)S(1)}, bf16[2,128,1024]{2,1,0:T(8,128)(2,1)}, u32[]{:S(2)}, u32[]{:S(2)}) collective-permute-start(bf16[2,128,1024]{2,1,0:T(8,128)(2,1)S(1)} %collective-permute-done.4.refs_0_), channel_id=1, source_target_pairs={{0,1},{1,0},{2,3},{3,2},{4,5},{5,4},{6,7},{7,6},{8,9},{9,8},{10,11... | collective-permute-start | bytes 1572872 | tf_op jit(solution)/shard_map/ppermute | solution.py:22
  118.0 16.1 %collective-permute-start.14 = (bf16[2,128,1024]{2,1,0:T(8,128)(2,1)}, bf16[2,128,1024]{2,1,0:T(8,128)(2,1)}, u32[]{:S(2)}, u32[]{:S(2)}) collective-permute-start(bf16[2,128,1024]{2,1,0:T(8,128)(2,1)} %collective-permute-done.12.refs_0_), channel_id=1, source_target_pairs={{0,2},{2,0},{1,3},{3,1},{4,6},{6,4},{5,7},{7,5},{8,10},{10,8},{9,1... | collective-permute-start | bytes 1572872 | tf_op jit(solution)/shard_map/ppermute | solution.py:22
  119.3 15.0 %collective-permute-start.7 = (bf16[2,128,1024]{2,1,0:T(8,128)(2,1)}, bf16[2,128,1024]{2,1,0:T(8,128)(2,1)}, u32[]{:S(2)}, u32[]{:S(2)}) collective-permute-start(bf16[2,128,1024]{2,1,0:T(8,128)(2,1)} %collective-permute-done.6.refs_2_), channel_id=1, source_target_pairs={{0,1},{1,0},{2,3},{3,2},{4,5},{5,4},{6,7},{7,6},{8,9},{9,8},{10,11... | collective-permute-start | bytes 1572872 | tf_op jit(solution)/shard_map/ppermute | solution.py:22
  120.5 25.2 %collective-permute-start.9 = (bf16[2,128,1024]{2,1,0:T(8,128)(2,1)}, bf16[2,128,1024]{2,1,0:T(8,128)(2,1)S(1)}, u32[]{:S(2)}, u32[]{:S(2)}) collective-permute-start(bf16[2,128,1024]{2,1,0:T(8,128)(2,1)} %collective-permute-done.8.refs_0_), channel_id=1, source_target_pairs={{0,1},{1,0},{2,3},{3,2},{4,5},{5,4},{6,7},{7,6},{8,9},{9,8},{10,11... | collective-permute-start | bytes 1572872 | tf_op jit(solution)/shard_map/ppermute | solution.py:22
  120.8 24.9 %collective-permute-start.11 = (bf16[2,128,1024]{2,1,0:T(8,128)(2,1)}, bf16[2,128,1024]{2,1,0:T(8,128)(2,1)S(1)}, u32[]{:S(2)}, u32[]{:S(2)}) collective-permute-start(bf16[2,128,1024]{2,1,0:T(8,128)(2,1)} %collective-permute-done.10.refs_2_), channel_id=1, source_target_pairs={{0,1},{1,0},{2,3},{3,2},{4,5},{5,4},{6,7},{7,6},{8,9},{9,8},{10,11... | collective-permute-start | bytes 1572872 | tf_op jit(solution)/shard_map/ppermute | solution.py:22
  133.7 23.3 %collective-permute-start.13 = (bf16[2,128,1024]{2,1,0:T(8,128)(2,1)}, bf16[2,128,1024]{2,1,0:T(8,128)(2,1)S(1)}, u32[]{:S(2)}, u32[]{:S(2)}) collective-permute-start(bf16[2,128,1024]{2,1,0:T(8,128)(2,1)} %collective-permute-done.12.refs_0_), channel_id=1, source_target_pairs={{0,1},{1,0},{2,3},{3,2},{4,5},{5,4},{6,7},{7,6},{8,9},{9,8},{10,11... | collective-permute-start | bytes 1572872 | tf_op jit(solution)/shard_map/ppermute | solution.py:22
  134.1 22.9 %collective-permute-start.15 = (bf16[2,128,1024]{2,1,0:T(8,128)(2,1)}, bf16[2,128,1024]{2,1,0:T(8,128)(2,1)S(1)}, u32[]{:S(2)}, u32[]{:S(2)}) collective-permute-start(bf16[2,128,1024]{2,1,0:T(8,128)(2,1)} %collective-permute-done.14.refs_2_), channel_id=1, source_target_pairs={{0,1},{1,0},{2,3},{3,2},{4,5},{5,4},{6,7},{7,6},{8,9},{9,8},{10,11... | collective-permute-start | bytes 1572872 | tf_op jit(solution)/shard_map/ppermute | solution.py:22
  221.1 26.2 %copy-start.1 = (bf16[2,4000]{1,0:T(2,128)(2,1)S(1)}, bf16[2,4000]{1,0:T(2,128)(2,1)}, u32[]{:S(2)}) copy-start(bf16[2,4000]{1,0:T(2,128)(2,1)} %param.18) | copy-start | bytes 48004
  221.2 2.0 collective-permute-start.16
  223.3 8.4 %collective-permute-start.17 = (f32[32,16,128]{2,1,0:T(8,128)S(1)}, f32[32,16,128]{2,1,0:T(8,128)S(1)}, u32[]{:S(2)}, u32[]{:S(2)}) collective-permute-start(f32[32,16,128]{2,1,0:T(8,128)S(1)} %dynamic-slice_bitcast_fusion.1), channel_id=1, source_target_pairs={{0,2},{2,0},{1,3},{3,1},{4,6},{6,4},{5,7},{7,5},{8,10},{10,8},{9,1... | collective-permute-start | bytes 786440 | tf_op jit(solution)/shard_map/ppermute | solution.py:22
  232.5 6.6 %collective-permute-start.18 = (bf16[16,16,128]{2,1,0:T(8,128)(2,1)S(1)}, bf16[16,16,128]{2,1,0:T(8,128)(2,1)S(1)}, u32[]{:S(2)}, u32[]{:S(2)}) collective-permute-start(bf16[16,16,128]{2,1,0:T(8,128)(2,1)S(1)} %get-tuple-element.15), channel_id=1, source_target_pairs={{0,4},{4,8},{8,12},{12,0},{1,5},{5,9},{9,13},{13,1},{2,6},{6,10},{... | collective-permute-start | bytes 196616 | tf_op jit(solution)/shard_map/ppermute | solution.py:22
  232.5 7.8 %collective-permute-start.19 = (bf16[16,16,128]{2,1,0:T(8,128)(2,1)S(1)}, bf16[16,16,128]{2,1,0:T(8,128)(2,1)S(1)}, u32[]{:S(2)}, u32[]{:S(2)}) collective-permute-start(bf16[16,16,128]{2,1,0:T(8,128)(2,1)S(1)} %get-tuple-element.17), channel_id=1, source_target_pairs={{0,8},{4,12},{8,0},{12,4},{1,9},{5,13},{9,1},{13,5},{2,10},{6,14},... | collective-permute-start | bytes 196616 | tf_op jit(solution)/shard_map/ppermute | solution.py:22
  234.4 6.0 %collective-permute-start.20 = (bf16[16,16,128]{2,1,0:T(8,128)(2,1)S(1)}, bf16[16,16,128]{2,1,0:T(8,128)(2,1)S(1)}, u32[]{:S(2)}, u32[]{:S(2)}) collective-permute-start(bf16[16,16,128]{2,1,0:T(8,128)(2,1)S(1)} %get-tuple-element.16), channel_id=1, source_target_pairs={{0,12},{4,0},{8,4},{12,8},{1,13},{5,1},{9,5},{13,9},{2,14},{6,2},{... | collective-permute-start | bytes 196616 | tf_op jit(solution)/shard_map/ppermute | solution.py:22
  (21 other events, 69.1 us)
Sparse Core Ops, SparseCore 0:
  11.7 196.9 all-gather.3

commit v2 on v1

--- a/solution.py
+++ b/solution.py
@@ -36,11 +36,12 @@
     return pieces
 
 
-def valence_columns(valence, valence_head, selector, core, width, last):
+def valence_columns(valence, valence_head, selector, core, width, last, chunks):
     parts, points, pairs, columns = valence.shape
     head_at = columns - last * width
-
-    def kernel(core_ref, valence_ref, head_ref, selector_ref, out_ref):
+    each = points // chunks
+
+    def kernel(core_ref, valence_ref, head_ref, selector_ref, *out_refs):
         column = lax.broadcasted_iota(jnp.int32, (pairs, width), 1)
         at_last = core_ref[0] == last
         limit = jnp.where(at_last, head_at, width)
@@ -51,11 +52,11 @@
             rows = jnp.where(column < limit, rows, 0.0)
             rows = jnp.where(column == head_column, head, rows)
             moved = jnp.dot(selector_ref[...], rows.astype(bf16), preferred_element_type=f32)
-            out_ref[0, point] = moved.astype(bf16)
+            out_refs[point // each][0, point % each] = moved.astype(bf16)
 
     return pl.pallas_call(
         kernel,
-        out_shape=jax.ShapeDtypeStruct((parts, points, pairs, width), bf16),
+        out_shape=[jax.ShapeDtypeStruct((parts, each, pairs, width), bf16)] * chunks,
         grid_spec=pltpu.PrefetchScalarGridSpec(
             num_scalar_prefetch=1,
             grid=(parts,),
@@ -64,14 +65,24 @@
                 pl.BlockSpec((1, points, pairs, 1), lambda x, core: (x, 0, 0, 0)),
                 pl.BlockSpec((pairs, pairs), lambda x, core: (0, 0)),
             ],
-            out_specs=pl.BlockSpec((1, points, pairs, width), lambda x, core: (x, 0, 0, 0)),
+            out_specs=[pl.BlockSpec((1, each, pairs, width), lambda x, core: (x, 0, 0, 0))] * chunks,
         ),
         compiler_params=pltpu.CompilerParams(vmem_limit_bytes=VMEM_BYTES),
         name="valence_columns",
     )(core.reshape(1), valence, valence_head[..., None], selector)
 
 
-def screen_product(places, pieces, right, per_index, half):
+def along_line(x, name):
+    count = lax.axis_size(name)
+    below, above, steps = x, x, []
+    for step in range(1, count):
+        below = lax.ppermute(below, name, [(s, s + 1) for s in range(step - 1, count - 1)])
+        above = lax.ppermute(above, name, [(s, s - 1) for s in range(1, count - step + 1)])
+        steps.append((below, above))
+    return steps
+
+
+def screen_product(places, pieces, right, per_index, half, store, blocks):
     _, deep, width = right.shape
     planes = deep // 2
     rows = per_index * half
@@ -82,7 +93,7 @@
     tile = min(256, width)
 
     def kernel(place_ref, *refs):
-        piece_refs, right_ref, out_ref, left_ref = refs[:count], refs[count], refs[count + 1], refs[count + 2]
+        piece_refs, right_ref, out_ref, left_ref = refs[:count], refs[count], refs[-2], refs[-1]
 
         @pl.when((pl.program_id(0) == 0) & (pl.program_id(1) == 0))
         def _():
@@ -99,16 +110,22 @@
                     out_ref[pw * per_index + point, band, 0] = total[start : start + half]
 
     whole = pl.BlockSpec((2, rows, planes), lambda x, n, place: (0, 0, 0))
+    kept = [] if store is None else [store]
     return pl.pallas_call(
         kernel,
-        out_shape=jax.ShapeDtypeStruct((points, bands, 2, half, width), bf16),
+        out_shape=jax.ShapeDtypeStruct((blocks * points, bands, 2, half, width), bf16),
         grid_spec=pltpu.PrefetchScalarGridSpec(
             num_scalar_prefetch=1,
             grid=(2, width // tile),
-            in_specs=[whole] * count + [pl.BlockSpec((1, deep, tile), lambda x, n, place: (x, 0, n))],
-            out_specs=pl.BlockSpec((points, bands, 1, half, tile), lambda x, n, place: (0, 0, x, 0, n)),
+            in_specs=[whole] * count
+            + [pl.BlockSpec((1, deep, tile), lambda x, n, place: (x, 0, n))]
+            + [pl.BlockSpec(memory_space=pl.ANY)] * len(kept),
+            out_specs=pl.BlockSpec(
+                (points, bands, 1, half, tile), lambda x, n, place: (place[count], 0, x, 0, n)
+            ),
             scratch_shapes=[pltpu.VMEM((count * rows, deep), bf16)],
         ),
+        input_output_aliases={count + 2: 0} if kept else {},
         compiler_params=pltpu.CompilerParams(vmem_limit_bytes=VMEM_BYTES),
         cost_estimate=pl.CostEstimate(
             flops=2 * count * rows * deep * width * 2,
@@ -116,52 +133,68 @@
             transcendentals=0,
         ),
         name="screen_product",
-    )(places, *pieces, right)
-
-
-def contract(rows, product, gathered):
-    points, bands, _, half, width = product.shape
-    _, _, stored, pairs, _ = gathered.shape
-    group = 4 if points % 4 == 0 else 1
-
-    def kernel(row_ref, product_ref, *refs):
-        out_ref = refs[group]
+    )(places, *pieces, right, *kept)
+
+
+def contract(row_ids, sides, store, below, above):
+    _, bands, _, half, width = store.shape
+    _, each, pairs, _ = below[0].shape
+    chunks, slots = len(below), sides.shape[0]
+    given = list(below) + list(above)
+
+    def kernel(row_ref, side_ref, *refs):
+        store_refs, valence_refs, out_ref = refs[:each], refs[each:-1], refs[-1]
         lane = lax.broadcasted_iota(jnp.int32, (half, 2 * pairs), 1)
-        for index in range(group):
-            left = product_ref[index].reshape(bands * 2 * half, width)
-            right = refs[index][0, :, 0].reshape(2 * pairs, width)
-            square = lax.dot_general(left, right, (((1,), (1,)), ((), ())), preferred_element_type=f32)
-            for band in range(bands):
-                first = square[2 * band * half : (2 * band + 1) * half]
-                second = square[(2 * band + 1) * half : (2 * band + 2) * half]
-                turned = pltpu.roll(second, pairs, 1)
-                total = first + jnp.where(lane < pairs, -turned, turned)
-                out_ref[index, band * half : (band + 1) * half, :] = total
-
-    def valence_spec(index):
+        side = side_ref[pl.program_id(0)]
+
+        def rows_of(valence_ref):
+            for index in range(each):
+                left = store_refs[index][0].reshape(bands * 2 * half, width)
+                right = valence_ref[:, index].reshape(2 * pairs, width)
+                square = lax.dot_general(left, right, (((1,), (1,)), ((), ())), preferred_element_type=f32)
+                for band in range(bands):
+                    first = square[2 * band * half : (2 * band + 1) * half]
+                    second = square[(2 * band + 1) * half : (2 * band + 2) * half]
+                    turned = pltpu.roll(second, pairs, 1)
+                    total = first + jnp.where(lane < pairs, -turned, turned)
+                    out_ref[index, band * half : (band + 1) * half, :] = total
+
+        for place in range(len(given)):
+
+            @pl.when((side == place // chunks) & (pl.program_id(1) == place % chunks))
+            def _(place=place):
+                rows_of(valence_refs[place])
+
+        @pl.when(side == 2)
+        def _():
+            out_ref[...] = jnp.zeros_like(out_ref)
+
+    def store_spec(index):
         return pl.BlockSpec(
-            (1, 2, 1, pairs, width),
-            lambda step, row: (row[step * group + index] // stored, 0, row[step * group + index] % stored, 0, 0),
+            (1, bands, 2, half, width),
+            lambda slot, chunk, row, side: (row[(slot * chunks + chunk) * each + index], 0, 0, 0, 0),
         )
 
+    whole = pl.BlockSpec((2, each, pairs, width), lambda slot, chunk, row, side: (0, 0, 0, 0))
     return pl.pallas_call(
         kernel,
-        out_shape=jax.ShapeDtypeStruct((points, bands * half, 2 * pairs), f32),
+        out_shape=jax.ShapeDtypeStruct((slots * chunks * each, bands * half, 2 * pairs), f32),
         grid_spec=pltpu.PrefetchScalarGridSpec(
-            num_scalar_prefetch=1,
-            grid=(points // group,),
-            in_specs=[pl.BlockSpec((group, bands, 2, half, width), lambda step, row: (step, 0, 0, 0, 0))]
-            + [valence_spec(index) for index in range(group)],
-            out_specs=pl.BlockSpec((group, bands * half, 2 * pairs), lambda step, row: (step, 0, 0)),
+            num_scalar_prefetch=2,
+            grid=(slots, chunks),
+            in_specs=[store_spec(index) for index in range(each)] + [whole] * len(given),
+            out_specs=pl.BlockSpec(
+                (each, bands * half, 2 * pairs), lambda slot, chunk, row, side: (slot * chunks + chunk, 0, 0)
+            ),
         ),
         compiler_params=pltpu.CompilerParams(vmem_limit_bytes=VMEM_BYTES),
         cost_estimate=pl.CostEstimate(
-            flops=2 * points * bands * 2 * half * 2 * pairs * width,
-            bytes_accessed=2 * points * width * (bands * 2 * half + 2 * pairs),
+            flops=2 * slots * chunks * each * bands * 2 * half * 2 * pairs * width,
+            bytes_accessed=2 * slots * chunks * each * width * (bands * 2 * half + 2 * pairs),
             transcendentals=0,
         ),
         name="contract",
-    )(rows, product, *([gathered] * group))
+    )(row_ids, sides, *([store] * each), *given)
 
 
 def on_device(
@@ -194,8 +227,9 @@
     head_at = columns - last * width
 
     selector = (pair_select[:, None] == jnp.arange(pairs)[None, :]).astype(bf16)
-    own_valence = valence_columns(valence, valence_head, selector, band, width, last)
-    gathered = lax.all_gather(own_valence, "kpt", axis=0)
+    chunks = 2 if points % 2 == 0 else 1
+    own_valence = valence_columns(valence, valence_head, selector, band, width, last, chunks)
+    lines = [along_line(chunk, "kpt") for chunk in own_valence]
 
     plane = jnp.arange(deep)
     is_head = (plane >= block) & (plane < block + HEAD_PARTS)
@@ -256,37 +290,55 @@
 
     live = jnp.where(jnp.arange(neighbors.shape[1])[None, :] < counts[:, None], weights, 0.0)
     all_points = kpt_count * points
-    match = neighbors[:, :, None] == jnp.arange(all_points)[None, None, :]
-    stencil = jnp.sum(jnp.where(match, live[:, :, None], 0.0), axis=1)
-
-    products = []
+    point_of_row = jnp.sum(
+        jnp.where(partner[None, :] == jnp.arange(all_points)[:, None], jnp.arange(all_points)[None, :], 0), axis=1
+    ).astype(jnp.int32)
+
+    store = None
     for shift in range(kpt_count):
         piece = block_for((kpt + shift) % kpt_count)
         if shift:
             piece = shifted(piece, "kpt", shift)
         pieces = [own for across in share(piece, "pw") for own in share(across, "band")]
-        products.append(screen_product(places, pieces, right, per_index, half))
-
-    totals = []
-    stencils = []
-    for shift in range(kpt_count):
-        source = (kpt - shift) % kpt_count
-        row_ids = lax.dynamic_slice_in_dim(partner, source * points, points, 0)
-        totals.append(contract(row_ids, products[shift], gathered))
-        stencils.append(lax.dynamic_slice_in_dim(stencil, source * points, points, 1))
-    body = jnp.concatenate(totals, axis=0)
-    stencil = jnp.concatenate(stencils, axis=1)
+        source = ((kpt - shift) % kpt_count).astype(jnp.int32)
+        store = screen_product(
+            jnp.append(places, source), pieces, right, per_index, half, store, kpt_count
+        )
 
     lanes = 2 * pairs
-    body = body.reshape(all_points, band_count, half, lanes)
-    body = sum(deal(jnp.moveaxis(body, 1, 0), "band"))
     kept = half // pw_count
-    body = body.reshape(all_points, pw_count, kept, lanes)
-    body = sum(deal(jnp.moveaxis(body, 1, 0), "pw"))
-    fine = jnp.dot(stencil, body.reshape(all_points, kept * lanes), precision=highest)
+
+    def fine_part(sides, owners, below, above):
+        owners = jnp.stack(owners)
+        sides = jnp.stack(sides).astype(jnp.int32)
+        live_slot = jnp.repeat(sides < 2, points)
+        row_ids = (owners[:, None] * points + jnp.arange(points)[None, :]).reshape(-1)
+        row_ids = jnp.where(live_slot, jnp.take(point_of_row, row_ids, mode="clip"), 0)
+        body = contract(row_ids, sides, store, below, above)
+        body = body.reshape(-1, band_count, half, lanes)
+        body = sum(deal(jnp.moveaxis(body, 1, 0), "band"))
+        body = body.reshape(-1, pw_count, kept, lanes)
+        body = sum(deal(jnp.moveaxis(body, 1, 0), "pw"))
+        match = (neighbors[:, :, None] == row_ids[None, None, :]) & live_slot[None, None, :]
+        stencil = jnp.sum(jnp.where(match, live[:, :, None], 0.0), axis=1)
+        return jnp.dot(stencil, body.reshape(-1, kept * lanes), precision=highest)
+
+    fine = fine_part([jnp.zeros((), jnp.int32)], [kpt], own_valence, [])
+    for step in range(1, kpt_count):
+        below = [line[step - 1][0] for line in lines]
+        above = [line[step - 1][1] for line in lines]
+        has_below, has_above = kpt >= step, kpt + step < kpt_count
+        if 2 * step < kpt_count:
+            sides = [jnp.where(has_below, 0, 2), jnp.where(has_above, 1, 2)]
+            owners = [kpt - step, kpt + step]
+        else:
+            sides = [jnp.where(has_below, 0, jnp.where(has_above, 1, 2))]
+            owners = [jnp.where(has_below, kpt - step, kpt + step)]
+        fine = fine + fine_part(sides, owners, below, above)
+
     fine_here = neighbors.shape[0] // kpt_count
-    fine = fine.astype(bf16).reshape(kpt_count, fine_here, kept, lanes)
-    fine = sum(piece.astype(f32) for piece in deal(fine, "kpt"))
+    fine = fine.reshape(kpt_count, fine_here, kept, lanes)
+    fine = sum(deal(fine, "kpt"))
     fine = lax.all_gather(fine, "pw", axis=0)
     fine = fine.reshape(pw_count, fine_here, kept, 2, pairs)
     return jnp.transpose(fine, (3, 1, 0, 2, 4)).reshape(2, fine_here, half * pairs)

time: 255 us -> 252 us (0.988)
  waiting for transfers between devices: 125 us -> 93 us
  starting transfers between devices: 21.2 us -> 43.6 us
  between operations: 13.9 us -> 0.87 us
  other arithmetic: 19.6 us -> 27.3 us
  Pallas kernels: 55 us -> 61.3 us
  local copies, waits for them, and re-layouts: 12.8 us -> 16.4 us
    all_gather x1 -> x0, waiting for transfers between devices: 40.4 us -> none  [on_device(): gathered = lax.all_gather(own_valence, 'kpt', axis=0)]
    ppermute x0 -> x12, starting transfers between devices: none -> 21.3 us  [the longest x6 13.6 us: along_line(): lax.ppermute(below, name, [(s, s + 1) for s in range(step - 1, count - 1)])]
    ppermute x0 -> x12, waiting for transfers between devices: none -> 21.2 us  [the longest x6 21.2 us: along_line(): lax.ppermute(above, name, [(s, s - 1) for s in range(1, count - step + 1)])]
    ppermute x21 -> x27, waiting for transfers between devices: 85 us -> 71.7 us  [shifted(): return lax.ppermute(x, name, pairs)]
    pallas_call x9, Pallas kernels: 55 us -> 61.3 us  [the longest x4 43.6 us: screen_product(): pl.pallas_call(kernel, out_shape=jax.ShapeDtypeStruct((blocks * points, b...]
    unnamed x47 -> x41, local copies, waits for them, and re-layouts: 8.87 us -> 5.66 us
    neg x1, other arithmetic: 0.14 us -> 3.12 us  [on_device(): -screen[0]]
    gather x0 -> x4, local copies, waits for them, and re-layouts: none -> 2.59 us  [fine_part(): jnp.take(point_of_row, row_ids, mode='clip')]
  transfers between devices with their start and end apart: 22 -> 39, of which waited for: 8 -> 15; matrix products, arithmetic and copies ran while one was open for 8% -> 15% of each run, Pallas kernels for 16% -> 22%
where the time goes in v2:
time: 252 us; the launch traced here: 251 us
  waiting for transfers between devices  93 us (37%)
  Pallas kernels  61.3 us (24%)
  starting transfers between devices  43.6 us (17%)
  other arithmetic  27.3 us (11%)
  local copies, waits for them, and re-layouts  16.4 us (7%)
  blocking collectives  5.64 us (2%)
    ppermute x27, waiting for transfers between devices, shifted(): return lax.ppermute(x, name, pairs)  71.7 us
    pallas_call x4, Pallas kernels, screen_product(): pl.pallas_call(kernel, out_shape=jax.ShapeDtypeStruct((blocks * points, b...  43.6 us
    ppermute x27, starting transfers between devices, shifted(): return lax.ppermute(x, name, pairs)  22.3 us
    ppermute x6, waiting for transfers between devices, along_line(): lax.ppermute(above, name, [(s, s - 1) for s in range(1, count - step + 1)])  21.2 us
    pallas_call x4, Pallas kernels, contract(): pl.pallas_call(kernel, out_shape=jax.ShapeDtypeStruct((slots * chunks * e...  14.5 us
    ppermute x6, starting transfers between devices, along_line(): lax.ppermute(below, name, [(s, s + 1) for s in range(step - 1, count - 1)])  13.6 us
    another operation x2, other arithmetic, on_device(): jnp.stack([jnp.concatenate([screen[0], screen[1]], axis=0), jnp.concatena...  11.5 us
    ppermute x6, starting transfers between devices, along_line(): lax.ppermute(above, name, [(s, s - 1) for s in range(1, count - step + 1)])  7.72 us
  transfers between devices with their start and end apart: 39, of which 15 were waited for; matrix products, arithmetic and copies ran while one was open for 15% of the time, Pallas kernels for 22%

profile of v2, /device:TPU:0, one launch (start us, length us, event | category | flops | bytes accessed | tf_op | source)
XLA Modules:
  0.0 250.5 jit_solution(14215326890052339141)
XLA Ops:
  4.8 5.0 %collective-permute-start.18 = (bf16[2,4,64,1024]{3,2,1,0:T(8,128)(2,1)}, bf16[2,4,64,1024]{3,2,1,0:T(8,128)(2,1)S(1)}, u32[]{:S(2)}, u32[]{:S(2)}) collective-permute-start(bf16[2,4,64,1024]{3,2,1,0:T(8,128)(2,1)} %get-tuple-element.7.refs_4_), channel_id=1, source_target_pairs={{0,4},{4,8},{8,12},{1,5},{5,9},{9,13},{2,6},{6,10},{10,14},{3,7},{... | collective-permute-start | bytes 3145736 | tf_op jit(solution)/shard_map/ppermute | solution.py:79
  11.1 5.5 %collective-permute-start.19 = (bf16[2,4,64,1024]{3,2,1,0:T(8,128)(2,1)}, bf16[2,4,64,1024]{3,2,1,0:T(8,128)(2,1)}, u32[]{:S(2)}, u32[]{:S(2)}) collective-permute-start(bf16[2,4,64,1024]{3,2,1,0:T(8,128)(2,1)} %get-tuple-element.8.refs_5_), channel_id=1, source_target_pairs={{0,4},{4,8},{8,12},{1,5},{5,9},{9,13},{2,6},{6,10},{10,14},{3,7},{... | collective-permute-start | bytes 3145736 | tf_op jit(solution)/shard_map/ppermute | solution.py:79
  27.2 4.6 %fusion.1 = bf16[2,1024,1024]{2,1,0:T(8,128)(2,1)} fusion(s32[]{:T(128)S(6)} %select_n.368, bf16[2,1000,2000]{2,1,0:T(8,128)(2,1)} %param.17, pred[1024]{0:T(1024)(128)(4,1)S(1)} %get-tuple-element.32, pred[1024]{0:T(1024)(128)(4,1)S(1)} %get-tuple-element.33, bf16[2,1024]{1,0:T(2,128)(2,1)S(1)} %broadcast_select_fusion, bf16[2,1024]{1,0:T(2,128)(2,1)S(1)} %fusion.36), kind=kLoop, calls=%fused_computation.7 | loop fusion | flops 4194304 | bytes 12204548 | tf_op jit(solution)/shard_map/jit(_where)/select_n | solution.py:273
  35.7 11.8 %collective-permute-done = bf16[2,2,128,1024]{3,2,1,0:T(8,128)(2,1)S(1)} collective-permute-done((bf16[2,2,128,1024]{3,2,1,0:T(8,128)(2,1)}, bf16[2,2,128,1024]{3,2,1,0:T(8,128)(2,1)S(1)}, u32[]{:S(2)}, u32[]{:S(2)}) %collective-permute-start) | collective-permute-done | bytes 1048608 | tf_op jit(solution)/shard_map/ppermute | solution.py:22
  63.8 10.0 %collective-permute-done.9.refs_0_ = bf16[2,128,1024]{2,1,0:T(8,128)(2,1)S(1)} collective-permute-done((bf16[2,128,1024]{2,1,0:T(8,128)(2,1)}, bf16[2,128,1024]{2,1,0:T(8,128)(2,1)S(1)}, u32[]{:S(2)}, u32[]{:S(2)}) %collective-permute-start.9) | collective-permute-done | bytes 524320 | tf_op jit(solution)/shard_map/ppermute | solution.py:22
  75.3 3.9 %maximum_bitcast_fusion = (bf16[1,2048,1024]{2,1,0:T(8,128)(2,1)}, bf16[1,2048,1024]{2,1,0:T(8,128)(2,1)}) fusion(bf16[1024,1024]{1,0:T(8,128)(2,1)S(1)} %get-tuple-element.15, bf16[1024,1024]{1,0:T(8,128)(2,1)S(1)} %get-tuple-element.14, bf16[1024,1024]{1,0:T(8,128)(2,1)S(1)} %copy-done.8), kind=kLoop, calls=%fused_computation.8 | loop fusion | flops 16777216 | bytes 14680064 | tf_op jit(solution)/shard_map/stack | solution.py:276
  80.0 14.8 %collective-permute-done.5.refs_0_ = bf16[2,128,1024]{2,1,0:T(8,128)(2,1)} collective-permute-done((bf16[2,128,1024]{2,1,0:T(8,128)(2,1)S(1)}, bf16[2,128,1024]{2,1,0:T(8,128)(2,1)}, u32[]{:S(2)}, u32[]{:S(2)}) %collective-permute-start.5) | collective-permute-done | bytes 524320 | tf_op jit(solution)/shard_map/ppermute | solution.py:22
  98.0 7.5 %pad_maximum_fusion.refs_4_ = bf16[2,2048,1024]{2,1,0:T(8,128)(2,1)} fusion(bf16[1,2048,1024]{2,1,0:T(8,128)(2,1)} %get-tuple-element.21, bf16[1,2048,1024]{2,1,0:T(8,128)(2,1)} %get-tuple-element.20), kind=kLoop, calls=%fused_computation.4 | loop fusion | flops 4194304 | bytes 16777216 | tf_op jit(solution)/shard_map/stack | solution.py:276
  106.7 3.3 %collective-permute-done.7.refs_2_ = bf16[2,128,1024]{2,1,0:T(8,128)(2,1)} collective-permute-done((bf16[2,128,1024]{2,1,0:T(8,128)(2,1)}, bf16[2,128,1024]{2,1,0:T(8,128)(2,1)}, u32[]{:S(2)}, u32[]{:S(2)}) %collective-permute-start.7) | collective-permute-done | bytes 524320 | tf_op jit(solution)/shard_map/ppermute | solution.py:22
  111.8 8.5 %collective-permute-done.3.refs_2_ = bf16[2,128,1024]{2,1,0:T(8,128)(2,1)} collective-permute-done((bf16[2,128,1024]{2,1,0:T(8,128)(2,1)}, bf16[2,128,1024]{2,1,0:T(8,128)(2,1)}, u32[]{:S(2)}, u32[]{:S(2)}) %collective-permute-start.3) | collective-permute-done | bytes 524320 | tf_op jit(solution)/shard_map/ppermute | solution.py:22
  124.4 10.7 %screen_product.4.refs_5_ = bf16[32,2,2,32,1024]{4,3,2,1,0:T(8,128)(2,1)} custom-call(s32[5]{0:T(128)S(1)} %concatenate.38.place_ref, bf16[2,128,1024]{2,1,0:T(8,128)(2,1)S(1)} %get-tuple-element.16.refs_0_, bf16[2,128,1024]{2,1,0:T(8,128)(2,1)S(1)} %copy-done.3, bf16[2,128,1024]{2,1,0:T(8,128)(2,1)} %collective-permute-done.14.refs_2_, ...), custom_call_target="tpu_custom_call" | custom-call | flops 4294967296 | bytes 10485760 | tf_op jit(solution)/shard_map/screen_product/pallas_call | solution.py:114
  136.4 10.9 %screen_product.5.refs_5_ = bf16[32,2,2,32,1024]{4,3,2,1,0:T(8,128)(2,1)} custom-call(s32[5]{0:T(128)S(1)} %concatenate.37.place_ref, bf16[2,128,1024]{2,1,0:T(8,128)(2,1)S(1)} %collective-permute-done.9.refs_0_, bf16[2,128,1024]{2,1,0:T(8,128)(2,1)S(1)} %copy-done.7, ...), custom_call_target="tpu_custom_call", output_to_operand_aliasing={{}: (6, {})} | custom-call | flops 4294967296 | bytes 10485760 | tf_op jit(solution)/shard_map/screen_product/pallas_call | solution.py:114
  147.3 11.2 %screen_product.6.refs_5_ = bf16[32,2,2,32,1024]{4,3,2,1,0:T(8,128)(2,1)} custom-call(s32[5]{0:T(128)S(1)} %concatenate.36.place_ref, bf16[2,128,1024]{2,1,0:T(8,128)(2,1)} %collective-permute-done.5.refs_0_, bf16[2,128,1024]{2,1,0:T(8,128)(2,1)} %collective-permute-done.6.refs_1_, ...), custom_call_target="tpu_custom_call", output_to_operand_aliasing={{}: (6, {})} | custom-call | flops 4294967296 | bytes 10485760 | tf_op jit(solution)/shard_map/screen_product/pallas_call | solution.py:114
  161.4 11.0 %screen_product.7.refs_0_.refs_1_.refs_2_.refs_3_ = bf16[32,2,2,32,1024]{4,3,2,1,0:T(8,128)(2,1)} custom-call(s32[5]{0:T(128)S(1)} %concatenate.32.place_ref, bf16[2,128,1024]{2,1,0:T(8,128)(2,1)} %collective-permute-done.1.refs_0_, bf16[2,128,1024]{2,1,0:T(8,128)(2,1)} %collective-permute-done.2.refs_1_, ...), custom_call_target="tpu_custom_call", output_to_operand_aliasing={{}: (6, {})} | custom-call | flops 4294967296 | bytes 10485760 | tf_op jit(solution)/shard_map/screen_product/pallas_call | solution.py:114
  172.4 3.9 %collective-permute-done.27.refs_7_ = bf16[2,4,64,1024]{3,2,1,0:T(8,128)(2,1)S(1)} collective-permute-done((bf16[2,4,64,1024]{3,2,1,0:T(8,128)(2,1)}, bf16[2,4,64,1024]{3,2,1,0:T(8,128)(2,1)S(1)}, u32[]{:S(2)}, u32[]{:S(2)}) %collective-permute-start.27) | collective-permute-done | bytes 1048608 | tf_op jit(solution)/shard_map/ppermute | solution.py:80
  179.3 3.7 %contract.4 = f32[8,64,128]{2,1,0:T(8,128)S(1)} custom-call(s32[8]{0:T(128)S(1)} %gather_fusion, s32[1]{0:T(128)} %constant.386.clone.1.side_ref, bf16[32,2,2,32,1024]{4,3,2,1,0:T(8,128)(2,1)} %screen_product.7.refs_0_.refs_1_.refs_2_.refs_3_, bf16[32,2,2,32,1024]{4,3,2,1,0:T(8,128)(2,1)} %screen_product.7.refs_0_.refs_1_.refs_2_.refs_3_, ...), custom_call_target="tpu_custom_call" | custom-call | flops 268435456 | bytes 4194304 | tf_op jit(solution)/shard_map/contract/pallas_call | solution.py:179
  183.6 4.9 %contract.5 = f32[16,64,128]{2,1,0:T(8,128)S(1)} custom-call(s32[16]{0:T(128)S(1)} %broadcast_select_fusion.6.row_ref, s32[2]{0:T(128)S(1)} %get-tuple-element.13.side_ref, bf16[32,2,2,32,1024]{4,3,2,1,0:T(8,128)(2,1)} %screen_product.7.refs_0_.refs_1_.refs_2_.refs_3_, bf16[32,2,2,32,1024]{4,3,2,1,0:T(8,128)(2,1)} %screen_product.7.refs_0_.refs_1_.refs_2_.refs_3_, ...), custom_call_target="tpu_custom_call" | custom-call | flops 536870912 | bytes 8388608 | tf_op jit(solution)/shard_map/contract/pallas_call | solution.py:179
  189.9 3.3 %collective-permute-done.29 = f32[8,16,128]{2,1,0:T(8,128)S(1)} collective-permute-done((f32[8,16,128]{2,1,0:T(8,128)S(1)}, f32[8,16,128]{2,1,0:T(8,128)S(1)}, u32[]{:S(2)}, u32[]{:S(2)}) %collective-permute-start.29) | collective-permute-done | bytes 65568 | tf_op jit(solution)/shard_map/ppermute | solution.py:22
  200.0 3.8 %collective-permute-done.23 = f32[16,16,128]{2,1,0:T(8,128)S(1)} collective-permute-done((f32[16,16,128]{2,1,0:T(8,128)S(1)}, f32[16,16,128]{2,1,0:T(8,128)S(1)}, u32[]{:S(2)}, u32[]{:S(2)}) %collective-permute-start.23) | collective-permute-done | bytes 131104 | tf_op jit(solution)/shard_map/ppermute | solution.py:22
  204.5 17.4 %collective-permute-done.33.refs_7_ = bf16[2,4,64,1024]{3,2,1,0:T(8,128)(2,1)S(1)} collective-permute-done((bf16[2,4,64,1024]{3,2,1,0:T(8,128)(2,1)S(1)}, bf16[2,4,64,1024]{3,2,1,0:T(8,128)(2,1)S(1)}, u32[]{:S(2)}, u32[]{:S(2)}) %collective-permute-start.33) | collective-permute-done | bytes 1048608 | tf_op jit(solution)/shard_map/ppermute | solution.py:80
  231.6 3.7 %collective-permute-start.38 = (f32[16,16,128]{2,1,0:T(8,128)S(1)}, f32[16,16,128]{2,1,0:T(8,128)S(1)}, u32[]{:S(2)}, u32[]{:S(2)}) collective-permute-start(f32[16,16,128]{2,1,0:T(8,128)S(1)} %get-tuple-element.25), channel_id=1, source_target_pairs={{0,12},{4,0},{8,4},{12,8},{1,13},{5,1},{9,5},{13,9},{2,14},{6,2},{... | collective-permute-start | bytes 393224 | tf_op jit(solution)/shard_map/ppermute | solution.py:22
  235.4 4.5 %collective-permute-done.36 = f32[16,16,128]{2,1,0:T(8,128)S(1)} collective-permute-done((f32[16,16,128]{2,1,0:T(8,128)S(1)}, f32[16,16,128]{2,1,0:T(8,128)S(1)}, u32[]{:S(2)}, u32[]{:S(2)}) %collective-permute-start.36) | collective-permute-done | bytes 131104 | tf_op jit(solution)/shard_map/ppermute | solution.py:22
  239.8 3.7 %collective-permute-done.37 = f32[16,16,128]{2,1,0:T(8,128)S(1)} collective-permute-done((f32[16,16,128]{2,1,0:T(8,128)S(1)}, f32[16,16,128]{2,1,0:T(8,128)S(1)}, u32[]{:S(2)}, u32[]{:S(2)}) %collective-permute-start.37) | collective-permute-done | bytes 131104 | tf_op jit(solution)/shard_map/ppermute | solution.py:22
  243.6 5.6 %all-gather = f32[32,16,128]{2,1,0:T(8,128)S(1)} all-gather(f32[16,16,128]{2,1,0:T(8,128)S(1)} %fusion.19), channel_id=2, replica_groups=mesh['grp'=2,'kpt'=4,'pw'=2,'band'=2] {'pw'}, dimensions={0}, use_global_device_ids=true | all-gather | bytes 393216 | tf_op jit(solution)/shard_map/all_gather | solution.py:342
  (178 shorter events, 76.6 us)
Async XLA Ops:
  4.8 48.4 %collective-permute-start.18 = (bf16[2,4,64,1024]{3,2,1,0:T(8,128)(2,1)}, bf16[2,4,64,1024]{3,2,1,0:T(8,128)(2,1)S(1)}, u32[]{:S(2)}, u32[]{:S(2)}) collective-permute-start(bf16[2,4,64,1024]{3,2,1,0:T(8,128)(2,1)} %get-tuple-element.7.refs_4_), channel_id=1, source_target_pairs={{0,4},{4,8},{8,12},{1,5},{5,9},{9,13},{2,6},{6,10},{10,14},{3,7},{... | collective-permute-start | bytes 3145736 | tf_op jit(solution)/shard_map/ppermute | solution.py:79
  9.8 48.8 %collective-permute-start.20 = (bf16[2,4,64,1024]{3,2,1,0:T(8,128)(2,1)}, bf16[2,4,64,1024]{3,2,1,0:T(8,128)(2,1)S(1)}, u32[]{:S(2)}, u32[]{:S(2)}) collective-permute-start(bf16[2,4,64,1024]{3,2,1,0:T(8,128)(2,1)} %get-tuple-element.7.refs_4_), channel_id=1, source_target_pairs={{4,0},{8,4},{12,8},{5,1},{9,5},{13,9},{6,2},{10,6},{14,10},{7,3},{... | collective-permute-start | bytes 3145736 | tf_op jit(solution)/shard_map/ppermute | solution.py:80
  11.1 47.5 %collective-permute-start.19 = (bf16[2,4,64,1024]{3,2,1,0:T(8,128)(2,1)}, bf16[2,4,64,1024]{3,2,1,0:T(8,128)(2,1)}, u32[]{:S(2)}, u32[]{:S(2)}) collective-permute-start(bf16[2,4,64,1024]{3,2,1,0:T(8,128)(2,1)} %get-tuple-element.8.refs_5_), channel_id=1, source_target_pairs={{0,4},{4,8},{8,12},{1,5},{5,9},{9,13},{2,6},{6,10},{10,14},{3,7},{... | collective-permute-start | bytes 3145736 | tf_op jit(solution)/shard_map/ppermute | solution.py:79
  16.6 44.7 %collective-permute-start.21 = (bf16[2,4,64,1024]{3,2,1,0:T(8,128)(2,1)}, bf16[2,4,64,1024]{3,2,1,0:T(8,128)(2,1)}, u32[]{:S(2)}, u32[]{:S(2)}) collective-permute-start(bf16[2,4,64,1024]{3,2,1,0:T(8,128)(2,1)} %get-tuple-element.8.refs_5_), channel_id=1, source_target_pairs={{4,0},{8,4},{12,8},{5,1},{9,5},{13,9},{6,2},{10,6},{14,10},{7,3},{... | collective-permute-start | bytes 3145736 | tf_op jit(solution)/shard_map/ppermute | solution.py:80
  23.2 24.3 %collective-permute-start = (bf16[2,2,128,1024]{3,2,1,0:T(8,128)(2,1)}, bf16[2,2,128,1024]{3,2,1,0:T(8,128)(2,1)S(1)}, u32[]{:S(2)}, u32[]{:S(2)}) collective-permute-start(bf16[2,2,128,1024]{3,2,1,0:T(8,128)(2,1)} %get-tuple-element.22), channel_id=1, source_target_pairs={{0,2},{2,0},{1,3},{3,1},{4,6},{6,4},{5,7},{7,5},{8,10},{10,8},{9,1... | collective-permute-start | bytes 3145736 | tf_op jit(solution)/shard_map/ppermute | solution.py:22
  58.6 20.7 %collective-permute-start.13 = (bf16[2,128,1024]{2,1,0:T(8,128)(2,1)S(1)}, bf16[2,128,1024]{2,1,0:T(8,128)(2,1)S(1)}, u32[]{:S(2)}, u32[]{:S(2)}) collective-permute-start(bf16[2,128,1024]{2,1,0:T(8,128)(2,1)S(1)} %get-tuple-element.16.refs_0_), channel_id=1, source_target_pairs={{0,1},{1,0},{2,3},{3,2},{4,5},{5,4},{6,7},{7,6},{8,9},{9,8},{10,11... | collective-permute-start | bytes 1572872 | tf_op jit(solution)/shard_map/ppermute | solution.py:22
  58.7 36.2 %collective-permute-start.5 = (bf16[2,128,1024]{2,1,0:T(8,128)(2,1)S(1)}, bf16[2,128,1024]{2,1,0:T(8,128)(2,1)}, u32[]{:S(2)}, u32[]{:S(2)}) collective-permute-start(bf16[2,128,1024]{2,1,0:T(8,128)(2,1)S(1)} %copy-done.11), channel_id=1, source_target_pairs={{0,8},{4,12},{8,0},{12,4},{1,9},{5,13},{9,1},{13,5},{2,10},{6,14},... | collective-permute-start | bytes 1572872 | tf_op jit(solution)/shard_map/ppermute | solution.py:22
  61.3 34.9 %collective-permute-start.1 = (bf16[2,128,1024]{2,1,0:T(8,128)(2,1)S(1)}, bf16[2,128,1024]{2,1,0:T(8,128)(2,1)}, u32[]{:S(2)}, u32[]{:S(2)}) collective-permute-start(bf16[2,128,1024]{2,1,0:T(8,128)(2,1)S(1)} %copy-done.10), channel_id=1, source_target_pairs={{0,12},{4,0},{8,4},{12,8},{1,13},{5,1},{9,5},{13,9},{2,14},{6,2},{... | collective-permute-start | bytes 1572872 | tf_op jit(solution)/shard_map/ppermute | solution.py:22
  63.8 32.5 %collective-permute-start.15 = (bf16[2,128,1024]{2,1,0:T(8,128)(2,1)}, bf16[2,128,1024]{2,1,0:T(8,128)(2,1)S(1)}, u32[]{:S(2)}, u32[]{:S(2)}) collective-permute-start(bf16[2,128,1024]{2,1,0:T(8,128)(2,1)} %collective-permute-done.14.refs_2_), channel_id=1, source_target_pairs={{0,1},{1,0},{2,3},{3,2},{4,5},{5,4},{6,7},{7,6},{8,9},{9,8},{10,11... | collective-permute-start | bytes 1572872 | tf_op jit(solution)/shard_map/ppermute | solution.py:22
  73.8 24.0 %collective-permute-start.11 = (bf16[2,128,1024]{2,1,0:T(8,128)(2,1)S(1)}, bf16[2,128,1024]{2,1,0:T(8,128)(2,1)}, u32[]{:S(2)}, u32[]{:S(2)}) collective-permute-start(bf16[2,128,1024]{2,1,0:T(8,128)(2,1)S(1)} %collective-permute-done.9.refs_0_), channel_id=1, source_target_pairs={{0,2},{2,0},{1,3},{3,1},{4,6},{6,4},{5,7},{7,5},{8,10},{10,8},{9,1... | collective-permute-start | bytes 1572872 | tf_op jit(solution)/shard_map/ppermute | solution.py:22
  80.0 25.5 %collective-permute-start.10 = (bf16[2,128,1024]{2,1,0:T(8,128)(2,1)S(1)}, bf16[2,128,1024]{2,1,0:T(8,128)(2,1)S(1)}, u32[]{:S(2)}, u32[]{:S(2)}) collective-permute-start(bf16[2,128,1024]{2,1,0:T(8,128)(2,1)S(1)} %collective-permute-done.9.refs_0_), channel_id=1, source_target_pairs={{0,1},{1,0},{2,3},{3,2},{4,5},{5,4},{6,7},{7,6},{8,9},{9,8},{10,11... | collective-permute-start | bytes 1572872 | tf_op jit(solution)/shard_map/ppermute | solution.py:22
  97.1 23.2 %collective-permute-start.3 = (bf16[2,128,1024]{2,1,0:T(8,128)(2,1)}, bf16[2,128,1024]{2,1,0:T(8,128)(2,1)}, u32[]{:S(2)}, u32[]{:S(2)}) collective-permute-start(bf16[2,128,1024]{2,1,0:T(8,128)(2,1)} %collective-permute-done.1.refs_0_), channel_id=1, source_target_pairs={{0,2},{2,0},{1,3},{3,1},{4,6},{6,4},{5,7},{7,5},{8,10},{10,8},{9,1... | collective-permute-start | bytes 1572872 | tf_op jit(solution)/shard_map/ppermute | solution.py:22
  97.8 23.2 %collective-permute-start.2 = (bf16[2,128,1024]{2,1,0:T(8,128)(2,1)}, bf16[2,128,1024]{2,1,0:T(8,128)(2,1)}, u32[]{:S(2)}, u32[]{:S(2)}) collective-permute-start(bf16[2,128,1024]{2,1,0:T(8,128)(2,1)} %collective-permute-done.1.refs_0_), channel_id=1, source_target_pairs={{0,1},{1,0},{2,3},{3,2},{4,5},{5,4},{6,7},{7,6},{8,9},{9,8},{10,11... | collective-permute-start | bytes 1572872 | tf_op jit(solution)/shard_map/ppermute | solution.py:22
  106.4 28.7 %collective-permute-start.12 = (bf16[2,128,1024]{2,1,0:T(8,128)(2,1)}, bf16[2,128,1024]{2,1,0:T(8,128)(2,1)}, u32[]{:S(2)}, u32[]{:S(2)}) collective-permute-start(bf16[2,128,1024]{2,1,0:T(8,128)(2,1)} %collective-permute-done.11.refs_2_), channel_id=1, source_target_pairs={{0,1},{1,0},{2,3},{3,2},{4,5},{5,4},{6,7},{7,6},{8,9},{9,8},{10,11... | collective-permute-start | bytes 1572872 | tf_op jit(solution)/shard_map/ppermute | solution.py:22
  109.9 26.4 %collective-permute-start.8 = (bf16[2,128,1024]{2,1,0:T(8,128)(2,1)}, bf16[2,128,1024]{2,1,0:T(8,128)(2,1)}, u32[]{:S(2)}, u32[]{:S(2)}) collective-permute-start(bf16[2,128,1024]{2,1,0:T(8,128)(2,1)} %collective-permute-done.7.refs_2_), channel_id=1, source_target_pairs={{0,1},{1,0},{2,3},{3,2},{4,5},{5,4},{6,7},{7,6},{8,9},{9,8},{10,11... | collective-permute-start | bytes 1572872 | tf_op jit(solution)/shard_map/ppermute | solution.py:22
  111.1 47.4 %collective-permute-start.24 = (bf16[2,4,64,1024]{3,2,1,0:T(8,128)(2,1)S(1)}, bf16[2,4,64,1024]{3,2,1,0:T(8,128)(2,1)S(1)}, u32[]{:S(2)}, u32[]{:S(2)}) collective-permute-start(bf16[2,4,64,1024]{3,2,1,0:T(8,128)(2,1)S(1)} %collective-permute-done.18.refs_4_), channel_id=1, source_target_pairs={{4,8},{8,12},{5,9},{9,13},{6,10},{10,14},{7,11},{11,15},{20,24},{2... | collective-permute-start | bytes 3145736 | tf_op jit(solution)/shard_map/ppermute | solution.py:79
  120.2 38.9 %collective-permute-start.25 = (bf16[2,4,64,1024]{3,2,1,0:T(8,128)(2,1)}, bf16[2,4,64,1024]{3,2,1,0:T(8,128)(2,1)S(1)}, u32[]{:S(2)}, u32[]{:S(2)}) collective-permute-start(bf16[2,4,64,1024]{3,2,1,0:T(8,128)(2,1)} %collective-permute-done.19.refs_5_), channel_id=1, source_target_pairs={{4,8},{8,12},{5,9},{9,13},{6,10},{10,14},{7,11},{11,15},{20,24},{2... | collective-permute-start | bytes 3145736 | tf_op jit(solution)/shard_map/ppermute | solution.py:79
  121.0 39.1 %collective-permute-start.26 = (bf16[2,4,64,1024]{3,2,1,0:T(8,128)(2,1)S(1)}, bf16[2,4,64,1024]{3,2,1,0:T(8,128)(2,1)S(1)}, u32[]{:S(2)}, u32[]{:S(2)}) collective-permute-start(bf16[2,4,64,1024]{3,2,1,0:T(8,128)(2,1)S(1)} %collective-permute-done.20.refs_6_), channel_id=1, source_target_pairs={{4,0},{8,4},{5,1},{9,5},{6,2},{10,6},{7,3},{11,7},{20,16},{24,20},... | collective-permute-start | bytes 3145736 | tf_op jit(solution)/shard_map/ppermute | solution.py:80
  135.0 41.2 %collective-permute-start.27 = (bf16[2,4,64,1024]{3,2,1,0:T(8,128)(2,1)}, bf16[2,4,64,1024]{3,2,1,0:T(8,128)(2,1)S(1)}, u32[]{:S(2)}, u32[]{:S(2)}) collective-permute-start(bf16[2,4,64,1024]{3,2,1,0:T(8,128)(2,1)} %collective-permute-done.21.refs_7_), channel_id=1, source_target_pairs={{4,0},{8,4},{5,1},{9,5},{6,2},{10,6},{7,3},{11,7},{20,16},{24,20},... | collective-permute-start | bytes 3145736 | tf_op jit(solution)/shard_map/ppermute | solution.py:80
  136.3 25.1 %collective-permute-start.4 = (bf16[2,128,1024]{2,1,0:T(8,128)(2,1)}, bf16[2,128,1024]{2,1,0:T(8,128)(2,1)S(1)}, u32[]{:S(2)}, u32[]{:S(2)}) collective-permute-start(bf16[2,128,1024]{2,1,0:T(8,128)(2,1)} %collective-permute-done.3.refs_2_), channel_id=1, source_target_pairs={{0,1},{1,0},{2,3},{3,2},{4,5},{5,4},{6,7},{7,6},{8,9},{9,8},{10,11... | collective-permute-start | bytes 1572872 | tf_op jit(solution)/shard_map/ppermute | solution.py:22
  158.4 46.1 %collective-permute-start.30 = (bf16[2,4,64,1024]{3,2,1,0:T(8,128)(2,1)S(1)}, bf16[2,4,64,1024]{3,2,1,0:T(8,128)(2,1)S(1)}, u32[]{:S(2)}, u32[]{:S(2)}) collective-permute-start(bf16[2,4,64,1024]{3,2,1,0:T(8,128)(2,1)S(1)} %collective-permute-done.24.refs_4_), channel_id=1, source_target_pairs={{8,12},{9,13},{10,14},{11,15},{24,28},{25,29},{26,30},{27,31}} | collective-permute-start | bytes 3145736 | tf_op jit(solution)/shard_map/ppermute | solution.py:79
  159.2 45.3 %collective-permute-start.31 = (bf16[2,4,64,1024]{3,2,1,0:T(8,128)(2,1)S(1)}, bf16[2,4,64,1024]{3,2,1,0:T(8,128)(2,1)S(1)}, u32[]{:S(2)}, u32[]{:S(2)}) collective-permute-start(bf16[2,4,64,1024]{3,2,1,0:T(8,128)(2,1)S(1)} %collective-permute-done.25.refs_5_), channel_id=1, source_target_pairs={{8,12},{9,13},{10,14},{11,15},{24,28},{25,29},{26,30},{27,31}} | collective-permute-start | bytes 3145736 | tf_op jit(solution)/shard_map/ppermute | solution.py:79
  160.1 44.4 %collective-permute-start.32 = (bf16[2,4,64,1024]{3,2,1,0:T(8,128)(2,1)S(1)}, bf16[2,4,64,1024]{3,2,1,0:T(8,128)(2,1)S(1)}, u32[]{:S(2)}, u32[]{:S(2)}) collective-permute-start(bf16[2,4,64,1024]{3,2,1,0:T(8,128)(2,1)S(1)} %collective-permute-done.26.refs_6_), channel_id=1, source_target_pairs={{4,0},{5,1},{6,2},{7,3},{20,16},{21,17},{22,18},{23,19}} | collective-permute-start | bytes 3145736 | tf_op jit(solution)/shard_map/ppermute | solution.py:80
  193.2 28.7 %collective-permute-start.33 = (bf16[2,4,64,1024]{3,2,1,0:T(8,128)(2,1)S(1)}, bf16[2,4,64,1024]{3,2,1,0:T(8,128)(2,1)S(1)}, u32[]{:S(2)}, u32[]{:S(2)}) collective-permute-start(bf16[2,4,64,1024]{3,2,1,0:T(8,128)(2,1)S(1)} %collective-permute-done.27.refs_7_), channel_id=1, source_target_pairs={{4,0},{5,1},{6,2},{7,3},{20,16},{21,17},{22,18},{23,19}} | collective-permute-start | bytes 3145736 | tf_op jit(solution)/shard_map/ppermute | solution.py:80
  (35 other events, 321.3 us)

commit v3 on v2

v3 whole, which is shorter than its diff:
```python
import jax
import jax.numpy as jnp
from jax import lax
from jax.experimental import pallas as pl
from jax.experimental.pallas import tpu as pltpu
from jax.sharding import PartitionSpec as P

highest = lax.Precision.HIGHEST
f32 = jnp.float32
bf16 = jnp.bfloat16
HEAD_PARTS = 3
VMEM_BYTES = 48 * 1024 * 1024


def round_up(value, step):
    return -(-value // step) * step


def shifted(x, name, shift):
    count = lax.axis_size(name)
    pairs = [(source, (source + shift) % count) for source in range(count)]
    return lax.ppermute(x, name, pairs)


def after(x, others):
    return lax.optimization_barrier((x, others))[0]


def share(x, name):
    return [x] + [shifted(x, name, shift) for shift in range(1, lax.axis_size(name))]


def deal(x, name):
    count = lax.axis_size(name)
    me = lax.axis_index(name)
    pieces = []
    for shift in range(count):
        piece = lax.dynamic_index_in_dim(x, (me + shift) % count, 0, keepdims=False)
        pieces.append(shifted(piece, name, shift) if shift else piece)
    return pieces


def valence_columns(valence, valence_head, selector, core, width, last):
    parts, points, pairs, columns = valence.shape
    head_at = columns - last * width

    def kernel(core_ref, valence_ref, head_ref, selector_ref, out_ref):
        column = lax.broadcasted_iota(jnp.int32, (pairs, width), 1)
        at_last = core_ref[0] == last
        limit = jnp.where(at_last, head_at, width)
        head_column = jnp.where(at_last, head_at, width)
        for point in range(points):
            rows = valence_ref[0, point].astype(f32)
            head = jnp.broadcast_to(head_ref[0, point].astype(f32), (pairs, width))
            rows = jnp.where(column < limit, rows, 0.0)
            rows = jnp.where(column == head_column, head, rows)
            moved = jnp.dot(selector_ref[...], rows.astype(bf16), preferred_element_type=f32)
            out_ref[0, point] = moved.astype(bf16)

    return pl.pallas_call(
        kernel,
        out_shape=jax.ShapeDtypeStruct((parts, points, pairs, width), bf16),
        grid_spec=pltpu.PrefetchScalarGridSpec(
            num_scalar_prefetch=1,
            grid=(parts,),
            in_specs=[
                pl.BlockSpec((1, points, pairs, width), lambda x, core: (x, 0, 0, core[0])),
                pl.BlockSpec((1, points, pairs, 1), lambda x, core: (x, 0, 0, 0)),
                pl.BlockSpec((pairs, pairs), lambda x, core: (0, 0)),
            ],
            out_specs=pl.BlockSpec((1, points, pairs, width), lambda x, core: (x, 0, 0, 0)),
        ),
        compiler_params=pltpu.CompilerParams(vmem_limit_bytes=VMEM_BYTES),
        name="valence_columns",
    )(core.reshape(1), valence, valence_head[..., None], selector)


def along_line(below, above, name, step):
    count = lax.axis_size(name)
    below = lax.ppermute(below, name, [(s, s + 1) for s in range(step - 1, count - 1)])
    above = lax.ppermute(above, name, [(s, s - 1) for s in range(1, count - step + 1)])
    return below, above


def screen_product(places, pieces, right, per_index, half, store, blocks):
    _, deep, width = right.shape
    planes = deep // 2
    rows = per_index * half
    count = len(pieces)
    sources = pieces[0].shape[0]
    bands = 2
    pw_count = count // bands
    points = pw_count * per_index
    tile = min(256, width)

    def kernel(place_ref, *refs):
        piece_refs, right_ref, out_ref, left_ref = refs[:count], refs[count], refs[-2], refs[-1]

        @pl.when((pl.program_id(1) == 0) & (pl.program_id(2) == 0))
        def _():
            for index in range(count):
                start = pl.multiple_of(place_ref[index] * rows, rows)
                left_ref[pl.ds(start, rows), 0:planes] = piece_refs[index][0, 0]
                left_ref[pl.ds(start, rows), planes:deep] = piece_refs[index][0, 1]

        total = jnp.dot(left_ref[...], right_ref[0], preferred_element_type=f32).astype(bf16)
        for pw in range(pw_count):
            for band in range(bands):
                for point in range(per_index):
                    start = (pw * bands + band) * rows + point * half
                    out_ref[pw * per_index + point, band, 0] = total[start : start + half]

    whole = pl.BlockSpec((1, 2, rows, planes), lambda s, x, n, place: (s, 0, 0, 0))
    kept = [] if store is None else [store]
    return pl.pallas_call(
        kernel,
        out_shape=jax.ShapeDtypeStruct((blocks * points, bands, 2, half, width), bf16),
        grid_spec=pltpu.PrefetchScalarGridSpec(
            num_scalar_prefetch=1,
            grid=(sources, 2, width // tile),
            in_specs=[whole] * count
            + [pl.BlockSpec((1, deep, tile), lambda s, x, n, place: (x, 0, n))]
            + [pl.BlockSpec(memory_space=pl.ANY)] * len(kept),
            out_specs=pl.BlockSpec(
                (points, bands, 1, half, tile), lambda s, x, n, place: (place[count + s], 0, x, 0, n)
            ),
            scratch_shapes=[pltpu.VMEM((count * rows, deep), bf16)],
        ),
        input_output_aliases={count + 2: 0} if kept else {},
        compiler_params=pltpu.CompilerParams(vmem_limit_bytes=VMEM_BYTES),
        cost_estimate=pl.CostEstimate(flops=1, bytes_accessed=1, transcendentals=0),
        name="screen_product",
    )(places, *pieces, right, *kept)


def contract(row_ids, sides, owners, store, valences, body, blocks):
    _, bands, _, half, width = store.shape
    _, points, pairs, _ = valences[0].shape
    slots = sides.shape[0]
    group = 4 if points % 4 == 0 else 1
    steps = points // group

    def kernel(row_ref, side_ref, owner_ref, *refs):
        store_refs, valence_refs, out_ref = refs[:group], refs[group : group + len(valences)], refs[-1]
        lane = lax.broadcasted_iota(jnp.int32, (half, 2 * pairs), 1)
        side = side_ref[pl.program_id(0)]
        step = pl.program_id(1)

        def rows_of(valence_ref):
            for index in range(group):
                left = store_refs[index][0].reshape(bands * 2 * half, width)
                right = valence_ref[:, step * group + index].reshape(2 * pairs, width)
                square = lax.dot_general(left, right, (((1,), (1,)), ((), ())), preferred_element_type=f32)
                for band in range(bands):
                    first = square[2 * band * half : (2 * band + 1) * half]
                    second = square[(2 * band + 1) * half : (2 * band + 2) * half]
                    turned = pltpu.roll(second, pairs, 1)
                    total = first + jnp.where(lane < pairs, -turned, turned)
                    out_ref[index, band * half : (band + 1) * half, :] = total

        for place in range(len(valences)):

            @pl.when(side == place)
            def _(place=place):
                rows_of(valence_refs[place])

    def store_spec(index):
        return pl.BlockSpec(
            (1, bands, 2, half, width),
            lambda slot, step, row, side, owner: (row[slot * points + step * group + index], 0, 0, 0, 0),
        )

    whole = pl.BlockSpec((2, points, pairs, width), lambda slot, step, row, side, owner: (0, 0, 0, 0))
    kept = [] if body is None else [body]
    return pl.pallas_call(
        kernel,
        out_shape=jax.ShapeDtypeStruct((blocks * points, bands * half, 2 * pairs), f32),
        grid_spec=pltpu.PrefetchScalarGridSpec(
            num_scalar_prefetch=3,
            grid=(slots, steps),
            in_specs=[store_spec(index) for index in range(group)]
            + [whole] * len(valences)
            + [pl.BlockSpec(memory_space=pl.ANY)] * len(kept),
            out_specs=pl.BlockSpec(
                (group, bands * half, 2 * pairs),
                lambda slot, step, row, side, owner: (owner[slot] * steps + step, 0, 0),
            ),
        ),
        input_output_aliases={3 + group + len(valences): 0} if kept else {},
        compiler_params=pltpu.CompilerParams(vmem_limit_bytes=VMEM_BYTES),
        cost_estimate=pl.CostEstimate(flops=1, bytes_accessed=1, transcendentals=0),
        name="contract",
    )(row_ids, sides, owners, *([store] * group), *valences, *kept)


def on_device(
    conduction,
    conduction_head,
    valence,
    valence_head,
    screened,
    wing_column,
    wing_row,
    head_value,
    partner,
    pair_select,
    neighbors,
    weights,
    counts,
):
    points = conduction.shape[1]
    half = conduction.shape[2]
    pairs = valence.shape[2]
    block, columns = screened.shape[1], screened.shape[2]
    kpt_count, pw_count, band_count = lax.axis_size("kpt"), lax.axis_size("pw"), lax.axis_size("band")
    kpt, pw, band = lax.axis_index("kpt"), lax.axis_index("pw"), lax.axis_index("band")
    per_index = points // pw_count
    rows = per_index * half
    blocks_here = columns // block
    deep = round_up(block + HEAD_PARTS, 128)
    width = round_up(-(-(columns + 1) // band_count), 128)
    last = band_count - 1
    head_at = columns - last * width

    plane = jnp.arange(deep)
    is_head = (plane >= block) & (plane < block + HEAD_PARTS)
    cut = []
    for index in range(blocks_here):
        padded = jnp.pad(
            conduction[..., index * block : (index + 1) * block], ((0, 0), (0, 0), (0, 0), (0, deep - block))
        )
        cut.append(jnp.where(is_head, conduction_head[..., None], padded))
    cut = jnp.stack(cut).reshape(blocks_here, 2, pw_count, rows, deep)
    selector = (pair_select[:, None] == jnp.arange(pairs)[None, :]).astype(bf16)
    own_valence = valence_columns(valence, valence_head, selector, after(band, cut), width, last)

    dealt = deal(jnp.moveaxis(cut, 2, 0), "pw")
    by_owner = []
    for owner in range(pw_count):
        blocks_of = dealt[0]
        for shift in range(1, pw_count):
            blocks_of = jnp.where((pw - owner) % pw_count == shift, dealt[shift], blocks_of)
        by_owner.append(blocks_of)
    by_block = jnp.concatenate(by_owner, axis=0)
    arrived = deal(by_block, "kpt")
    own_block = arrived[0]
    middle = kpt_count // 2 + 1

    screen = jnp.pad(screened, ((0, 0), (0, deep - block), (0, band_count * width - columns)))
    screen = lax.dynamic_slice_in_dim(screen, band * width, width, 2)
    row_part = jnp.pad(wing_row, ((0, 0), (0, band_count * width - columns)))
    row_part = lax.dynamic_slice_in_dim(row_part, band * width, width, 1)
    first_kpt = kpt == 0
    row_part = jnp.where(first_kpt, row_part, 0)
    corner = []
    rest = head_value
    for _ in range(HEAD_PARTS):
        part = lax.reduce_precision(rest, 8, 7)
        corner.append(jnp.where(first_kpt, part, 0.0))
        rest = rest - part
    corner = jnp.stack(corner, axis=1).astype(bf16)
    column_part = jnp.concatenate(
        [lax.dynamic_slice_in_dim(wing_column, kpt * block, block, 1), corner], axis=1
    )
    column_part = jnp.pad(column_part, ((0, 0), (0, deep - block - HEAD_PARTS)))
    has_column = (pw == 0) & (band == last)
    screen = jnp.where(plane[None, :, None] == block, row_part[:, None, :], screen)
    screen = jnp.where(
        (jnp.arange(width)[None, None, :] == head_at) & has_column, column_part[:, :, None], screen
    )
    right = jnp.stack(
        [
            jnp.concatenate([screen[0], screen[1]], axis=0),
            jnp.concatenate([screen[1], -screen[0]], axis=0),
        ]
    )

    places = jnp.stack(
        [
            ((pw - pw_shift) % pw_count) * band_count + (band - band_shift) % band_count
            for pw_shift in range(pw_count)
            for band_shift in range(band_count)
        ]
    ).astype(jnp.int32)

    live = jnp.where(jnp.arange(neighbors.shape[1])[None, :] < counts[:, None], weights, 0.0)
    all_points = kpt_count * points
    point_of_row = jnp.sum(
        jnp.where(partner[None, :] == jnp.arange(all_points)[:, None], jnp.arange(all_points)[None, :], 0), axis=1
    ).astype(jnp.int32)

    line = [along_line(own_valence, own_valence, "kpt", 1)]
    own_pieces = [own for across in share(own_block[None], "pw") for own in share(across, "band")]
    line.append(along_line(*after(line[0], [own_pieces, arrived[1:middle]]), "kpt", 2))

    pieces = [own_pieces]
    groups = [[0], list(range(1, middle)), list(range(middle, kpt_count))]
    for shifts in groups[1:]:
        group = jnp.stack(after([arrived[shift] for shift in shifts], line[0]))
        pieces.append([own for across in share(group, "pw") for own in share(across, "band")])

    store = None
    for index, shifts in enumerate(groups):
        sources = jnp.stack([((kpt - shift) % kpt_count).astype(jnp.int32) for shift in shifts])
        store = screen_product(
            jnp.append(places, sources), pieces[index], right, per_index, half, store, kpt_count
        )
        if index == 0:
            gates = [store, pieces[1:]]
            for step in range(3, kpt_count):
                line.append(along_line(*after(line[-1], gates), "kpt", step))
            right = after(right, line[1])

    lanes = 2 * pairs
    kept = half // pw_count

    def add_blocks(body, sides, owners, valences):
        sides, owners = jnp.stack(sides).astype(jnp.int32), jnp.stack(owners).astype(jnp.int32)
        row_ids = (owners[:, None] * points + jnp.arange(points)[None, :]).reshape(-1)
        row_ids = jnp.take(point_of_row, row_ids, mode="clip")
        return contract(row_ids, sides, owners, store, valences, body, kpt_count)

    body = add_blocks(None, [jnp.zeros((), jnp.int32)], [kpt], [own_valence])
    for step in range(1, kpt_count):
        has_below, has_above = kpt >= step, kpt + step < kpt_count
        if 2 * step < kpt_count:
            sides = [jnp.where(has_below, 0, 2), jnp.where(has_above, 1, 2)]
            owners = [jnp.where(has_below, kpt - step, kpt), jnp.where(has_above, kpt + step, kpt)]
        else:
            sides = [jnp.where(has_below, 0, jnp.where(has_above, 1, 2))]
            owners = [jnp.where(has_below, kpt - step, jnp.where(has_above, kpt + step, kpt))]
        body = add_blocks(body, sides, owners, [*line[step - 1], own_valence])

    match = neighbors[:, :, None] == point_of_row[None, None, :]
    stencil = jnp.sum(jnp.where(match, live[:, :, None], 0.0), axis=1)
    body = body.reshape(all_points, band_count, half, lanes)
    body = sum(deal(jnp.moveaxis(body, 1, 0), "band"))
    body = body.reshape(all_points, pw_count, kept, lanes)
    body = sum(deal(jnp.moveaxis(body, 1, 0), "pw"))
    fine_here = neighbors.shape[0] // kpt_count
    fine = jnp.dot(stencil, body.reshape(all_points, kept * lanes), precision=highest)
    fine = sum(deal(fine.reshape(kpt_count, fine_here, kept, lanes), "kpt"))
    fine = lax.all_gather(fine, "pw", axis=0)
    fine = fine.reshape(pw_count, fine_here, kept, 2, pairs)
    return jnp.transpose(fine, (3, 1, 0, 2, 4)).reshape(2, fine_here, half * pairs)


def solution(mesh):
    return jax.shard_map(
        on_device,
        mesh=mesh,
        in_specs=(
            P("grp", "kpt", "band", "pw"),
            P("grp", "kpt", "band"),
            P("grp", "kpt", None, "pw"),
            P("grp", "kpt", None),
            P("grp", "kpt", "pw"),
            P("grp", None),
            P("grp", "pw"),
            P("grp"),
            P("grp"),
            P(),
            P(),
            P(),
            P(),
        ),
        out_specs=P("grp", "kpt", "band"),
        check_vma=False,
    )
```

time: 252 us -> 251 us (level)
  waiting for transfers between devices: 93 us -> 113 us
  starting transfers between devices: 43.6 us -> 31 us
  local copies, waits for them, and re-layouts: 16.4 us -> 10.8 us
  other arithmetic: 27.3 us -> 23.4 us
  Pallas kernels: 61.3 us -> 64 us
    ppermute x27 -> x18, waiting for transfers between devices: 71.7 us -> 113 us  [shifted(): return lax.ppermute(x, name, pairs)]
    ppermute x6 -> x3, waiting for transfers between devices: 21.2 us -> 0.01 us  [along_line(): lax.ppermute(above, name, [(s, s - 1) for s in range(1, count - step + 1)])]
    ppermute x6 -> x3, starting transfers between devices: 13.6 us -> 8.95 us  [along_line(): lax.ppermute(below, name, [(s, s + 1) for s in range(step - 1, count - 1)])]
    ppermute x27 -> x18, starting transfers between devices: 22.3 us -> 18.1 us  [shifted(): return lax.ppermute(x, name, pairs)]
    pallas_call x5, Pallas kernels: 17.6 us -> 21.8 us  [the longest x4 19.6 us: contract(): pl.pallas_call(kernel, out_shape=jax.ShapeDtypeStruct((blocks * points, b...]
    ppermute x6 -> x3, starting transfers between devices: 7.72 us -> 4.02 us  [along_line(): lax.ppermute(above, name, [(s, s - 1) for s in range(1, count - step + 1)])]
    squeeze x1 -> x0, other arithmetic: 3.27 us -> none  [block_for(): lax.dynamic_index_in_dim(lax.dynamic_index_in_dim(dealt, (pw - owner) % p...]
    neg x1, other arithmetic: 3.12 us -> 0.14 us  [on_device(): -screen[0]]
  transfers between devices with their start and end apart: 39 -> 24, of which waited for: 15 -> 9; matrix products, arithmetic and copies ran while one was open for 15% -> 10% of each run, Pallas kernels for 22% -> 24%
where the time goes in v3:
time: 251 us; the launch traced here: 249 us
  waiting for transfers between devices  113 us (45%)
  Pallas kernels  64 us (25%)
  starting transfers between devices  31 us (12%)
  other arithmetic  23.4 us (9%)
  local copies, waits for them, and re-layouts  10.8 us (4%)
  blocking collectives  6 us (2%)
    ppermute x18, waiting for transfers between devices, shifted(): return lax.ppermute(x, name, pairs)  113 us
    pallas_call x3, Pallas kernels, screen_product(): pl.pallas_call(kernel, out_shape=jax.ShapeDtypeStruct((blocks * points, b...  42.1 us
    pallas_call x4, Pallas kernels, contract(): pl.pallas_call(kernel, out_shape=jax.ShapeDtypeStruct((blocks * points, b...  19.6 us
    ppermute x18, starting transfers between devices, shifted(): return lax.ppermute(x, name, pairs)  18.1 us
    another operation x2, other arithmetic, on_device(): jnp.stack([jnp.concatenate([screen[0], screen[1]], axis=0), jnp.concatena...  11.3 us
    ppermute x3, starting transfers between devices, along_line(): lax.ppermute(below, name, [(s, s + 1) for s in range(step - 1, count - 1)])  8.95 us
    all_gather x1, blocking collectives, on_device(): fine = lax.all_gather(fine, 'pw', axis=0)  6 us
  transfers between devices with their start and end apart: 24, of which 9 were waited for; matrix products, arithmetic and copies ran while one was open for 10% of the time, Pallas kernels for 24%

profile of v3, /device:TPU:0, one launch (start us, length us, event | category | flops | bytes accessed | tf_op | source)
XLA Modules:
  0.0 249.4 jit_solution(13552853851291702898)
XLA Ops:
  5.7 2.9 %collective-permute-start = (bf16[2,2,128,1024]{3,2,1,0:T(8,128)(2,1)}, bf16[2,2,128,1024]{3,2,1,0:T(8,128)(2,1)}, u32[]{:S(2)}, u32[]{:S(2)}) collective-permute-start(bf16[2,2,128,1024]{3,2,1,0:T(8,128)(2,1)} %dynamic-slice_bitcast_fusion), channel_id=1, source_target_pairs={{0,2},{2,0},{1,3},{3,1},{4,6},{6,4},{5,7},{7,5},{8,10},{10,8},{9,1... | collective-permute-start | bytes 3145736 | tf_op jit(solution)/shard_map/ppermute | solution.py:22
  9.0 2.3 valence_columns.1.refs_4_.refs_6_
  11.3 4.8 %collective-permute-start.2 = (bf16[2,8,64,1024]{3,2,1,0:T(8,128)(2,1)S(1)}, bf16[2,8,64,1024]{3,2,1,0:T(8,128)(2,1)}, u32[]{:S(2)}, u32[]{:S(2)}) collective-permute-start(bf16[2,8,64,1024]{3,2,1,0:T(8,128)(2,1)S(1)} %valence_columns.1.refs_4_.refs_6_), channel_id=1, source_target_pairs={{0,4},{4,8},{8,12},{1,5},{5,9},{9,13},{2,6},{6,10},{10,14},{3,7},{... | collective-permute-start | bytes 6291464 | tf_op jit(solution)/shard_map/ppermute | solution.py:80
  17.5 14.7 %collective-permute-done = bf16[2,2,128,1024]{3,2,1,0:T(8,128)(2,1)} collective-permute-done((bf16[2,2,128,1024]{3,2,1,0:T(8,128)(2,1)}, bf16[2,2,128,1024]{3,2,1,0:T(8,128)(2,1)}, u32[]{:S(2)}, u32[]{:S(2)}) %collective-permute-start) | collective-permute-done | bytes 1048608 | tf_op jit(solution)/shard_map/ppermute | solution.py:22
  39.3 2.6 %collective-permute-start.11 = (bf16[2,128,1024]{2,1,0:T(8,128)(2,1)}, bf16[2,128,1024]{2,1,0:T(8,128)(2,1)S(1)}, u32[]{:S(2)}, u32[]{:S(2)}) collective-permute-start(bf16[2,128,1024]{2,1,0:T(8,128)(2,1)} %get-tuple-element.29), channel_id=1, source_target_pairs={{0,8},{4,12},{8,0},{12,4},{1,9},{5,13},{9,1},{13,5},{2,10},{6,14},... | collective-permute-start | bytes 1572872 | tf_op jit(solution)/shard_map/ppermute | solution.py:22
  41.9 36.7 %collective-permute-done.10 = bf16[2,128,1024]{2,1,0:T(8,128)(2,1)S(1)} collective-permute-done((bf16[2,128,1024]{2,1,0:T(8,128)(2,1)}, bf16[2,128,1024]{2,1,0:T(8,128)(2,1)S(1)}, u32[]{:S(2)}, u32[]{:S(2)}) %collective-permute-start.10) | collective-permute-done | bytes 524320 | tf_op jit(solution)/shard_map/ppermute | solution.py:22
  79.1 19.9 %collective-permute-done.11 = bf16[2,128,1024]{2,1,0:T(8,128)(2,1)S(1)} collective-permute-done((bf16[2,128,1024]{2,1,0:T(8,128)(2,1)}, bf16[2,128,1024]{2,1,0:T(8,128)(2,1)S(1)}, u32[]{:S(2)}, u32[]{:S(2)}) %collective-permute-start.11) | collective-permute-done | bytes 524320 | tf_op jit(solution)/shard_map/ppermute | solution.py:22
  105.2 9.0 %collective-permute-done.1 = bf16[2,128,1024]{2,1,0:T(8,128)(2,1)} collective-permute-done((bf16[2,128,1024]{2,1,0:T(8,128)(2,1)}, bf16[2,128,1024]{2,1,0:T(8,128)(2,1)}, u32[]{:S(2)}, u32[]{:S(2)}) %collective-permute-start.1) | collective-permute-done | bytes 524320 | tf_op jit(solution)/shard_map/ppermute | solution.py:22
  114.7 3.3 %fusion.1 = bf16[2,1024,1024]{2,1,0:T(8,128)(2,1)S(1)} fusion(s32[]{:T(128)S(6)} %select_n.259, bf16[2,1000,2000]{2,1,0:T(8,128)(2,1)} %param.17, pred[1024]{0:T(1024)(128)(4,1)S(1)} %get-tuple-element.44, pred[1024]{0:T(1024)(128)(4,1)S(1)} %get-tuple-element.45, bf16[2,1024]{1,0:T(2,128)(2,1)S(1)} %broadcast_select_fusion, bf16[2,1024]{1,0:T(2,128)(2,1)S(1)} %fusion.20), kind=kLoop, calls=%fused_computation.7 | loop fusion | flops 4194304 | bytes 12204548 | tf_op jit(solution)/shard_map/jit(_where)/select_n | solution.py:268
  118.5 16.6 %collective-permute-done.5.refs_2_ = bf16[1,2,128,1024]{3,2,1,0:T(8,128)(2,1)} collective-permute-done((bf16[1,2,128,1024]{3,2,1,0:T(8,128)(2,1)}, bf16[1,2,128,1024]{3,2,1,0:T(8,128)(2,1)}, u32[]{:S(2)}, u32[]{:S(2)}) %collective-permute-start.5) | collective-permute-done | bytes 524320 | tf_op jit(solution)/shard_map/ppermute | solution.py:22
  136.6 3.8 %maximum_bitcast_fusion = (bf16[1,2048,1024]{2,1,0:T(8,128)(2,1)}, bf16[1,2048,1024]{2,1,0:T(8,128)(2,1)}) fusion(bf16[1024,1024]{1,0:T(8,128)(2,1)S(1)} %get-tuple-element.26, bf16[1024,1024]{1,0:T(8,128)(2,1)S(1)} %get-tuple-element.25, bf16[1024,1024]{1,0:T(8,128)(2,1)S(1)} %fusion.29), kind=kLoop, calls=%fused_computation.8 | loop fusion | flops 16777216 | bytes 14680064 | tf_op jit(solution)/shard_map/stack | solution.py:271
  140.4 7.5 %pad_maximum_fusion.refs_4_ = bf16[2,2048,1024]{2,1,0:T(8,128)(2,1)} fusion(bf16[1,2048,1024]{2,1,0:T(8,128)(2,1)} %get-tuple-element.34, bf16[1,2048,1024]{2,1,0:T(8,128)(2,1)} %get-tuple-element.33), kind=kLoop, calls=%fused_computation.4 | loop fusion | flops 4194304 | bytes 16777216 | tf_op jit(solution)/shard_map/stack | solution.py:271
  148.0 11.2 %screen_product.3.refs_5_ = bf16[32,2,2,32,1024]{4,3,2,1,0:T(8,128)(2,1)} custom-call(s32[5]{0:T(128)S(1)} %concatenate.38.place_ref, bf16[1,2,128,1024]{3,2,1,0:T(8,128)(2,1)} %get-tuple-element.31.refs_0_, bf16[1,2,128,1024]{3,2,1,0:T(8,128)(2,1)} %collective-permute-done.7.refs_1_, bf16[1,2,128,1024]{3,2,1,0:T(8,128)(2,1)} %collective-permute-done.8.refs_2_, ...), custom_call_target="tpu_custom_call" | custom-call | flops 1 | bytes 1 | tf_op jit(solution)/shard_map/screen_product/pallas_call | solution.py:115
  166.1 20.0 %screen_product.4.refs_5_ = bf16[32,2,2,32,1024]{4,3,2,1,0:T(8,128)(2,1)} custom-call(s32[6]{0:T(128)S(1)} %concatenate.37.place_ref, bf16[2,2,128,1024]{3,2,1,0:T(8,128)(2,1)S(1)} %pad_maximum_fusion.2.refs_0_, bf16[2,2,128,1024]{3,2,1,0:T(8,128)(2,1)} %collective-permute-done.14.refs_1_, ...), custom_call_target="tpu_custom_call", output_to_operand_aliasing={{}: (6, {})} | custom-call | flops 1 | bytes 1 | tf_op jit(solution)/shard_map/screen_product/pallas_call | solution.py:115
  187.1 11.0 %screen_product.5.refs_0_.refs_1_.refs_2_.refs_3_ = bf16[32,2,2,32,1024]{4,3,2,1,0:T(8,128)(2,1)} custom-call(s32[5]{0:T(128)S(1)} %concatenate.32.place_ref, bf16[1,2,128,1024]{3,2,1,0:T(8,128)(2,1)} %bitcast.18.refs_0_, bf16[1,2,128,1024]{3,2,1,0:T(8,128)(2,1)S(1)} %copy-done.4, ...), custom_call_target="tpu_custom_call", output_to_operand_aliasing={{}: (6, {})} | custom-call | flops 1 | bytes 1 | tf_op jit(solution)/shard_map/screen_product/pallas_call | solution.py:115
  198.1 2.9 %contract.4.refs_7_ = f32[32,64,128]{2,1,0:T(8,128)S(1)} custom-call(s32[8]{0:T(128)S(1)} %gather_fusion.3, s32[1]{0:T(128)} %constant.184.clone.1.side_ref, s32[1]{0:T(128)} %bitcast.41.owner_ref, bf16[32,2,2,32,1024]{4,3,2,1,0:T(8,128)(2,1)} %screen_product.5.refs_0_.refs_1_.refs_2_.refs_3_, ...), custom_call_target="tpu_custom_call" | custom-call | flops 1 | bytes 1 | tf_op jit(solution)/shard_map/contract/pallas_call | solution.py:175
  201.0 6.8 %contract.5.refs_7_ = f32[32,64,128]{2,1,0:T(8,128)S(1)} custom-call(s32[16]{0:T(128)S(1)} %gather_fusion.2, s32[2]{0:T(128)S(1)} %pad_add_fusion.1.side_ref, s32[2]{0:T(128)S(1)} %get-tuple-element.24.owner_ref, bf16[32,2,2,32,1024]{4,3,2,1,0:T(8,128)(2,1)} %screen_product.5.refs_0_.refs_1_.refs_2_.refs_3_, ...), custom_call_target="tpu_custom_call", output_to_operand_aliasing={{}: (10, {})} | custom-call | flops 1 | bytes 1 | tf_op jit(solution)/shard_map/contract/pallas_call | solution.py:175
  207.8 4.9 %contract.6.refs_7_ = f32[32,64,128]{2,1,0:T(8,128)S(1)} custom-call(s32[8]{0:T(128)S(1)} %gather_fusion.1, s32[1]{0:T(128)} %bitcast.34.side_ref, s32[1]{0:T(128)} %bitcast.35.owner_ref, bf16[32,2,2,32,1024]{4,3,2,1,0:T(8,128)(2,1)} %screen_product.5.refs_0_.refs_1_.refs_2_.refs_3_, ...), custom_call_target="tpu_custom_call", output_to_operand_aliasing={{}: (10, {})} | custom-call | flops 1 | bytes 1 | tf_op jit(solution)/shard_map/contract/pallas_call | solution.py:175
  212.8 4.9 %contract.7 = f32[32,64,128]{2,1,0:T(8,128)S(1)} custom-call(s32[8]{0:T(128)S(1)} %gather_fusion, s32[1]{0:T(128)} %bitcast.4.side_ref, s32[1]{0:T(128)} %bitcast.5.owner_ref, bf16[32,2,2,32,1024]{4,3,2,1,0:T(8,128)(2,1)} %screen_product.5.refs_0_.refs_1_.refs_2_.refs_3_, ...), custom_call_target="tpu_custom_call", output_to_operand_aliasing={{}: (10, {})} | custom-call | flops 1 | bytes 1 | tf_op jit(solution)/shard_map/contract/pallas_call | solution.py:175
  220.9 7.8 %collective-permute-done.20 = f32[32,16,128]{2,1,0:T(8,128)S(1)} collective-permute-done((f32[32,16,128]{2,1,0:T(8,128)S(1)}, f32[32,16,128]{2,1,0:T(8,128)S(1)}, u32[]{:S(2)}, u32[]{:S(2)}) %collective-permute-start.20) | collective-permute-done | bytes 262176 | tf_op jit(solution)/shard_map/ppermute | solution.py:22
  229.5 3.4 %collective-permute-start.21 = (f32[16,16,128]{2,1,0:T(8,128)S(1)}, f32[16,16,128]{2,1,0:T(8,128)S(1)}, u32[]{:S(2)}, u32[]{:S(2)}) collective-permute-start(f32[16,16,128]{2,1,0:T(8,128)S(1)} %bitcast.120), channel_id=1, source_target_pairs={{0,4},{4,8},{8,12},{12,0},{1,5},{5,9},{9,13},{13,1},{2,6},{6,10},{... | collective-permute-start | bytes 393224 | tf_op jit(solution)/shard_map/ppermute | solution.py:22
  233.1 2.4 collective-permute-start.23
  237.4 4.6 %collective-permute-done.22 = f32[16,16,128]{2,1,0:T(8,128)S(1)} collective-permute-done((f32[16,16,128]{2,1,0:T(8,128)S(1)}, f32[16,16,128]{2,1,0:T(8,128)S(1)}, u32[]{:S(2)}, u32[]{:S(2)}) %collective-permute-start.22) | collective-permute-done | bytes 131104 | tf_op jit(solution)/shard_map/ppermute | solution.py:22
  242.1 6.0 %all-gather = f32[32,16,128]{2,1,0:T(8,128)S(1)} all-gather(f32[16,16,128]{2,1,0:T(8,128)S(1)} %fusion.12), channel_id=2, replica_groups=mesh['grp'=2,'kpt'=4,'pw'=2,'band'=2] {'pw'}, dimensions={0}, use_global_device_ids=true | all-gather | bytes 393216 | tf_op jit(solution)/shard_map/all_gather | solution.py:343
  (126 shorter events, 38.6 us)
Async XLA Ops:
  5.7 26.4 %collective-permute-start = (bf16[2,2,128,1024]{3,2,1,0:T(8,128)(2,1)}, bf16[2,2,128,1024]{3,2,1,0:T(8,128)(2,1)}, u32[]{:S(2)}, u32[]{:S(2)}) collective-permute-start(bf16[2,2,128,1024]{3,2,1,0:T(8,128)(2,1)} %dynamic-slice_bitcast_fusion), channel_id=1, source_target_pairs={{0,2},{2,0},{1,3},{3,1},{4,6},{6,4},{5,7},{7,5},{8,10},{10,8},{9,1... | collective-permute-start | bytes 3145736 | tf_op jit(solution)/shard_map/ppermute | solution.py:22
  11.3 88.2 %collective-permute-start.2 = (bf16[2,8,64,1024]{3,2,1,0:T(8,128)(2,1)S(1)}, bf16[2,8,64,1024]{3,2,1,0:T(8,128)(2,1)}, u32[]{:S(2)}, u32[]{:S(2)}) collective-permute-start(bf16[2,8,64,1024]{3,2,1,0:T(8,128)(2,1)S(1)} %valence_columns.1.refs_4_.refs_6_), channel_id=1, source_target_pairs={{0,4},{4,8},{8,12},{1,5},{5,9},{9,13},{2,6},{6,10},{10,14},{3,7},{... | collective-permute-start | bytes 6291464 | tf_op jit(solution)/shard_map/ppermute | solution.py:80
  16.1 83.4 %collective-permute-start.3 = (bf16[2,8,64,1024]{3,2,1,0:T(8,128)(2,1)S(1)}, bf16[2,8,64,1024]{3,2,1,0:T(8,128)(2,1)}, u32[]{:S(2)}, u32[]{:S(2)}) collective-permute-start(bf16[2,8,64,1024]{3,2,1,0:T(8,128)(2,1)S(1)} %valence_columns.1.refs_4_.refs_6_), channel_id=1, source_target_pairs={{4,0},{8,4},{12,8},{5,1},{9,5},{13,9},{6,2},{10,6},{14,10},{7,3},{... | collective-permute-start | bytes 6291464 | tf_op jit(solution)/shard_map/ppermute | solution.py:81
  36.0 42.6 %collective-permute-start.10 = (bf16[2,128,1024]{2,1,0:T(8,128)(2,1)}, bf16[2,128,1024]{2,1,0:T(8,128)(2,1)S(1)}, u32[]{:S(2)}, u32[]{:S(2)}) collective-permute-start(bf16[2,128,1024]{2,1,0:T(8,128)(2,1)} %get-tuple-element.32), channel_id=1, source_target_pairs={{0,4},{4,8},{8,12},{12,0},{1,5},{5,9},{9,13},{13,1},{2,6},{6,10},{... | collective-permute-start | bytes 1572872 | tf_op jit(solution)/shard_map/ppermute | solution.py:22
  37.8 40.8 %collective-permute-start.8 = (bf16[1,2,128,1024]{3,2,1,0:T(8,128)(2,1)}, bf16[1,2,128,1024]{3,2,1,0:T(8,128)(2,1)}, u32[]{:S(2)}, u32[]{:S(2)}) collective-permute-start(bf16[1,2,128,1024]{3,2,1,0:T(8,128)(2,1)} %get-tuple-element.31.refs_0_), channel_id=1, source_target_pairs={{0,2},{2,0},{1,3},{3,1},{4,6},{6,4},{5,7},{7,5},{8,10},{10,8},{9,1... | collective-permute-start | bytes 1572872 | tf_op jit(solution)/shard_map/ppermute | solution.py:22
  39.3 59.7 %collective-permute-start.11 = (bf16[2,128,1024]{2,1,0:T(8,128)(2,1)}, bf16[2,128,1024]{2,1,0:T(8,128)(2,1)S(1)}, u32[]{:S(2)}, u32[]{:S(2)}) collective-permute-start(bf16[2,128,1024]{2,1,0:T(8,128)(2,1)} %get-tuple-element.29), channel_id=1, source_target_pairs={{0,8},{4,12},{8,0},{12,4},{1,9},{5,13},{9,1},{13,5},{2,10},{6,14},... | collective-permute-start | bytes 1572872 | tf_op jit(solution)/shard_map/ppermute | solution.py:22
  78.6 23.2 %collective-permute-start.7 = (bf16[1,2,128,1024]{3,2,1,0:T(8,128)(2,1)}, bf16[1,2,128,1024]{3,2,1,0:T(8,128)(2,1)}, u32[]{:S(2)}, u32[]{:S(2)}) collective-permute-start(bf16[1,2,128,1024]{3,2,1,0:T(8,128)(2,1)} %get-tuple-element.31.refs_0_), channel_id=1, source_target_pairs={{0,1},{1,0},{2,3},{3,2},{4,5},{5,4},{6,7},{7,6},{8,9},{9,8},{10,11... | collective-permute-start | bytes 1572872 | tf_op jit(solution)/shard_map/ppermute | solution.py:22
  78.6 23.2 %collective-permute-start.9 = (bf16[1,2,128,1024]{3,2,1,0:T(8,128)(2,1)}, bf16[1,2,128,1024]{3,2,1,0:T(8,128)(2,1)}, u32[]{:S(2)}, u32[]{:S(2)}) collective-permute-start(bf16[1,2,128,1024]{3,2,1,0:T(8,128)(2,1)} %collective-permute-done.8.refs_2_), channel_id=1, source_target_pairs={{0,1},{1,0},{2,3},{3,2},{4,5},{5,4},{6,7},{7,6},{8,9},{9,8},{10,11... | collective-permute-start | bytes 1572872 | tf_op jit(solution)/shard_map/ppermute | solution.py:22
  99.0 15.2 %collective-permute-start.1 = (bf16[2,128,1024]{2,1,0:T(8,128)(2,1)}, bf16[2,128,1024]{2,1,0:T(8,128)(2,1)}, u32[]{:S(2)}, u32[]{:S(2)}) collective-permute-start(bf16[2,128,1024]{2,1,0:T(8,128)(2,1)} %get-tuple-element.30), channel_id=1, source_target_pairs={{0,12},{4,0},{8,4},{12,8},{1,13},{5,1},{9,5},{13,9},{2,14},{6,2},{... | collective-permute-start | bytes 1572872 | tf_op jit(solution)/shard_map/ppermute | solution.py:22
  101.1 34.0 %collective-permute-start.15 = (bf16[2,2,128,1024]{3,2,1,0:T(8,128)(2,1)S(1)}, bf16[2,2,128,1024]{3,2,1,0:T(8,128)(2,1)}, u32[]{:S(2)}, u32[]{:S(2)}) collective-permute-start(bf16[2,2,128,1024]{3,2,1,0:T(8,128)(2,1)S(1)} %pad_maximum_fusion.2.refs_0_), channel_id=1, source_target_pairs={{0,2},{2,0},{1,3},{3,1},{4,6},{6,4},{5,7},{7,5},{8,10},{10,8},{9,1... | collective-permute-start | bytes 3145736 | tf_op jit(solution)/shard_map/ppermute | solution.py:22
  101.8 57.3 %collective-permute-start.12 = (bf16[2,8,64,1024]{3,2,1,0:T(8,128)(2,1)}, bf16[2,8,64,1024]{3,2,1,0:T(8,128)(2,1)}, u32[]{:S(2)}, u32[]{:S(2)}) collective-permute-start(bf16[2,8,64,1024]{3,2,1,0:T(8,128)(2,1)} %collective-permute-done.2.refs_4_), channel_id=1, source_target_pairs={{4,8},{8,12},{5,9},{9,13},{6,10},{10,14},{7,11},{11,15},{20,24},{2... | collective-permute-start | bytes 6291464 | tf_op jit(solution)/shard_map/ppermute | solution.py:80
  103.9 55.3 %collective-permute-start.13 = (bf16[2,8,64,1024]{3,2,1,0:T(8,128)(2,1)}, bf16[2,8,64,1024]{3,2,1,0:T(8,128)(2,1)}, u32[]{:S(2)}, u32[]{:S(2)}) collective-permute-start(bf16[2,8,64,1024]{3,2,1,0:T(8,128)(2,1)} %collective-permute-done.3.refs_5_), channel_id=1, source_target_pairs={{4,0},{8,4},{5,1},{9,5},{6,2},{10,6},{7,3},{11,7},{20,16},{24,20},... | collective-permute-start | bytes 6291464 | tf_op jit(solution)/shard_map/ppermute | solution.py:81
  114.2 20.9 %collective-permute-start.5 = (bf16[1,2,128,1024]{3,2,1,0:T(8,128)(2,1)}, bf16[1,2,128,1024]{3,2,1,0:T(8,128)(2,1)}, u32[]{:S(2)}, u32[]{:S(2)}) collective-permute-start(bf16[1,2,128,1024]{3,2,1,0:T(8,128)(2,1)} %bitcast.18.refs_0_), channel_id=1, source_target_pairs={{0,2},{2,0},{1,3},{3,1},{4,6},{6,4},{5,7},{7,5},{8,10},{10,8},{9,1... | collective-permute-start | bytes 1572872 | tf_op jit(solution)/shard_map/ppermute | solution.py:22
  118.0 17.8 %collective-permute-start.4 = (bf16[1,2,128,1024]{3,2,1,0:T(8,128)(2,1)}, bf16[1,2,128,1024]{3,2,1,0:T(8,128)(2,1)S(1)}, u32[]{:S(2)}, u32[]{:S(2)}) collective-permute-start(bf16[1,2,128,1024]{3,2,1,0:T(8,128)(2,1)} %bitcast.18.refs_0_), channel_id=1, source_target_pairs={{0,1},{1,0},{2,3},{3,2},{4,5},{5,4},{6,7},{7,6},{8,9},{9,8},{10,11... | collective-permute-start | bytes 1572872 | tf_op jit(solution)/shard_map/ppermute | solution.py:22
  135.1 24.0 %collective-permute-start.14 = (bf16[2,2,128,1024]{3,2,1,0:T(8,128)(2,1)S(1)}, bf16[2,2,128,1024]{3,2,1,0:T(8,128)(2,1)}, u32[]{:S(2)}, u32[]{:S(2)}) collective-permute-start(bf16[2,2,128,1024]{3,2,1,0:T(8,128)(2,1)S(1)} %pad_maximum_fusion.2.refs_0_), channel_id=1, source_target_pairs={{0,1},{1,0},{2,3},{3,2},{4,5},{5,4},{6,7},{7,6},{8,9},{9,8},{10,11... | collective-permute-start | bytes 3145736 | tf_op jit(solution)/shard_map/ppermute | solution.py:22
  135.1 24.0 %collective-permute-start.16 = (bf16[2,2,128,1024]{3,2,1,0:T(8,128)(2,1)}, bf16[2,2,128,1024]{3,2,1,0:T(8,128)(2,1)}, u32[]{:S(2)}, u32[]{:S(2)}) collective-permute-start(bf16[2,2,128,1024]{3,2,1,0:T(8,128)(2,1)} %collective-permute-done.15.refs_2_), channel_id=1, source_target_pairs={{0,1},{1,0},{2,3},{3,2},{4,5},{5,4},{6,7},{7,6},{8,9},{9,8},{10,11... | collective-permute-start | bytes 3145736 | tf_op jit(solution)/shard_map/ppermute | solution.py:22
  136.6 22.5 %collective-permute-start.6 = (bf16[1,2,128,1024]{3,2,1,0:T(8,128)(2,1)}, bf16[1,2,128,1024]{3,2,1,0:T(8,128)(2,1)}, u32[]{:S(2)}, u32[]{:S(2)}) collective-permute-start(bf16[1,2,128,1024]{3,2,1,0:T(8,128)(2,1)} %collective-permute-done.5.refs_2_), channel_id=1, source_target_pairs={{0,1},{1,0},{2,3},{3,2},{4,5},{5,4},{6,7},{7,6},{8,9},{9,8},{10,11... | collective-permute-start | bytes 1572872 | tf_op jit(solution)/shard_map/ppermute | solution.py:22
  159.2 53.6 %collective-permute-start.17 = (bf16[2,8,64,1024]{3,2,1,0:T(8,128)(2,1)}, bf16[2,8,64,1024]{3,2,1,0:T(8,128)(2,1)}, u32[]{:S(2)}, u32[]{:S(2)}) collective-permute-start(bf16[2,8,64,1024]{3,2,1,0:T(8,128)(2,1)} %collective-permute-done.12.refs_4_), channel_id=1, source_target_pairs={{8,12},{9,13},{10,14},{11,15},{24,28},{25,29},{26,30},{27,31}} | collective-permute-start | bytes 6291464 | tf_op jit(solution)/shard_map/ppermute | solution.py:80
  161.2 51.5 %collective-permute-start.18 = (bf16[2,8,64,1024]{3,2,1,0:T(8,128)(2,1)}, bf16[2,8,64,1024]{3,2,1,0:T(8,128)(2,1)}, u32[]{:S(2)}, u32[]{:S(2)}) collective-permute-start(bf16[2,8,64,1024]{3,2,1,0:T(8,128)(2,1)} %collective-permute-done.13.refs_5_), channel_id=1, source_target_pairs={{4,0},{5,1},{6,2},{7,3},{20,16},{21,17},{22,18},{23,19}} | collective-permute-start | bytes 6291464 | tf_op jit(solution)/shard_map/ppermute | solution.py:81
  217.8 2.1 collective-permute-start.19
  220.1 8.7 %collective-permute-start.20 = (f32[32,16,128]{2,1,0:T(8,128)S(1)}, f32[32,16,128]{2,1,0:T(8,128)S(1)}, u32[]{:S(2)}, u32[]{:S(2)}) collective-permute-start(f32[32,16,128]{2,1,0:T(8,128)S(1)} %dynamic-slice_bitcast_fusion.2), channel_id=1, source_target_pairs={{0,2},{2,0},{1,3},{3,1},{4,6},{6,4},{5,7},{7,5},{8,10},{10,8},{9,1... | collective-permute-start | bytes 786440 | tf_op jit(solution)/shard_map/ppermute | solution.py:22
  229.5 7.9 %collective-permute-start.21 = (f32[16,16,128]{2,1,0:T(8,128)S(1)}, f32[16,16,128]{2,1,0:T(8,128)S(1)}, u32[]{:S(2)}, u32[]{:S(2)}) collective-permute-start(f32[16,16,128]{2,1,0:T(8,128)S(1)} %bitcast.120), channel_id=1, source_target_pairs={{0,4},{4,8},{8,12},{12,0},{1,5},{5,9},{9,13},{13,1},{2,6},{6,10},{... | collective-permute-start | bytes 393224 | tf_op jit(solution)/shard_map/ppermute | solution.py:22
  232.9 9.1 %collective-permute-start.22 = (f32[16,16,128]{2,1,0:T(8,128)S(1)}, f32[16,16,128]{2,1,0:T(8,128)S(1)}, u32[]{:S(2)}, u32[]{:S(2)}) collective-permute-start(f32[16,16,128]{2,1,0:T(8,128)S(1)} %bitcast.121), channel_id=1, source_target_pairs={{0,8},{4,12},{8,0},{12,4},{1,9},{5,13},{9,1},{13,5},{2,10},{6,14},... | collective-permute-start | bytes 393224 | tf_op jit(solution)/shard_map/ppermute | solution.py:22
  233.1 9.0 %collective-permute-start.23 = (f32[16,16,128]{2,1,0:T(8,128)S(1)}, f32[16,16,128]{2,1,0:T(8,128)S(1)}, u32[]{:S(2)}, u32[]{:S(2)}) collective-permute-start(f32[16,16,128]{2,1,0:T(8,128)S(1)} %bitcast.122), channel_id=1, source_target_pairs={{0,12},{4,0},{8,4},{12,8},{1,13},{5,1},{9,5},{13,9},{2,14},{6,2},{... | collective-permute-start | bytes 393224 | tf_op jit(solution)/shard_map/ppermute | solution.py:22
  (18 other events, 475.5 us)

commit v4 on v3

--- a/solution.py
+++ b/solution.py
@@ -91,7 +91,7 @@
     bands = 2
     pw_count = count // bands
     points = pw_count * per_index
-    tile = min(256, width)
+    tile = 512 if width % 512 == 0 else min(256, width)
 
     def kernel(place_ref, *refs):
         piece_refs, right_ref, out_ref, left_ref = refs[:count], refs[count], refs[-2], refs[-1]
@@ -137,19 +137,18 @@
     _, bands, _, half, width = store.shape
     _, points, pairs, _ = valences[0].shape
     slots = sides.shape[0]
-    group = 4 if points % 4 == 0 else 1
+    group = 2 if points % 2 == 0 else 1
     steps = points // group
 
     def kernel(row_ref, side_ref, owner_ref, *refs):
         store_refs, valence_refs, out_ref = refs[:group], refs[group : group + len(valences)], refs[-1]
         lane = lax.broadcasted_iota(jnp.int32, (half, 2 * pairs), 1)
         side = side_ref[pl.program_id(0)]
-        step = pl.program_id(1)
 
         def rows_of(valence_ref):
             for index in range(group):
                 left = store_refs[index][0].reshape(bands * 2 * half, width)
-                right = valence_ref[:, step * group + index].reshape(2 * pairs, width)
+                right = valence_ref[:, index].reshape(2 * pairs, width)
                 square = lax.dot_general(left, right, (((1,), (1,)), ((), ())), preferred_element_type=f32)
                 for band in range(bands):
                     first = square[2 * band * half : (2 * band + 1) * half]
@@ -170,7 +169,12 @@
             lambda slot, step, row, side, owner: (row[slot * points + step * group + index], 0, 0, 0, 0),
         )
 
-    whole = pl.BlockSpec((2, points, pairs, width), lambda slot, step, row, side, owner: (0, 0, 0, 0))
+    def valence_spec(place):
+        return pl.BlockSpec(
+            (2, group, pairs, width),
+            lambda slot, step, row, side, owner: (0, jnp.where(side[slot] == place, step, 0), 0, 0),
+        )
+
     kept = [] if body is None else [body]
     return pl.pallas_call(
         kernel,
@@ -179,7 +183,7 @@
             num_scalar_prefetch=3,
             grid=(slots, steps),
             in_specs=[store_spec(index) for index in range(group)]
-            + [whole] * len(valences)
+            + [valence_spec(place) for place in range(len(valences))]
             + [pl.BlockSpec(memory_space=pl.ANY)] * len(kept),
             out_specs=pl.BlockSpec(
                 (group, bands * half, 2 * pairs),
@@ -222,6 +226,10 @@
     last = band_count - 1
     head_at = columns - last * width
 
+    selector = (pair_select[:, None] == jnp.arange(pairs)[None, :]).astype(bf16)
+    own_valence = valence_columns(valence, valence_head, selector, band, width, last)
+    line = [along_line(own_valence, own_valence, "kpt", 1)]
+
     plane = jnp.arange(deep)
     is_head = (plane >= block) & (plane < block + HEAD_PARTS)
     cut = []
@@ -231,9 +239,6 @@
         )
         cut.append(jnp.where(is_head, conduction_head[..., None], padded))
     cut = jnp.stack(cut).reshape(blocks_here, 2, pw_count, rows, deep)
-    selector = (pair_select[:, None] == jnp.arange(pairs)[None, :]).astype(bf16)
-    own_valence = valence_columns(valence, valence_head, selector, after(band, cut), width, last)
-
     dealt = deal(jnp.moveaxis(cut, 2, 0), "pw")
     by_owner = []
     for owner in range(pw_count):
@@ -289,27 +294,24 @@
         jnp.where(partner[None, :] == jnp.arange(all_points)[:, None], jnp.arange(all_points)[None, :], 0), axis=1
     ).astype(jnp.int32)
 
-    line = [along_line(own_valence, own_valence, "kpt", 1)]
-    own_pieces = [own for across in share(own_block[None], "pw") for own in share(across, "band")]
-    line.append(along_line(*after(line[0], [own_pieces, arrived[1:middle]]), "kpt", 2))
-
-    pieces = [own_pieces]
-    groups = [[0], list(range(1, middle)), list(range(middle, kpt_count))]
-    for shifts in groups[1:]:
-        group = jnp.stack(after([arrived[shift] for shift in shifts], line[0]))
-        pieces.append([own for across in share(group, "pw") for own in share(across, "band")])
-
-    store = None
-    for index, shifts in enumerate(groups):
+    def spread(group):
+        return [own for across in share(group, "pw") for own in share(across, "band")]
+
+    def product(shifts, pieces, right, store):
         sources = jnp.stack([((kpt - shift) % kpt_count).astype(jnp.int32) for shift in shifts])
-        store = screen_product(
-            jnp.append(places, sources), pieces[index], right, per_index, half, store, kpt_count
-        )
-        if index == 0:
-            gates = [store, pieces[1:]]
-            for step in range(3, kpt_count):
-                line.append(along_line(*after(line[-1], gates), "kpt", step))
-            right = after(right, line[1])
+        where = jnp.append(places, sources)
+        return screen_product(where, pieces, right, per_index, half, store, kpt_count)
+
+    near, far = list(range(1, middle)), list(range(middle, kpt_count))
+    store = product([0], spread(own_block[None]), right, None)
+    line.append(along_line(*after(line[0], store), "kpt", 2))
+    near_group = jnp.stack(after([arrived[shift] for shift in near], [store, line[0]]))
+    near_pieces = spread(near_group)
+    far_pieces = spread(jnp.stack([arrived[shift] for shift in far]))
+    store = product(near, near_pieces, right, store)
+    for step in range(3, kpt_count):
+        line.append(along_line(*after(line[-1], [store, far_pieces]), "kpt", step))
+    store = product(far, far_pieces, after(right, line[1]), store)
 
     lanes = 2 * pairs
     kept = half // pw_count

time: 251 us -> 276 us (1.100)
  waiting for transfers between devices: 113 us -> 143 us
  Pallas kernels: 64 us -> 57.9 us
    ppermute x3, waiting for transfers between devices: 0.01 us -> 18.8 us  [along_line(): lax.ppermute(above, name, [(s, s - 1) for s in range(1, count - step + 1)])]
    ppermute x18, waiting for transfers between devices: 113 us -> 124 us  [shifted(): return lax.ppermute(x, name, pairs)]
    pallas_call x3, Pallas kernels: 42.1 us -> 34.1 us  [screen_product(): pl.pallas_call(kernel, out_shape=jax.ShapeDtypeStruct((blocks * points, b...]
    ppermute x18, starting transfers between devices: 18.1 us -> 13.7 us  [shifted(): return lax.ppermute(x, name, pairs)]
  transfers between devices with their start and end apart: 24 -> 24, of which waited for: 9 -> 11; matrix products, arithmetic and copies ran while one was open for 10% -> 11% of each run, Pallas kernels for 24% -> 19%
where the time goes in v4:
time: 276 us; the launch traced here: 275 us
  waiting for transfers between devices  143 us (52%)
  Pallas kernels  57.9 us (21%)
  starting transfers between devices  28.7 us (10%)
  other arithmetic  25.5 us (9%)
  local copies, waits for them, and re-layouts  13.3 us (5%)
  blocking collectives  5.64 us (2%)
    ppermute x18, waiting for transfers between devices, shifted(): return lax.ppermute(x, name, pairs)  124 us
    pallas_call x3, Pallas kernels, screen_product(): pl.pallas_call(kernel, out_shape=jax.ShapeDtypeStruct((blocks * points, b...  34.1 us
    pallas_call x4, Pallas kernels, contract(): pl.pallas_call(kernel, out_shape=jax.ShapeDtypeStruct((blocks * points, b...  21.5 us
    ppermute x3, waiting for transfers between devices, along_line(): lax.ppermute(above, name, [(s, s - 1) for s in range(1, count - step + 1)])  18.8 us
    ppermute x18, starting transfers between devices, shifted(): return lax.ppermute(x, name, pairs)  13.7 us
    another operation x2, other arithmetic, on_device(): jnp.stack([jnp.concatenate([screen[0], screen[1]], axis=0), jnp.concatena...  11.3 us
    ppermute x3, starting transfers between devices, along_line(): lax.ppermute(below, name, [(s, s + 1) for s in range(step - 1, count - 1)])  11 us
    all_gather x1, blocking collectives, on_device(): fine = lax.all_gather(fine, 'pw', axis=0)  5.64 us
  transfers between devices with their start and end apart: 24, of which 11 were waited for; matrix products, arithmetic and copies ran while one was open for 11% of the time, Pallas kernels for 19%

profile of v4, /device:TPU:0, one launch (start us, length us, event | category | flops | bytes accessed | tf_op | source)
XLA Modules:
  0.0 274.8 jit_solution(787126377058823564)
XLA Ops:
  5.3 6.9 %collective-permute-start.5 = (bf16[2,8,64,1024]{3,2,1,0:T(8,128)(2,1)S(1)}, bf16[2,8,64,1024]{3,2,1,0:T(8,128)(2,1)}, u32[]{:S(2)}, u32[]{:S(2)}) collective-permute-start(bf16[2,8,64,1024]{3,2,1,0:T(8,128)(2,1)S(1)} %valence_columns.1.refs_2_.refs_4_), channel_id=1, source_target_pairs={{0,4},{4,8},{8,12},{1,5},{5,9},{9,13},{2,6},{6,10},{10,14},{3,7},{... | collective-permute-start | bytes 6291464 | tf_op jit(solution)/shard_map/ppermute | solution.py:80
  12.2 2.9 %slice.16 = bf16[2,8,32,1000]{3,2,1,0:T(8,128)(2,1)} slice(bf16[2,8,32,2000]{3,2,1,0:T(8,128)(2,1)} %param.13), slice={[0:2], [0:8], [0:32], [1000:2000]} | slice | bytes 2048000 | tf_op jit(solution)/shard_map/slice | solution.py:238
  21.7 4.7 %fusion.1 = bf16[2,1024,1024]{2,1,0:T(8,128)(2,1)} fusion(s32[]{:T(128)S(6)} %select_n.259, bf16[2,1000,2000]{2,1,0:T(8,128)(2,1)} %param.17, pred[1024]{0:T(1024)(128)(4,1)S(1)} %get-tuple-element.40, pred[1024]{0:T(1024)(128)(4,1)S(1)} %get-tuple-element.41, bf16[2,1024]{1,0:T(2,128)(2,1)S(1)} %broadcast_select_fusion.2, bf16[2,1024]{1,0:T(2,128)(2,1)S(1)} %fusion.24), kind=kLoop, calls=%fused_computation.7 | loop fusion | flops 4194304 | bytes 12204548 | tf_op jit(solution)/shard_map/jit(_where)/select_n | solution.py:273
  26.3 17.8 %collective-permute-done = bf16[2,2,128,1024]{3,2,1,0:T(8,128)(2,1)} collective-permute-done((bf16[2,2,128,1024]{3,2,1,0:T(8,128)(2,1)}, bf16[2,2,128,1024]{3,2,1,0:T(8,128)(2,1)}, u32[]{:S(2)}, u32[]{:S(2)}) %collective-permute-start) | collective-permute-done | bytes 1048608 | tf_op jit(solution)/shard_map/ppermute | solution.py:22
  52.5 7.5 %collective-permute-done.8.refs_2_ = bf16[1,2,128,1024]{3,2,1,0:T(8,128)(2,1)S(1)} collective-permute-done((bf16[1,2,128,1024]{3,2,1,0:T(8,128)(2,1)S(1)}, bf16[1,2,128,1024]{3,2,1,0:T(8,128)(2,1)S(1)}, u32[]{:S(2)}, u32[]{:S(2)}) %collective-permute-start.8) | collective-permute-done | bytes 524320 | tf_op jit(solution)/shard_map/ppermute | solution.py:22
  61.0 3.8 %maximum_bitcast_fusion = (bf16[1,2048,1024]{2,1,0:T(8,128)(2,1)}, bf16[1,2048,1024]{2,1,0:T(8,128)(2,1)}) fusion(bf16[1024,1024]{1,0:T(8,128)(2,1)S(1)} %get-tuple-element.22, bf16[1024,1024]{1,0:T(8,128)(2,1)S(1)} %get-tuple-element.21, bf16[1024,1024]{1,0:T(8,128)(2,1)S(1)} %fusion.33), kind=kLoop, calls=%fused_computation.8 | loop fusion | flops 16777216 | bytes 14680064 | tf_op jit(solution)/shard_map/stack | solution.py:276
  64.9 7.5 %pad_maximum_fusion.refs_4_ = bf16[2,2048,1024]{2,1,0:T(8,128)(2,1)} fusion(bf16[1,2048,1024]{2,1,0:T(8,128)(2,1)} %get-tuple-element.30, bf16[1,2048,1024]{2,1,0:T(8,128)(2,1)} %get-tuple-element.29), kind=kLoop, calls=%fused_computation.4 | loop fusion | flops 4194304 | bytes 16777216 | tf_op jit(solution)/shard_map/stack | solution.py:276
  72.4 8.9 %screen_product.3.refs_5_ = bf16[32,2,2,32,1024]{4,3,2,1,0:T(8,128)(2,1)} custom-call(s32[5]{0:T(128)S(1)} %concatenate.37.place_ref, bf16[1,2,128,1024]{3,2,1,0:T(8,128)(2,1)S(1)} %get-tuple-element.27.refs_0_, bf16[1,2,128,1024]{3,2,1,0:T(8,128)(2,1)S(1)} %copy-done.6, bf16[1,2,128,1024]{3,2,1,0:T(8,128)(2,1)S(1)} %collective-permute-done.8.refs_2_, ...), custom_call_target="tpu_custom_call" | custom-call | flops 1 | bytes 1 | tf_op jit(solution)/shard_map/screen_product/pallas_call | solution.py:115
  81.4 8.2 %collective-permute-done.13 = bf16[2,128,1024]{2,1,0:T(8,128)(2,1)} collective-permute-done((bf16[2,128,1024]{2,1,0:T(8,128)(2,1)}, bf16[2,128,1024]{2,1,0:T(8,128)(2,1)}, u32[]{:S(2)}, u32[]{:S(2)}) %collective-permute-start.13) | collective-permute-done | bytes 524320 | tf_op jit(solution)/shard_map/ppermute | solution.py:22
  95.9 19.1 %collective-permute-done.15.refs_2_ = bf16[2,2,128,1024]{3,2,1,0:T(8,128)(2,1)} collective-permute-done((bf16[2,2,128,1024]{3,2,1,0:T(8,128)(2,1)S(1)}, bf16[2,2,128,1024]{3,2,1,0:T(8,128)(2,1)}, u32[]{:S(2)}, u32[]{:S(2)}) %collective-permute-start.15) | collective-permute-done | bytes 1048608 | tf_op jit(solution)/shard_map/ppermute | solution.py:22
  115.0 42.2 %collective-permute-done.1 = bf16[2,128,1024]{2,1,0:T(8,128)(2,1)} collective-permute-done((bf16[2,128,1024]{2,1,0:T(8,128)(2,1)S(1)}, bf16[2,128,1024]{2,1,0:T(8,128)(2,1)}, u32[]{:S(2)}, u32[]{:S(2)}) %collective-permute-start.1) | collective-permute-done | bytes 524320 | tf_op jit(solution)/shard_map/ppermute | solution.py:22
  157.8 11.1 %collective-permute-done.3.refs_2_ = bf16[1,2,128,1024]{3,2,1,0:T(8,128)(2,1)} collective-permute-done((bf16[1,2,128,1024]{3,2,1,0:T(8,128)(2,1)}, bf16[1,2,128,1024]{3,2,1,0:T(8,128)(2,1)}, u32[]{:S(2)}, u32[]{:S(2)}) %collective-permute-start.3) | collective-permute-done | bytes 524320 | tf_op jit(solution)/shard_map/ppermute | solution.py:22
  171.7 15.8 %screen_product.4.refs_5_ = bf16[32,2,2,32,1024]{4,3,2,1,0:T(8,128)(2,1)} custom-call(s32[6]{0:T(128)S(1)} %concatenate.38.place_ref, bf16[2,2,128,1024]{3,2,1,0:T(8,128)(2,1)S(1)} %pad_maximum_fusion.1.refs_0_, bf16[2,2,128,1024]{3,2,1,0:T(8,128)(2,1)S(1)} %copy-done.4, ...), custom_call_target="tpu_custom_call", output_to_operand_aliasing={{}: (6, {})} | custom-call | flops 1 | bytes 1 | tf_op jit(solution)/shard_map/screen_product/pallas_call | solution.py:115
  194.3 9.4 %screen_product.5.refs_0_.refs_1_ = bf16[32,2,2,32,1024]{4,3,2,1,0:T(8,128)(2,1)} custom-call(s32[5]{0:T(128)S(1)} %concatenate.32.place_ref, bf16[1,2,128,1024]{3,2,1,0:T(8,128)(2,1)} %bitcast.16.refs_0_, bf16[1,2,128,1024]{3,2,1,0:T(8,128)(2,1)} %collective-permute-done.2.refs_1_, ...), custom_call_target="tpu_custom_call", output_to_operand_aliasing={{}: (6, {})} | custom-call | flops 1 | bytes 1 | tf_op jit(solution)/shard_map/screen_product/pallas_call | solution.py:115
  203.6 3.9 %contract.4.refs_5_ = f32[32,64,128]{2,1,0:T(8,128)S(1)} custom-call(s32[8]{0:T(128)S(1)} %gather_fusion.3, s32[1]{0:T(128)} %constant.184.clone.1.side_ref, s32[1]{0:T(128)} %bitcast.41.owner_ref, bf16[32,2,2,32,1024]{4,3,2,1,0:T(8,128)(2,1)} %screen_product.5.refs_0_.refs_1_, bf16[32,2,2,32,1024]{4,3,2,1,0:T(8,128)(2,1)} %screen_product.5.refs_0_.refs_1_, ...), custom_call_target="tpu_custom_call" | custom-call | flops 1 | bytes 1 | tf_op jit(solution)/shard_map/contract/pallas_call | solution.py:179
  207.6 8.2 %contract.5.refs_5_ = f32[32,64,128]{2,1,0:T(8,128)S(1)} custom-call(s32[16]{0:T(128)S(1)} %gather_fusion.2, s32[2]{0:T(128)S(1)} %pad_add_fusion.1.side_ref, s32[2]{0:T(128)S(1)} %get-tuple-element.20.owner_ref, bf16[32,2,2,32,1024]{4,3,2,1,0:T(8,128)(2,1)} %screen_product.5.refs_0_.refs_1_, ...), custom_call_target="tpu_custom_call", output_to_operand_aliasing={{}: (8, {})} | custom-call | flops 1 | bytes 1 | tf_op jit(solution)/shard_map/contract/pallas_call | solution.py:179
  215.7 4.7 %contract.6.refs_5_ = f32[32,64,128]{2,1,0:T(8,128)S(1)} custom-call(s32[8]{0:T(128)S(1)} %gather_fusion.1, s32[1]{0:T(128)} %bitcast.34.side_ref, s32[1]{0:T(128)} %bitcast.35.owner_ref, bf16[32,2,2,32,1024]{4,3,2,1,0:T(8,128)(2,1)} %screen_product.5.refs_0_.refs_1_, ...), custom_call_target="tpu_custom_call", output_to_operand_aliasing={{}: (8, {})} | custom-call | flops 1 | bytes 1 | tf_op jit(solution)/shard_map/contract/pallas_call | solution.py:179
  220.5 18.8 %collective-permute-done.18.refs_3_ = bf16[2,8,64,1024]{3,2,1,0:T(8,128)(2,1)} collective-permute-done((bf16[2,8,64,1024]{3,2,1,0:T(8,128)(2,1)}, bf16[2,8,64,1024]{3,2,1,0:T(8,128)(2,1)}, u32[]{:S(2)}, u32[]{:S(2)}) %collective-permute-start.18) | collective-permute-done | bytes 2097184 | tf_op jit(solution)/shard_map/ppermute | solution.py:81
  239.3 4.7 %contract.7 = f32[32,64,128]{2,1,0:T(8,128)S(1)} custom-call(s32[8]{0:T(128)S(1)} %gather_fusion, s32[1]{0:T(128)} %bitcast.4.side_ref, s32[1]{0:T(128)} %bitcast.5.owner_ref, bf16[32,2,2,32,1024]{4,3,2,1,0:T(8,128)(2,1)} %screen_product.5.refs_0_.refs_1_, ...), custom_call_target="tpu_custom_call", output_to_operand_aliasing={{}: (8, {})} | custom-call | flops 1 | bytes 1 | tf_op jit(solution)/shard_map/contract/pallas_call | solution.py:179
  247.0 7.6 %collective-permute-done.20 = f32[32,16,128]{2,1,0:T(8,128)S(1)} collective-permute-done((f32[32,16,128]{2,1,0:T(8,128)S(1)}, f32[32,16,128]{2,1,0:T(8,128)S(1)}, u32[]{:S(2)}, u32[]{:S(2)}) %collective-permute-start.20) | collective-permute-done | bytes 262176 | tf_op jit(solution)/shard_map/ppermute | solution.py:22
  255.6 3.7 %collective-permute-start.23 = (f32[16,16,128]{2,1,0:T(8,128)S(1)}, f32[16,16,128]{2,1,0:T(8,128)S(1)}, u32[]{:S(2)}, u32[]{:S(2)}) collective-permute-start(f32[16,16,128]{2,1,0:T(8,128)S(1)} %bitcast.125), channel_id=1, source_target_pairs={{0,12},{4,0},{8,4},{12,8},{1,13},{5,1},{9,5},{13,9},{2,14},{6,2},{... | collective-permute-start | bytes 393224 | tf_op jit(solution)/shard_map/ppermute | solution.py:22
  259.3 4.5 %collective-permute-done.21 = f32[16,16,128]{2,1,0:T(8,128)S(1)} collective-permute-done((f32[16,16,128]{2,1,0:T(8,128)S(1)}, f32[16,16,128]{2,1,0:T(8,128)S(1)}, u32[]{:S(2)}, u32[]{:S(2)}) %collective-permute-start.21) | collective-permute-done | bytes 131104 | tf_op jit(solution)/shard_map/ppermute | solution.py:22
  263.8 4.0 %collective-permute-done.22 = f32[16,16,128]{2,1,0:T(8,128)S(1)} collective-permute-done((f32[16,16,128]{2,1,0:T(8,128)S(1)}, f32[16,16,128]{2,1,0:T(8,128)S(1)}, u32[]{:S(2)}, u32[]{:S(2)}) %collective-permute-start.22) | collective-permute-done | bytes 131104 | tf_op jit(solution)/shard_map/ppermute | solution.py:22
  267.9 5.6 %all-gather = f32[32,16,128]{2,1,0:T(8,128)S(1)} all-gather(f32[16,16,128]{2,1,0:T(8,128)S(1)} %fusion.16), channel_id=2, replica_groups=mesh['grp'=2,'kpt'=4,'pw'=2,'band'=2] {'pw'}, dimensions={0}, use_global_device_ids=true | all-gather | bytes 393216 | tf_op jit(solution)/shard_map/all_gather | solution.py:345
  (126 shorter events, 42.8 us)
Async XLA Ops:
  4.0 85.5 %collective-permute-start.6 = (bf16[2,8,64,1024]{3,2,1,0:T(8,128)(2,1)S(1)}, bf16[2,8,64,1024]{3,2,1,0:T(8,128)(2,1)}, u32[]{:S(2)}, u32[]{:S(2)}) collective-permute-start(bf16[2,8,64,1024]{3,2,1,0:T(8,128)(2,1)S(1)} %valence_columns.1.refs_2_.refs_4_), channel_id=1, source_target_pairs={{4,0},{8,4},{12,8},{5,1},{9,5},{13,9},{6,2},{10,6},{14,10},{7,3},{... | collective-permute-start | bytes 6291464 | tf_op jit(solution)/shard_map/ppermute | solution.py:81
  5.3 84.2 %collective-permute-start.5 = (bf16[2,8,64,1024]{3,2,1,0:T(8,128)(2,1)S(1)}, bf16[2,8,64,1024]{3,2,1,0:T(8,128)(2,1)}, u32[]{:S(2)}, u32[]{:S(2)}) collective-permute-start(bf16[2,8,64,1024]{3,2,1,0:T(8,128)(2,1)S(1)} %valence_columns.1.refs_2_.refs_4_), channel_id=1, source_target_pairs={{0,4},{4,8},{8,12},{1,5},{5,9},{9,13},{2,6},{6,10},{10,14},{3,7},{... | collective-permute-start | bytes 6291464 | tf_op jit(solution)/shard_map/ppermute | solution.py:80
  19.2 24.9 %collective-permute-start = (bf16[2,2,128,1024]{3,2,1,0:T(8,128)(2,1)}, bf16[2,2,128,1024]{3,2,1,0:T(8,128)(2,1)}, u32[]{:S(2)}, u32[]{:S(2)}) collective-permute-start(bf16[2,2,128,1024]{3,2,1,0:T(8,128)(2,1)} %fusion.5), channel_id=1, source_target_pairs={{0,2},{2,0},{1,3},{3,1},{4,6},{6,4},{5,7},{7,5},{8,10},{10,8},{9,1... | collective-permute-start | bytes 3145736 | tf_op jit(solution)/shard_map/ppermute | solution.py:22
  47.6 12.5 %collective-permute-start.8 = (bf16[1,2,128,1024]{3,2,1,0:T(8,128)(2,1)S(1)}, bf16[1,2,128,1024]{3,2,1,0:T(8,128)(2,1)S(1)}, u32[]{:S(2)}, u32[]{:S(2)}) collective-permute-start(bf16[1,2,128,1024]{3,2,1,0:T(8,128)(2,1)S(1)} %get-tuple-element.27.refs_0_), channel_id=1, source_target_pairs={{0,2},{2,0},{1,3},{3,1},{4,6},{6,4},{5,7},{7,5},{8,10},{10,8},{9,1... | collective-permute-start | bytes 1572872 | tf_op jit(solution)/shard_map/ppermute | solution.py:22
  49.2 11.0 %collective-permute-start.7 = (bf16[1,2,128,1024]{3,2,1,0:T(8,128)(2,1)S(1)}, bf16[1,2,128,1024]{3,2,1,0:T(8,128)(2,1)S(1)}, u32[]{:S(2)}, u32[]{:S(2)}) collective-permute-start(bf16[1,2,128,1024]{3,2,1,0:T(8,128)(2,1)S(1)} %get-tuple-element.27.refs_0_), channel_id=1, source_target_pairs={{0,1},{1,0},{2,3},{3,2},{4,5},{5,4},{6,7},{7,6},{8,9},{9,8},{10,11... | collective-permute-start | bytes 1572872 | tf_op jit(solution)/shard_map/ppermute | solution.py:22
  49.8 39.7 %collective-permute-start.13 = (bf16[2,128,1024]{2,1,0:T(8,128)(2,1)}, bf16[2,128,1024]{2,1,0:T(8,128)(2,1)}, u32[]{:S(2)}, u32[]{:S(2)}) collective-permute-start(bf16[2,128,1024]{2,1,0:T(8,128)(2,1)} %get-tuple-element.25), channel_id=1, source_target_pairs={{0,8},{4,12},{8,0},{12,4},{1,9},{5,13},{9,1},{13,5},{2,10},{6,14},... | collective-permute-start | bytes 1572872 | tf_op jit(solution)/shard_map/ppermute | solution.py:22
  60.0 29.5 %collective-permute-start.12 = (bf16[2,128,1024]{2,1,0:T(8,128)(2,1)}, bf16[2,128,1024]{2,1,0:T(8,128)(2,1)}, u32[]{:S(2)}, u32[]{:S(2)}) collective-permute-start(bf16[2,128,1024]{2,1,0:T(8,128)(2,1)} %get-tuple-element.28), channel_id=1, source_target_pairs={{0,4},{4,8},{8,12},{12,0},{1,5},{5,9},{9,13},{13,1},{2,6},{6,10},{... | collective-permute-start | bytes 1572872 | tf_op jit(solution)/shard_map/ppermute | solution.py:22
  61.0 11.4 %collective-permute-start.9 = (bf16[1,2,128,1024]{3,2,1,0:T(8,128)(2,1)S(1)}, bf16[1,2,128,1024]{3,2,1,0:T(8,128)(2,1)}, u32[]{:S(2)}, u32[]{:S(2)}) collective-permute-start(bf16[1,2,128,1024]{3,2,1,0:T(8,128)(2,1)S(1)} %collective-permute-done.8.refs_2_), channel_id=1, source_target_pairs={{0,1},{1,0},{2,3},{3,2},{4,5},{5,4},{6,7},{7,6},{8,9},{9,8},{10,11... | collective-permute-start | bytes 1572872 | tf_op jit(solution)/shard_map/ppermute | solution.py:22
  90.8 24.2 %collective-permute-start.15 = (bf16[2,2,128,1024]{3,2,1,0:T(8,128)(2,1)S(1)}, bf16[2,2,128,1024]{3,2,1,0:T(8,128)(2,1)}, u32[]{:S(2)}, u32[]{:S(2)}) collective-permute-start(bf16[2,2,128,1024]{3,2,1,0:T(8,128)(2,1)S(1)} %pad_maximum_fusion.1.refs_0_), channel_id=1, source_target_pairs={{0,2},{2,0},{1,3},{3,1},{4,6},{6,4},{5,7},{7,5},{8,10},{10,8},{9,1... | collective-permute-start | bytes 3145736 | tf_op jit(solution)/shard_map/ppermute | solution.py:22
  92.4 95.1 %collective-permute-start.10 = (bf16[2,8,64,1024]{3,2,1,0:T(8,128)(2,1)}, bf16[2,8,64,1024]{3,2,1,0:T(8,128)(2,1)}, u32[]{:S(2)}, u32[]{:S(2)}) collective-permute-start(bf16[2,8,64,1024]{3,2,1,0:T(8,128)(2,1)} %collective-permute-done.5.refs_2_), channel_id=1, source_target_pairs={{4,8},{8,12},{5,9},{9,13},{6,10},{10,14},{7,11},{11,15},{20,24},{2... | collective-permute-start | bytes 6291464 | tf_op jit(solution)/shard_map/ppermute | solution.py:80
  94.4 93.0 %collective-permute-start.11 = (bf16[2,8,64,1024]{3,2,1,0:T(8,128)(2,1)}, bf16[2,8,64,1024]{3,2,1,0:T(8,128)(2,1)}, u32[]{:S(2)}, u32[]{:S(2)}) collective-permute-start(bf16[2,8,64,1024]{3,2,1,0:T(8,128)(2,1)} %collective-permute-done.6.refs_3_), channel_id=1, source_target_pairs={{4,0},{8,4},{5,1},{9,5},{6,2},{10,6},{7,3},{11,7},{20,16},{24,20},... | collective-permute-start | bytes 6291464 | tf_op jit(solution)/shard_map/ppermute | solution.py:81
  95.7 61.5 %collective-permute-start.1 = (bf16[2,128,1024]{2,1,0:T(8,128)(2,1)S(1)}, bf16[2,128,1024]{2,1,0:T(8,128)(2,1)}, u32[]{:S(2)}, u32[]{:S(2)}) collective-permute-start(bf16[2,128,1024]{2,1,0:T(8,128)(2,1)S(1)} %copy-done.9), channel_id=1, source_target_pairs={{0,12},{4,0},{8,4},{12,8},{1,13},{5,1},{9,5},{13,9},{2,14},{6,2},{... | collective-permute-start | bytes 1572872 | tf_op jit(solution)/shard_map/ppermute | solution.py:22
  95.8 73.1 %collective-permute-start.14 = (bf16[2,2,128,1024]{3,2,1,0:T(8,128)(2,1)S(1)}, bf16[2,2,128,1024]{3,2,1,0:T(8,128)(2,1)S(1)}, u32[]{:S(2)}, u32[]{:S(2)}) collective-permute-start(bf16[2,2,128,1024]{3,2,1,0:T(8,128)(2,1)S(1)} %pad_maximum_fusion.1.refs_0_), channel_id=1, source_target_pairs={{0,1},{1,0},{2,3},{3,2},{4,5},{5,4},{6,7},{7,6},{8,9},{9,8},{10,11... | collective-permute-start | bytes 3145736 | tf_op jit(solution)/shard_map/ppermute | solution.py:22
  115.0 55.4 %collective-permute-start.16 = (bf16[2,2,128,1024]{3,2,1,0:T(8,128)(2,1)}, bf16[2,2,128,1024]{3,2,1,0:T(8,128)(2,1)}, u32[]{:S(2)}, u32[]{:S(2)}) collective-permute-start(bf16[2,2,128,1024]{3,2,1,0:T(8,128)(2,1)} %collective-permute-done.15.refs_2_), channel_id=1, source_target_pairs={{0,1},{1,0},{2,3},{3,2},{4,5},{5,4},{6,7},{7,6},{8,9},{9,8},{10,11... | collective-permute-start | bytes 3145736 | tf_op jit(solution)/shard_map/ppermute | solution.py:22
  157.3 11.6 %collective-permute-start.3 = (bf16[1,2,128,1024]{3,2,1,0:T(8,128)(2,1)}, bf16[1,2,128,1024]{3,2,1,0:T(8,128)(2,1)}, u32[]{:S(2)}, u32[]{:S(2)}) collective-permute-start(bf16[1,2,128,1024]{3,2,1,0:T(8,128)(2,1)} %bitcast.16.refs_0_), channel_id=1, source_target_pairs={{0,2},{2,0},{1,3},{3,1},{4,6},{6,4},{5,7},{7,5},{8,10},{10,8},{9,1... | collective-permute-start | bytes 1572872 | tf_op jit(solution)/shard_map/ppermute | solution.py:22
  168.8 18.6 %collective-permute-start.2 = (bf16[1,2,128,1024]{3,2,1,0:T(8,128)(2,1)}, bf16[1,2,128,1024]{3,2,1,0:T(8,128)(2,1)}, u32[]{:S(2)}, u32[]{:S(2)}) collective-permute-start(bf16[1,2,128,1024]{3,2,1,0:T(8,128)(2,1)} %bitcast.16.refs_0_), channel_id=1, source_target_pairs={{0,1},{1,0},{2,3},{3,2},{4,5},{5,4},{6,7},{7,6},{8,9},{9,8},{10,11... | collective-permute-start | bytes 1572872 | tf_op jit(solution)/shard_map/ppermute | solution.py:22
  169.8 17.6 %collective-permute-start.4 = (bf16[1,2,128,1024]{3,2,1,0:T(8,128)(2,1)}, bf16[1,2,128,1024]{3,2,1,0:T(8,128)(2,1)}, u32[]{:S(2)}, u32[]{:S(2)}) collective-permute-start(bf16[1,2,128,1024]{3,2,1,0:T(8,128)(2,1)} %collective-permute-done.3.refs_2_), channel_id=1, source_target_pairs={{0,1},{1,0},{2,3},{3,2},{4,5},{5,4},{6,7},{7,6},{8,9},{9,8},{10,11... | collective-permute-start | bytes 1572872 | tf_op jit(solution)/shard_map/ppermute | solution.py:22
  187.5 33.0 %collective-permute-start.17 = (bf16[2,8,64,1024]{3,2,1,0:T(8,128)(2,1)}, bf16[2,8,64,1024]{3,2,1,0:T(8,128)(2,1)}, u32[]{:S(2)}, u32[]{:S(2)}) collective-permute-start(bf16[2,8,64,1024]{3,2,1,0:T(8,128)(2,1)} %collective-permute-done.10.refs_2_), channel_id=1, source_target_pairs={{8,12},{9,13},{10,14},{11,15},{24,28},{25,29},{26,30},{27,31}} | collective-permute-start | bytes 6291464 | tf_op jit(solution)/shard_map/ppermute | solution.py:80
  189.5 49.7 %collective-permute-start.18 = (bf16[2,8,64,1024]{3,2,1,0:T(8,128)(2,1)}, bf16[2,8,64,1024]{3,2,1,0:T(8,128)(2,1)}, u32[]{:S(2)}, u32[]{:S(2)}) collective-permute-start(bf16[2,8,64,1024]{3,2,1,0:T(8,128)(2,1)} %collective-permute-done.11.refs_3_), channel_id=1, source_target_pairs={{4,0},{5,1},{6,2},{7,3},{20,16},{21,17},{22,18},{23,19}} | collective-permute-start | bytes 6291464 | tf_op jit(solution)/shard_map/ppermute | solution.py:81
  244.1 2.0 collective-permute-start.19
  246.2 8.4 %collective-permute-start.20 = (f32[32,16,128]{2,1,0:T(8,128)S(1)}, f32[32,16,128]{2,1,0:T(8,128)S(1)}, u32[]{:S(2)}, u32[]{:S(2)}) collective-permute-start(f32[32,16,128]{2,1,0:T(8,128)S(1)} %dynamic-slice_bitcast_fusion.1), channel_id=1, source_target_pairs={{0,2},{2,0},{1,3},{3,1},{4,6},{6,4},{5,7},{7,5},{8,10},{10,8},{9,1... | collective-permute-start | bytes 786440 | tf_op jit(solution)/shard_map/ppermute | solution.py:22
  255.5 8.3 %collective-permute-start.21 = (f32[16,16,128]{2,1,0:T(8,128)S(1)}, f32[16,16,128]{2,1,0:T(8,128)S(1)}, u32[]{:S(2)}, u32[]{:S(2)}) collective-permute-start(f32[16,16,128]{2,1,0:T(8,128)S(1)} %bitcast.127), channel_id=1, source_target_pairs={{0,4},{4,8},{8,12},{12,0},{1,5},{5,9},{9,13},{13,1},{2,6},{6,10},{... | collective-permute-start | bytes 393224 | tf_op jit(solution)/shard_map/ppermute | solution.py:22
  255.5 12.3 %collective-permute-start.22 = (f32[16,16,128]{2,1,0:T(8,128)S(1)}, f32[16,16,128]{2,1,0:T(8,128)S(1)}, u32[]{:S(2)}, u32[]{:S(2)}) collective-permute-start(f32[16,16,128]{2,1,0:T(8,128)S(1)} %bitcast.126), channel_id=1, source_target_pairs={{0,8},{4,12},{8,0},{12,4},{1,9},{5,13},{9,1},{13,5},{2,10},{6,14},... | collective-permute-start | bytes 393224 | tf_op jit(solution)/shard_map/ppermute | solution.py:22
  255.6 12.2 %collective-permute-start.23 = (f32[16,16,128]{2,1,0:T(8,128)S(1)}, f32[16,16,128]{2,1,0:T(8,128)S(1)}, u32[]{:S(2)}, u32[]{:S(2)}) collective-permute-start(f32[16,16,128]{2,1,0:T(8,128)S(1)} %bitcast.125), channel_id=1, source_target_pairs={{0,12},{4,0},{8,4},{12,8},{1,13},{5,1},{9,5},{13,9},{2,14},{6,2},{... | collective-permute-start | bytes 393224 | tf_op jit(solution)/shard_map/ppermute | solution.py:22
  (18 other events, 389.3 us)

commit v5 on v4

--- a/solution.py
+++ b/solution.py
@@ -226,27 +226,28 @@
     last = band_count - 1
     head_at = columns - last * width
 
+    halves = jnp.moveaxis(conduction.reshape(2, pw_count, per_index, half, columns), 1, 0)
+    first = halves if pw_count == 1 else lax.dynamic_index_in_dim(halves, (pw + 1) % pw_count, 0, keepdims=False)
+    dealt = deal(halves, "pw")
+
     selector = (pair_select[:, None] == jnp.arange(pairs)[None, :]).astype(bf16)
-    own_valence = valence_columns(valence, valence_head, selector, band, width, last)
+    own_valence = valence_columns(valence, valence_head, selector, after(band, first), width, last)
     line = [along_line(own_valence, own_valence, "kpt", 1)]
 
     plane = jnp.arange(deep)
     is_head = (plane >= block) & (plane < block + HEAD_PARTS)
-    cut = []
-    for index in range(blocks_here):
-        padded = jnp.pad(
-            conduction[..., index * block : (index + 1) * block], ((0, 0), (0, 0), (0, 0), (0, deep - block))
-        )
-        cut.append(jnp.where(is_head, conduction_head[..., None], padded))
-    cut = jnp.stack(cut).reshape(blocks_here, 2, pw_count, rows, deep)
-    dealt = deal(jnp.moveaxis(cut, 2, 0), "pw")
-    by_owner = []
+    heads = lax.dynamic_slice_in_dim(conduction_head, pw * per_index, per_index, 1)
+    by_block = []
     for owner in range(pw_count):
-        blocks_of = dealt[0]
+        whole = dealt[0]
         for shift in range(1, pw_count):
-            blocks_of = jnp.where((pw - owner) % pw_count == shift, dealt[shift], blocks_of)
-        by_owner.append(blocks_of)
-    by_block = jnp.concatenate(by_owner, axis=0)
+            whole = jnp.where((pw - owner) % pw_count == shift, dealt[shift], whole)
+        for index in range(blocks_here):
+            cut = jnp.pad(
+                whole[..., index * block : (index + 1) * block], ((0, 0), (0, 0), (0, 0), (0, deep - block))
+            )
+            by_block.append(jnp.where(is_head, heads[..., None], cut).reshape(2, rows, deep))
+    by_block = jnp.stack(by_block)
     arrived = deal(by_block, "kpt")
     own_block = arrived[0]
     middle = kpt_count // 2 + 1
@@ -304,9 +305,9 @@
 
     near, far = list(range(1, middle)), list(range(middle, kpt_count))
     store = product([0], spread(own_block[None]), right, None)
-    line.append(along_line(*after(line[0], store), "kpt", 2))
     near_group = jnp.stack(after([arrived[shift] for shift in near], [store, line[0]]))
     near_pieces = spread(near_group)
+    line.append(along_line(*after(line[0], [store, near_group, [arrived[shift] for shift in far]]), "kpt", 2))
     far_pieces = spread(jnp.stack([arrived[shift] for shift in far]))
     store = product(near, near_pieces, right, store)
     for step in range(3, kpt_count):
@@ -316,13 +317,20 @@
     lanes = 2 * pairs
     kept = half // pw_count
 
-    def add_blocks(body, sides, owners, valences):
-        sides, owners = jnp.stack(sides).astype(jnp.int32), jnp.stack(owners).astype(jnp.int32)
+    def add_blocks(body, sides, owners, valences, targets, blocks):
+        sides, owners = jnp.stack(sides).astype(jnp.int32), jnp.stack(owners)
+        targets = jnp.stack(targets).astype(jnp.int32)
         row_ids = (owners[:, None] * points + jnp.arange(points)[None, :]).reshape(-1)
         row_ids = jnp.take(point_of_row, row_ids, mode="clip")
-        return contract(row_ids, sides, owners, store, valences, body, kpt_count)
-
-    body = add_blocks(None, [jnp.zeros((), jnp.int32)], [kpt], [own_valence])
+        return contract(row_ids, sides, targets, store, valences, body, blocks)
+
+    def summed(body):
+        body = body.reshape(-1, band_count, half, lanes)
+        body = sum(deal(jnp.moveaxis(body, 1, 0), "band"))
+        body = body.reshape(-1, pw_count, kept, lanes)
+        return sum(deal(jnp.moveaxis(body, 1, 0), "pw")).reshape(-1, kept * lanes)
+
+    body = add_blocks(None, [jnp.zeros((), jnp.int32)], [kpt], [own_valence], [kpt], kpt_count)
     for step in range(1, kpt_count):
         has_below, has_above = kpt >= step, kpt + step < kpt_count
         if 2 * step < kpt_count:
@@ -331,16 +339,20 @@
         else:
             sides = [jnp.where(has_below, 0, jnp.where(has_above, 1, 2))]
             owners = [jnp.where(has_below, kpt - step, jnp.where(has_above, kpt + step, kpt))]
-        body = add_blocks(body, sides, owners, [*line[step - 1], own_valence])
+        valences = [*line[step - 1], own_valence]
+        if step < kpt_count - 1:
+            body = add_blocks(body, sides, owners, valences, owners, kpt_count)
+    early = summed(body)
+    last_owner = owners[-1]
+    late = summed(add_blocks(None, sides[-1:], owners[-1:], valences, [jnp.zeros((), jnp.int32)], 1))
 
     match = neighbors[:, :, None] == point_of_row[None, None, :]
     stencil = jnp.sum(jnp.where(match, live[:, :, None], 0.0), axis=1)
-    body = body.reshape(all_points, band_count, half, lanes)
-    body = sum(deal(jnp.moveaxis(body, 1, 0), "band"))
-    body = body.reshape(all_points, pw_count, kept, lanes)
-    body = sum(deal(jnp.moveaxis(body, 1, 0), "pw"))
+    is_late = jnp.arange(all_points) // points == last_owner
+    fine = jnp.dot(stencil, jnp.where(is_late[:, None], 0.0, early), precision=highest)
+    late_stencil = lax.dynamic_slice_in_dim(stencil, last_owner * points, points, 1)
+    fine = fine + jnp.dot(late_stencil, late, precision=highest)
     fine_here = neighbors.shape[0] // kpt_count
-    fine = jnp.dot(stencil, body.reshape(all_points, kept * lanes), precision=highest)
     fine = sum(deal(fine.reshape(kpt_count, fine_here, kept, lanes), "kpt"))
     fine = lax.all_gather(fine, "pw", axis=0)
     fine = fine.reshape(pw_count, fine_here, kept, 2, pairs)

time: 276 us -> 246 us (0.89)
  waiting for transfers between devices: 143 us -> 114 us
  other arithmetic: 25.5 us -> 18.3 us
  starting transfers between devices: 28.7 us -> 33.2 us
    ppermute x18 -> x20, waiting for transfers between devices: 124 us -> 88.7 us  [shifted(): return lax.ppermute(x, name, pairs)]
    ppermute x3, waiting for transfers between devices: 18.8 us -> 25.4 us  [along_line(): lax.ppermute(above, name, [(s, s - 1) for s in range(1, count - step + 1)])]
    ppermute x18 -> x20, starting transfers between devices: 13.7 us -> 19.1 us  [shifted(): return lax.ppermute(x, name, pairs)]
    squeeze x2 -> x7, local copies, waits for them, and re-layouts: 0.07 us -> 3.78 us  [deal(): piece = lax.dynamic_index_in_dim(x, (me + shift) % count, 0, keepdims=False)]
    select_n x1, other arithmetic: 4.65 us -> 1.67 us  [on_device(): jnp.where((jnp.arange(width)[None, None, :] == head_at) & has_column, col...]
    squeeze x2 -> x0, other arithmetic: 2.82 us -> none  [deal(): piece = lax.dynamic_index_in_dim(x, (me + shift) % count, 0, keepdims=False)]
  transfers between devices with their start and end apart: 24 -> 26, of which waited for: 11 -> 12; matrix products, arithmetic and copies ran while one was open for 11% -> 10% of each run, Pallas kernels for 19% -> 24%
where the time goes in v5:
time: 246 us; the launch traced here: 245 us
  waiting for transfers between devices  114 us (46%)
  Pallas kernels  57.9 us (24%)
  starting transfers between devices  33.2 us (13%)
  other arithmetic  18.3 us (7%)
  local copies, waits for them, and re-layouts  14.4 us (6%)
  blocking collectives  5.65 us (2%)
    ppermute x20, waiting for transfers between devices, shifted(): return lax.ppermute(x, name, pairs)  88.7 us
    pallas_call x3, Pallas kernels, screen_product(): pl.pallas_call(kernel, out_shape=jax.ShapeDtypeStruct((blocks * points, b...  34.1 us
    ppermute x3, waiting for transfers between devices, along_line(): lax.ppermute(above, name, [(s, s - 1) for s in range(1, count - step + 1)])  25.4 us
    pallas_call x4, Pallas kernels, contract(): pl.pallas_call(kernel, out_shape=jax.ShapeDtypeStruct((blocks * points, b...  21.5 us
    ppermute x20, starting transfers between devices, shifted(): return lax.ppermute(x, name, pairs)  19.1 us
    another operation x2, other arithmetic, on_device(): jnp.stack([jnp.concatenate([screen[0], screen[1]], axis=0), jnp.concatena...  11.3 us
    ppermute x3, starting transfers between devices, along_line(): lax.ppermute(below, name, [(s, s + 1) for s in range(step - 1, count - 1)])  10 us
    all_gather x1, blocking collectives, on_device(): fine = lax.all_gather(fine, 'pw', axis=0)  5.65 us
  transfers between devices with their start and end apart: 26, of which 12 were waited for; matrix products, arithmetic and copies ran while one was open for 10% of the time, Pallas kernels for 24%

profile of v5, /device:TPU:0, one launch (start us, length us, event | category | flops | bytes accessed | tf_op | source)
XLA Modules:
  0.0 245.5 jit_solution(10027311934175606778)
XLA Ops:
  2.4 2.9 %collective-permute-start = (bf16[2,4,32,2000]{3,2,1,0:T(8,128)(2,1)}, bf16[2,4,32,2000]{3,2,1,0:T(8,128)(2,1)S(1)}, u32[]{:S(2)}, u32[]{:S(2)}) collective-permute-start(bf16[2,4,32,2000]{3,2,1,0:T(8,128)(2,1)} %dynamic-slice_bitcast_fusion), channel_id=1, source_target_pairs={{0,2},{2,0},{1,3},{3,1},{4,6},{6,4},{5,7},{7,5},{8,10},{10,8},{9,1... | collective-permute-start | bytes 3072008 | tf_op jit(solution)/shard_map/ppermute | solution.py:22
  10.7 5.9 %collective-permute-start.5 = (bf16[2,8,64,1024]{3,2,1,0:T(8,128)(2,1)S(1)}, bf16[2,8,64,1024]{3,2,1,0:T(8,128)(2,1)}, u32[]{:S(2)}, u32[]{:S(2)}) collective-permute-start(bf16[2,8,64,1024]{3,2,1,0:T(8,128)(2,1)S(1)} %valence_columns.1.refs_2_.refs_4_), channel_id=1, source_target_pairs={{0,4},{4,8},{8,12},{1,5},{5,9},{9,13},{2,6},{6,10},{10,14},{3,7},{... | collective-permute-start | bytes 6291464 | tf_op jit(solution)/shard_map/ppermute | solution.py:80
  17.2 11.5 %collective-permute-done = bf16[2,4,32,2000]{3,2,1,0:T(8,128)(2,1)S(1)} collective-permute-done((bf16[2,4,32,2000]{3,2,1,0:T(8,128)(2,1)}, bf16[2,4,32,2000]{3,2,1,0:T(8,128)(2,1)S(1)}, u32[]{:S(2)}, u32[]{:S(2)}) %collective-permute-start) | collective-permute-done | bytes 1024032 | tf_op jit(solution)/shard_map/ppermute | solution.py:22
  36.9 9.2 %collective-permute-done.8.refs_2_ = bf16[1,2,128,1024]{3,2,1,0:T(8,128)(2,1)S(1)} collective-permute-done((bf16[1,2,128,1024]{3,2,1,0:T(8,128)(2,1)S(1)}, bf16[1,2,128,1024]{3,2,1,0:T(8,128)(2,1)S(1)}, u32[]{:S(2)}, u32[]{:S(2)}) %collective-permute-start.8) | collective-permute-done | bytes 524320 | tf_op jit(solution)/shard_map/ppermute | solution.py:22
  46.3 2.6 %collective-permute-start.11 = (bf16[2,128,1024]{2,1,0:T(8,128)(2,1)}, bf16[2,128,1024]{2,1,0:T(8,128)(2,1)}, u32[]{:S(2)}, u32[]{:S(2)}) collective-permute-start(bf16[2,128,1024]{2,1,0:T(8,128)(2,1)} %get-tuple-element.27), channel_id=1, source_target_pairs={{0,8},{4,12},{8,0},{12,4},{1,9},{5,13},{9,1},{13,5},{2,10},{6,14},... | collective-permute-start | bytes 1572872 | tf_op jit(solution)/shard_map/ppermute | solution.py:22
  51.2 3.8 %maximum_bitcast_fusion = (bf16[1,2048,1024]{2,1,0:T(8,128)(2,1)}, bf16[1,2048,1024]{2,1,0:T(8,128)(2,1)}) fusion(bf16[1024,1024]{1,0:T(8,128)(2,1)S(1)} %get-tuple-element.24, bf16[1024,1024]{1,0:T(8,128)(2,1)S(1)} %get-tuple-element.23, bf16[1024,1024]{1,0:T(8,128)(2,1)S(1)} %fusion.32), kind=kLoop, calls=%fused_computation.8 | loop fusion | flops 16777216 | bytes 14680064 | tf_op jit(solution)/shard_map/stack | solution.py:277
  57.2 7.5 %pad_maximum_fusion.refs_4_ = bf16[2,2048,1024]{2,1,0:T(8,128)(2,1)} fusion(bf16[1,2048,1024]{2,1,0:T(8,128)(2,1)} %get-tuple-element.32, bf16[1,2048,1024]{2,1,0:T(8,128)(2,1)} %get-tuple-element.31), kind=kLoop, calls=%fused_computation.4 | loop fusion | flops 4194304 | bytes 16777216 | tf_op jit(solution)/shard_map/stack | solution.py:277
  65.9 8.9 %screen_product.3.refs_5_ = bf16[32,2,2,32,1024]{4,3,2,1,0:T(8,128)(2,1)} custom-call(s32[5]{0:T(128)S(1)} %concatenate.32.place_ref, bf16[1,2,128,1024]{3,2,1,0:T(8,128)(2,1)S(1)} %get-tuple-element.29.refs_0_, bf16[1,2,128,1024]{3,2,1,0:T(8,128)(2,1)S(1)} %copy-done.6, bf16[1,2,128,1024]{3,2,1,0:T(8,128)(2,1)S(1)} %collective-permute-done.8.refs_2_, ...), custom_call_target="tpu_custom_call" | custom-call | flops 1 | bytes 1 | tf_op jit(solution)/shard_map/screen_product/pallas_call | solution.py:115
  74.8 19.9 %collective-permute-done.11 = bf16[2,128,1024]{2,1,0:T(8,128)(2,1)} collective-permute-done((bf16[2,128,1024]{2,1,0:T(8,128)(2,1)}, bf16[2,128,1024]{2,1,0:T(8,128)(2,1)}, u32[]{:S(2)}, u32[]{:S(2)}) %collective-permute-start.11) | collective-permute-done | bytes 524320 | tf_op jit(solution)/shard_map/ppermute | solution.py:22
  100.0 18.4 %collective-permute-done.15.refs_2_ = bf16[2,2,128,1024]{3,2,1,0:T(8,128)(2,1)} collective-permute-done((bf16[2,2,128,1024]{3,2,1,0:T(8,128)(2,1)S(1)}, bf16[2,2,128,1024]{3,2,1,0:T(8,128)(2,1)}, u32[]{:S(2)}, u32[]{:S(2)}) %collective-permute-start.15) | collective-permute-done | bytes 1048608 | tf_op jit(solution)/shard_map/ppermute | solution.py:22
  118.9 14.1 %collective-permute-done.3.refs_2_ = bf16[1,2,128,1024]{3,2,1,0:T(8,128)(2,1)} collective-permute-done((bf16[1,2,128,1024]{3,2,1,0:T(8,128)(2,1)}, bf16[1,2,128,1024]{3,2,1,0:T(8,128)(2,1)}, u32[]{:S(2)}, u32[]{:S(2)}) %collective-permute-start.3) | collective-permute-done | bytes 524320 | tf_op jit(solution)/shard_map/ppermute | solution.py:22
  135.9 15.8 %screen_product.4.refs_5_ = bf16[32,2,2,32,1024]{4,3,2,1,0:T(8,128)(2,1)} custom-call(s32[6]{0:T(128)S(1)} %concatenate.33.place_ref, bf16[2,2,128,1024]{3,2,1,0:T(8,128)(2,1)S(1)} %pad_maximum_fusion.2.refs_0_, bf16[2,2,128,1024]{3,2,1,0:T(8,128)(2,1)S(1)} %copy-done.4, ...), custom_call_target="tpu_custom_call", output_to_operand_aliasing={{}: (6, {})} | custom-call | flops 1 | bytes 1 | tf_op jit(solution)/shard_map/screen_product/pallas_call | solution.py:115
  151.8 8.0 %collective-permute-done.13.refs_3_ = bf16[2,8,64,1024]{3,2,1,0:T(8,128)(2,1)} collective-permute-done((bf16[2,8,64,1024]{3,2,1,0:T(8,128)(2,1)}, bf16[2,8,64,1024]{3,2,1,0:T(8,128)(2,1)}, u32[]{:S(2)}, u32[]{:S(2)}) %collective-permute-start.13) | collective-permute-done | bytes 2097184 | tf_op jit(solution)/shard_map/ppermute | solution.py:81
  165.7 9.4 %screen_product.5.refs_0_.refs_1_ = bf16[32,2,2,32,1024]{4,3,2,1,0:T(8,128)(2,1)} custom-call(s32[5]{0:T(128)S(1)} %concatenate.28.place_ref, bf16[1,2,128,1024]{3,2,1,0:T(8,128)(2,1)} %bitcast.16.refs_0_, bf16[1,2,128,1024]{3,2,1,0:T(8,128)(2,1)} %collective-permute-done.2.refs_1_, ...), custom_call_target="tpu_custom_call", output_to_operand_aliasing={{}: (6, {})} | custom-call | flops 1 | bytes 1 | tf_op jit(solution)/shard_map/screen_product/pallas_call | solution.py:115
  175.1 3.9 %contract.4.refs_5_ = f32[32,64,128]{2,1,0:T(8,128)S(1)} custom-call(s32[8]{0:T(128)S(1)} %gather_fusion.2, s32[1]{0:T(128)} %constant.224.clone.1.side_ref.owner_ref, s32[1]{0:T(128)} %bitcast.38.owner_ref, bf16[32,2,2,32,1024]{4,3,2,1,0:T(8,128)(2,1)} %screen_product.5.refs_0_.refs_1_, bf16[32,2,2,32,1024]{4,3,2,1,0:T(8,128)(2,1)} %screen_product.5.refs_0_.refs_1_, ...), custom_call_target="tpu_custom_call" | custom-call | flops 1 | bytes 1 | tf_op jit(solution)/shard_map/contract/pallas_call | solution.py:179
  179.1 8.2 %contract.5.refs_5_ = f32[32,64,128]{2,1,0:T(8,128)S(1)} custom-call(s32[16]{0:T(128)S(1)} %gather_fusion.1, s32[2]{0:T(128)S(1)} %pad_add_fusion.1.side_ref, s32[2]{0:T(128)S(1)} %get-tuple-element.22.owner_ref, bf16[32,2,2,32,1024]{4,3,2,1,0:T(8,128)(2,1)} %screen_product.5.refs_0_.refs_1_, ...), custom_call_target="tpu_custom_call", output_to_operand_aliasing={{}: (8, {})} | custom-call | flops 1 | bytes 1 | tf_op jit(solution)/shard_map/contract/pallas_call | solution.py:179
  187.3 4.7 %contract.6 = f32[32,64,128]{2,1,0:T(8,128)S(1)} custom-call(s32[8]{0:T(128)S(1)} %gather_fusion, s32[1]{0:T(128)} %bitcast.1.side_ref, s32[1]{0:T(128)} %bitcast.2.owner_ref, bf16[32,2,2,32,1024]{4,3,2,1,0:T(8,128)(2,1)} %screen_product.5.refs_0_.refs_1_, ...), custom_call_target="tpu_custom_call", output_to_operand_aliasing={{}: (8, {})} | custom-call | flops 1 | bytes 1 | tf_op jit(solution)/shard_map/contract/pallas_call | solution.py:179
  196.5 17.4 %collective-permute-done.20.refs_3_ = bf16[2,8,64,1024]{3,2,1,0:T(8,128)(2,1)} collective-permute-done((bf16[2,8,64,1024]{3,2,1,0:T(8,128)(2,1)}, bf16[2,8,64,1024]{3,2,1,0:T(8,128)(2,1)}, u32[]{:S(2)}, u32[]{:S(2)}) %collective-permute-start.20) | collective-permute-done | bytes 2097184 | tf_op jit(solution)/shard_map/ppermute | solution.py:81
  213.9 4.7 %contract.7 = f32[8,64,128]{2,1,0:T(8,128)S(1)} custom-call(s32[8]{0:T(128)S(1)} %gather_fusion.3, s32[1]{0:T(128)} %bitcast.46.side_ref, s32[1]{0:T(128)} %constant.224.clone.1.side_ref.owner_ref, bf16[32,2,2,32,1024]{4,3,2,1,0:T(8,128)(2,1)} %screen_product.5.refs_0_.refs_1_, bf16[32,2,2,32,1024]{4,3,2,1,0:T(8,128)(2,1)} %screen_product.5.refs_0_.refs_1_, ...), custom_call_target="tpu_custom_call" | custom-call | flops 1 | bytes 1 | tf_op jit(solution)/shard_map/contract/pallas_call | solution.py:179
  221.4 3.0 %collective-permute-done.22 = f32[8,16,128]{2,1,0:T(8,128)S(1)} collective-permute-done((f32[8,16,128]{2,1,0:T(8,128)S(1)}, f32[8,16,128]{2,1,0:T(8,128)S(1)}, u32[]{:S(2)}, u32[]{:S(2)}) %collective-permute-start.22) | collective-permute-done | bytes 65568 | tf_op jit(solution)/shard_map/ppermute | solution.py:22
  225.3 3.8 %collective-permute-start.25 = (f32[16,16,128]{2,1,0:T(8,128)S(1)}, f32[16,16,128]{2,1,0:T(8,128)S(1)}, u32[]{:S(2)}, u32[]{:S(2)}) collective-permute-start(f32[16,16,128]{2,1,0:T(8,128)S(1)} %get-tuple-element.34), channel_id=1, source_target_pairs={{0,12},{4,0},{8,4},{12,8},{1,13},{5,1},{9,5},{13,9},{2,14},{6,2},{... | collective-permute-start | bytes 393224 | tf_op jit(solution)/shard_map/ppermute | solution.py:22
  229.1 4.5 %collective-permute-done.23 = f32[16,16,128]{2,1,0:T(8,128)S(1)} collective-permute-done((f32[16,16,128]{2,1,0:T(8,128)S(1)}, f32[16,16,128]{2,1,0:T(8,128)S(1)}, u32[]{:S(2)}, u32[]{:S(2)}) %collective-permute-start.23) | collective-permute-done | bytes 131104 | tf_op jit(solution)/shard_map/ppermute | solution.py:22
  233.6 4.9 %collective-permute-done.24 = f32[16,16,128]{2,1,0:T(8,128)S(1)} collective-permute-done((f32[16,16,128]{2,1,0:T(8,128)S(1)}, f32[16,16,128]{2,1,0:T(8,128)S(1)}, u32[]{:S(2)}, u32[]{:S(2)}) %collective-permute-start.24) | collective-permute-done | bytes 131104 | tf_op jit(solution)/shard_map/ppermute | solution.py:22
  238.6 5.7 %all-gather = f32[32,16,128]{2,1,0:T(8,128)S(1)} all-gather(f32[16,16,128]{2,1,0:T(8,128)S(1)} %fusion.8), channel_id=2, replica_groups=mesh['grp'=2,'kpt'=4,'pw'=2,'band'=2] {'pw'}, dimensions={0}, use_global_device_ids=true | all-gather | bytes 393216 | tf_op jit(solution)/shard_map/all_gather | solution.py:357
  (135 shorter events, 46.1 us)
Async XLA Ops:
  2.4 26.3 %collective-permute-start = (bf16[2,4,32,2000]{3,2,1,0:T(8,128)(2,1)}, bf16[2,4,32,2000]{3,2,1,0:T(8,128)(2,1)S(1)}, u32[]{:S(2)}, u32[]{:S(2)}) collective-permute-start(bf16[2,4,32,2000]{3,2,1,0:T(8,128)(2,1)} %dynamic-slice_bitcast_fusion), channel_id=1, source_target_pairs={{0,2},{2,0},{1,3},{3,1},{4,6},{6,4},{5,7},{7,5},{8,10},{10,8},{9,1... | collective-permute-start | bytes 3072008 | tf_op jit(solution)/shard_map/ppermute | solution.py:22
  9.3 85.4 %collective-permute-start.6 = (bf16[2,8,64,1024]{3,2,1,0:T(8,128)(2,1)S(1)}, bf16[2,8,64,1024]{3,2,1,0:T(8,128)(2,1)}, u32[]{:S(2)}, u32[]{:S(2)}) collective-permute-start(bf16[2,8,64,1024]{3,2,1,0:T(8,128)(2,1)S(1)} %valence_columns.1.refs_2_.refs_4_), channel_id=1, source_target_pairs={{4,0},{8,4},{12,8},{5,1},{9,5},{13,9},{6,2},{10,6},{14,10},{7,3},{... | collective-permute-start | bytes 6291464 | tf_op jit(solution)/shard_map/ppermute | solution.py:81
  10.7 84.0 %collective-permute-start.5 = (bf16[2,8,64,1024]{3,2,1,0:T(8,128)(2,1)S(1)}, bf16[2,8,64,1024]{3,2,1,0:T(8,128)(2,1)}, u32[]{:S(2)}, u32[]{:S(2)}) collective-permute-start(bf16[2,8,64,1024]{3,2,1,0:T(8,128)(2,1)S(1)} %valence_columns.1.refs_2_.refs_4_), channel_id=1, source_target_pairs={{0,4},{4,8},{8,12},{1,5},{5,9},{9,13},{2,6},{6,10},{10,14},{3,7},{... | collective-permute-start | bytes 6291464 | tf_op jit(solution)/shard_map/ppermute | solution.py:80
  32.9 13.2 %collective-permute-start.8 = (bf16[1,2,128,1024]{3,2,1,0:T(8,128)(2,1)S(1)}, bf16[1,2,128,1024]{3,2,1,0:T(8,128)(2,1)S(1)}, u32[]{:S(2)}, u32[]{:S(2)}) collective-permute-start(bf16[1,2,128,1024]{3,2,1,0:T(8,128)(2,1)S(1)} %get-tuple-element.29.refs_0_), channel_id=1, source_target_pairs={{0,2},{2,0},{1,3},{3,1},{4,6},{6,4},{5,7},{7,5},{8,10},{10,8},{9,1... | collective-permute-start | bytes 1572872 | tf_op jit(solution)/shard_map/ppermute | solution.py:22
  36.3 12.5 %collective-permute-start.7 = (bf16[1,2,128,1024]{3,2,1,0:T(8,128)(2,1)S(1)}, bf16[1,2,128,1024]{3,2,1,0:T(8,128)(2,1)S(1)}, u32[]{:S(2)}, u32[]{:S(2)}) collective-permute-start(bf16[1,2,128,1024]{3,2,1,0:T(8,128)(2,1)S(1)} %get-tuple-element.29.refs_0_), channel_id=1, source_target_pairs={{0,1},{1,0},{2,3},{3,2},{4,5},{5,4},{6,7},{7,6},{8,9},{9,8},{10,11... | collective-permute-start | bytes 1572872 | tf_op jit(solution)/shard_map/ppermute | solution.py:22
  46.1 8.9 %collective-permute-start.9 = (bf16[1,2,128,1024]{3,2,1,0:T(8,128)(2,1)S(1)}, bf16[1,2,128,1024]{3,2,1,0:T(8,128)(2,1)}, u32[]{:S(2)}, u32[]{:S(2)}) collective-permute-start(bf16[1,2,128,1024]{3,2,1,0:T(8,128)(2,1)S(1)} %collective-permute-done.8.refs_2_), channel_id=1, source_target_pairs={{0,1},{1,0},{2,3},{3,2},{4,5},{5,4},{6,7},{7,6},{8,9},{9,8},{10,11... | collective-permute-start | bytes 1572872 | tf_op jit(solution)/shard_map/ppermute | solution.py:22
  46.3 48.4 %collective-permute-start.11 = (bf16[2,128,1024]{2,1,0:T(8,128)(2,1)}, bf16[2,128,1024]{2,1,0:T(8,128)(2,1)}, u32[]{:S(2)}, u32[]{:S(2)}) collective-permute-start(bf16[2,128,1024]{2,1,0:T(8,128)(2,1)} %get-tuple-element.27), channel_id=1, source_target_pairs={{0,8},{4,12},{8,0},{12,4},{1,9},{5,13},{9,1},{13,5},{2,10},{6,14},... | collective-permute-start | bytes 1572872 | tf_op jit(solution)/shard_map/ppermute | solution.py:22
  49.6 45.0 %collective-permute-start.10 = (bf16[2,128,1024]{2,1,0:T(8,128)(2,1)}, bf16[2,128,1024]{2,1,0:T(8,128)(2,1)}, u32[]{:S(2)}, u32[]{:S(2)}) collective-permute-start(bf16[2,128,1024]{2,1,0:T(8,128)(2,1)} %get-tuple-element.28), channel_id=1, source_target_pairs={{0,4},{4,8},{8,12},{12,0},{1,5},{5,9},{9,13},{13,1},{2,6},{6,10},{... | collective-permute-start | bytes 1572872 | tf_op jit(solution)/shard_map/ppermute | solution.py:22
  55.0 41.6 %collective-permute-start.1 = (bf16[2,128,1024]{2,1,0:T(8,128)(2,1)}, bf16[2,128,1024]{2,1,0:T(8,128)(2,1)}, u32[]{:S(2)}, u32[]{:S(2)}) collective-permute-start(bf16[2,128,1024]{2,1,0:T(8,128)(2,1)} %get-tuple-element.30), channel_id=1, source_target_pairs={{0,12},{4,0},{8,4},{12,8},{1,13},{5,1},{9,5},{13,9},{2,14},{6,2},{... | collective-permute-start | bytes 1572872 | tf_op jit(solution)/shard_map/ppermute | solution.py:22
  96.0 22.4 %collective-permute-start.15 = (bf16[2,2,128,1024]{3,2,1,0:T(8,128)(2,1)S(1)}, bf16[2,2,128,1024]{3,2,1,0:T(8,128)(2,1)}, u32[]{:S(2)}, u32[]{:S(2)}) collective-permute-start(bf16[2,2,128,1024]{3,2,1,0:T(8,128)(2,1)S(1)} %pad_maximum_fusion.2.refs_0_), channel_id=1, source_target_pairs={{0,2},{2,0},{1,3},{3,1},{4,6},{6,4},{5,7},{7,5},{8,10},{10,8},{9,1... | collective-permute-start | bytes 3145736 | tf_op jit(solution)/shard_map/ppermute | solution.py:22
  96.6 55.1 %collective-permute-start.12 = (bf16[2,8,64,1024]{3,2,1,0:T(8,128)(2,1)}, bf16[2,8,64,1024]{3,2,1,0:T(8,128)(2,1)}, u32[]{:S(2)}, u32[]{:S(2)}) collective-permute-start(bf16[2,8,64,1024]{3,2,1,0:T(8,128)(2,1)} %collective-permute-done.5.refs_2_), channel_id=1, source_target_pairs={{4,8},{8,12},{5,9},{9,13},{6,10},{10,14},{7,11},{11,15},{20,24},{2... | collective-permute-start | bytes 6291464 | tf_op jit(solution)/shard_map/ppermute | solution.py:80
  98.7 61.1 %collective-permute-start.13 = (bf16[2,8,64,1024]{3,2,1,0:T(8,128)(2,1)}, bf16[2,8,64,1024]{3,2,1,0:T(8,128)(2,1)}, u32[]{:S(2)}, u32[]{:S(2)}) collective-permute-start(bf16[2,8,64,1024]{3,2,1,0:T(8,128)(2,1)} %collective-permute-done.6.refs_3_), channel_id=1, source_target_pairs={{4,0},{8,4},{5,1},{9,5},{6,2},{10,6},{7,3},{11,7},{20,16},{24,20},... | collective-permute-start | bytes 6291464 | tf_op jit(solution)/shard_map/ppermute | solution.py:81
  99.9 33.1 %collective-permute-start.14 = (bf16[2,2,128,1024]{3,2,1,0:T(8,128)(2,1)S(1)}, bf16[2,2,128,1024]{3,2,1,0:T(8,128)(2,1)S(1)}, u32[]{:S(2)}, u32[]{:S(2)}) collective-permute-start(bf16[2,2,128,1024]{3,2,1,0:T(8,128)(2,1)S(1)} %pad_maximum_fusion.2.refs_0_), channel_id=1, source_target_pairs={{0,1},{1,0},{2,3},{3,2},{4,5},{5,4},{6,7},{7,6},{8,9},{9,8},{10,11... | collective-permute-start | bytes 3145736 | tf_op jit(solution)/shard_map/ppermute | solution.py:22
  118.4 16.3 %collective-permute-start.16 = (bf16[2,2,128,1024]{3,2,1,0:T(8,128)(2,1)}, bf16[2,2,128,1024]{3,2,1,0:T(8,128)(2,1)}, u32[]{:S(2)}, u32[]{:S(2)}) collective-permute-start(bf16[2,2,128,1024]{3,2,1,0:T(8,128)(2,1)} %collective-permute-done.15.refs_2_), channel_id=1, source_target_pairs={{0,1},{1,0},{2,3},{3,2},{4,5},{5,4},{6,7},{7,6},{8,9},{9,8},{10,11... | collective-permute-start | bytes 3145736 | tf_op jit(solution)/shard_map/ppermute | solution.py:22
  118.4 14.7 %collective-permute-start.3 = (bf16[1,2,128,1024]{3,2,1,0:T(8,128)(2,1)}, bf16[1,2,128,1024]{3,2,1,0:T(8,128)(2,1)}, u32[]{:S(2)}, u32[]{:S(2)}) collective-permute-start(bf16[1,2,128,1024]{3,2,1,0:T(8,128)(2,1)} %bitcast.16.refs_0_), channel_id=1, source_target_pairs={{0,2},{2,0},{1,3},{3,1},{4,6},{6,4},{5,7},{7,5},{8,10},{10,8},{9,1... | collective-permute-start | bytes 1572872 | tf_op jit(solution)/shard_map/ppermute | solution.py:22
  133.1 18.7 %collective-permute-start.2 = (bf16[1,2,128,1024]{3,2,1,0:T(8,128)(2,1)}, bf16[1,2,128,1024]{3,2,1,0:T(8,128)(2,1)}, u32[]{:S(2)}, u32[]{:S(2)}) collective-permute-start(bf16[1,2,128,1024]{3,2,1,0:T(8,128)(2,1)} %bitcast.16.refs_0_), channel_id=1, source_target_pairs={{0,1},{1,0},{2,3},{3,2},{4,5},{5,4},{6,7},{7,6},{8,9},{9,8},{10,11... | collective-permute-start | bytes 1572872 | tf_op jit(solution)/shard_map/ppermute | solution.py:22
  134.0 17.7 %collective-permute-start.4 = (bf16[1,2,128,1024]{3,2,1,0:T(8,128)(2,1)}, bf16[1,2,128,1024]{3,2,1,0:T(8,128)(2,1)}, u32[]{:S(2)}, u32[]{:S(2)}) collective-permute-start(bf16[1,2,128,1024]{3,2,1,0:T(8,128)(2,1)} %collective-permute-done.3.refs_2_), channel_id=1, source_target_pairs={{0,1},{1,0},{2,3},{3,2},{4,5},{5,4},{6,7},{7,6},{8,9},{9,8},{10,11... | collective-permute-start | bytes 1572872 | tf_op jit(solution)/shard_map/ppermute | solution.py:22
  159.7 36.7 %collective-permute-start.19 = (bf16[2,8,64,1024]{3,2,1,0:T(8,128)(2,1)}, bf16[2,8,64,1024]{3,2,1,0:T(8,128)(2,1)}, u32[]{:S(2)}, u32[]{:S(2)}) collective-permute-start(bf16[2,8,64,1024]{3,2,1,0:T(8,128)(2,1)} %collective-permute-done.12.refs_2_), channel_id=1, source_target_pairs={{8,12},{9,13},{10,14},{11,15},{24,28},{25,29},{26,30},{27,31}} | collective-permute-start | bytes 6291464 | tf_op jit(solution)/shard_map/ppermute | solution.py:80
  161.8 52.1 %collective-permute-start.20 = (bf16[2,8,64,1024]{3,2,1,0:T(8,128)(2,1)}, bf16[2,8,64,1024]{3,2,1,0:T(8,128)(2,1)}, u32[]{:S(2)}, u32[]{:S(2)}) collective-permute-start(bf16[2,8,64,1024]{3,2,1,0:T(8,128)(2,1)} %collective-permute-done.13.refs_3_), channel_id=1, source_target_pairs={{4,0},{5,1},{6,2},{7,3},{20,16},{21,17},{22,18},{23,19}} | collective-permute-start | bytes 6291464 | tf_op jit(solution)/shard_map/ppermute | solution.py:81
  194.2 24.6 %collective-permute-start.18 = (f32[32,16,128]{2,1,0:T(8,128)S(1)}, f32[32,16,128]{2,1,0:T(8,128)S(1)}, u32[]{:S(2)}, u32[]{:S(2)}) collective-permute-start(f32[32,16,128]{2,1,0:T(8,128)S(1)} %dynamic-slice_bitcast_fusion.5), channel_id=1, source_target_pairs={{0,2},{2,0},{1,3},{3,1},{4,6},{6,4},{5,7},{7,5},{8,10},{10,8},{9,1... | collective-permute-start | bytes 786440 | tf_op jit(solution)/shard_map/ppermute | solution.py:22
  220.1 4.3 %collective-permute-start.22 = (f32[8,16,128]{2,1,0:T(8,128)S(1)}, f32[8,16,128]{2,1,0:T(8,128)S(1)}, u32[]{:S(2)}, u32[]{:S(2)}) collective-permute-start(f32[8,16,128]{2,1,0:T(8,128)S(1)} %dynamic-slice_bitcast_fusion.10), channel_id=1, source_target_pairs={{0,2},{2,0},{1,3},{3,1},{4,6},{6,4},{5,7},{7,5},{8,10},{10,8},{9,1... | collective-permute-start | bytes 196616 | tf_op jit(solution)/shard_map/ppermute | solution.py:22
  225.2 8.4 %collective-permute-start.23 = (f32[16,16,128]{2,1,0:T(8,128)S(1)}, f32[16,16,128]{2,1,0:T(8,128)S(1)}, u32[]{:S(2)}, u32[]{:S(2)}) collective-permute-start(f32[16,16,128]{2,1,0:T(8,128)S(1)} %get-tuple-element.33), channel_id=1, source_target_pairs={{0,4},{4,8},{8,12},{12,0},{1,5},{5,9},{9,13},{13,1},{2,6},{6,10},{... | collective-permute-start | bytes 393224 | tf_op jit(solution)/shard_map/ppermute | solution.py:22
  225.3 8.3 %collective-permute-start.25 = (f32[16,16,128]{2,1,0:T(8,128)S(1)}, f32[16,16,128]{2,1,0:T(8,128)S(1)}, u32[]{:S(2)}, u32[]{:S(2)}) collective-permute-start(f32[16,16,128]{2,1,0:T(8,128)S(1)} %get-tuple-element.34), channel_id=1, source_target_pairs={{0,12},{4,0},{8,4},{12,8},{1,13},{5,1},{9,5},{13,9},{2,14},{6,2},{... | collective-permute-start | bytes 393224 | tf_op jit(solution)/shard_map/ppermute | solution.py:22
  229.1 9.4 %collective-permute-start.24 = (f32[16,16,128]{2,1,0:T(8,128)S(1)}, f32[16,16,128]{2,1,0:T(8,128)S(1)}, u32[]{:S(2)}, u32[]{:S(2)}) collective-permute-start(f32[16,16,128]{2,1,0:T(8,128)S(1)} %get-tuple-element.35), channel_id=1, source_target_pairs={{0,8},{4,12},{8,0},{12,4},{1,9},{5,13},{9,1},{13,5},{2,10},{6,14},... | collective-permute-start | bytes 393224 | tf_op jit(solution)/shard_map/ppermute | solution.py:22
  (19 other events, 345.5 us)

commit v6 on v5

--- a/solution.py
+++ b/solution.py
@@ -75,11 +75,25 @@
     )(core.reshape(1), valence, valence_head[..., None], selector)
 
 
-def along_line(below, above, name, step):
-    count = lax.axis_size(name)
-    below = lax.ppermute(below, name, [(s, s + 1) for s in range(step - 1, count - 1)])
-    above = lax.ppermute(above, name, [(s, s - 1) for s in range(1, count - step + 1)])
-    return below, above
+def one_way(below, above, pairs_below, pairs_above, name):
+    senders = [pair[0] for pair in pairs_below + pairs_above]
+    takers = [pair[1] for pair in pairs_below + pairs_above]
+    if len(set(senders)) < len(senders) or len(set(takers)) < len(takers):
+        return lax.ppermute(below, name, pairs_below), lax.ppermute(above, name, pairs_above)
+    sent = below
+    if above is not below:
+        sends_below = jnp.isin(lax.axis_index(name), jnp.array([pair[0] for pair in pairs_below]))
+        sent = jnp.where(sends_below, below, above)
+    moved = lax.ppermute(sent, name, pairs_below + pairs_above)
+    return moved, moved
+
+
+def line_pairs(count, step):
+    below = [(s, s + 1) for s in range(step - 1, count - 1)]
+    above = [(s, s - 1) for s in range(1, count - step + 1)]
+    to_ends = [[pair for pair in below if pair[1] == count - 1], [pair for pair in above if pair[1] == 0]]
+    to_others = [[pair for pair in below if pair[1] < count - 1], [pair for pair in above if pair[1] > 0]]
+    return to_ends, to_others
 
 
 def screen_product(places, pieces, right, per_index, half, store, blocks):
@@ -135,15 +149,24 @@
 
 def contract(row_ids, sides, owners, store, valences, body, blocks):
     _, bands, _, half, width = store.shape
-    _, points, pairs, _ = valences[0].shape
+    _, _, pairs, _ = valences[0][0].shape
+    points = sum(part.shape[1] for part in valences[0])
     slots = sides.shape[0]
     group = 2 if points % 2 == 0 else 1
     steps = points // group
+    given, places = [], []
+    for side, parts in enumerate(valences):
+        first = 0
+        for part in parts:
+            given.append(part)
+            places.append((side, first, first + part.shape[1] // group))
+            first = places[-1][2]
 
     def kernel(row_ref, side_ref, owner_ref, *refs):
-        store_refs, valence_refs, out_ref = refs[:group], refs[group : group + len(valences)], refs[-1]
+        store_refs, valence_refs, out_ref = refs[:group], refs[group : group + len(given)], refs[-1]
         lane = lax.broadcasted_iota(jnp.int32, (half, 2 * pairs), 1)
         side = side_ref[pl.program_id(0)]
+        step = pl.program_id(1)
 
         def rows_of(valence_ref):
             for index in range(group):
@@ -157,11 +180,11 @@
                     total = first + jnp.where(lane < pairs, -turned, turned)
                     out_ref[index, band * half : (band + 1) * half, :] = total
 
-        for place in range(len(valences)):
-
-            @pl.when(side == place)
-            def _(place=place):
-                rows_of(valence_refs[place])
+        for valence_ref, (place, first, end) in zip(valence_refs, places):
+
+            @pl.when((side == place) & (step >= first) & (step < end))
+            def _(valence_ref=valence_ref):
+                rows_of(valence_ref)
 
     def store_spec(index):
         return pl.BlockSpec(
@@ -169,10 +192,15 @@
             lambda slot, step, row, side, owner: (row[slot * points + step * group + index], 0, 0, 0, 0),
         )
 
-    def valence_spec(place):
+    def valence_spec(place, first, end):
         return pl.BlockSpec(
             (2, group, pairs, width),
-            lambda slot, step, row, side, owner: (0, jnp.where(side[slot] == place, step, 0), 0, 0),
+            lambda slot, step, row, side, owner: (
+                0,
+                jnp.where((side[slot] == place) & (step >= first) & (step < end), step - first, 0),
+                0,
+                0,
+            ),
         )
 
     kept = [] if body is None else [body]
@@ -183,18 +211,18 @@
             num_scalar_prefetch=3,
             grid=(slots, steps),
             in_specs=[store_spec(index) for index in range(group)]
-            + [valence_spec(place) for place in range(len(valences))]
+            + [valence_spec(*place) for place in places]
             + [pl.BlockSpec(memory_space=pl.ANY)] * len(kept),
             out_specs=pl.BlockSpec(
                 (group, bands * half, 2 * pairs),
                 lambda slot, step, row, side, owner: (owner[slot] * steps + step, 0, 0),
             ),
         ),
-        input_output_aliases={3 + group + len(valences): 0} if kept else {},
+        input_output_aliases={3 + group + len(given): 0} if kept else {},
         compiler_params=pltpu.CompilerParams(vmem_limit_bytes=VMEM_BYTES),
         cost_estimate=pl.CostEstimate(flops=1, bytes_accessed=1, transcendentals=0),
         name="contract",
-    )(row_ids, sides, owners, *([store] * group), *valences, *kept)
+    )(row_ids, sides, owners, *([store] * group), *given, *kept)
 
 
 def on_device(
@@ -232,7 +260,10 @@
 
     selector = (pair_select[:, None] == jnp.arange(pairs)[None, :]).astype(bf16)
     own_valence = valence_columns(valence, valence_head, selector, after(band, first), width, last)
-    line = [along_line(own_valence, own_valence, "kpt", 1)]
+    step_one = [
+        lax.ppermute(own_valence, "kpt", [(s, s + 1) for s in range(kpt_count - 1)]),
+        lax.ppermute(own_valence, "kpt", [(s, s - 1) for s in range(1, kpt_count)]),
+    ]
 
     plane = jnp.arange(deep)
     is_head = (plane >= block) & (plane < block + HEAD_PARTS)
@@ -305,14 +336,34 @@
 
     near, far = list(range(1, middle)), list(range(middle, kpt_count))
     store = product([0], spread(own_block[None]), right, None)
-    near_group = jnp.stack(after([arrived[shift] for shift in near], [store, line[0]]))
+    first_half = points // 2
+    held = after(step_one, store)
+    held = [[value[:, :first_half] for value in held], [value[:, first_half:] for value in held]]
+    near_group = jnp.stack(after([arrived[shift] for shift in near], [store, step_one]))
     near_pieces = spread(near_group)
-    line.append(along_line(*after(line[0], [store, near_group, [arrived[shift] for shift in far]]), "kpt", 2))
-    far_pieces = spread(jnp.stack([arrived[shift] for shift in far]))
+    far_across = share(jnp.stack([arrived[shift] for shift in far]), "pw")
+    ready = [near_group, [arrived[shift] for shift in far]]
+    ends, others = {}, {}
+
+    def move(step, part, gates):
+        below, above = held[part]
+        values = [after(below, gates)] * 2 if above is below else after([below, above], gates)
+        to_ends, to_others = line_pairs(kpt_count, step)
+        if step == 2 and part == 0:
+            ends[step, part] = one_way(*held[part], *to_ends, "kpt")
+            values = after(values, ends[step, part])
+        else:
+            ends[step, part] = one_way(*values, *to_ends, "kpt")
+        if step < kpt_count - 1:
+            held[part] = others[step, part] = one_way(*values, *to_others, "kpt")
+
+    move(2, 0, ready)
+    move(2, 1, [ready, ends[2, 0]])
     store = product(near, near_pieces, right, store)
-    for step in range(3, kpt_count):
-        line.append(along_line(*after(line[-1], [store, far_pieces]), "kpt", step))
-    store = product(far, far_pieces, after(right, line[1]), store)
+    if kpt_count > 3:
+        move(3, 0, [store, ends[2, 1]])
+    far_pieces = [own for across in after(far_across, store) for own in share(across, "band")]
+    store = product(far, far_pieces, after(right, others[2, 0]), store)
 
     lanes = 2 * pairs
     kept = half // pw_count
@@ -330,21 +381,53 @@
         body = body.reshape(-1, pw_count, kept, lanes)
         return sum(deal(jnp.moveaxis(body, 1, 0), "pw")).reshape(-1, kept * lanes)
 
-    body = add_blocks(None, [jnp.zeros((), jnp.int32)], [kpt], [own_valence], [kpt], kpt_count)
-    for step in range(1, kpt_count):
-        has_below, has_above = kpt >= step, kpt + step < kpt_count
+    has_below = [kpt >= step for step in range(kpt_count)]
+    has_above = [kpt + step < kpt_count for step in range(kpt_count)]
+
+    def blocks_of(step):
+        if step == 1:
+            return [[value] for value in step_one] + [[own_valence]], 0, 1
+        places, index = [], {}
+        for name, moved in (("ends", ends), ("others", others)):
+            if (step, 0) not in moved:
+                continue
+            pair = moved[step, 0], moved[step, 1]
+            for side in range(2):
+                if side and pair[0][1] is pair[0][0]:
+                    index[name, side] = index[name, 0]
+                    continue
+                index[name, side] = len(places)
+                places.append([pair[0][side], pair[1][side]])
+        from_below = jnp.where(kpt == kpt_count - 1, index["ends", 0], index.get(("others", 0), 0))
+        from_above = jnp.where(kpt == 0, index["ends", 1], index.get(("others", 1), 0))
+        return places + [[own_valence]], from_below, from_above
+
+    def slots_of(step):
+        places, from_below, from_above = blocks_of(step)
+        none = len(places) - 1
+        below = jnp.where(has_below[step], from_below, none), jnp.where(has_below[step], kpt - step, kpt)
+        above = jnp.where(has_above[step], from_above, none), jnp.where(has_above[step], kpt + step, kpt)
         if 2 * step < kpt_count:
-            sides = [jnp.where(has_below, 0, 2), jnp.where(has_above, 1, 2)]
-            owners = [jnp.where(has_below, kpt - step, kpt), jnp.where(has_above, kpt + step, kpt)]
-        else:
-            sides = [jnp.where(has_below, 0, jnp.where(has_above, 1, 2))]
-            owners = [jnp.where(has_below, kpt - step, jnp.where(has_above, kpt + step, kpt))]
-        valences = [*line[step - 1], own_valence]
-        if step < kpt_count - 1:
-            body = add_blocks(body, sides, owners, valences, owners, kpt_count)
+            return places, [below[0], above[0]], [below[1], above[1]]
+        return places, [jnp.where(has_below[step], below[0], above[0])], [jnp.where(has_below[step], below[1], above[1])]
+
+    body = add_blocks(None, [jnp.zeros((), jnp.int32)], [kpt], [[own_valence]], [kpt], kpt_count)
+    for step in range(1, kpt_count - 1):
+        places_here, sides, owners = slots_of(step)
+        if step == 2:
+            body = after(body, ends[3, 0])
+        body = add_blocks(body, sides, owners, places_here, owners, kpt_count)
+        if step == 1:
+            if kpt_count > 3:
+                move(3, 1, body)
+            for later in range(4, kpt_count):
+                move(later, 0, body)
+                move(later, 1, body)
     early = summed(body)
-    last_owner = owners[-1]
-    late = summed(add_blocks(None, sides[-1:], owners[-1:], valences, [jnp.zeros((), jnp.int32)], 1))
+    places_here, sides, owners = slots_of(kpt_count - 1)
+    last_owner = owners[0]
+    places_here[0] = after(places_here[0], early)
+    late = summed(add_blocks(None, sides, owners, places_here, [jnp.zeros((), jnp.int32)], 1))
 
     match = neighbors[:, :, None] == point_of_row[None, None, :]
     stencil = jnp.sum(jnp.where(match, live[:, :, None], 0.0), axis=1)

time: 246 us -> 256 us (1.041)
  other arithmetic: 18.3 us -> 28.6 us
    select_n x0 -> x2, other arithmetic: none -> 5.34 us  [one_way(): sent = jnp.where(sends_below, below, above)]
    slice x0 -> x1, other arithmetic: none -> 4.58 us  [on_device(): value[:, first_half:]]
    ppermute x6 -> x8, starting transfers between devices: 14.2 us -> 15.8 us  [the longest x6 8.62 us: one_way(): moved = lax.ppermute(sent, name, pairs_below + pairs_above)]
    ppermute x6 -> x8, waiting for transfers between devices: 25.4 us -> 24.5 us  [the longest x6 24.5 us: one_way(): moved = lax.ppermute(sent, name, pairs_below + pairs_above)]
  transfers between devices with their start and end apart: 26 -> 28, of which waited for: 12 -> 12; matrix products, arithmetic and copies ran while one was open for 10% -> 14% of each run, Pallas kernels for 24% -> 23%
where the time goes in v6:
time: 256 us; the launch traced here: 255 us
  waiting for transfers between devices  112 us (44%)
  Pallas kernels  58.3 us (23%)
  starting transfers between devices  34.4 us (13%)
  other arithmetic  28.6 us (11%)
  local copies, waits for them, and re-layouts  13.4 us (5%)
  blocking collectives  5.64 us (2%)
    ppermute x20, waiting for transfers between devices, shifted(): return lax.ppermute(x, name, pairs)  87.6 us
    pallas_call x3, Pallas kernels, screen_product(): pl.pallas_call(kernel, out_shape=jax.ShapeDtypeStruct((blocks * points, b...  33.9 us
    ppermute x6, waiting for transfers between devices, one_way(): moved = lax.ppermute(sent, name, pairs_below + pairs_above)  24.5 us
    pallas_call x4, Pallas kernels, contract(): pl.pallas_call(kernel, out_shape=jax.ShapeDtypeStruct((blocks * points, b...  22.1 us
    ppermute x20, starting transfers between devices, shifted(): return lax.ppermute(x, name, pairs)  18.6 us
    another operation x2, other arithmetic, on_device(): jnp.stack([jnp.concatenate([screen[0], screen[1]], axis=0), jnp.concatena...  11.4 us
    ppermute x6, starting transfers between devices, one_way(): moved = lax.ppermute(sent, name, pairs_below + pairs_above)  8.62 us
    ppermute x1, starting transfers between devices, on_device(): lax.ppermute(own_valence, 'kpt', [(s, s + 1) for s in range(kpt_count - 1)])  5.91 us
  transfers between devices with their start and end apart: 28, of which 12 were waited for; matrix products, arithmetic and copies ran while one was open for 14% of the time, Pallas kernels for 23%

profile of v6, /device:TPU:0, one launch (start us, length us, event | category | flops | bytes accessed | tf_op | source)
XLA Modules:
  0.0 254.5 jit_solution(2025223181673577575)
XLA Ops:
  10.6 5.9 %collective-permute-start.8 = (bf16[2,8,64,1024]{3,2,1,0:T(8,128)(2,1)S(1)}, bf16[2,8,64,1024]{3,2,1,0:T(8,128)(2,1)}, u32[]{:S(2)}, u32[]{:S(2)}) collective-permute-start(bf16[2,8,64,1024]{3,2,1,0:T(8,128)(2,1)S(1)} %valence_columns.1.refs_2_.refs_4_.refs_6_), channel_id=1, source_target_pairs={{0,4},{4,8},{8,12},{1,5},{5,9},{9,13},{2,6},{6,10},{10,14},{3,7},{... | collective-permute-start | bytes 6291464 | tf_op jit(solution)/shard_map/ppermute | solution.py:264
  17.2 3.5 %fusion.1 = bf16[2,1024,1024]{2,1,0:T(8,128)(2,1)S(1)} fusion(s32[]{:T(128)S(6)} %select_n.367, bf16[2,1000,2000]{2,1,0:T(8,128)(2,1)} %param.21, pred[1024]{0:T(1024)(128)(4,1)S(1)} %get-tuple-element.72, pred[1024]{0:T(1024)(128)(4,1)S(1)} %get-tuple-element.73, bf16[2,1024]{1,0:T(2,128)(2,1)S(1)} %broadcast_select_fusion.4, bf16[2,1024]{1,0:T(2,128)(2,1)S(1)} %fusion.21), kind=kLoop, calls=%fused_computation.7 | loop fusion | flops 4194304 | bytes 12204548 | tf_op jit(solution)/shard_map/jit(_where)/select_n | solution.py:305
  20.6 8.1 %collective-permute-done = bf16[2,4,32,2000]{3,2,1,0:T(8,128)(2,1)S(1)} collective-permute-done((bf16[2,4,32,2000]{3,2,1,0:T(8,128)(2,1)}, bf16[2,4,32,2000]{3,2,1,0:T(8,128)(2,1)S(1)}, u32[]{:S(2)}, u32[]{:S(2)}) %collective-permute-start) | collective-permute-done | bytes 1024032 | tf_op jit(solution)/shard_map/ppermute | solution.py:22
  33.9 10.8 %collective-permute-done.6.refs_2_ = bf16[1,2,128,1024]{3,2,1,0:T(8,128)(2,1)S(1)} collective-permute-done((bf16[1,2,128,1024]{3,2,1,0:T(8,128)(2,1)S(1)}, bf16[1,2,128,1024]{3,2,1,0:T(8,128)(2,1)S(1)}, u32[]{:S(2)}, u32[]{:S(2)}) %collective-permute-start.6) | collective-permute-done | bytes 524320 | tf_op jit(solution)/shard_map/ppermute | solution.py:22
  44.7 3.8 %maximum_bitcast_fusion = (bf16[1,2048,1024]{2,1,0:T(8,128)(2,1)}, bf16[1,2048,1024]{2,1,0:T(8,128)(2,1)}) fusion(bf16[1024,1024]{1,0:T(8,128)(2,1)S(1)} %get-tuple-element.46, bf16[1024,1024]{1,0:T(8,128)(2,1)S(1)} %get-tuple-element.45, bf16[1024,1024]{1,0:T(8,128)(2,1)S(1)} %fusion.32), kind=kLoop, calls=%fused_computation.8 | loop fusion | flops 16777216 | bytes 14680064 | tf_op jit(solution)/shard_map/stack | solution.py:308
  48.6 7.6 %pad_maximum_fusion.refs_4_ = bf16[2,2048,1024]{2,1,0:T(8,128)(2,1)} fusion(bf16[1,2048,1024]{2,1,0:T(8,128)(2,1)} %get-tuple-element.57, bf16[1,2048,1024]{2,1,0:T(8,128)(2,1)} %get-tuple-element.56), kind=kLoop, calls=%fused_computation.4 | loop fusion | flops 4194304 | bytes 16777216 | tf_op jit(solution)/shard_map/stack | solution.py:308
  60.3 9.1 %screen_product.3.refs_5_ = bf16[32,2,2,32,1024]{4,3,2,1,0:T(8,128)(2,1)} custom-call(s32[5]{0:T(128)S(1)} %concatenate.30.place_ref, bf16[1,2,128,1024]{3,2,1,0:T(8,128)(2,1)S(1)} %get-tuple-element.58.refs_0_, bf16[1,2,128,1024]{3,2,1,0:T(8,128)(2,1)} %collective-permute-done.5.refs_1_, bf16[1,2,128,1024]{3,2,1,0:T(8,128)(2,1)S(1)} %collective-permute-done.6.refs_2_, ...), custom_call_target="tpu_custom_call" | custom-call | flops 1 | bytes 1 | tf_op jit(solution)/shard_map/screen_product/pallas_call | solution.py:129
  69.4 4.6 %fusion.33 = (bf16[2,4,64,1024]{3,2,1,0:T(8,128)(2,1)}, bf16[2,4,64,1024]{3,2,1,0:T(8,128)(2,1)}, bf16[2,4,64,1024]{3,2,1,0:T(8,128)(2,1)}, bf16[2,4,64,1024]{3,2,1,0:T(8,128)(2,1)}, bf16[2,4,64,1024]{3,2,1,0:T(8,128)(2,1)}) fusion(bf16[2,8,64,1024]{3,2,1,0:T(8,128)(2,1)} %collective-permute-done.9.refs_3_, ...), kind=kLoop, calls=%fused_computation.110 | loop fusion | flops 524288 | bytes 9437185 | tf_op jit(solution)/shard_map/slice | solution.py:341
  75.3 18.7 %collective-permute-done.4 = bf16[2,128,1024]{2,1,0:T(8,128)(2,1)S(1)} collective-permute-done((bf16[2,128,1024]{2,1,0:T(8,128)(2,1)S(1)}, bf16[2,128,1024]{2,1,0:T(8,128)(2,1)S(1)}, u32[]{:S(2)}, u32[]{:S(2)}) %collective-permute-start.4) | collective-permute-done | bytes 524320 | tf_op jit(solution)/shard_map/ppermute | solution.py:22
  95.6 32.1 %collective-permute-done.1 = bf16[2,128,1024]{2,1,0:T(8,128)(2,1)} collective-permute-done((bf16[2,128,1024]{2,1,0:T(8,128)(2,1)}, bf16[2,128,1024]{2,1,0:T(8,128)(2,1)}, u32[]{:S(2)}, u32[]{:S(2)}) %collective-permute-start.1) | collective-permute-done | bytes 524320 | tf_op jit(solution)/shard_map/ppermute | solution.py:22
  131.7 3.0 %broadcast_select_fusion.2 = (bf16[2,4,64,1024]{3,2,1,0:T(8,128)(2,1)}, bf16[2,4,64,1024]{3,2,1,0:T(8,128)(2,1)}) fusion(bf16[2,4,64,1024]{3,2,1,0:T(8,128)(2,1)} %get-tuple-element.36, bf16[2,4,64,1024]{3,2,1,0:T(8,128)(2,1)} %get-tuple-element.37, pred[]{:T(512)S(6)} %eq.161, pred[]{:T(512)S(6)} %eq.162), kind=kLoop, calls=%fused_computation.21 | loop fusion | flops 1048576 | bytes 4194306 | tf_op jit(solution)/shard_map/jit(_where)/select_n | solution.py:86
  141.6 15.8 %screen_product.4.refs_5_ = bf16[32,2,2,32,1024]{4,3,2,1,0:T(8,128)(2,1)} custom-call(s32[6]{0:T(128)S(1)} %concatenate.29.place_ref, bf16[2,2,128,1024]{3,2,1,0:T(8,128)(2,1)S(1)} %pad_maximum_fusion.2.refs_0_, bf16[2,2,128,1024]{3,2,1,0:T(8,128)(2,1)S(1)} %copy-done.5, ...), custom_call_target="tpu_custom_call", output_to_operand_aliasing={{}: (6, {})} | custom-call | flops 1 | bytes 1 | tf_op jit(solution)/shard_map/screen_product/pallas_call | solution.py:129
  157.3 5.2 %collective-permute-done.17.refs_3_ = bf16[2,4,64,1024]{3,2,1,0:T(8,128)(2,1)} collective-permute-done((bf16[2,4,64,1024]{3,2,1,0:T(8,128)(2,1)}, bf16[2,4,64,1024]{3,2,1,0:T(8,128)(2,1)}, u32[]{:S(2)}, u32[]{:S(2)}) %collective-permute-start.17) | collective-permute-done | bytes 1048608 | tf_op jit(solution)/shard_map/ppermute | solution.py:87
  167.1 9.1 %screen_product.5.refs_0_.refs_1_ = bf16[32,2,2,32,1024]{4,3,2,1,0:T(8,128)(2,1)} custom-call(s32[5]{0:T(128)S(1)} %concatenate.28.place_ref, bf16[1,2,128,1024]{3,2,1,0:T(8,128)(2,1)} %bitcast.16.refs_0_, bf16[1,2,128,1024]{3,2,1,0:T(8,128)(2,1)S(1)} %collective-permute-done.13.refs_1_, ...), custom_call_target="tpu_custom_call", output_to_operand_aliasing={{}: (6, {})} | custom-call | flops 1 | bytes 1 | tf_op jit(solution)/shard_map/screen_product/pallas_call | solution.py:129
  176.2 3.9 %contract.4.refs_5_ = f32[32,64,128]{2,1,0:T(8,128)S(1)} custom-call(s32[8]{0:T(128)S(1)} %gather_fusion.2, s32[1]{0:T(128)} %constant.233.clone.1.side_ref.owner_ref, s32[1]{0:T(128)} %bitcast.38.owner_ref, bf16[32,2,2,32,1024]{4,3,2,1,0:T(8,128)(2,1)} %screen_product.5.refs_0_.refs_1_, bf16[32,2,2,32,1024]{4,3,2,1,0:T(8,128)(2,1)} %screen_product.5.refs_0_.refs_1_, ...), custom_call_target="tpu_custom_call" | custom-call | flops 1 | bytes 1 | tf_op jit(solution)/shard_map/contract/pallas_call | solution.py:207
  180.1 8.2 %contract.5.refs_7_ = f32[32,64,128]{2,1,0:T(8,128)S(1)} custom-call(s32[16]{0:T(128)S(1)} %gather_fusion.1, s32[2]{0:T(128)S(1)} %pad_add_fusion.1.side_ref, s32[2]{0:T(128)S(1)} %get-tuple-element.44.owner_ref, bf16[32,2,2,32,1024]{4,3,2,1,0:T(8,128)(2,1)} %screen_product.5.refs_0_.refs_1_, ...), custom_call_target="tpu_custom_call", output_to_operand_aliasing={{}: (8, {})} | custom-call | flops 1 | bytes 1 | tf_op jit(solution)/shard_map/contract/pallas_call | solution.py:207
  190.5 5.3 %contract.6 = f32[32,64,128]{2,1,0:T(8,128)S(1)} custom-call(s32[8]{0:T(128)S(1)} %gather_fusion, s32[1]{0:T(128)} %bitcast.1.side_ref, s32[1]{0:T(128)} %bitcast.2.owner_ref, bf16[32,2,2,32,1024]{4,3,2,1,0:T(8,128)(2,1)} %screen_product.5.refs_0_.refs_1_, ...), custom_call_target="tpu_custom_call", output_to_operand_aliasing={{}: (10, {})} | custom-call | flops 1 | bytes 1 | tf_op jit(solution)/shard_map/contract/pallas_call | solution.py:207
  197.6 19.3 %collective-permute-done.22.refs_3_ = bf16[2,4,64,1024]{3,2,1,0:T(8,128)(2,1)} collective-permute-done((bf16[2,4,64,1024]{3,2,1,0:T(8,128)(2,1)}, bf16[2,4,64,1024]{3,2,1,0:T(8,128)(2,1)}, u32[]{:S(2)}, u32[]{:S(2)}) %collective-permute-start.22) | collective-permute-done | bytes 1048608 | tf_op jit(solution)/shard_map/ppermute | solution.py:87
  217.0 4.6 %contract.7 = f32[8,64,128]{2,1,0:T(8,128)S(1)} custom-call(s32[8]{0:T(128)S(1)} %gather_fusion.3, s32[1]{0:T(128)} %bitcast.46.side_ref, s32[1]{0:T(128)} %constant.233.clone.1.side_ref.owner_ref, bf16[32,2,2,32,1024]{4,3,2,1,0:T(8,128)(2,1)} %screen_product.5.refs_0_.refs_1_, bf16[32,2,2,32,1024]{4,3,2,1,0:T(8,128)(2,1)} %screen_product.5.refs_0_.refs_1_, ...), custom_call_target="tpu_custom_call" | custom-call | flops 1 | bytes 1 | tf_op jit(solution)/shard_map/contract/pallas_call | solution.py:207
  225.1 8.0 %collective-permute-done.24 = f32[8,16,128]{2,1,0:T(8,128)S(1)} collective-permute-done((f32[8,16,128]{2,1,0:T(8,128)S(1)}, f32[8,16,128]{2,1,0:T(8,128)S(1)}, u32[]{:S(2)}, u32[]{:S(2)}) %collective-permute-start.24) | collective-permute-done | bytes 65568 | tf_op jit(solution)/shard_map/ppermute | solution.py:22
  234.6 3.8 %collective-permute-start.27 = (f32[16,16,128]{2,1,0:T(8,128)S(1)}, f32[16,16,128]{2,1,0:T(8,128)S(1)}, u32[]{:S(2)}, u32[]{:S(2)}) collective-permute-start(f32[16,16,128]{2,1,0:T(8,128)S(1)} %get-tuple-element.63), channel_id=1, source_target_pairs={{0,12},{4,0},{8,4},{12,8},{1,13},{5,1},{9,5},{13,9},{2,14},{6,2},{... | collective-permute-start | bytes 393224 | tf_op jit(solution)/shard_map/ppermute | solution.py:22
  238.4 4.4 %collective-permute-done.25 = f32[16,16,128]{2,1,0:T(8,128)S(1)} collective-permute-done((f32[16,16,128]{2,1,0:T(8,128)S(1)}, f32[16,16,128]{2,1,0:T(8,128)S(1)}, u32[]{:S(2)}, u32[]{:S(2)}) %collective-permute-start.25) | collective-permute-done | bytes 131104 | tf_op jit(solution)/shard_map/ppermute | solution.py:22
  244.3 3.2 %collective-permute-done.26 = f32[16,16,128]{2,1,0:T(8,128)S(1)} collective-permute-done((f32[16,16,128]{2,1,0:T(8,128)S(1)}, f32[16,16,128]{2,1,0:T(8,128)S(1)}, u32[]{:S(2)}, u32[]{:S(2)}) %collective-permute-start.26) | collective-permute-done | bytes 131104 | tf_op jit(solution)/shard_map/ppermute | solution.py:22
  247.6 5.6 %all-gather = f32[32,16,128]{2,1,0:T(8,128)S(1)} all-gather(f32[16,16,128]{2,1,0:T(8,128)S(1)} %fusion.8), channel_id=2, replica_groups=mesh['grp'=2,'kpt'=4,'pw'=2,'band'=2] {'pw'}, dimensions={0}, use_global_device_ids=true | all-gather | bytes 393216 | tf_op jit(solution)/shard_map/all_gather | solution.py:440
  (141 shorter events, 50.2 us)
Async XLA Ops:
  2.4 26.3 %collective-permute-start = (bf16[2,4,32,2000]{3,2,1,0:T(8,128)(2,1)}, bf16[2,4,32,2000]{3,2,1,0:T(8,128)(2,1)S(1)}, u32[]{:S(2)}, u32[]{:S(2)}) collective-permute-start(bf16[2,4,32,2000]{3,2,1,0:T(8,128)(2,1)} %dynamic-slice_bitcast_fusion), channel_id=1, source_target_pairs={{0,2},{2,0},{1,3},{3,1},{4,6},{6,4},{5,7},{7,5},{8,10},{10,8},{9,1... | collective-permute-start | bytes 3072008 | tf_op jit(solution)/shard_map/ppermute | solution.py:22
  9.3 60.2 %collective-permute-start.9 = (bf16[2,8,64,1024]{3,2,1,0:T(8,128)(2,1)S(1)}, bf16[2,8,64,1024]{3,2,1,0:T(8,128)(2,1)}, u32[]{:S(2)}, u32[]{:S(2)}) collective-permute-start(bf16[2,8,64,1024]{3,2,1,0:T(8,128)(2,1)S(1)} %valence_columns.1.refs_2_.refs_4_.refs_6_), channel_id=1, source_target_pairs={{4,0},{8,4},{12,8},{5,1},{9,5},{13,9},{6,2},{10,6},{14,10},{7,3},{... | collective-permute-start | bytes 6291464 | tf_op jit(solution)/shard_map/ppermute | solution.py:265
  10.6 58.9 %collective-permute-start.8 = (bf16[2,8,64,1024]{3,2,1,0:T(8,128)(2,1)S(1)}, bf16[2,8,64,1024]{3,2,1,0:T(8,128)(2,1)}, u32[]{:S(2)}, u32[]{:S(2)}) collective-permute-start(bf16[2,8,64,1024]{3,2,1,0:T(8,128)(2,1)S(1)} %valence_columns.1.refs_2_.refs_4_.refs_6_), channel_id=1, source_target_pairs={{0,4},{4,8},{8,12},{1,5},{5,9},{9,13},{2,6},{6,10},{10,14},{3,7},{... | collective-permute-start | bytes 6291464 | tf_op jit(solution)/shard_map/ppermute | solution.py:264
  31.5 13.2 %collective-permute-start.6 = (bf16[1,2,128,1024]{3,2,1,0:T(8,128)(2,1)S(1)}, bf16[1,2,128,1024]{3,2,1,0:T(8,128)(2,1)S(1)}, u32[]{:S(2)}, u32[]{:S(2)}) collective-permute-start(bf16[1,2,128,1024]{3,2,1,0:T(8,128)(2,1)S(1)} %get-tuple-element.58.refs_0_), channel_id=1, source_target_pairs={{0,2},{2,0},{1,3},{3,1},{4,6},{6,4},{5,7},{7,5},{8,10},{10,8},{9,1... | collective-permute-start | bytes 1572872 | tf_op jit(solution)/shard_map/ppermute | solution.py:22
  33.8 24.9 %collective-permute-start.5 = (bf16[1,2,128,1024]{3,2,1,0:T(8,128)(2,1)S(1)}, bf16[1,2,128,1024]{3,2,1,0:T(8,128)(2,1)}, u32[]{:S(2)}, u32[]{:S(2)}) collective-permute-start(bf16[1,2,128,1024]{3,2,1,0:T(8,128)(2,1)S(1)} %get-tuple-element.58.refs_0_), channel_id=1, source_target_pairs={{0,1},{1,0},{2,3},{3,2},{4,5},{5,4},{6,7},{7,6},{8,9},{9,8},{10,11... | collective-permute-start | bytes 1572872 | tf_op jit(solution)/shard_map/ppermute | solution.py:22
  44.7 15.6 %collective-permute-start.7 = (bf16[1,2,128,1024]{3,2,1,0:T(8,128)(2,1)S(1)}, bf16[1,2,128,1024]{3,2,1,0:T(8,128)(2,1)}, u32[]{:S(2)}, u32[]{:S(2)}) collective-permute-start(bf16[1,2,128,1024]{3,2,1,0:T(8,128)(2,1)S(1)} %collective-permute-done.6.refs_2_), channel_id=1, source_target_pairs={{0,1},{1,0},{2,3},{3,2},{4,5},{5,4},{6,7},{7,6},{8,9},{9,8},{10,11... | collective-permute-start | bytes 1572872 | tf_op jit(solution)/shard_map/ppermute | solution.py:22
  56.2 37.8 %collective-permute-start.4 = (bf16[2,128,1024]{2,1,0:T(8,128)(2,1)S(1)}, bf16[2,128,1024]{2,1,0:T(8,128)(2,1)S(1)}, u32[]{:S(2)}, u32[]{:S(2)}) collective-permute-start(bf16[2,128,1024]{2,1,0:T(8,128)(2,1)S(1)} %copy-done.8), channel_id=1, source_target_pairs={{0,8},{4,12},{8,0},{12,4},{1,9},{5,13},{9,1},{13,5},{2,10},{6,14},... | collective-permute-start | bytes 1572872 | tf_op jit(solution)/shard_map/ppermute | solution.py:22
  58.7 35.3 %collective-permute-start.3 = (bf16[2,128,1024]{2,1,0:T(8,128)(2,1)S(1)}, bf16[2,128,1024]{2,1,0:T(8,128)(2,1)S(1)}, u32[]{:S(2)}, u32[]{:S(2)}) collective-permute-start(bf16[2,128,1024]{2,1,0:T(8,128)(2,1)S(1)} %copy-done.7), channel_id=1, source_target_pairs={{0,4},{4,8},{8,12},{12,0},{1,5},{5,9},{9,13},{13,1},{2,6},{6,10},{... | collective-permute-start | bytes 1572872 | tf_op jit(solution)/shard_map/ppermute | solution.py:22
  74.0 53.7 %collective-permute-start.15 = (bf16[2,4,64,1024]{3,2,1,0:T(8,128)(2,1)}, bf16[2,4,64,1024]{3,2,1,0:T(8,128)(2,1)}, u32[]{:S(2)}, u32[]{:S(2)}) collective-permute-start(bf16[2,4,64,1024]{3,2,1,0:T(8,128)(2,1)} %get-tuple-element.52), channel_id=1, source_target_pairs={{8,12},{4,0},{9,13},{5,1},{10,14},{6,2},{11,15},{7,3},{24,28},{20,... | collective-permute-start | bytes 3145736 | tf_op jit(solution)/shard_map/ppermute | solution.py:87
  94.1 37.6 %collective-permute-start.11 = (bf16[2,2,128,1024]{3,2,1,0:T(8,128)(2,1)S(1)}, bf16[2,2,128,1024]{3,2,1,0:T(8,128)(2,1)}, u32[]{:S(2)}, u32[]{:S(2)}) collective-permute-start(bf16[2,2,128,1024]{3,2,1,0:T(8,128)(2,1)S(1)} %pad_maximum_fusion.2.refs_0_), channel_id=1, source_target_pairs={{0,2},{2,0},{1,3},{3,1},{4,6},{6,4},{5,7},{7,5},{8,10},{10,8},{9,1... | collective-permute-start | bytes 3145736 | tf_op jit(solution)/shard_map/ppermute | solution.py:22
  95.6 32.1 %collective-permute-start.1 = (bf16[2,128,1024]{2,1,0:T(8,128)(2,1)}, bf16[2,128,1024]{2,1,0:T(8,128)(2,1)}, u32[]{:S(2)}, u32[]{:S(2)}) collective-permute-start(bf16[2,128,1024]{2,1,0:T(8,128)(2,1)} %get-tuple-element.61), channel_id=1, source_target_pairs={{0,12},{4,0},{8,4},{12,8},{1,13},{5,1},{9,5},{13,9},{2,14},{6,2},{... | collective-permute-start | bytes 1572872 | tf_op jit(solution)/shard_map/ppermute | solution.py:22
  95.6 41.9 %collective-permute-start.10 = (bf16[2,2,128,1024]{3,2,1,0:T(8,128)(2,1)S(1)}, bf16[2,2,128,1024]{3,2,1,0:T(8,128)(2,1)S(1)}, u32[]{:S(2)}, u32[]{:S(2)}) collective-permute-start(bf16[2,2,128,1024]{3,2,1,0:T(8,128)(2,1)S(1)} %pad_maximum_fusion.2.refs_0_), channel_id=1, source_target_pairs={{0,1},{1,0},{2,3},{3,2},{4,5},{5,4},{6,7},{7,6},{8,9},{9,8},{10,11... | collective-permute-start | bytes 3145736 | tf_op jit(solution)/shard_map/ppermute | solution.py:22
  130.0 27.3 %collective-permute-start.16 = (bf16[2,4,64,1024]{3,2,1,0:T(8,128)(2,1)}, bf16[2,4,64,1024]{3,2,1,0:T(8,128)(2,1)}, u32[]{:S(2)}, u32[]{:S(2)}) collective-permute-start(bf16[2,4,64,1024]{3,2,1,0:T(8,128)(2,1)} %broadcast_select_fusion.3), channel_id=1, source_target_pairs={{4,8},{8,4},{5,9},{9,5},{6,10},{10,6},{7,11},{11,7},{20,24},{24,20... | collective-permute-start | bytes 3145736 | tf_op jit(solution)/shard_map/ppermute | solution.py:87
  131.7 8.6 %collective-permute-start.12 = (bf16[2,2,128,1024]{3,2,1,0:T(8,128)(2,1)}, bf16[2,2,128,1024]{3,2,1,0:T(8,128)(2,1)}, u32[]{:S(2)}, u32[]{:S(2)}) collective-permute-start(bf16[2,2,128,1024]{3,2,1,0:T(8,128)(2,1)} %collective-permute-done.11.refs_2_), channel_id=1, source_target_pairs={{0,1},{1,0},{2,3},{3,2},{4,5},{5,4},{6,7},{7,6},{8,9},{9,8},{10,11... | collective-permute-start | bytes 3145736 | tf_op jit(solution)/shard_map/ppermute | solution.py:22
  134.8 27.8 %collective-permute-start.17 = (bf16[2,4,64,1024]{3,2,1,0:T(8,128)(2,1)}, bf16[2,4,64,1024]{3,2,1,0:T(8,128)(2,1)}, u32[]{:S(2)}, u32[]{:S(2)}) collective-permute-start(bf16[2,4,64,1024]{3,2,1,0:T(8,128)(2,1)} %get-tuple-element.50), channel_id=1, source_target_pairs={{8,12},{4,0},{9,13},{5,1},{10,14},{6,2},{11,15},{7,3},{24,28},{20,... | collective-permute-start | bytes 3145736 | tf_op jit(solution)/shard_map/ppermute | solution.py:87
  136.0 28.2 %collective-permute-start.2 = (bf16[1,2,128,1024]{3,2,1,0:T(8,128)(2,1)}, bf16[1,2,128,1024]{3,2,1,0:T(8,128)(2,1)}, u32[]{:S(2)}, u32[]{:S(2)}) collective-permute-start(bf16[1,2,128,1024]{3,2,1,0:T(8,128)(2,1)} %bitcast.16.refs_0_), channel_id=1, source_target_pairs={{0,2},{2,0},{1,3},{3,1},{4,6},{6,4},{5,7},{7,5},{8,10},{10,8},{9,1... | collective-permute-start | bytes 1572872 | tf_op jit(solution)/shard_map/ppermute | solution.py:22
  138.5 49.8 %collective-permute-start.18 = (bf16[2,4,64,1024]{3,2,1,0:T(8,128)(2,1)}, bf16[2,4,64,1024]{3,2,1,0:T(8,128)(2,1)}, u32[]{:S(2)}, u32[]{:S(2)}) collective-permute-start(bf16[2,4,64,1024]{3,2,1,0:T(8,128)(2,1)} %get-tuple-element.49), channel_id=1, source_target_pairs={{4,8},{8,4},{5,9},{9,5},{6,10},{10,6},{7,11},{11,7},{20,24},{24,20... | collective-permute-start | bytes 3145736 | tf_op jit(solution)/shard_map/ppermute | solution.py:87
  162.5 27.9 %collective-permute-start.19 = (bf16[2,4,64,1024]{3,2,1,0:T(8,128)(2,1)}, bf16[2,4,64,1024]{3,2,1,0:T(8,128)(2,1)}, u32[]{:S(2)}, u32[]{:S(2)}) collective-permute-start(bf16[2,4,64,1024]{3,2,1,0:T(8,128)(2,1)} %collective-permute-done.16.refs_4_), channel_id=1, source_target_pairs={{8,12},{4,0},{9,13},{5,1},{10,14},{6,2},{11,15},{7,3},{24,28},{20,... | collective-permute-start | bytes 3145736 | tf_op jit(solution)/shard_map/ppermute | solution.py:87
  188.4 28.6 %collective-permute-start.22 = (bf16[2,4,64,1024]{3,2,1,0:T(8,128)(2,1)}, bf16[2,4,64,1024]{3,2,1,0:T(8,128)(2,1)}, u32[]{:S(2)}, u32[]{:S(2)}) collective-permute-start(bf16[2,4,64,1024]{3,2,1,0:T(8,128)(2,1)} %collective-permute-done.18.refs_5_), channel_id=1, source_target_pairs={{8,12},{4,0},{9,13},{5,1},{10,14},{6,2},{11,15},{7,3},{24,28},{20,... | collective-permute-start | bytes 3145736 | tf_op jit(solution)/shard_map/ppermute | solution.py:87
  196.7 25.0 %collective-permute-start.20 = (f32[32,32,128]{2,1,0:T(8,128)}, f32[32,32,128]{2,1,0:T(8,128)}, u32[]{:S(2)}, u32[]{:S(2)}) collective-permute-start(f32[32,32,128]{2,1,0:T(8,128)} %dynamic-slice_bitcast_fusion.1), channel_id=1, source_target_pairs={{0,1},{1,0},{2,3},{3,2},{4,5},{5,4},{6,7},{7,6},{8,9},{9,8},{10,11... | collective-permute-start | bytes 1572872 | tf_op jit(solution)/shard_map/ppermute | solution.py:22
  222.9 10.2 %collective-permute-start.21 = (f32[32,16,128]{2,1,0:T(8,128)S(1)}, f32[32,16,128]{2,1,0:T(8,128)S(1)}, u32[]{:S(2)}, u32[]{:S(2)}) collective-permute-start(f32[32,16,128]{2,1,0:T(8,128)S(1)} %dynamic-slice_bitcast_fusion.5), channel_id=1, source_target_pairs={{0,2},{2,0},{1,3},{3,1},{4,6},{6,4},{5,7},{7,5},{8,10},{10,8},{9,1... | collective-permute-start | bytes 786440 | tf_op jit(solution)/shard_map/ppermute | solution.py:22
  224.4 8.6 %collective-permute-start.24 = (f32[8,16,128]{2,1,0:T(8,128)S(1)}, f32[8,16,128]{2,1,0:T(8,128)S(1)}, u32[]{:S(2)}, u32[]{:S(2)}) collective-permute-start(f32[8,16,128]{2,1,0:T(8,128)S(1)} %dynamic-slice_bitcast_fusion.10), channel_id=1, source_target_pairs={{0,2},{2,0},{1,3},{3,1},{4,6},{6,4},{5,7},{7,5},{8,10},{10,8},{9,1... | collective-permute-start | bytes 196616 | tf_op jit(solution)/shard_map/ppermute | solution.py:22
  234.6 9.7 %collective-permute-start.27 = (f32[16,16,128]{2,1,0:T(8,128)S(1)}, f32[16,16,128]{2,1,0:T(8,128)S(1)}, u32[]{:S(2)}, u32[]{:S(2)}) collective-permute-start(f32[16,16,128]{2,1,0:T(8,128)S(1)} %get-tuple-element.63), channel_id=1, source_target_pairs={{0,12},{4,0},{8,4},{12,8},{1,13},{5,1},{9,5},{13,9},{2,14},{6,2},{... | collective-permute-start | bytes 393224 | tf_op jit(solution)/shard_map/ppermute | solution.py:22
  238.4 9.1 %collective-permute-start.26 = (f32[16,16,128]{2,1,0:T(8,128)S(1)}, f32[16,16,128]{2,1,0:T(8,128)S(1)}, u32[]{:S(2)}, u32[]{:S(2)}) collective-permute-start(f32[16,16,128]{2,1,0:T(8,128)S(1)} %get-tuple-element.64), channel_id=1, source_target_pairs={{0,8},{4,12},{8,0},{12,4},{1,9},{5,13},{9,1},{13,5},{2,10},{6,14},... | collective-permute-start | bytes 393224 | tf_op jit(solution)/shard_map/ppermute | solution.py:22
  (21 other events, 390.7 us)

commit v7 on v6

--- a/solution.py
+++ b/solution.py
@@ -254,16 +254,15 @@
     last = band_count - 1
     head_at = columns - last * width
 
-    halves = jnp.moveaxis(conduction.reshape(2, pw_count, per_index, half, columns), 1, 0)
-    first = halves if pw_count == 1 else lax.dynamic_index_in_dim(halves, (pw + 1) % pw_count, 0, keepdims=False)
-    dealt = deal(halves, "pw")
-
     selector = (pair_select[:, None] == jnp.arange(pairs)[None, :]).astype(bf16)
-    own_valence = valence_columns(valence, valence_head, selector, after(band, first), width, last)
+    own_valence = valence_columns(valence, valence_head, selector, band, width, last)
     step_one = [
         lax.ppermute(own_valence, "kpt", [(s, s + 1) for s in range(kpt_count - 1)]),
         lax.ppermute(own_valence, "kpt", [(s, s - 1) for s in range(1, kpt_count)]),
     ]
+
+    halves = jnp.moveaxis(conduction.reshape(2, pw_count, per_index, half, columns), 1, 0)
+    dealt = deal(halves, "pw")
 
     plane = jnp.arange(deep)
     is_head = (plane >= block) & (plane < block + HEAD_PARTS)
@@ -335,35 +334,30 @@
         return screen_product(where, pieces, right, per_index, half, store, kpt_count)
 
     near, far = list(range(1, middle)), list(range(middle, kpt_count))
+    distant = [arrived[shift] for shift in far]
     store = product([0], spread(own_block[None]), right, None)
-    first_half = points // 2
-    held = after(step_one, store)
-    held = [[value[:, :first_half] for value in held], [value[:, first_half:] for value in held]]
-    near_group = jnp.stack(after([arrived[shift] for shift in near], [store, step_one]))
+    near_group = jnp.stack(after([arrived[shift] for shift in near], [store, step_one, distant]))
     near_pieces = spread(near_group)
-    far_across = share(jnp.stack([arrived[shift] for shift in far]), "pw")
-    ready = [near_group, [arrived[shift] for shift in far]]
-    ends, others = {}, {}
-
-    def move(step, part, gates):
-        below, above = held[part]
-        values = [after(below, gates)] * 2 if above is below else after([below, above], gates)
+    far_across = share(jnp.stack(distant), "pw")
+    to_ends, to_others = line_pairs(kpt_count, 2)
+    early_rows = max(points // 4, 1)
+    first_part = one_way(*[value[:, :early_rows] for value in step_one], *to_ends, "kpt")
+    held = after(step_one, [near_group, distant, first_part])
+    ends = {2: [first_part, one_way(*[value[:, early_rows:] for value in held], *to_ends, "kpt")]}
+    others = {}
+    if kpt_count > 3:
+        others[2] = [one_way(*held, *to_others, "kpt")]
+    store = product(near, near_pieces, right, store)
+    for step in range(3, kpt_count):
+        below, above = others[step - 1][0]
+        gates = [store, ends[2]]
+        below, above = [after(below, gates)] * 2 if above is below else after([below, above], gates)
         to_ends, to_others = line_pairs(kpt_count, step)
-        if step == 2 and part == 0:
-            ends[step, part] = one_way(*held[part], *to_ends, "kpt")
-            values = after(values, ends[step, part])
-        else:
-            ends[step, part] = one_way(*values, *to_ends, "kpt")
+        ends[step] = [one_way(below, above, *to_ends, "kpt")]
         if step < kpt_count - 1:
-            held[part] = others[step, part] = one_way(*values, *to_others, "kpt")
-
-    move(2, 0, ready)
-    move(2, 1, [ready, ends[2, 0]])
-    store = product(near, near_pieces, right, store)
-    if kpt_count > 3:
-        move(3, 0, [store, ends[2, 1]])
+            others[step] = [one_way(below, above, *to_others, "kpt")]
     far_pieces = [own for across in after(far_across, store) for own in share(across, "band")]
-    store = product(far, far_pieces, after(right, others[2, 0]), store)
+    store = product(far, far_pieces, after(right, others.get(2, ends[2])), store)
 
     lanes = 2 * pairs
     kept = half // pw_count
@@ -389,15 +383,15 @@
             return [[value] for value in step_one] + [[own_valence]], 0, 1
         places, index = [], {}
         for name, moved in (("ends", ends), ("others", others)):
-            if (step, 0) not in moved:
+            if step not in moved:
                 continue
-            pair = moved[step, 0], moved[step, 1]
+            parts = moved[step]
             for side in range(2):
-                if side and pair[0][1] is pair[0][0]:
+                if side and parts[0][1] is parts[0][0]:
                     index[name, side] = index[name, 0]
                     continue
                 index[name, side] = len(places)
-                places.append([pair[0][side], pair[1][side]])
+                places.append([part[side] for part in parts])
         from_below = jnp.where(kpt == kpt_count - 1, index["ends", 0], index.get(("others", 0), 0))
         from_above = jnp.where(kpt == 0, index["ends", 1], index.get(("others", 1), 0))
         return places + [[own_valence]], from_below, from_above
@@ -414,19 +408,10 @@
     body = add_blocks(None, [jnp.zeros((), jnp.int32)], [kpt], [[own_valence]], [kpt], kpt_count)
     for step in range(1, kpt_count - 1):
         places_here, sides, owners = slots_of(step)
-        if step == 2:
-            body = after(body, ends[3, 0])
         body = add_blocks(body, sides, owners, places_here, owners, kpt_count)
-        if step == 1:
-            if kpt_count > 3:
-                move(3, 1, body)
-            for later in range(4, kpt_count):
-                move(later, 0, body)
-                move(later, 1, body)
     early = summed(body)
     places_here, sides, owners = slots_of(kpt_count - 1)
     last_owner = owners[0]
-    places_here[0] = after(places_here[0], early)
     late = summed(add_blocks(None, sides, owners, places_here, [jnp.zeros((), jnp.int32)], 1))
 
     match = neighbors[:, :, None] == point_of_row[None, None, :]
@@ -437,9 +422,15 @@
     fine = fine + jnp.dot(late_stencil, late, precision=highest)
     fine_here = neighbors.shape[0] // kpt_count
     fine = sum(deal(fine.reshape(kpt_count, fine_here, kept, lanes), "kpt"))
-    fine = lax.all_gather(fine, "pw", axis=0)
-    fine = fine.reshape(pw_count, fine_here, kept, 2, pairs)
-    return jnp.transpose(fine, (3, 1, 0, 2, 4)).reshape(2, fine_here, half * pairs)
+    gathered = share(fine, "pw")
+    whole = []
+    for owner in range(pw_count):
+        part = gathered[0]
+        for shift in range(1, pw_count):
+            part = jnp.where((pw - owner) % pw_count == shift, gathered[shift], part)
+        whole.append(part)
+    fine = jnp.concatenate(whole, axis=1).reshape(fine_here, half, 2, pairs)
+    return jnp.transpose(fine, (2, 0, 1, 3)).reshape(2, fine_here, half * pairs)
 
 
 def solution(mesh):

time: 256 us -> 235 us (0.918)
  waiting for transfers between devices: 112 us -> 95.8 us
  blocking collectives: 5.64 us -> 0 us
    ppermute x20 -> x21, waiting for transfers between devices: 87.6 us -> 59.1 us  [shifted(): return lax.ppermute(x, name, pairs)]
    ppermute x6 -> x4, waiting for transfers between devices: 24.5 us -> 36.7 us  [one_way(): moved = lax.ppermute(sent, name, pairs_below + pairs_above)]
    all_gather x1 -> x0, blocking collectives: 5.64 us -> none  [on_device(): fine = lax.all_gather(fine, 'pw', axis=0)]
    slice x1 -> x0, other arithmetic: 4.58 us -> none  [on_device(): value[:, first_half:]]
    ppermute x6 -> x4, starting transfers between devices: 8.62 us -> 6.08 us  [one_way(): moved = lax.ppermute(sent, name, pairs_below + pairs_above)]
    select_n x2 -> x3, other arithmetic: 5.34 us -> 7.81 us  [one_way(): sent = jnp.where(sends_below, below, above)]
    ppermute x20 -> x21, starting transfers between devices: 18.6 us -> 18.4 us  [shifted(): return lax.ppermute(x, name, pairs)]
  transfers between devices with their start and end apart: 28 -> 27, of which waited for: 12 -> 17; matrix products, arithmetic and copies ran while one was open for 14% -> 18% of each run, Pallas kernels for 23% -> 24%
where the time goes in v7:
time: 235 us; the launch traced here: 234 us
  waiting for transfers between devices  95.8 us (41%)
  Pallas kernels  57.5 us (24%)
  starting transfers between devices  32.8 us (14%)
  other arithmetic  31 us (13%)
  local copies, waits for them, and re-layouts  15.1 us (6%)
    ppermute x21, waiting for transfers between devices, shifted(): return lax.ppermute(x, name, pairs)  59.1 us
    ppermute x4, waiting for transfers between devices, one_way(): moved = lax.ppermute(sent, name, pairs_below + pairs_above)  36.7 us
    pallas_call x3, Pallas kernels, screen_product(): pl.pallas_call(kernel, out_shape=jax.ShapeDtypeStruct((blocks * points, b...  33.8 us
    pallas_call x4, Pallas kernels, contract(): pl.pallas_call(kernel, out_shape=jax.ShapeDtypeStruct((blocks * points, b...  21.4 us
    ppermute x21, starting transfers between devices, shifted(): return lax.ppermute(x, name, pairs)  18.4 us
    another operation x2, other arithmetic, on_device(): jnp.stack([jnp.concatenate([screen[0], screen[1]], axis=0), jnp.concatena...  13.4 us
    select_n x3, other arithmetic, one_way(): sent = jnp.where(sends_below, below, above)  7.81 us
    ppermute x1, starting transfers between devices, on_device(): lax.ppermute(own_valence, 'kpt', [(s, s + 1) for s in range(kpt_count - 1)])  6.92 us
  transfers between devices with their start and end apart: 27, of which 17 were waited for; matrix products, arithmetic and copies ran while one was open for 18% of the time, Pallas kernels for 24%

profile of v7, /device:TPU:0, one launch (start us, length us, event | category | flops | bytes accessed | tf_op | source)
XLA Modules:
  0.0 234.0 jit_solution(8388213971927121574)
XLA Ops:
  5.4 6.9 %collective-permute-start.8 = (bf16[2,8,64,1024]{3,2,1,0:T(8,128)(2,1)S(1)}, bf16[2,8,64,1024]{3,2,1,0:T(8,128)(2,1)}, u32[]{:S(2)}, u32[]{:S(2)}) collective-permute-start(bf16[2,8,64,1024]{3,2,1,0:T(8,128)(2,1)S(1)} %valence_columns.1.refs_2_.refs_4_.refs_5_.refs_3_), channel_id=1, source_target_pairs={{0,4},{4,8},{8,12},{1,5},{5,9},{9,13},{2,6},{6,10},{10,14},{3,7},{... | collective-permute-start | bytes 6291464 | tf_op jit(solution)/shard_map/ppermute | solution.py:260
  17.1 3.3 %fusion.1 = bf16[2,1024,1024]{2,1,0:T(8,128)(2,1)S(1)} fusion(s32[]{:T(128)S(6)} %select_n.381, bf16[2,1000,2000]{2,1,0:T(8,128)(2,1)} %param.20, pred[1024]{0:T(1024)(128)(4,1)S(1)} %get-tuple-element.45, pred[1024]{0:T(1024)(128)(4,1)S(1)} %get-tuple-element.46, bf16[2,1024]{1,0:T(2,128)(2,1)S(1)} %broadcast_select_fusion.3, bf16[2,1024]{1,0:T(2,128)(2,1)S(1)} %fusion.21), kind=kLoop, calls=%fused_computation.7 | loop fusion | flops 4194304 | bytes 12204548 | tf_op jit(solution)/shard_map/jit(_where)/select_n | solution.py:304
  22.9 16.6 %collective-permute-done = bf16[2,4,32,2000]{3,2,1,0:T(8,128)(2,1)S(1)} collective-permute-done((bf16[2,4,32,2000]{3,2,1,0:T(8,128)(2,1)}, bf16[2,4,32,2000]{3,2,1,0:T(8,128)(2,1)S(1)}, u32[]{:S(2)}, u32[]{:S(2)}) %collective-permute-start) | collective-permute-done | bytes 1024032 | tf_op jit(solution)/shard_map/ppermute | solution.py:22
  45.7 5.8 %maximum_bitcast_fusion = (bf16[1,2048,1024]{2,1,0:T(8,128)(2,1)}, bf16[1,2048,1024]{2,1,0:T(8,128)(2,1)}) fusion(bf16[1024,1024]{1,0:T(8,128)(2,1)} %get-tuple-element.24, bf16[1024,1024]{1,0:T(8,128)(2,1)} %get-tuple-element.23, bf16[1024,1024]{1,0:T(8,128)(2,1)} %fusion.32), kind=kLoop, calls=%fused_computation.8 | loop fusion | flops 16777216 | bytes 14680064 | tf_op jit(solution)/shard_map/stack | solution.py:307
  55.2 3.7 %collective-permute-start.1 = (bf16[2,128,1024]{2,1,0:T(8,128)(2,1)}, bf16[2,128,1024]{2,1,0:T(8,128)(2,1)S(1)}, u32[]{:S(2)}, u32[]{:S(2)}) collective-permute-start(bf16[2,128,1024]{2,1,0:T(8,128)(2,1)} %get-tuple-element.32), channel_id=1, source_target_pairs={{0,12},{4,0},{8,4},{12,8},{1,13},{5,1},{9,5},{13,9},{2,14},{6,2},{... | collective-permute-start | bytes 1572872 | tf_op jit(solution)/shard_map/ppermute | solution.py:22
  61.5 7.5 %pad_maximum_fusion.refs_4_ = bf16[2,2048,1024]{2,1,0:T(8,128)(2,1)} fusion(bf16[1,2048,1024]{2,1,0:T(8,128)(2,1)} %get-tuple-element.28, bf16[1,2048,1024]{2,1,0:T(8,128)(2,1)} %get-tuple-element.27), kind=kLoop, calls=%fused_computation.4 | loop fusion | flops 4194304 | bytes 16777216 | tf_op jit(solution)/shard_map/stack | solution.py:307
  69.0 8.8 %screen_product.3.refs_5_ = bf16[32,2,2,32,1024]{4,3,2,1,0:T(8,128)(2,1)} custom-call(s32[5]{0:T(128)S(1)} %concatenate.33.place_ref, bf16[1,2,128,1024]{3,2,1,0:T(8,128)(2,1)S(1)} %get-tuple-element.29.refs_0_, bf16[1,2,128,1024]{3,2,1,0:T(8,128)(2,1)S(1)} %collective-permute-done.5.refs_1_, bf16[1,2,128,1024]{3,2,1,0:T(8,128)(2,1)S(1)} %collective-permute-done.6.refs_2_, ...), custom_call_target="tpu_custom_call" | custom-call | flops 1 | bytes 1 | tf_op jit(solution)/shard_map/screen_product/pallas_call | solution.py:129
  77.9 11.8 %collective-permute-done.4 = bf16[2,128,1024]{2,1,0:T(8,128)(2,1)S(1)} collective-permute-done((bf16[2,128,1024]{2,1,0:T(8,128)(2,1)}, bf16[2,128,1024]{2,1,0:T(8,128)(2,1)S(1)}, u32[]{:S(2)}, u32[]{:S(2)}) %collective-permute-start.4) | collective-permute-done | bytes 524320 | tf_op jit(solution)/shard_map/ppermute | solution.py:22
  93.5 8.0 %collective-permute-done.15.refs_2_ = bf16[2,2,64,1024]{3,2,1,0:T(8,128)(2,1)S(1)} collective-permute-done((bf16[2,2,64,1024]{3,2,1,0:T(8,128)(2,1)S(1)}, bf16[2,2,64,1024]{3,2,1,0:T(8,128)(2,1)S(1)}, u32[]{:S(2)}, u32[]{:S(2)}) %collective-permute-start.15) | collective-permute-done | bytes 524320 | tf_op jit(solution)/shard_map/ppermute | solution.py:87
  101.5 3.3 %broadcast_select_fusion = bf16[2,8,64,1024]{3,2,1,0:T(8,128)(2,1)} fusion(bf16[2,8,64,1024]{3,2,1,0:T(8,128)(2,1)} %collective-permute-done.8.refs_2_, bf16[2,8,64,1024]{3,2,1,0:T(8,128)(2,1)} %collective-permute-done.9.refs_3_, pred[]{:T(512)S(6)} %eq.160), kind=kLoop, calls=%fused_computation.14 | loop fusion | flops 1048576 | bytes 6291457 | tf_op jit(solution)/shard_map/jit(_where)/select_n | solution.py:86
  106.9 3.2 %slice_select_fusion = bf16[2,6,64,1024]{3,2,1,0:T(8,128)(2,1)} fusion(bf16[2,8,64,1024]{3,2,1,0:T(8,128)(2,1)} %collective-permute-done.9.refs_3_, bf16[2,8,64,1024]{3,2,1,0:T(8,128)(2,1)} %collective-permute-done.8.refs_2_, pred[]{:T(512)S(6)} %eq.161), kind=kLoop, calls=%fused_computation.15 | loop fusion | flops 786432 | bytes 4718593 | tf_op jit(solution)/shard_map/jit(_where)/select_n | solution.py:86
  111.5 4.6 %collective-permute-done.11.refs_2_ = bf16[2,2,128,1024]{3,2,1,0:T(8,128)(2,1)} collective-permute-done((bf16[2,2,128,1024]{3,2,1,0:T(8,128)(2,1)S(1)}, bf16[2,2,128,1024]{3,2,1,0:T(8,128)(2,1)}, u32[]{:S(2)}, u32[]{:S(2)}) %collective-permute-start.11) | collective-permute-done | bytes 1048608 | tf_op jit(solution)/shard_map/ppermute | solution.py:22
  119.1 16.1 %screen_product.4.refs_5_ = bf16[32,2,2,32,1024]{4,3,2,1,0:T(8,128)(2,1)} custom-call(s32[6]{0:T(128)S(1)} %concatenate.32.place_ref, bf16[2,2,128,1024]{3,2,1,0:T(8,128)(2,1)S(1)} %pad_maximum_fusion.2.refs_0_, bf16[2,2,128,1024]{3,2,1,0:T(8,128)(2,1)} %collective-permute-done.10.refs_1_, ...), custom_call_target="tpu_custom_call", output_to_operand_aliasing={{}: (6, {})} | custom-call | flops 1 | bytes 1 | tf_op jit(solution)/shard_map/screen_product/pallas_call | solution.py:129
  135.2 15.5 %collective-permute-done.17.refs_3_ = bf16[2,6,64,1024]{3,2,1,0:T(8,128)(2,1)} collective-permute-done((bf16[2,6,64,1024]{3,2,1,0:T(8,128)(2,1)}, bf16[2,6,64,1024]{3,2,1,0:T(8,128)(2,1)}, u32[]{:S(2)}, u32[]{:S(2)}) %collective-permute-start.17) | collective-permute-done | bytes 1572896 | tf_op jit(solution)/shard_map/ppermute | solution.py:87
  157.2 8.9 %screen_product.5.refs_0_.refs_1_ = bf16[32,2,2,32,1024]{4,3,2,1,0:T(8,128)(2,1)} custom-call(s32[5]{0:T(128)S(1)} %concatenate.31.place_ref, bf16[1,2,128,1024]{3,2,1,0:T(8,128)(2,1)S(1)} %bitcast.116, bf16[1,2,128,1024]{3,2,1,0:T(8,128)(2,1)S(1)} %collective-permute-done.13.refs_1_, ...), custom_call_target="tpu_custom_call", output_to_operand_aliasing={{}: (6, {})} | custom-call | flops 1 | bytes 1 | tf_op jit(solution)/shard_map/screen_product/pallas_call | solution.py:129
  166.2 3.9 %contract.4.refs_5_ = f32[32,64,128]{2,1,0:T(8,128)S(1)} custom-call(s32[8]{0:T(128)S(1)} %gather_fusion.2, s32[1]{0:T(128)} %constant.232.clone.1.side_ref.owner_ref, s32[1]{0:T(128)} %bitcast.38.owner_ref, bf16[32,2,2,32,1024]{4,3,2,1,0:T(8,128)(2,1)} %screen_product.5.refs_0_.refs_1_, bf16[32,2,2,32,1024]{4,3,2,1,0:T(8,128)(2,1)} %screen_product.5.refs_0_.refs_1_, ...), custom_call_target="tpu_custom_call" | custom-call | flops 1 | bytes 1 | tf_op jit(solution)/shard_map/contract/pallas_call | solution.py:207
  170.1 8.2 %contract.5.refs_6_ = f32[32,64,128]{2,1,0:T(8,128)S(1)} custom-call(s32[16]{0:T(128)S(1)} %gather_fusion.1, s32[2]{0:T(128)S(1)} %pad_add_fusion.1.side_ref, s32[2]{0:T(128)S(1)} %get-tuple-element.22.owner_ref, bf16[32,2,2,32,1024]{4,3,2,1,0:T(8,128)(2,1)} %screen_product.5.refs_0_.refs_1_, ...), custom_call_target="tpu_custom_call", output_to_operand_aliasing={{}: (8, {})} | custom-call | flops 1 | bytes 1 | tf_op jit(solution)/shard_map/contract/pallas_call | solution.py:207
  178.4 4.8 %contract.6 = f32[32,64,128]{2,1,0:T(8,128)S(1)} custom-call(s32[8]{0:T(128)S(1)} %gather_fusion, s32[1]{0:T(128)} %bitcast.1.side_ref, s32[1]{0:T(128)} %bitcast.2.owner_ref, bf16[32,2,2,32,1024]{4,3,2,1,0:T(8,128)(2,1)} %screen_product.5.refs_0_.refs_1_, ...), custom_call_target="tpu_custom_call", output_to_operand_aliasing={{}: (9, {})} | custom-call | flops 1 | bytes 1 | tf_op jit(solution)/shard_map/contract/pallas_call | solution.py:207
  189.7 13.2 %collective-permute-done.20.refs_2_ = bf16[2,8,64,1024]{3,2,1,0:T(8,128)(2,1)} collective-permute-done((bf16[2,8,64,1024]{3,2,1,0:T(8,128)(2,1)}, bf16[2,8,64,1024]{3,2,1,0:T(8,128)(2,1)}, u32[]{:S(2)}, u32[]{:S(2)}) %collective-permute-start.20) | collective-permute-done | bytes 2097184 | tf_op jit(solution)/shard_map/ppermute | solution.py:87
  202.8 4.4 %contract.7 = f32[8,64,128]{2,1,0:T(8,128)S(1)} custom-call(s32[8]{0:T(128)S(1)} %gather_fusion.3, s32[1]{0:T(128)} %bitcast.46.side_ref, s32[1]{0:T(128)} %constant.232.clone.1.side_ref.owner_ref, bf16[32,2,2,32,1024]{4,3,2,1,0:T(8,128)(2,1)} %screen_product.5.refs_0_.refs_1_, bf16[32,2,2,32,1024]{4,3,2,1,0:T(8,128)(2,1)} %screen_product.5.refs_0_.refs_1_, ...), custom_call_target="tpu_custom_call" | custom-call | flops 1 | bytes 1 | tf_op jit(solution)/shard_map/contract/pallas_call | solution.py:207
  213.9 3.8 %collective-permute-start.25 = (f32[16,16,128]{2,1,0:T(8,128)S(1)}, f32[16,16,128]{2,1,0:T(8,128)S(1)}, u32[]{:S(2)}, u32[]{:S(2)}) collective-permute-start(f32[16,16,128]{2,1,0:T(8,128)S(1)} %get-tuple-element.34), channel_id=1, source_target_pairs={{0,12},{4,0},{8,4},{12,8},{1,13},{5,1},{9,5},{13,9},{2,14},{6,2},{... | collective-permute-start | bytes 393224 | tf_op jit(solution)/shard_map/ppermute | solution.py:22
  217.7 4.5 %collective-permute-done.23 = f32[16,16,128]{2,1,0:T(8,128)S(1)} collective-permute-done((f32[16,16,128]{2,1,0:T(8,128)S(1)}, f32[16,16,128]{2,1,0:T(8,128)S(1)}, u32[]{:S(2)}, u32[]{:S(2)}) %collective-permute-start.23) | collective-permute-done | bytes 131104 | tf_op jit(solution)/shard_map/ppermute | solution.py:22
  222.2 5.4 %collective-permute-done.24 = f32[16,16,128]{2,1,0:T(8,128)S(1)} collective-permute-done((f32[16,16,128]{2,1,0:T(8,128)S(1)}, f32[16,16,128]{2,1,0:T(8,128)S(1)}, u32[]{:S(2)}, u32[]{:S(2)}) %collective-permute-start.24) | collective-permute-done | bytes 131104 | tf_op jit(solution)/shard_map/ppermute | solution.py:22
  228.2 4.4 %collective-permute-done.26 = f32[16,16,128]{2,1,0:T(8,128)S(1)} collective-permute-done((f32[16,16,128]{2,1,0:T(8,128)S(1)}, f32[16,16,128]{2,1,0:T(8,128)S(1)}, u32[]{:S(2)}, u32[]{:S(2)}) %collective-permute-start.26) | collective-permute-done | bytes 131104 | tf_op jit(solution)/shard_map/ppermute | solution.py:22
  (144 shorter events, 56.5 us)
Async XLA Ops:
  4.0 51.2 %collective-permute-start.9 = (bf16[2,8,64,1024]{3,2,1,0:T(8,128)(2,1)S(1)}, bf16[2,8,64,1024]{3,2,1,0:T(8,128)(2,1)}, u32[]{:S(2)}, u32[]{:S(2)}) collective-permute-start(bf16[2,8,64,1024]{3,2,1,0:T(8,128)(2,1)S(1)} %valence_columns.1.refs_2_.refs_4_.refs_5_.refs_3_), channel_id=1, source_target_pairs={{4,0},{8,4},{12,8},{5,1},{9,5},{13,9},{6,2},{10,6},{14,10},{7,3},{... | collective-permute-start | bytes 6291464 | tf_op jit(solution)/shard_map/ppermute | solution.py:261
  5.4 53.5 %collective-permute-start.8 = (bf16[2,8,64,1024]{3,2,1,0:T(8,128)(2,1)S(1)}, bf16[2,8,64,1024]{3,2,1,0:T(8,128)(2,1)}, u32[]{:S(2)}, u32[]{:S(2)}) collective-permute-start(bf16[2,8,64,1024]{3,2,1,0:T(8,128)(2,1)S(1)} %valence_columns.1.refs_2_.refs_4_.refs_5_.refs_3_), channel_id=1, source_target_pairs={{0,4},{4,8},{8,12},{1,5},{5,9},{9,13},{2,6},{6,10},{10,14},{3,7},{... | collective-permute-start | bytes 6291464 | tf_op jit(solution)/shard_map/ppermute | solution.py:260
  14.6 24.8 %collective-permute-start = (bf16[2,4,32,2000]{3,2,1,0:T(8,128)(2,1)}, bf16[2,4,32,2000]{3,2,1,0:T(8,128)(2,1)S(1)}, u32[]{:S(2)}, u32[]{:S(2)}) collective-permute-start(bf16[2,4,32,2000]{3,2,1,0:T(8,128)(2,1)} %dynamic-slice_bitcast_fusion), channel_id=1, source_target_pairs={{0,2},{2,0},{1,3},{3,1},{4,6},{6,4},{5,7},{7,5},{8,10},{10,8},{9,1... | collective-permute-start | bytes 3072008 | tf_op jit(solution)/shard_map/ppermute | solution.py:22
  42.5 12.6 %collective-permute-start.6 = (bf16[1,2,128,1024]{3,2,1,0:T(8,128)(2,1)S(1)}, bf16[1,2,128,1024]{3,2,1,0:T(8,128)(2,1)S(1)}, u32[]{:S(2)}, u32[]{:S(2)}) collective-permute-start(bf16[1,2,128,1024]{3,2,1,0:T(8,128)(2,1)S(1)} %get-tuple-element.29.refs_0_), channel_id=1, source_target_pairs={{0,2},{2,0},{1,3},{3,1},{4,6},{6,4},{5,7},{7,5},{8,10},{10,8},{9,1... | collective-permute-start | bytes 1572872 | tf_op jit(solution)/shard_map/ppermute | solution.py:22
  45.7 14.5 %collective-permute-start.5 = (bf16[1,2,128,1024]{3,2,1,0:T(8,128)(2,1)S(1)}, bf16[1,2,128,1024]{3,2,1,0:T(8,128)(2,1)S(1)}, u32[]{:S(2)}, u32[]{:S(2)}) collective-permute-start(bf16[1,2,128,1024]{3,2,1,0:T(8,128)(2,1)S(1)} %get-tuple-element.29.refs_0_), channel_id=1, source_target_pairs={{0,1},{1,0},{2,3},{3,2},{4,5},{5,4},{6,7},{7,6},{8,9},{9,8},{10,11... | collective-permute-start | bytes 1572872 | tf_op jit(solution)/shard_map/ppermute | solution.py:22
  51.5 38.2 %collective-permute-start.4 = (bf16[2,128,1024]{2,1,0:T(8,128)(2,1)}, bf16[2,128,1024]{2,1,0:T(8,128)(2,1)S(1)}, u32[]{:S(2)}, u32[]{:S(2)}) collective-permute-start(bf16[2,128,1024]{2,1,0:T(8,128)(2,1)} %get-tuple-element.30), channel_id=1, source_target_pairs={{0,8},{4,12},{8,0},{12,4},{1,9},{5,13},{9,1},{13,5},{2,10},{6,14},... | collective-permute-start | bytes 1572872 | tf_op jit(solution)/shard_map/ppermute | solution.py:22
  55.1 34.6 %collective-permute-start.3 = (bf16[2,128,1024]{2,1,0:T(8,128)(2,1)}, bf16[2,128,1024]{2,1,0:T(8,128)(2,1)}, u32[]{:S(2)}, u32[]{:S(2)}) collective-permute-start(bf16[2,128,1024]{2,1,0:T(8,128)(2,1)} %get-tuple-element.31), channel_id=1, source_target_pairs={{0,4},{4,8},{8,12},{12,0},{1,5},{5,9},{9,13},{13,1},{2,6},{6,10},{... | collective-permute-start | bytes 1572872 | tf_op jit(solution)/shard_map/ppermute | solution.py:22
  55.2 35.7 %collective-permute-start.1 = (bf16[2,128,1024]{2,1,0:T(8,128)(2,1)}, bf16[2,128,1024]{2,1,0:T(8,128)(2,1)S(1)}, u32[]{:S(2)}, u32[]{:S(2)}) collective-permute-start(bf16[2,128,1024]{2,1,0:T(8,128)(2,1)} %get-tuple-element.32), channel_id=1, source_target_pairs={{0,12},{4,0},{8,4},{12,8},{1,13},{5,1},{9,5},{13,9},{2,14},{6,2},{... | collective-permute-start | bytes 1572872 | tf_op jit(solution)/shard_map/ppermute | solution.py:22
  58.9 10.1 %collective-permute-start.7 = (bf16[1,2,128,1024]{3,2,1,0:T(8,128)(2,1)S(1)}, bf16[1,2,128,1024]{3,2,1,0:T(8,128)(2,1)S(1)}, u32[]{:S(2)}, u32[]{:S(2)}) collective-permute-start(bf16[1,2,128,1024]{3,2,1,0:T(8,128)(2,1)S(1)} %collective-permute-done.6.refs_2_), channel_id=1, source_target_pairs={{0,1},{1,0},{2,3},{3,2},{4,5},{5,4},{6,7},{7,6},{8,9},{9,8},{10,11... | collective-permute-start | bytes 1572872 | tf_op jit(solution)/shard_map/ppermute | solution.py:22
  60.2 41.3 %collective-permute-start.15 = (bf16[2,2,64,1024]{3,2,1,0:T(8,128)(2,1)S(1)}, bf16[2,2,64,1024]{3,2,1,0:T(8,128)(2,1)S(1)}, u32[]{:S(2)}, u32[]{:S(2)}) collective-permute-start(bf16[2,2,64,1024]{3,2,1,0:T(8,128)(2,1)S(1)} %slice_select_fusion.1), channel_id=1, source_target_pairs={{8,12},{4,0},{9,13},{5,1},{10,14},{6,2},{11,15},{7,3},{24,28},{20,... | collective-permute-start | bytes 1572872 | tf_op jit(solution)/shard_map/ppermute | solution.py:87
  92.2 23.9 %collective-permute-start.11 = (bf16[2,2,128,1024]{3,2,1,0:T(8,128)(2,1)S(1)}, bf16[2,2,128,1024]{3,2,1,0:T(8,128)(2,1)}, u32[]{:S(2)}, u32[]{:S(2)}) collective-permute-start(bf16[2,2,128,1024]{3,2,1,0:T(8,128)(2,1)S(1)} %pad_maximum_fusion.2.refs_0_), channel_id=1, source_target_pairs={{0,2},{2,0},{1,3},{3,1},{4,6},{6,4},{5,7},{7,5},{8,10},{10,8},{9,1... | collective-permute-start | bytes 3145736 | tf_op jit(solution)/shard_map/ppermute | solution.py:22
  104.9 45.9 %collective-permute-start.16 = (bf16[2,8,64,1024]{3,2,1,0:T(8,128)(2,1)}, bf16[2,8,64,1024]{3,2,1,0:T(8,128)(2,1)}, u32[]{:S(2)}, u32[]{:S(2)}) collective-permute-start(bf16[2,8,64,1024]{3,2,1,0:T(8,128)(2,1)} %broadcast_select_fusion), channel_id=1, source_target_pairs={{4,8},{8,4},{5,9},{9,5},{6,10},{10,6},{7,11},{11,7},{20,24},{24,20... | collective-permute-start | bytes 6291464 | tf_op jit(solution)/shard_map/ppermute | solution.py:87
  110.1 40.6 %collective-permute-start.17 = (bf16[2,6,64,1024]{3,2,1,0:T(8,128)(2,1)}, bf16[2,6,64,1024]{3,2,1,0:T(8,128)(2,1)}, u32[]{:S(2)}, u32[]{:S(2)}) collective-permute-start(bf16[2,6,64,1024]{3,2,1,0:T(8,128)(2,1)} %slice_select_fusion), channel_id=1, source_target_pairs={{8,12},{4,0},{9,13},{5,1},{10,14},{6,2},{11,15},{7,3},{24,28},{20,... | collective-permute-start | bytes 4718600 | tf_op jit(solution)/shard_map/ppermute | solution.py:87
  111.4 5.5 %collective-permute-start.10 = (bf16[2,2,128,1024]{3,2,1,0:T(8,128)(2,1)S(1)}, bf16[2,2,128,1024]{3,2,1,0:T(8,128)(2,1)}, u32[]{:S(2)}, u32[]{:S(2)}) collective-permute-start(bf16[2,2,128,1024]{3,2,1,0:T(8,128)(2,1)S(1)} %pad_maximum_fusion.2.refs_0_), channel_id=1, source_target_pairs={{0,1},{1,0},{2,3},{3,2},{4,5},{5,4},{6,7},{7,6},{8,9},{9,8},{10,11... | collective-permute-start | bytes 3145736 | tf_op jit(solution)/shard_map/ppermute | solution.py:22
  116.1 3.0 %collective-permute-start.12 = (bf16[2,2,128,1024]{3,2,1,0:T(8,128)(2,1)}, bf16[2,2,128,1024]{3,2,1,0:T(8,128)(2,1)}, u32[]{:S(2)}, u32[]{:S(2)}) collective-permute-start(bf16[2,2,128,1024]{3,2,1,0:T(8,128)(2,1)} %collective-permute-done.11.refs_2_), channel_id=1, source_target_pairs={{0,1},{1,0},{2,3},{3,2},{4,5},{5,4},{6,7},{7,6},{8,9},{9,8},{10,11... | collective-permute-start | bytes 3145736 | tf_op jit(solution)/shard_map/ppermute | solution.py:22
  116.2 37.0 %collective-permute-start.2 = (bf16[1,2,128,1024]{3,2,1,0:T(8,128)(2,1)}, bf16[1,2,128,1024]{3,2,1,0:T(8,128)(2,1)}, u32[]{:S(2)}, u32[]{:S(2)}) collective-permute-start(bf16[1,2,128,1024]{3,2,1,0:T(8,128)(2,1)} %bitcast.114), channel_id=1, source_target_pairs={{0,2},{2,0},{1,3},{3,1},{4,6},{6,4},{5,7},{7,5},{8,10},{10,8},{9,1... | collective-permute-start | bytes 1572872 | tf_op jit(solution)/shard_map/ppermute | solution.py:22
  150.7 52.1 %collective-permute-start.20 = (bf16[2,8,64,1024]{3,2,1,0:T(8,128)(2,1)}, bf16[2,8,64,1024]{3,2,1,0:T(8,128)(2,1)}, u32[]{:S(2)}, u32[]{:S(2)}) collective-permute-start(bf16[2,8,64,1024]{3,2,1,0:T(8,128)(2,1)} %collective-permute-done.16.refs_4_), channel_id=1, source_target_pairs={{8,12},{4,0},{9,13},{5,1},{10,14},{6,2},{11,15},{7,3},{24,28},{20,... | collective-permute-start | bytes 6291464 | tf_op jit(solution)/shard_map/ppermute | solution.py:87
  153.3 2.9 %collective-permute-start.14 = (bf16[1,2,128,1024]{3,2,1,0:T(8,128)(2,1)}, bf16[1,2,128,1024]{3,2,1,0:T(8,128)(2,1)S(1)}, u32[]{:S(2)}, u32[]{:S(2)}) collective-permute-start(bf16[1,2,128,1024]{3,2,1,0:T(8,128)(2,1)} %collective-permute-done.2.refs_2_), channel_id=1, source_target_pairs={{0,1},{1,0},{2,3},{3,2},{4,5},{5,4},{6,7},{7,6},{8,9},{9,8},{10,11... | collective-permute-start | bytes 1572872 | tf_op jit(solution)/shard_map/ppermute | solution.py:22
  188.3 19.0 %collective-permute-start.19 = (f32[32,16,128]{2,1,0:T(8,128)S(1)}, f32[32,16,128]{2,1,0:T(8,128)S(1)}, u32[]{:S(2)}, u32[]{:S(2)}) collective-permute-start(f32[32,16,128]{2,1,0:T(8,128)S(1)} %dynamic-slice_bitcast_fusion.5), channel_id=1, source_target_pairs={{0,2},{2,0},{1,3},{3,1},{4,6},{6,4},{5,7},{7,5},{8,10},{10,8},{9,1... | collective-permute-start | bytes 786440 | tf_op jit(solution)/shard_map/ppermute | solution.py:22
  208.7 4.3 %collective-permute-start.22 = (f32[8,16,128]{2,1,0:T(8,128)S(1)}, f32[8,16,128]{2,1,0:T(8,128)S(1)}, u32[]{:S(2)}, u32[]{:S(2)}) collective-permute-start(f32[8,16,128]{2,1,0:T(8,128)S(1)} %dynamic-slice_bitcast_fusion.10), channel_id=1, source_target_pairs={{0,2},{2,0},{1,3},{3,1},{4,6},{6,4},{5,7},{7,5},{8,10},{10,8},{9,1... | collective-permute-start | bytes 196616 | tf_op jit(solution)/shard_map/ppermute | solution.py:22
  213.8 8.4 %collective-permute-start.23 = (f32[16,16,128]{2,1,0:T(8,128)S(1)}, f32[16,16,128]{2,1,0:T(8,128)S(1)}, u32[]{:S(2)}, u32[]{:S(2)}) collective-permute-start(f32[16,16,128]{2,1,0:T(8,128)S(1)} %get-tuple-element.33), channel_id=1, source_target_pairs={{0,4},{4,8},{8,12},{12,0},{1,5},{5,9},{9,13},{13,1},{2,6},{6,10},{... | collective-permute-start | bytes 393224 | tf_op jit(solution)/shard_map/ppermute | solution.py:22
  213.9 8.3 %collective-permute-start.25 = (f32[16,16,128]{2,1,0:T(8,128)S(1)}, f32[16,16,128]{2,1,0:T(8,128)S(1)}, u32[]{:S(2)}, u32[]{:S(2)}) collective-permute-start(f32[16,16,128]{2,1,0:T(8,128)S(1)} %get-tuple-element.34), channel_id=1, source_target_pairs={{0,12},{4,0},{8,4},{12,8},{1,13},{5,1},{9,5},{13,9},{2,14},{6,2},{... | collective-permute-start | bytes 393224 | tf_op jit(solution)/shard_map/ppermute | solution.py:22
  217.7 9.9 %collective-permute-start.24 = (f32[16,16,128]{2,1,0:T(8,128)S(1)}, f32[16,16,128]{2,1,0:T(8,128)S(1)}, u32[]{:S(2)}, u32[]{:S(2)}) collective-permute-start(f32[16,16,128]{2,1,0:T(8,128)S(1)} %get-tuple-element.35), channel_id=1, source_target_pairs={{0,8},{4,12},{8,0},{12,4},{1,9},{5,13},{9,1},{13,5},{2,10},{6,14},... | collective-permute-start | bytes 393224 | tf_op jit(solution)/shard_map/ppermute | solution.py:22
  227.6 5.0 %collective-permute-start.26 = (f32[16,16,128]{2,1,0:T(8,128)S(1)}, f32[16,16,128]{2,1,0:T(8,128)S(1)}, u32[]{:S(2)}, u32[]{:S(2)}) collective-permute-start(f32[16,16,128]{2,1,0:T(8,128)S(1)} %fusion.8), channel_id=1, source_target_pairs={{0,2},{2,0},{1,3},{3,1},{4,6},{6,4},{5,7},{7,5},{8,10},{10,8},{9,1... | collective-permute-start | bytes 393224 | tf_op jit(solution)/shard_map/ppermute | solution.py:22
  (22 other events, 354.3 us)

commit v8 on v7

--- a/solution.py
+++ b/solution.py
@@ -75,16 +75,17 @@
     )(core.reshape(1), valence, valence_head[..., None], selector)
 
 
-def one_way(below, above, pairs_below, pairs_above, name):
+def one_way(below, above, pairs_below, pairs_above, name, gates=()):
     senders = [pair[0] for pair in pairs_below + pairs_above]
     takers = [pair[1] for pair in pairs_below + pairs_above]
     if len(set(senders)) < len(senders) or len(set(takers)) < len(takers):
+        below, above = after((below, above), gates)
         return lax.ppermute(below, name, pairs_below), lax.ppermute(above, name, pairs_above)
     sent = below
     if above is not below:
         sends_below = jnp.isin(lax.axis_index(name), jnp.array([pair[0] for pair in pairs_below]))
         sent = jnp.where(sends_below, below, above)
-    moved = lax.ppermute(sent, name, pairs_below + pairs_above)
+    moved = lax.ppermute(after(sent, gates), name, pairs_below + pairs_above)
     return moved, moved
 
 
@@ -342,20 +343,19 @@
     to_ends, to_others = line_pairs(kpt_count, 2)
     early_rows = max(points // 4, 1)
     first_part = one_way(*[value[:, :early_rows] for value in step_one], *to_ends, "kpt")
-    held = after(step_one, [near_group, distant, first_part])
-    ends = {2: [first_part, one_way(*[value[:, early_rows:] for value in held], *to_ends, "kpt")]}
+    gates = [near_group, distant, first_part]
+    ends = {2: [first_part, one_way(*[value[:, early_rows:] for value in step_one], *to_ends, "kpt", gates)]}
     others = {}
     if kpt_count > 3:
-        others[2] = [one_way(*held, *to_others, "kpt")]
+        others[2] = [one_way(*step_one, *to_others, "kpt", gates)]
     store = product(near, near_pieces, right, store)
     for step in range(3, kpt_count):
         below, above = others[step - 1][0]
         gates = [store, ends[2]]
-        below, above = [after(below, gates)] * 2 if above is below else after([below, above], gates)
         to_ends, to_others = line_pairs(kpt_count, step)
-        ends[step] = [one_way(below, above, *to_ends, "kpt")]
+        ends[step] = [one_way(below, above, *to_ends, "kpt", gates)]
         if step < kpt_count - 1:
-            others[step] = [one_way(below, above, *to_others, "kpt")]
+            others[step] = [one_way(below, above, *to_others, "kpt", gates)]
     far_pieces = [own for across in after(far_across, store) for own in share(across, "band")]
     store = product(far, far_pieces, after(right, others.get(2, ends[2])), store)
 
@@ -421,7 +421,9 @@
     late_stencil = lax.dynamic_slice_in_dim(stencil, last_owner * points, points, 1)
     fine = fine + jnp.dot(late_stencil, late, precision=highest)
     fine_here = neighbors.shape[0] // kpt_count
-    fine = sum(deal(fine.reshape(kpt_count, fine_here, kept, lanes), "kpt"))
+    fine = fine.reshape(kpt_count, fine_here, kept, lanes)
+    own_fine = lax.dynamic_index_in_dim(fine, kpt, 0, keepdims=False)
+    fine = own_fine + sum(piece.astype(f32) for piece in deal(fine.astype(bf16), "kpt")[1:])
     gathered = share(fine, "pw")
     whole = []
     for owner in range(pw_count):

time: 235 us -> 228 us (0.970)
  waiting for transfers between devices: 95.8 us -> 83.5 us
    ppermute x4, waiting for transfers between devices: 36.7 us -> 14.9 us  [one_way(): moved = lax.ppermute(after(sent, gates), name, pairs_below + pairs_above)]
    ppermute x21, waiting for transfers between devices: 59.1 us -> 66.9 us  [shifted(): return lax.ppermute(x, name, pairs)]
    ppermute x21, starting transfers between devices: 18.4 us -> 21.1 us  [shifted(): return lax.ppermute(x, name, pairs)]
  transfers between devices with their start and end apart: 27 -> 27, of which waited for: 17 -> 15; matrix products, arithmetic and copies ran while one was open for 18% -> 19% of each run, Pallas kernels for 24% -> 25%
where the time goes in v8:
time: 228 us; the launch traced here: 227 us
  waiting for transfers between devices  83.5 us (37%)
  Pallas kernels  57.9 us (25%)
  starting transfers between devices  34.8 us (15%)
  other arithmetic  31.6 us (14%)
  local copies, waits for them, and re-layouts  16.9 us (7%)
    ppermute x21, waiting for transfers between devices, shifted(): return lax.ppermute(x, name, pairs)  66.9 us
    pallas_call x3, Pallas kernels, screen_product(): pl.pallas_call(kernel, out_shape=jax.ShapeDtypeStruct((blocks * points, b...  34.1 us
    pallas_call x4, Pallas kernels, contract(): pl.pallas_call(kernel, out_shape=jax.ShapeDtypeStruct((blocks * points, b...  21.6 us
    ppermute x21, starting transfers between devices, shifted(): return lax.ppermute(x, name, pairs)  21.1 us
    ppermute x4, waiting for transfers between devices, one_way(): moved = lax.ppermute(after(sent, gates), name, pairs_below + pairs_above)  14.9 us
    another operation x2, other arithmetic, on_device(): jnp.stack([jnp.concatenate([screen[0], screen[1]], axis=0), jnp.concatena...  13.3 us
    select_n x3, other arithmetic, one_way(): sent = jnp.where(sends_below, below, above)  8.44 us
    ppermute x1, starting transfers between devices, on_device(): lax.ppermute(own_valence, 'kpt', [(s, s + 1) for s in range(kpt_count - 1)])  6.42 us
  transfers between devices with their start and end apart: 27, of which 15 were waited for; matrix products, arithmetic and copies ran while one was open for 19% of the time, Pallas kernels for 25%

profile of v8, /device:TPU:0, one launch (start us, length us, event | category | flops | bytes accessed | tf_op | source)
XLA Modules:
  0.0 226.7 jit_solution(1302324624248500732)
XLA Ops:
  4.0 6.4 %collective-permute-start.8 = (bf16[2,8,64,1024]{3,2,1,0:T(8,128)(2,1)S(1)}, bf16[2,8,64,1024]{3,2,1,0:T(8,128)(2,1)}, u32[]{:S(2)}, u32[]{:S(2)}) collective-permute-start(bf16[2,8,64,1024]{3,2,1,0:T(8,128)(2,1)S(1)} %valence_columns.1.refs_2_.refs_4_.refs_5_.refs_3_), channel_id=1, source_target_pairs={{0,4},{4,8},{8,12},{1,5},{5,9},{9,13},{2,6},{6,10},{10,14},{3,7},{... | collective-permute-start | bytes 6291464 | tf_op jit(solution)/shard_map/ppermute | solution.py:261
  16.1 3.3 %fusion.1 = bf16[2,1024,1024]{2,1,0:T(8,128)(2,1)S(1)} fusion(s32[]{:T(128)S(6)} %select_n.382, bf16[2,1000,2000]{2,1,0:T(8,128)(2,1)} %param.20, pred[1024]{0:T(1024)(128)(4,1)S(1)} %get-tuple-element.45, pred[1024]{0:T(1024)(128)(4,1)S(1)} %get-tuple-element.46, bf16[2,1024]{1,0:T(2,128)(2,1)S(1)} %broadcast_select_fusion.3, bf16[2,1024]{1,0:T(2,128)(2,1)S(1)} %fusion.19), kind=kLoop, calls=%fused_computation.7 | loop fusion | flops 4194304 | bytes 12204548 | tf_op jit(solution)/shard_map/jit(_where)/select_n | solution.py:305
  21.9 17.0 %collective-permute-done = bf16[2,4,32,2000]{3,2,1,0:T(8,128)(2,1)S(1)} collective-permute-done((bf16[2,4,32,2000]{3,2,1,0:T(8,128)(2,1)}, bf16[2,4,32,2000]{3,2,1,0:T(8,128)(2,1)S(1)}, u32[]{:S(2)}, u32[]{:S(2)}) %collective-permute-start) | collective-permute-done | bytes 1024032 | tf_op jit(solution)/shard_map/ppermute | solution.py:22
  44.9 5.8 %maximum_bitcast_fusion = (bf16[1,2048,1024]{2,1,0:T(8,128)(2,1)}, bf16[1,2048,1024]{2,1,0:T(8,128)(2,1)}) fusion(bf16[1024,1024]{1,0:T(8,128)(2,1)} %get-tuple-element.24, bf16[1024,1024]{1,0:T(8,128)(2,1)} %get-tuple-element.23, bf16[1024,1024]{1,0:T(8,128)(2,1)} %fusion.30), kind=kLoop, calls=%fused_computation.8 | loop fusion | flops 16777216 | bytes 14680064 | tf_op jit(solution)/shard_map/stack | solution.py:308
  50.7 4.4 %collective-permute-start.1 = (bf16[2,128,1024]{2,1,0:T(8,128)(2,1)}, bf16[2,128,1024]{2,1,0:T(8,128)(2,1)S(1)}, u32[]{:S(2)}, u32[]{:S(2)}) collective-permute-start(bf16[2,128,1024]{2,1,0:T(8,128)(2,1)} %get-tuple-element.32), channel_id=1, source_target_pairs={{0,12},{4,0},{8,4},{12,8},{1,13},{5,1},{9,5},{13,9},{2,14},{6,2},{... | collective-permute-start | bytes 1572872 | tf_op jit(solution)/shard_map/ppermute | solution.py:22
  56.6 2.6 %collective-permute-start.4 = (bf16[2,128,1024]{2,1,0:T(8,128)(2,1)}, bf16[2,128,1024]{2,1,0:T(8,128)(2,1)}, u32[]{:S(2)}, u32[]{:S(2)}) collective-permute-start(bf16[2,128,1024]{2,1,0:T(8,128)(2,1)} %get-tuple-element.30), channel_id=1, source_target_pairs={{0,8},{4,12},{8,0},{12,4},{1,9},{5,13},{9,1},{13,5},{2,10},{6,14},... | collective-permute-start | bytes 1572872 | tf_op jit(solution)/shard_map/ppermute | solution.py:22
  60.9 7.5 %pad_maximum_fusion.refs_4_ = bf16[2,2048,1024]{2,1,0:T(8,128)(2,1)} fusion(bf16[1,2048,1024]{2,1,0:T(8,128)(2,1)} %get-tuple-element.28, bf16[1,2048,1024]{2,1,0:T(8,128)(2,1)} %get-tuple-element.27), kind=kLoop, calls=%fused_computation.4 | loop fusion | flops 4194304 | bytes 16777216 | tf_op jit(solution)/shard_map/stack | solution.py:308
  73.9 9.1 %screen_product.3.refs_5_ = bf16[32,2,2,32,1024]{4,3,2,1,0:T(8,128)(2,1)} custom-call(s32[5]{0:T(128)S(1)} %concatenate.33.place_ref, bf16[1,2,128,1024]{3,2,1,0:T(8,128)(2,1)S(1)} %get-tuple-element.29.refs_0_, bf16[1,2,128,1024]{3,2,1,0:T(8,128)(2,1)S(1)} %copy-done.7, bf16[1,2,128,1024]{3,2,1,0:T(8,128)(2,1)} %collective-permute-done.6.refs_2_, ...), custom_call_target="tpu_custom_call" | custom-call | flops 1 | bytes 1 | tf_op jit(solution)/shard_map/screen_product/pallas_call | solution.py:130
  84.2 20.0 %collective-permute-done.4 = bf16[2,128,1024]{2,1,0:T(8,128)(2,1)} collective-permute-done((bf16[2,128,1024]{2,1,0:T(8,128)(2,1)}, bf16[2,128,1024]{2,1,0:T(8,128)(2,1)}, u32[]{:S(2)}, u32[]{:S(2)}) %collective-permute-start.4) | collective-permute-done | bytes 524320 | tf_op jit(solution)/shard_map/ppermute | solution.py:22
  107.1 3.1 %broadcast_select_fusion = bf16[2,8,64,1024]{3,2,1,0:T(8,128)(2,1)} fusion(bf16[2,8,64,1024]{3,2,1,0:T(8,128)(2,1)} %collective-permute-done.8.refs_2_, bf16[2,8,64,1024]{3,2,1,0:T(8,128)(2,1)} %collective-permute-done.9.refs_3_, pred[]{:T(512)S(6)} %eq.159), kind=kLoop, calls=%fused_computation.14 | loop fusion | flops 1048576 | bytes 6291457 | tf_op jit(solution)/shard_map/jit(_where)/select_n | solution.py:87
  112.2 3.2 %slice_select_fusion = bf16[2,6,64,1024]{3,2,1,0:T(8,128)(2,1)} fusion(bf16[2,8,64,1024]{3,2,1,0:T(8,128)(2,1)} %collective-permute-done.9.refs_3_, bf16[2,8,64,1024]{3,2,1,0:T(8,128)(2,1)} %collective-permute-done.8.refs_2_, pred[]{:T(512)S(6)} %eq.160), kind=kLoop, calls=%fused_computation.15 | loop fusion | flops 786432 | bytes 4718593 | tf_op jit(solution)/shard_map/jit(_where)/select_n | solution.py:87
  116.8 12.5 %collective-permute-done.11.refs_2_ = bf16[2,2,128,1024]{3,2,1,0:T(8,128)(2,1)} collective-permute-done((bf16[2,2,128,1024]{3,2,1,0:T(8,128)(2,1)S(1)}, bf16[2,2,128,1024]{3,2,1,0:T(8,128)(2,1)}, u32[]{:S(2)}, u32[]{:S(2)}) %collective-permute-start.11) | collective-permute-done | bytes 1048608 | tf_op jit(solution)/shard_map/ppermute | solution.py:22
  132.3 16.1 %screen_product.4.refs_5_ = bf16[32,2,2,32,1024]{4,3,2,1,0:T(8,128)(2,1)} custom-call(s32[6]{0:T(128)S(1)} %concatenate.32.place_ref, bf16[2,2,128,1024]{3,2,1,0:T(8,128)(2,1)S(1)} %pad_maximum_fusion.2.refs_0_, bf16[2,2,128,1024]{3,2,1,0:T(8,128)(2,1)} %collective-permute-done.10.refs_1_, ...), custom_call_target="tpu_custom_call", output_to_operand_aliasing={{}: (6, {})} | custom-call | flops 1 | bytes 1 | tf_op jit(solution)/shard_map/screen_product/pallas_call | solution.py:130
  148.4 3.9 %collective-permute-done.17.refs_3_ = bf16[2,6,64,1024]{3,2,1,0:T(8,128)(2,1)} collective-permute-done((bf16[2,6,64,1024]{3,2,1,0:T(8,128)(2,1)}, bf16[2,6,64,1024]{3,2,1,0:T(8,128)(2,1)}, u32[]{:S(2)}, u32[]{:S(2)}) %collective-permute-start.17) | collective-permute-done | bytes 1572896 | tf_op jit(solution)/shard_map/ppermute | solution.py:88
  158.1 8.9 %screen_product.5.refs_0_.refs_1_ = bf16[32,2,2,32,1024]{4,3,2,1,0:T(8,128)(2,1)} custom-call(s32[5]{0:T(128)S(1)} %concatenate.31.place_ref, bf16[1,2,128,1024]{3,2,1,0:T(8,128)(2,1)S(1)} %bitcast.114, bf16[1,2,128,1024]{3,2,1,0:T(8,128)(2,1)S(1)} %collective-permute-done.13.refs_1_, ...), custom_call_target="tpu_custom_call", output_to_operand_aliasing={{}: (6, {})} | custom-call | flops 1 | bytes 1 | tf_op jit(solution)/shard_map/screen_product/pallas_call | solution.py:130
  167.0 3.9 %contract.4.refs_5_ = f32[32,64,128]{2,1,0:T(8,128)S(1)} custom-call(s32[8]{0:T(128)S(1)} %gather_fusion.2, s32[1]{0:T(128)} %constant.232.clone.1.side_ref.owner_ref, s32[1]{0:T(128)} %bitcast.38.owner_ref, bf16[32,2,2,32,1024]{4,3,2,1,0:T(8,128)(2,1)} %screen_product.5.refs_0_.refs_1_, bf16[32,2,2,32,1024]{4,3,2,1,0:T(8,128)(2,1)} %screen_product.5.refs_0_.refs_1_, ...), custom_call_target="tpu_custom_call" | custom-call | flops 1 | bytes 1 | tf_op jit(solution)/shard_map/contract/pallas_call | solution.py:208
  171.0 8.2 %contract.5.refs_6_ = f32[32,64,128]{2,1,0:T(8,128)S(1)} custom-call(s32[16]{0:T(128)S(1)} %gather_fusion.1, s32[2]{0:T(128)S(1)} %pad_add_fusion.1.side_ref, s32[2]{0:T(128)S(1)} %get-tuple-element.22.owner_ref, bf16[32,2,2,32,1024]{4,3,2,1,0:T(8,128)(2,1)} %screen_product.5.refs_0_.refs_1_, ...), custom_call_target="tpu_custom_call", output_to_operand_aliasing={{}: (8, {})} | custom-call | flops 1 | bytes 1 | tf_op jit(solution)/shard_map/contract/pallas_call | solution.py:208
  179.2 5.0 %contract.6 = f32[32,64,128]{2,1,0:T(8,128)S(1)} custom-call(s32[8]{0:T(128)S(1)} %gather_fusion, s32[1]{0:T(128)} %bitcast.1.side_ref, s32[1]{0:T(128)} %bitcast.2.owner_ref, bf16[32,2,2,32,1024]{4,3,2,1,0:T(8,128)(2,1)} %screen_product.5.refs_0_.refs_1_, ...), custom_call_target="tpu_custom_call", output_to_operand_aliasing={{}: (9, {})} | custom-call | flops 1 | bytes 1 | tf_op jit(solution)/shard_map/contract/pallas_call | solution.py:208
  190.7 11.0 %collective-permute-done.20.refs_2_ = bf16[2,8,64,1024]{3,2,1,0:T(8,128)(2,1)} collective-permute-done((bf16[2,8,64,1024]{3,2,1,0:T(8,128)(2,1)}, bf16[2,8,64,1024]{3,2,1,0:T(8,128)(2,1)}, u32[]{:S(2)}, u32[]{:S(2)}) %collective-permute-start.20) | collective-permute-done | bytes 2097184 | tf_op jit(solution)/shard_map/ppermute | solution.py:88
  201.7 4.4 %contract.7 = f32[8,64,128]{2,1,0:T(8,128)S(1)} custom-call(s32[8]{0:T(128)S(1)} %gather_fusion.3, s32[1]{0:T(128)} %bitcast.46.side_ref, s32[1]{0:T(128)} %constant.232.clone.1.side_ref.owner_ref, bf16[32,2,2,32,1024]{4,3,2,1,0:T(8,128)(2,1)} %screen_product.5.refs_0_.refs_1_, bf16[32,2,2,32,1024]{4,3,2,1,0:T(8,128)(2,1)} %screen_product.5.refs_0_.refs_1_, ...), custom_call_target="tpu_custom_call" | custom-call | flops 1 | bytes 1 | tf_op jit(solution)/shard_map/contract/pallas_call | solution.py:208
  208.9 3.0 %collective-permute-done.22 = f32[8,16,128]{2,1,0:T(8,128)S(1)} collective-permute-done((f32[8,16,128]{2,1,0:T(8,128)S(1)}, f32[8,16,128]{2,1,0:T(8,128)S(1)}, u32[]{:S(2)}, u32[]{:S(2)}) %collective-permute-start.22) | collective-permute-done | bytes 65568 | tf_op jit(solution)/shard_map/ppermute | solution.py:22
  212.8 2.9 %collective-permute-start.24 = (bf16[16,16,128]{2,1,0:T(8,128)(2,1)S(1)}, bf16[16,16,128]{2,1,0:T(8,128)(2,1)S(1)}, u32[]{:S(2)}, u32[]{:S(2)}) collective-permute-start(bf16[16,16,128]{2,1,0:T(8,128)(2,1)S(1)} %get-tuple-element.37), channel_id=1, source_target_pairs={{0,8},{4,12},{8,0},{12,4},{1,9},{5,13},{9,1},{13,5},{2,10},{6,14},... | collective-permute-start | bytes 196616 | tf_op jit(solution)/shard_map/ppermute | solution.py:22
  216.6 2.5 %collective-permute-done.23 = bf16[16,16,128]{2,1,0:T(8,128)(2,1)S(1)} collective-permute-done((bf16[16,16,128]{2,1,0:T(8,128)(2,1)S(1)}, bf16[16,16,128]{2,1,0:T(8,128)(2,1)S(1)}, u32[]{:S(2)}, u32[]{:S(2)}) %collective-permute-start.23) | collective-permute-done | bytes 65568 | tf_op jit(solution)/shard_map/ppermute | solution.py:22
  221.0 4.4 %collective-permute-done.26 = f32[16,16,128]{2,1,0:T(8,128)S(1)} collective-permute-done((f32[16,16,128]{2,1,0:T(8,128)S(1)}, f32[16,16,128]{2,1,0:T(8,128)S(1)}, u32[]{:S(2)}, u32[]{:S(2)}) %collective-permute-start.26) | collective-permute-done | bytes 131104 | tf_op jit(solution)/shard_map/ppermute | solution.py:22
  (145 shorter events, 56.9 us)
Async XLA Ops:
  4.0 52.7 %collective-permute-start.8 = (bf16[2,8,64,1024]{3,2,1,0:T(8,128)(2,1)S(1)}, bf16[2,8,64,1024]{3,2,1,0:T(8,128)(2,1)}, u32[]{:S(2)}, u32[]{:S(2)}) collective-permute-start(bf16[2,8,64,1024]{3,2,1,0:T(8,128)(2,1)S(1)} %valence_columns.1.refs_2_.refs_4_.refs_5_.refs_3_), channel_id=1, source_target_pairs={{0,4},{4,8},{8,12},{1,5},{5,9},{9,13},{2,6},{6,10},{10,14},{3,7},{... | collective-permute-start | bytes 6291464 | tf_op jit(solution)/shard_map/ppermute | solution.py:261
  10.4 50.5 %collective-permute-start.9 = (bf16[2,8,64,1024]{3,2,1,0:T(8,128)(2,1)S(1)}, bf16[2,8,64,1024]{3,2,1,0:T(8,128)(2,1)}, u32[]{:S(2)}, u32[]{:S(2)}) collective-permute-start(bf16[2,8,64,1024]{3,2,1,0:T(8,128)(2,1)S(1)} %valence_columns.1.refs_2_.refs_4_.refs_5_.refs_3_), channel_id=1, source_target_pairs={{4,0},{8,4},{12,8},{5,1},{9,5},{13,9},{6,2},{10,6},{14,10},{7,3},{... | collective-permute-start | bytes 6291464 | tf_op jit(solution)/shard_map/ppermute | solution.py:262
  14.0 24.8 %collective-permute-start = (bf16[2,4,32,2000]{3,2,1,0:T(8,128)(2,1)}, bf16[2,4,32,2000]{3,2,1,0:T(8,128)(2,1)S(1)}, u32[]{:S(2)}, u32[]{:S(2)}) collective-permute-start(bf16[2,4,32,2000]{3,2,1,0:T(8,128)(2,1)} %dynamic-slice_bitcast_fusion), channel_id=1, source_target_pairs={{0,2},{2,0},{1,3},{3,1},{4,6},{6,4},{5,7},{7,5},{8,10},{10,8},{9,1... | collective-permute-start | bytes 3072008 | tf_op jit(solution)/shard_map/ppermute | solution.py:22
  41.9 13.2 %collective-permute-start.6 = (bf16[1,2,128,1024]{3,2,1,0:T(8,128)(2,1)S(1)}, bf16[1,2,128,1024]{3,2,1,0:T(8,128)(2,1)}, u32[]{:S(2)}, u32[]{:S(2)}) collective-permute-start(bf16[1,2,128,1024]{3,2,1,0:T(8,128)(2,1)S(1)} %get-tuple-element.29.refs_0_), channel_id=1, source_target_pairs={{0,2},{2,0},{1,3},{3,1},{4,6},{6,4},{5,7},{7,5},{8,10},{10,8},{9,1... | collective-permute-start | bytes 1572872 | tf_op jit(solution)/shard_map/ppermute | solution.py:22
  50.7 19.9 %collective-permute-start.5 = (bf16[1,2,128,1024]{3,2,1,0:T(8,128)(2,1)S(1)}, bf16[1,2,128,1024]{3,2,1,0:T(8,128)(2,1)S(1)}, u32[]{:S(2)}, u32[]{:S(2)}) collective-permute-start(bf16[1,2,128,1024]{3,2,1,0:T(8,128)(2,1)S(1)} %get-tuple-element.29.refs_0_), channel_id=1, source_target_pairs={{0,1},{1,0},{2,3},{3,2},{4,5},{5,4},{6,7},{7,6},{8,9},{9,8},{10,11... | collective-permute-start | bytes 1572872 | tf_op jit(solution)/shard_map/ppermute | solution.py:22
  50.7 32.3 %collective-permute-start.1 = (bf16[2,128,1024]{2,1,0:T(8,128)(2,1)}, bf16[2,128,1024]{2,1,0:T(8,128)(2,1)S(1)}, u32[]{:S(2)}, u32[]{:S(2)}) collective-permute-start(bf16[2,128,1024]{2,1,0:T(8,128)(2,1)} %get-tuple-element.32), channel_id=1, source_target_pairs={{0,12},{4,0},{8,4},{12,8},{1,13},{5,1},{9,5},{13,9},{2,14},{6,2},{... | collective-permute-start | bytes 1572872 | tf_op jit(solution)/shard_map/ppermute | solution.py:22
  55.1 29.1 %collective-permute-start.3 = (bf16[2,128,1024]{2,1,0:T(8,128)(2,1)}, bf16[2,128,1024]{2,1,0:T(8,128)(2,1)}, u32[]{:S(2)}, u32[]{:S(2)}) collective-permute-start(bf16[2,128,1024]{2,1,0:T(8,128)(2,1)} %get-tuple-element.31), channel_id=1, source_target_pairs={{0,4},{4,8},{8,12},{12,0},{1,5},{5,9},{9,13},{13,1},{2,6},{6,10},{... | collective-permute-start | bytes 1572872 | tf_op jit(solution)/shard_map/ppermute | solution.py:22
  56.6 47.6 %collective-permute-start.4 = (bf16[2,128,1024]{2,1,0:T(8,128)(2,1)}, bf16[2,128,1024]{2,1,0:T(8,128)(2,1)}, u32[]{:S(2)}, u32[]{:S(2)}) collective-permute-start(bf16[2,128,1024]{2,1,0:T(8,128)(2,1)} %get-tuple-element.30), channel_id=1, source_target_pairs={{0,8},{4,12},{8,0},{12,4},{1,9},{5,13},{9,1},{13,5},{2,10},{6,14},... | collective-permute-start | bytes 1572872 | tf_op jit(solution)/shard_map/ppermute | solution.py:22
  60.9 11.9 %collective-permute-start.7 = (bf16[1,2,128,1024]{3,2,1,0:T(8,128)(2,1)}, bf16[1,2,128,1024]{3,2,1,0:T(8,128)(2,1)}, u32[]{:S(2)}, u32[]{:S(2)}) collective-permute-start(bf16[1,2,128,1024]{3,2,1,0:T(8,128)(2,1)} %collective-permute-done.6.refs_2_), channel_id=1, source_target_pairs={{0,1},{1,0},{2,3},{3,2},{4,5},{5,4},{6,7},{7,6},{8,9},{9,8},{10,11... | collective-permute-start | bytes 1572872 | tf_op jit(solution)/shard_map/ppermute | solution.py:22
  71.4 38.8 %collective-permute-start.15 = (bf16[2,2,64,1024]{3,2,1,0:T(8,128)(2,1)}, bf16[2,2,64,1024]{3,2,1,0:T(8,128)(2,1)}, u32[]{:S(2)}, u32[]{:S(2)}) collective-permute-start(bf16[2,2,64,1024]{3,2,1,0:T(8,128)(2,1)} %slice_select_fusion.1), channel_id=1, source_target_pairs={{8,12},{4,0},{9,13},{5,1},{10,14},{6,2},{11,15},{7,3},{24,28},{20,... | collective-permute-start | bytes 1572872 | tf_op jit(solution)/shard_map/ppermute | solution.py:88
  105.5 23.8 %collective-permute-start.11 = (bf16[2,2,128,1024]{3,2,1,0:T(8,128)(2,1)S(1)}, bf16[2,2,128,1024]{3,2,1,0:T(8,128)(2,1)}, u32[]{:S(2)}, u32[]{:S(2)}) collective-permute-start(bf16[2,2,128,1024]{3,2,1,0:T(8,128)(2,1)S(1)} %pad_maximum_fusion.2.refs_0_), channel_id=1, source_target_pairs={{0,2},{2,0},{1,3},{3,1},{4,6},{6,4},{5,7},{7,5},{8,10},{10,8},{9,1... | collective-permute-start | bytes 3145736 | tf_op jit(solution)/shard_map/ppermute | solution.py:22
  110.2 42.1 %collective-permute-start.16 = (bf16[2,8,64,1024]{3,2,1,0:T(8,128)(2,1)}, bf16[2,8,64,1024]{3,2,1,0:T(8,128)(2,1)}, u32[]{:S(2)}, u32[]{:S(2)}) collective-permute-start(bf16[2,8,64,1024]{3,2,1,0:T(8,128)(2,1)} %broadcast_select_fusion), channel_id=1, source_target_pairs={{4,8},{8,4},{5,9},{9,5},{6,10},{10,6},{7,11},{11,7},{20,24},{24,20... | collective-permute-start | bytes 6291464 | tf_op jit(solution)/shard_map/ppermute | solution.py:88
  115.5 36.8 %collective-permute-start.17 = (bf16[2,6,64,1024]{3,2,1,0:T(8,128)(2,1)}, bf16[2,6,64,1024]{3,2,1,0:T(8,128)(2,1)}, u32[]{:S(2)}, u32[]{:S(2)}) collective-permute-start(bf16[2,6,64,1024]{3,2,1,0:T(8,128)(2,1)} %slice_select_fusion), channel_id=1, source_target_pairs={{8,12},{4,0},{9,13},{5,1},{10,14},{6,2},{11,15},{7,3},{24,28},{20,... | collective-permute-start | bytes 4718600 | tf_op jit(solution)/shard_map/ppermute | solution.py:88
  116.8 14.2 %collective-permute-start.10 = (bf16[2,2,128,1024]{3,2,1,0:T(8,128)(2,1)S(1)}, bf16[2,2,128,1024]{3,2,1,0:T(8,128)(2,1)}, u32[]{:S(2)}, u32[]{:S(2)}) collective-permute-start(bf16[2,2,128,1024]{3,2,1,0:T(8,128)(2,1)S(1)} %pad_maximum_fusion.2.refs_0_), channel_id=1, source_target_pairs={{0,1},{1,0},{2,3},{3,2},{4,5},{5,4},{6,7},{7,6},{8,9},{9,8},{10,11... | collective-permute-start | bytes 3145736 | tf_op jit(solution)/shard_map/ppermute | solution.py:22
  129.3 3.0 %collective-permute-start.12 = (bf16[2,2,128,1024]{3,2,1,0:T(8,128)(2,1)}, bf16[2,2,128,1024]{3,2,1,0:T(8,128)(2,1)}, u32[]{:S(2)}, u32[]{:S(2)}) collective-permute-start(bf16[2,2,128,1024]{3,2,1,0:T(8,128)(2,1)} %collective-permute-done.11.refs_2_), channel_id=1, source_target_pairs={{0,1},{1,0},{2,3},{3,2},{4,5},{5,4},{6,7},{7,6},{8,9},{9,8},{10,11... | collective-permute-start | bytes 3145736 | tf_op jit(solution)/shard_map/ppermute | solution.py:22
  129.4 24.7 %collective-permute-start.2 = (bf16[1,2,128,1024]{3,2,1,0:T(8,128)(2,1)}, bf16[1,2,128,1024]{3,2,1,0:T(8,128)(2,1)}, u32[]{:S(2)}, u32[]{:S(2)}) collective-permute-start(bf16[1,2,128,1024]{3,2,1,0:T(8,128)(2,1)} %bitcast.112), channel_id=1, source_target_pairs={{0,2},{2,0},{1,3},{3,1},{4,6},{6,4},{5,7},{7,5},{8,10},{10,8},{9,1... | collective-permute-start | bytes 1572872 | tf_op jit(solution)/shard_map/ppermute | solution.py:22
  152.3 49.4 %collective-permute-start.20 = (bf16[2,8,64,1024]{3,2,1,0:T(8,128)(2,1)}, bf16[2,8,64,1024]{3,2,1,0:T(8,128)(2,1)}, u32[]{:S(2)}, u32[]{:S(2)}) collective-permute-start(bf16[2,8,64,1024]{3,2,1,0:T(8,128)(2,1)} %collective-permute-done.16.refs_4_), channel_id=1, source_target_pairs={{8,12},{4,0},{9,13},{5,1},{10,14},{6,2},{11,15},{7,3},{24,28},{20,... | collective-permute-start | bytes 6291464 | tf_op jit(solution)/shard_map/ppermute | solution.py:88
  154.2 2.9 %collective-permute-start.14 = (bf16[1,2,128,1024]{3,2,1,0:T(8,128)(2,1)}, bf16[1,2,128,1024]{3,2,1,0:T(8,128)(2,1)S(1)}, u32[]{:S(2)}, u32[]{:S(2)}) collective-permute-start(bf16[1,2,128,1024]{3,2,1,0:T(8,128)(2,1)} %collective-permute-done.2.refs_2_), channel_id=1, source_target_pairs={{0,1},{1,0},{2,3},{3,2},{4,5},{5,4},{6,7},{7,6},{8,9},{9,8},{10,11... | collective-permute-start | bytes 1572872 | tf_op jit(solution)/shard_map/ppermute | solution.py:22
  189.4 16.8 %collective-permute-start.19 = (f32[32,16,128]{2,1,0:T(8,128)S(1)}, f32[32,16,128]{2,1,0:T(8,128)S(1)}, u32[]{:S(2)}, u32[]{:S(2)}) collective-permute-start(f32[32,16,128]{2,1,0:T(8,128)S(1)} %dynamic-slice_bitcast_fusion.5), channel_id=1, source_target_pairs={{0,2},{2,0},{1,3},{3,1},{4,6},{6,4},{5,7},{7,5},{8,10},{10,8},{9,1... | collective-permute-start | bytes 786440 | tf_op jit(solution)/shard_map/ppermute | solution.py:22
  207.6 4.3 %collective-permute-start.22 = (f32[8,16,128]{2,1,0:T(8,128)S(1)}, f32[8,16,128]{2,1,0:T(8,128)S(1)}, u32[]{:S(2)}, u32[]{:S(2)}) collective-permute-start(f32[8,16,128]{2,1,0:T(8,128)S(1)} %dynamic-slice_bitcast_fusion.10), channel_id=1, source_target_pairs={{0,2},{2,0},{1,3},{3,1},{4,6},{6,4},{5,7},{7,5},{8,10},{10,8},{9,1... | collective-permute-start | bytes 196616 | tf_op jit(solution)/shard_map/ppermute | solution.py:22
  212.7 6.3 %collective-permute-start.23 = (bf16[16,16,128]{2,1,0:T(8,128)(2,1)S(1)}, bf16[16,16,128]{2,1,0:T(8,128)(2,1)S(1)}, u32[]{:S(2)}, u32[]{:S(2)}) collective-permute-start(bf16[16,16,128]{2,1,0:T(8,128)(2,1)S(1)} %get-tuple-element.35), channel_id=1, source_target_pairs={{0,4},{4,8},{8,12},{12,0},{1,5},{5,9},{9,13},{13,1},{2,6},{6,10},{... | collective-permute-start | bytes 196616 | tf_op jit(solution)/shard_map/ppermute | solution.py:22
  212.8 7.5 %collective-permute-start.24 = (bf16[16,16,128]{2,1,0:T(8,128)(2,1)S(1)}, bf16[16,16,128]{2,1,0:T(8,128)(2,1)S(1)}, u32[]{:S(2)}, u32[]{:S(2)}) collective-permute-start(bf16[16,16,128]{2,1,0:T(8,128)(2,1)S(1)} %get-tuple-element.37), channel_id=1, source_target_pairs={{0,8},{4,12},{8,0},{12,4},{1,9},{5,13},{9,1},{13,5},{2,10},{6,14},... | collective-permute-start | bytes 196616 | tf_op jit(solution)/shard_map/ppermute | solution.py:22
  215.7 4.6 %collective-permute-start.25 = (bf16[16,16,128]{2,1,0:T(8,128)(2,1)S(1)}, bf16[16,16,128]{2,1,0:T(8,128)(2,1)S(1)}, u32[]{:S(2)}, u32[]{:S(2)}) collective-permute-start(bf16[16,16,128]{2,1,0:T(8,128)(2,1)S(1)} %get-tuple-element.36), channel_id=1, source_target_pairs={{0,12},{4,0},{8,4},{12,8},{1,13},{5,1},{9,5},{13,9},{2,14},{6,2},{... | collective-permute-start | bytes 196616 | tf_op jit(solution)/shard_map/ppermute | solution.py:22
  220.4 5.0 %collective-permute-start.26 = (f32[16,16,128]{2,1,0:T(8,128)S(1)}, f32[16,16,128]{2,1,0:T(8,128)S(1)}, u32[]{:S(2)}, u32[]{:S(2)}) collective-permute-start(f32[16,16,128]{2,1,0:T(8,128)S(1)} %bitcast_add_fusion.2), channel_id=1, source_target_pairs={{0,2},{2,0},{1,3},{3,1},{4,6},{6,4},{5,7},{7,5},{8,10},{10,8},{9,1... | collective-permute-start | bytes 393224 | tf_op jit(solution)/shard_map/ppermute | solution.py:22
  (22 other events, 333.9 us)

commit v9 on v8

--- a/solution.py
+++ b/solution.py
@@ -279,9 +279,13 @@
             )
             by_block.append(jnp.where(is_head, heads[..., None], cut).reshape(2, rows, deep))
     by_block = jnp.stack(by_block)
-    arrived = deal(by_block, "kpt")
-    own_block = arrived[0]
     middle = kpt_count // 2 + 1
+    own_block = lax.dynamic_index_in_dim(by_block, kpt, 0, keepdims=False)
+    own_across = share(own_block[None], "pw")
+    arrived = [own_block]
+    for shift in range(1, kpt_count):
+        piece = lax.dynamic_index_in_dim(by_block, (kpt + shift) % kpt_count, 0, keepdims=False)
+        arrived.append(shifted(piece if shift < middle else after(piece, own_across), "kpt", shift))
 
     screen = jnp.pad(screened, ((0, 0), (0, deep - block), (0, band_count * width - columns)))
     screen = lax.dynamic_slice_in_dim(screen, band * width, width, 2)
@@ -326,8 +330,8 @@
         jnp.where(partner[None, :] == jnp.arange(all_points)[:, None], jnp.arange(all_points)[None, :], 0), axis=1
     ).astype(jnp.int32)
 
-    def spread(group):
-        return [own for across in share(group, "pw") for own in share(across, "band")]
+    def spread(across):
+        return [own for value in across for own in share(value, "band")]
 
     def product(shifts, pieces, right, store):
         sources = jnp.stack([((kpt - shift) % kpt_count).astype(jnp.int32) for shift in shifts])
@@ -336,27 +340,35 @@
 
     near, far = list(range(1, middle)), list(range(middle, kpt_count))
     distant = [arrived[shift] for shift in far]
-    store = product([0], spread(own_block[None]), right, None)
+    store = product([0], spread(own_across), right, None)
     near_group = jnp.stack(after([arrived[shift] for shift in near], [store, step_one, distant]))
-    near_pieces = spread(near_group)
+    near_pieces = spread(share(near_group, "pw"))
     far_across = share(jnp.stack(distant), "pw")
     to_ends, to_others = line_pairs(kpt_count, 2)
-    early_rows = max(points // 4, 1)
-    first_part = one_way(*[value[:, :early_rows] for value in step_one], *to_ends, "kpt")
-    gates = [near_group, distant, first_part]
-    ends = {2: [first_part, one_way(*[value[:, early_rows:] for value in step_one], *to_ends, "kpt", gates)]}
-    others = {}
+    few, more = max(points // 4, 1), max(points // 2, 1)
+
+    def rows_of(first, end):
+        return [value[:, first:end] for value in step_one]
+
+    ends, others = {2: [one_way(*rows_of(0, more), *to_ends, "kpt")]}, {}
     if kpt_count > 3:
-        others[2] = [one_way(*step_one, *to_others, "kpt", gates)]
+        others[2] = [one_way(*rows_of(0, few), *to_others, "kpt")]
+    gates = [near_group, distant, ends[2][0], others.get(2, [])[:1]]
+    if kpt_count > 3:
+        others[2].append(one_way(*rows_of(few, points), *to_others, "kpt", gates))
+    ends[2].append(one_way(*rows_of(more, points), *to_ends, "kpt", gates))
+    if kpt_count > 3:
+        ends[3] = [one_way(*others[2][0], *line_pairs(kpt_count, 3)[0], "kpt", [ends[2], near_pieces[0]])]
     store = product(near, near_pieces, right, store)
     for step in range(3, kpt_count):
-        below, above = others[step - 1][0]
-        gates = [store, ends[2]]
+        gates = [store, ends[2], ends[3][:1]]
         to_ends, to_others = line_pairs(kpt_count, step)
-        ends[step] = [one_way(below, above, *to_ends, "kpt", gates)]
+        sent = others[step - 1]
+        skip = 1 if step == 3 else 0
+        ends.setdefault(step, []).extend(one_way(*part, *to_ends, "kpt", gates) for part in sent[skip:])
         if step < kpt_count - 1:
-            others[step] = [one_way(below, above, *to_others, "kpt", gates)]
-    far_pieces = [own for across in after(far_across, store) for own in share(across, "band")]
+            others[step] = [one_way(*part, *to_others, "kpt", gates) for part in sent]
+    far_pieces = spread(after(far_across, store))
     store = product(far, far_pieces, after(right, others.get(2, ends[2])), store)
 
     lanes = 2 * pairs

time: 228 us -> 231 us (1.013)
  waiting for transfers between devices: 83.5 us -> 87 us
  starting transfers between devices: 34.8 us -> 37.9 us
  other arithmetic: 31.6 us -> 28.9 us
    ppermute x21, waiting for transfers between devices: 66.9 us -> 33.5 us  [shifted(): return lax.ppermute(x, name, pairs)]
    ppermute x4 -> x6, waiting for transfers between devices: 14.9 us -> 40.4 us  [one_way(): moved = lax.ppermute(after(sent, gates), name, pairs_below + pairs_above)]
    ppermute x1, waiting for transfers between devices: 1.74 us -> 13 us  [on_device(): lax.ppermute(own_valence, 'kpt', [(s, s - 1) for s in range(1, kpt_count)])]
    ppermute x4 -> x6, starting transfers between devices: 6.07 us -> 8.01 us  [one_way(): moved = lax.ppermute(after(sent, gates), name, pairs_below + pairs_above)]
  transfers between devices with their start and end apart: 27 -> 29, of which waited for: 15 -> 14; matrix products, arithmetic and copies ran while one was open for 19% -> 17% of each run, Pallas kernels for 25% -> 24%
where the time goes in v9:
time: 231 us; the launch traced here: 230 us
  waiting for transfers between devices  87 us (38%)
  Pallas kernels  58.1 us (25%)
  starting transfers between devices  37.9 us (16%)
  other arithmetic  28.9 us (13%)
  local copies, waits for them, and re-layouts  16.2 us (7%)
    ppermute x6, waiting for transfers between devices, one_way(): moved = lax.ppermute(after(sent, gates), name, pairs_below + pairs_above)  40.4 us
    pallas_call x3, Pallas kernels, screen_product(): pl.pallas_call(kernel, out_shape=jax.ShapeDtypeStruct((blocks * points, b...  34.1 us
    ppermute x21, waiting for transfers between devices, shifted(): return lax.ppermute(x, name, pairs)  33.5 us
    ppermute x21, starting transfers between devices, shifted(): return lax.ppermute(x, name, pairs)  22.2 us
    pallas_call x4, Pallas kernels, contract(): pl.pallas_call(kernel, out_shape=jax.ShapeDtypeStruct((blocks * points, b...  21.7 us
    ppermute x1, waiting for transfers between devices, on_device(): lax.ppermute(own_valence, 'kpt', [(s, s - 1) for s in range(1, kpt_count)])  13 us
    another operation x2, other arithmetic, on_device(): jnp.stack([jnp.concatenate([screen[0], screen[1]], axis=0), jnp.concatena...  11.3 us
    ppermute x6, starting transfers between devices, one_way(): moved = lax.ppermute(after(sent, gates), name, pairs_below + pairs_above)  8.01 us
  transfers between devices with their start and end apart: 29, of which 14 were waited for; matrix products, arithmetic and copies ran while one was open for 17% of the time, Pallas kernels for 24%

profile of v9, /device:TPU:0, one launch (start us, length us, event | category | flops | bytes accessed | tf_op | source)
XLA Modules:
  0.0 230.0 jit_solution(12149807198258815677)
XLA Ops:
  4.0 6.4 %collective-permute-start.8 = (bf16[2,8,64,1024]{3,2,1,0:T(8,128)(2,1)S(1)}, bf16[2,8,64,1024]{3,2,1,0:T(8,128)(2,1)}, u32[]{:S(2)}, u32[]{:S(2)}) collective-permute-start(bf16[2,8,64,1024]{3,2,1,0:T(8,128)(2,1)S(1)} %valence_columns.1.refs_2_.refs_4_.refs_6_), channel_id=1, source_target_pairs={{0,4},{4,8},{8,12},{1,5},{5,9},{9,13},{2,6},{6,10},{10,14},{3,7},{... | collective-permute-start | bytes 6291464 | tf_op jit(solution)/shard_map/ppermute | solution.py:261
  16.0 3.3 %fusion.1 = bf16[2,1024,1024]{2,1,0:T(8,128)(2,1)S(1)} fusion(s32[]{:T(128)S(6)} %select_n.384, bf16[2,1000,2000]{2,1,0:T(8,128)(2,1)} %param.21, pred[1024]{0:T(1024)(128)(4,1)S(1)} %get-tuple-element.51, pred[1024]{0:T(1024)(128)(4,1)S(1)} %get-tuple-element.52, bf16[2,1024]{1,0:T(2,128)(2,1)S(1)} %broadcast_select_fusion.2, bf16[2,1024]{1,0:T(2,128)(2,1)S(1)} %fusion.19), kind=kLoop, calls=%fused_computation.7 | loop fusion | flops 4194304 | bytes 12204548 | tf_op jit(solution)/shard_map/jit(_where)/select_n | solution.py:309
  19.4 2.7 %slice_bitcast_fusion.1 = (bf16[1024,1024]{1,0:T(8,128)(2,1)}, bf16[1024,1024]{1,0:T(8,128)(2,1)}) fusion(bf16[2,1024,1024]{2,1,0:T(8,128)(2,1)S(1)} %fusion.1), kind=kLoop, calls=%fused_computation.12 | loop fusion | bytes 8388608 | tf_op jit(solution)/shard_map/squeeze | solution.py:314
  22.7 16.1 %collective-permute-done = bf16[2,4,32,2000]{3,2,1,0:T(8,128)(2,1)S(1)} collective-permute-done((bf16[2,4,32,2000]{3,2,1,0:T(8,128)(2,1)}, bf16[2,4,32,2000]{3,2,1,0:T(8,128)(2,1)S(1)}, u32[]{:S(2)}, u32[]{:S(2)}) %collective-permute-start) | collective-permute-done | bytes 1024032 | tf_op jit(solution)/shard_map/ppermute | solution.py:22
  46.1 3.8 %maximum_bitcast_fusion = (bf16[1,2048,1024]{2,1,0:T(8,128)(2,1)}, bf16[1,2048,1024]{2,1,0:T(8,128)(2,1)}) fusion(bf16[1024,1024]{1,0:T(8,128)(2,1)S(1)} %copy-done.11, bf16[1024,1024]{1,0:T(8,128)(2,1)S(1)} %copy-done.10, bf16[1024,1024]{1,0:T(8,128)(2,1)S(1)} %fusion.30), kind=kLoop, calls=%fused_computation.8 | loop fusion | flops 16777216 | bytes 14680064 | tf_op jit(solution)/shard_map/stack | solution.py:312
  49.9 2.4 %collective-permute-start.4 = (bf16[2,128,1024]{2,1,0:T(8,128)(2,1)}, bf16[2,128,1024]{2,1,0:T(8,128)(2,1)}, u32[]{:S(2)}, u32[]{:S(2)}) collective-permute-start(bf16[2,128,1024]{2,1,0:T(8,128)(2,1)} %get-tuple-element.36), channel_id=1, source_target_pairs={{0,4},{4,8},{8,12},{12,0},{1,5},{5,9},{9,13},{13,1},{2,6},{6,10},{... | collective-permute-start | bytes 1572872 | tf_op jit(solution)/shard_map/ppermute | solution.py:22
  52.3 3.4 %collective-permute-done.1.refs_2_ = bf16[1,2,128,1024]{3,2,1,0:T(8,128)(2,1)S(1)} collective-permute-done((bf16[1,2,128,1024]{3,2,1,0:T(8,128)(2,1)S(1)}, bf16[1,2,128,1024]{3,2,1,0:T(8,128)(2,1)S(1)}, u32[]{:S(2)}, u32[]{:S(2)}) %collective-permute-start.1) | collective-permute-done | bytes 524320 | tf_op jit(solution)/shard_map/ppermute | solution.py:22
  57.4 2.7 %collective-permute-start.2 = (bf16[2,128,1024]{2,1,0:T(8,128)(2,1)}, bf16[2,128,1024]{2,1,0:T(8,128)(2,1)}, u32[]{:S(2)}, u32[]{:S(2)}) collective-permute-start(bf16[2,128,1024]{2,1,0:T(8,128)(2,1)} %get-tuple-element.15), channel_id=1, source_target_pairs={{0,12},{4,0},{8,4},{12,8},{1,13},{5,1},{9,5},{13,9},{2,14},{6,2},{... | collective-permute-start | bytes 1572872 | tf_op jit(solution)/shard_map/ppermute | solution.py:22
  60.1 13.0 %collective-permute-done.9.refs_3_ = bf16[2,8,64,1024]{3,2,1,0:T(8,128)(2,1)} collective-permute-done((bf16[2,8,64,1024]{3,2,1,0:T(8,128)(2,1)S(1)}, bf16[2,8,64,1024]{3,2,1,0:T(8,128)(2,1)}, u32[]{:S(2)}, u32[]{:S(2)}) %collective-permute-start.9) | collective-permute-done | bytes 2097184 | tf_op jit(solution)/shard_map/ppermute | solution.py:262
  73.1 3.4 %slice_select_fusion.1 = (bf16[2,4,64,1024]{3,2,1,0:T(8,128)(2,1)}, bf16[2,4,64,1024]{3,2,1,0:T(8,128)(2,1)S(1)}) fusion(bf16[2,8,64,1024]{3,2,1,0:T(8,128)(2,1)} %collective-permute-done.9.refs_3_, bf16[2,8,64,1024]{3,2,1,0:T(8,128)(2,1)} %collective-permute-done.8.refs_2_, pred[]{:T(512)S(6)} %eq.163), kind=kLoop, calls=%fused_computation.16 | loop fusion | flops 1048576 | bytes 6291457 | tf_op jit(solution)/shard_map/jit(_where)/select_n | solution.py:87
  77.8 7.5 %pad_maximum_fusion.refs_4_ = bf16[2,2048,1024]{2,1,0:T(8,128)(2,1)} fusion(bf16[1,2048,1024]{2,1,0:T(8,128)(2,1)} %get-tuple-element.34, bf16[1,2048,1024]{2,1,0:T(8,128)(2,1)} %get-tuple-element.33), kind=kLoop, calls=%fused_computation.4 | loop fusion | flops 4194304 | bytes 16777216 | tf_op jit(solution)/shard_map/stack | solution.py:312
  85.3 8.9 %screen_product.3.refs_5_ = bf16[32,2,2,32,1024]{4,3,2,1,0:T(8,128)(2,1)} custom-call(s32[5]{0:T(128)S(1)} %concatenate.33.place_ref, bf16[1,2,128,1024]{3,2,1,0:T(8,128)(2,1)S(1)} %get-tuple-element.37.refs_0_, bf16[1,2,128,1024]{3,2,1,0:T(8,128)(2,1)} %collective-permute-done.6.refs_1_, bf16[1,2,128,1024]{3,2,1,0:T(8,128)(2,1)S(1)} %collective-permute-done.1.refs_2_, ...), custom_call_target="tpu_custom_call" | custom-call | flops 1 | bytes 1 | tf_op jit(solution)/shard_map/screen_product/pallas_call | solution.py:130
  99.2 16.4 %collective-permute-done.16.refs_2_ = bf16[2,4,64,1024]{3,2,1,0:T(8,128)(2,1)S(1)} collective-permute-done((bf16[2,4,64,1024]{3,2,1,0:T(8,128)(2,1)S(1)}, bf16[2,4,64,1024]{3,2,1,0:T(8,128)(2,1)S(1)}, u32[]{:S(2)}, u32[]{:S(2)}) %collective-permute-start.16) | collective-permute-done | bytes 1048608 | tf_op jit(solution)/shard_map/ppermute | solution.py:88
  117.0 3.3 %slice_select_fusion = bf16[2,6,64,1024]{3,2,1,0:T(8,128)(2,1)} fusion(bf16[2,8,64,1024]{3,2,1,0:T(8,128)(2,1)} %collective-permute-done.9.refs_3_, bf16[2,8,64,1024]{3,2,1,0:T(8,128)(2,1)} %collective-permute-done.8.refs_2_, pred[]{:T(512)S(6)} %eq.162), kind=kLoop, calls=%fused_computation.14 | loop fusion | flops 786432 | bytes 4718593 | tf_op jit(solution)/shard_map/jit(_where)/select_n | solution.py:87
  124.9 20.3 %collective-permute-done.18.refs_3_ = bf16[2,4,64,1024]{3,2,1,0:T(8,128)(2,1)} collective-permute-done((bf16[2,4,64,1024]{3,2,1,0:T(8,128)(2,1)}, bf16[2,4,64,1024]{3,2,1,0:T(8,128)(2,1)}, u32[]{:S(2)}, u32[]{:S(2)}) %collective-permute-start.18) | collective-permute-done | bytes 1048608 | tf_op jit(solution)/shard_map/ppermute | solution.py:88
  147.0 16.1 %screen_product.4.refs_5_ = bf16[32,2,2,32,1024]{4,3,2,1,0:T(8,128)(2,1)} custom-call(s32[6]{0:T(128)S(1)} %concatenate.32.place_ref, bf16[2,2,128,1024]{3,2,1,0:T(8,128)(2,1)S(1)} %pad_maximum_fusion.2.refs_0_, bf16[2,2,128,1024]{3,2,1,0:T(8,128)(2,1)} %collective-permute-done.10.refs_1_, ...), custom_call_target="tpu_custom_call", output_to_operand_aliasing={{}: (6, {})} | custom-call | flops 1 | bytes 1 | tf_op jit(solution)/shard_map/screen_product/pallas_call | solution.py:130
  167.2 9.1 %screen_product.5.refs_0_.refs_1_ = bf16[32,2,2,32,1024]{4,3,2,1,0:T(8,128)(2,1)} custom-call(s32[5]{0:T(128)S(1)} %concatenate.31.place_ref, bf16[1,2,128,1024]{3,2,1,0:T(8,128)(2,1)} %bitcast.16.refs_0_, bf16[1,2,128,1024]{3,2,1,0:T(8,128)(2,1)S(1)} %collective-permute-done.13.refs_1_, ...), custom_call_target="tpu_custom_call", output_to_operand_aliasing={{}: (6, {})} | custom-call | flops 1 | bytes 1 | tf_op jit(solution)/shard_map/screen_product/pallas_call | solution.py:130
  176.3 3.9 %contract.4.refs_5_ = f32[32,64,128]{2,1,0:T(8,128)S(1)} custom-call(s32[8]{0:T(128)S(1)} %gather_fusion.2, s32[1]{0:T(128)} %constant.231.clone.1.side_ref.owner_ref, s32[1]{0:T(128)} %bitcast.38.owner_ref, bf16[32,2,2,32,1024]{4,3,2,1,0:T(8,128)(2,1)} %screen_product.5.refs_0_.refs_1_, bf16[32,2,2,32,1024]{4,3,2,1,0:T(8,128)(2,1)} %screen_product.5.refs_0_.refs_1_, ...), custom_call_target="tpu_custom_call" | custom-call | flops 1 | bytes 1 | tf_op jit(solution)/shard_map/contract/pallas_call | solution.py:208
  180.3 8.2 %contract.5.refs_7_ = f32[32,64,128]{2,1,0:T(8,128)S(1)} custom-call(s32[16]{0:T(128)S(1)} %gather_fusion.1, s32[2]{0:T(128)S(1)} %pad_add_fusion.1.side_ref, s32[2]{0:T(128)S(1)} %get-tuple-element.26.owner_ref, bf16[32,2,2,32,1024]{4,3,2,1,0:T(8,128)(2,1)} %screen_product.5.refs_0_.refs_1_, ...), custom_call_target="tpu_custom_call", output_to_operand_aliasing={{}: (8, {})} | custom-call | flops 1 | bytes 1 | tf_op jit(solution)/shard_map/contract/pallas_call | solution.py:208
  188.6 4.9 %contract.6 = f32[32,64,128]{2,1,0:T(8,128)S(1)} custom-call(s32[8]{0:T(128)S(1)} %gather_fusion, s32[1]{0:T(128)} %bitcast.1.side_ref, s32[1]{0:T(128)} %bitcast.2.owner_ref, bf16[32,2,2,32,1024]{4,3,2,1,0:T(8,128)(2,1)} %screen_product.5.refs_0_.refs_1_, ...), custom_call_target="tpu_custom_call", output_to_operand_aliasing={{}: (10, {})} | custom-call | flops 1 | bytes 1 | tf_op jit(solution)/shard_map/contract/pallas_call | solution.py:208
  200.9 3.7 %collective-permute-done.22.refs_3_ = bf16[2,6,64,1024]{3,2,1,0:T(8,128)(2,1)} collective-permute-done((bf16[2,6,64,1024]{3,2,1,0:T(8,128)(2,1)}, bf16[2,6,64,1024]{3,2,1,0:T(8,128)(2,1)}, u32[]{:S(2)}, u32[]{:S(2)}) %collective-permute-start.22) | collective-permute-done | bytes 1572896 | tf_op jit(solution)/shard_map/ppermute | solution.py:88
  204.6 4.6 %contract.7 = f32[8,64,128]{2,1,0:T(8,128)S(1)} custom-call(s32[8]{0:T(128)S(1)} %gather_fusion.3, s32[1]{0:T(128)} %bitcast.46.side_ref, s32[1]{0:T(128)} %constant.231.clone.1.side_ref.owner_ref, bf16[32,2,2,32,1024]{4,3,2,1,0:T(8,128)(2,1)} %screen_product.5.refs_0_.refs_1_, bf16[32,2,2,32,1024]{4,3,2,1,0:T(8,128)(2,1)} %screen_product.5.refs_0_.refs_1_, ...), custom_call_target="tpu_custom_call" | custom-call | flops 1 | bytes 1 | tf_op jit(solution)/shard_map/contract/pallas_call | solution.py:208
  219.7 2.5 %collective-permute-done.25 = bf16[16,16,128]{2,1,0:T(8,128)(2,1)S(1)} collective-permute-done((bf16[16,16,128]{2,1,0:T(8,128)(2,1)S(1)}, bf16[16,16,128]{2,1,0:T(8,128)(2,1)S(1)}, u32[]{:S(2)}, u32[]{:S(2)}) %collective-permute-start.25) | collective-permute-done | bytes 65568 | tf_op jit(solution)/shard_map/ppermute | solution.py:22
  225.2 3.5 %collective-permute-done.28 = f32[16,16,128]{2,1,0:T(8,128)S(1)} collective-permute-done((f32[16,16,128]{2,1,0:T(8,128)S(1)}, f32[16,16,128]{2,1,0:T(8,128)S(1)}, u32[]{:S(2)}, u32[]{:S(2)}) %collective-permute-start.28) | collective-permute-done | bytes 131104 | tf_op jit(solution)/shard_map/ppermute | solution.py:22
  (155 shorter events, 59.2 us)
Async XLA Ops:
  4.0 53.4 %collective-permute-start.8 = (bf16[2,8,64,1024]{3,2,1,0:T(8,128)(2,1)S(1)}, bf16[2,8,64,1024]{3,2,1,0:T(8,128)(2,1)}, u32[]{:S(2)}, u32[]{:S(2)}) collective-permute-start(bf16[2,8,64,1024]{3,2,1,0:T(8,128)(2,1)S(1)} %valence_columns.1.refs_2_.refs_4_.refs_6_), channel_id=1, source_target_pairs={{0,4},{4,8},{8,12},{1,5},{5,9},{9,13},{2,6},{6,10},{10,14},{3,7},{... | collective-permute-start | bytes 6291464 | tf_op jit(solution)/shard_map/ppermute | solution.py:261
  10.4 62.7 %collective-permute-start.9 = (bf16[2,8,64,1024]{3,2,1,0:T(8,128)(2,1)S(1)}, bf16[2,8,64,1024]{3,2,1,0:T(8,128)(2,1)}, u32[]{:S(2)}, u32[]{:S(2)}) collective-permute-start(bf16[2,8,64,1024]{3,2,1,0:T(8,128)(2,1)S(1)} %valence_columns.1.refs_2_.refs_4_.refs_6_), channel_id=1, source_target_pairs={{4,0},{8,4},{12,8},{5,1},{9,5},{13,9},{6,2},{10,6},{14,10},{7,3},{... | collective-permute-start | bytes 6291464 | tf_op jit(solution)/shard_map/ppermute | solution.py:262
  14.0 24.8 %collective-permute-start = (bf16[2,4,32,2000]{3,2,1,0:T(8,128)(2,1)}, bf16[2,4,32,2000]{3,2,1,0:T(8,128)(2,1)S(1)}, u32[]{:S(2)}, u32[]{:S(2)}) collective-permute-start(bf16[2,4,32,2000]{3,2,1,0:T(8,128)(2,1)} %dynamic-slice_bitcast_fusion), channel_id=1, source_target_pairs={{0,2},{2,0},{1,3},{3,1},{4,6},{6,4},{5,7},{7,5},{8,10},{10,8},{9,1... | collective-permute-start | bytes 3072008 | tf_op jit(solution)/shard_map/ppermute | solution.py:22
  43.1 12.6 %collective-permute-start.1 = (bf16[1,2,128,1024]{3,2,1,0:T(8,128)(2,1)S(1)}, bf16[1,2,128,1024]{3,2,1,0:T(8,128)(2,1)S(1)}, u32[]{:S(2)}, u32[]{:S(2)}) collective-permute-start(bf16[1,2,128,1024]{3,2,1,0:T(8,128)(2,1)S(1)} %get-tuple-element.37.refs_0_), channel_id=1, source_target_pairs={{0,2},{2,0},{1,3},{3,1},{4,6},{6,4},{5,7},{7,5},{8,10},{10,8},{9,1... | collective-permute-start | bytes 1572872 | tf_op jit(solution)/shard_map/ppermute | solution.py:22
  44.8 31.7 %collective-permute-start.6 = (bf16[1,2,128,1024]{3,2,1,0:T(8,128)(2,1)S(1)}, bf16[1,2,128,1024]{3,2,1,0:T(8,128)(2,1)}, u32[]{:S(2)}, u32[]{:S(2)}) collective-permute-start(bf16[1,2,128,1024]{3,2,1,0:T(8,128)(2,1)S(1)} %get-tuple-element.37.refs_0_), channel_id=1, source_target_pairs={{0,1},{1,0},{2,3},{3,2},{4,5},{5,4},{6,7},{7,6},{8,9},{9,8},{10,11... | collective-permute-start | bytes 1572872 | tf_op jit(solution)/shard_map/ppermute | solution.py:22
  49.9 44.3 %collective-permute-start.4 = (bf16[2,128,1024]{2,1,0:T(8,128)(2,1)}, bf16[2,128,1024]{2,1,0:T(8,128)(2,1)}, u32[]{:S(2)}, u32[]{:S(2)}) collective-permute-start(bf16[2,128,1024]{2,1,0:T(8,128)(2,1)} %get-tuple-element.36), channel_id=1, source_target_pairs={{0,4},{4,8},{8,12},{12,0},{1,5},{5,9},{9,13},{13,1},{2,6},{6,10},{... | collective-permute-start | bytes 1572872 | tf_op jit(solution)/shard_map/ppermute | solution.py:22
  55.7 38.7 %collective-permute-start.5 = (bf16[2,128,1024]{2,1,0:T(8,128)(2,1)}, bf16[2,128,1024]{2,1,0:T(8,128)(2,1)}, u32[]{:S(2)}, u32[]{:S(2)}) collective-permute-start(bf16[2,128,1024]{2,1,0:T(8,128)(2,1)} %get-tuple-element.35), channel_id=1, source_target_pairs={{0,8},{4,12},{8,0},{12,4},{1,9},{5,13},{9,1},{13,5},{2,10},{6,14},... | collective-permute-start | bytes 1572872 | tf_op jit(solution)/shard_map/ppermute | solution.py:22
  57.4 37.0 %collective-permute-start.2 = (bf16[2,128,1024]{2,1,0:T(8,128)(2,1)}, bf16[2,128,1024]{2,1,0:T(8,128)(2,1)}, u32[]{:S(2)}, u32[]{:S(2)}) collective-permute-start(bf16[2,128,1024]{2,1,0:T(8,128)(2,1)} %get-tuple-element.15), channel_id=1, source_target_pairs={{0,12},{4,0},{8,4},{12,8},{1,13},{5,1},{9,5},{13,9},{2,14},{6,2},{... | collective-permute-start | bytes 1572872 | tf_op jit(solution)/shard_map/ppermute | solution.py:22
  73.1 12.2 %collective-permute-start.7 = (bf16[1,2,128,1024]{3,2,1,0:T(8,128)(2,1)S(1)}, bf16[1,2,128,1024]{3,2,1,0:T(8,128)(2,1)S(1)}, u32[]{:S(2)}, u32[]{:S(2)}) collective-permute-start(bf16[1,2,128,1024]{3,2,1,0:T(8,128)(2,1)S(1)} %collective-permute-done.1.refs_2_), channel_id=1, source_target_pairs={{0,1},{1,0},{2,3},{3,2},{4,5},{5,4},{6,7},{7,6},{8,9},{9,8},{10,11... | collective-permute-start | bytes 1572872 | tf_op jit(solution)/shard_map/ppermute | solution.py:22
  76.5 39.1 %collective-permute-start.16 = (bf16[2,4,64,1024]{3,2,1,0:T(8,128)(2,1)S(1)}, bf16[2,4,64,1024]{3,2,1,0:T(8,128)(2,1)S(1)}, u32[]{:S(2)}, u32[]{:S(2)}) collective-permute-start(bf16[2,4,64,1024]{3,2,1,0:T(8,128)(2,1)S(1)} %get-tuple-element.28), channel_id=1, source_target_pairs={{8,12},{4,0},{9,13},{5,1},{10,14},{6,2},{11,15},{7,3},{24,28},{20,... | collective-permute-start | bytes 3145736 | tf_op jit(solution)/shard_map/ppermute | solution.py:88
  97.6 25.7 %collective-permute-start.11 = (bf16[2,2,128,1024]{3,2,1,0:T(8,128)(2,1)S(1)}, bf16[2,2,128,1024]{3,2,1,0:T(8,128)(2,1)}, u32[]{:S(2)}, u32[]{:S(2)}) collective-permute-start(bf16[2,2,128,1024]{3,2,1,0:T(8,128)(2,1)S(1)} %pad_maximum_fusion.2.refs_0_), channel_id=1, source_target_pairs={{0,2},{2,0},{1,3},{3,1},{4,6},{6,4},{5,7},{7,5},{8,10},{10,8},{9,1... | collective-permute-start | bytes 3145736 | tf_op jit(solution)/shard_map/ppermute | solution.py:22
  115.6 29.7 %collective-permute-start.18 = (bf16[2,4,64,1024]{3,2,1,0:T(8,128)(2,1)}, bf16[2,4,64,1024]{3,2,1,0:T(8,128)(2,1)}, u32[]{:S(2)}, u32[]{:S(2)}) collective-permute-start(bf16[2,4,64,1024]{3,2,1,0:T(8,128)(2,1)} %get-tuple-element.22), channel_id=1, source_target_pairs={{8,12},{4,0},{9,13},{5,1},{10,14},{6,2},{11,15},{7,3},{24,28},{20,... | collective-permute-start | bytes 3145736 | tf_op jit(solution)/shard_map/ppermute | solution.py:88
  120.2 44.7 %collective-permute-start.17 = (bf16[2,6,64,1024]{3,2,1,0:T(8,128)(2,1)}, bf16[2,6,64,1024]{3,2,1,0:T(8,128)(2,1)}, u32[]{:S(2)}, u32[]{:S(2)}) collective-permute-start(bf16[2,6,64,1024]{3,2,1,0:T(8,128)(2,1)} %slice_select_fusion), channel_id=1, source_target_pairs={{4,8},{8,4},{5,9},{9,5},{6,10},{10,6},{7,11},{11,7},{20,24},{24,20... | collective-permute-start | bytes 4718600 | tf_op jit(solution)/shard_map/ppermute | solution.py:88
  122.1 24.9 %collective-permute-start.10 = (bf16[2,2,128,1024]{3,2,1,0:T(8,128)(2,1)S(1)}, bf16[2,2,128,1024]{3,2,1,0:T(8,128)(2,1)}, u32[]{:S(2)}, u32[]{:S(2)}) collective-permute-start(bf16[2,2,128,1024]{3,2,1,0:T(8,128)(2,1)S(1)} %pad_maximum_fusion.2.refs_0_), channel_id=1, source_target_pairs={{0,1},{1,0},{2,3},{3,2},{4,5},{5,4},{6,7},{7,6},{8,9},{9,8},{10,11... | collective-permute-start | bytes 3145736 | tf_op jit(solution)/shard_map/ppermute | solution.py:22
  123.3 23.7 %collective-permute-start.12 = (bf16[2,2,128,1024]{3,2,1,0:T(8,128)(2,1)}, bf16[2,2,128,1024]{3,2,1,0:T(8,128)(2,1)}, u32[]{:S(2)}, u32[]{:S(2)}) collective-permute-start(bf16[2,2,128,1024]{3,2,1,0:T(8,128)(2,1)} %collective-permute-done.11.refs_2_), channel_id=1, source_target_pairs={{0,1},{1,0},{2,3},{3,2},{4,5},{5,4},{6,7},{7,6},{8,9},{9,8},{10,11... | collective-permute-start | bytes 3145736 | tf_op jit(solution)/shard_map/ppermute | solution.py:22
  123.3 39.8 %collective-permute-start.3 = (bf16[1,2,128,1024]{3,2,1,0:T(8,128)(2,1)}, bf16[1,2,128,1024]{3,2,1,0:T(8,128)(2,1)}, u32[]{:S(2)}, u32[]{:S(2)}) collective-permute-start(bf16[1,2,128,1024]{3,2,1,0:T(8,128)(2,1)} %bitcast.16.refs_0_), channel_id=1, source_target_pairs={{0,2},{2,0},{1,3},{3,1},{4,6},{6,4},{5,7},{7,5},{8,10},{10,8},{9,1... | collective-permute-start | bytes 1572872 | tf_op jit(solution)/shard_map/ppermute | solution.py:22
  145.2 19.8 %collective-permute-start.21 = (bf16[2,2,64,1024]{3,2,1,0:T(8,128)(2,1)}, bf16[2,2,64,1024]{3,2,1,0:T(8,128)(2,1)}, u32[]{:S(2)}, u32[]{:S(2)}) collective-permute-start(bf16[2,2,64,1024]{3,2,1,0:T(8,128)(2,1)} %copy-done.6), channel_id=1, source_target_pairs={{8,12},{4,0},{9,13},{5,1},{10,14},{6,2},{11,15},{7,3},{24,28},{20,... | collective-permute-start | bytes 1572872 | tf_op jit(solution)/shard_map/ppermute | solution.py:88
  165.0 39.6 %collective-permute-start.22 = (bf16[2,6,64,1024]{3,2,1,0:T(8,128)(2,1)}, bf16[2,6,64,1024]{3,2,1,0:T(8,128)(2,1)}, u32[]{:S(2)}, u32[]{:S(2)}) collective-permute-start(bf16[2,6,64,1024]{3,2,1,0:T(8,128)(2,1)} %collective-permute-done.17.refs_5_), channel_id=1, source_target_pairs={{8,12},{4,0},{9,13},{5,1},{10,14},{6,2},{11,15},{7,3},{24,28},{20,... | collective-permute-start | bytes 4718600 | tf_op jit(solution)/shard_map/ppermute | solution.py:88
  198.6 10.7 %collective-permute-start.20 = (f32[32,16,128]{2,1,0:T(8,128)S(1)}, f32[32,16,128]{2,1,0:T(8,128)S(1)}, u32[]{:S(2)}, u32[]{:S(2)}) collective-permute-start(f32[32,16,128]{2,1,0:T(8,128)S(1)} %dynamic-slice_bitcast_fusion.5), channel_id=1, source_target_pairs={{0,2},{2,0},{1,3},{3,1},{4,6},{6,4},{5,7},{7,5},{8,10},{10,8},{9,1... | collective-permute-start | bytes 786440 | tf_op jit(solution)/shard_map/ppermute | solution.py:22
  210.7 4.3 %collective-permute-start.24 = (f32[8,16,128]{2,1,0:T(8,128)S(1)}, f32[8,16,128]{2,1,0:T(8,128)S(1)}, u32[]{:S(2)}, u32[]{:S(2)}) collective-permute-start(f32[8,16,128]{2,1,0:T(8,128)S(1)} %dynamic-slice_bitcast_fusion.10), channel_id=1, source_target_pairs={{0,2},{2,0},{1,3},{3,1},{4,6},{6,4},{5,7},{7,5},{8,10},{10,8},{9,1... | collective-permute-start | bytes 196616 | tf_op jit(solution)/shard_map/ppermute | solution.py:22
  215.9 6.4 %collective-permute-start.25 = (bf16[16,16,128]{2,1,0:T(8,128)(2,1)S(1)}, bf16[16,16,128]{2,1,0:T(8,128)(2,1)S(1)}, u32[]{:S(2)}, u32[]{:S(2)}) collective-permute-start(bf16[16,16,128]{2,1,0:T(8,128)(2,1)S(1)} %get-tuple-element.41), channel_id=1, source_target_pairs={{0,4},{4,8},{8,12},{12,0},{1,5},{5,9},{9,13},{13,1},{2,6},{6,10},{... | collective-permute-start | bytes 196616 | tf_op jit(solution)/shard_map/ppermute | solution.py:22
  216.7 6.9 %collective-permute-start.26 = (bf16[16,16,128]{2,1,0:T(8,128)(2,1)S(1)}, bf16[16,16,128]{2,1,0:T(8,128)(2,1)S(1)}, u32[]{:S(2)}, u32[]{:S(2)}) collective-permute-start(bf16[16,16,128]{2,1,0:T(8,128)(2,1)S(1)} %get-tuple-element.43), channel_id=1, source_target_pairs={{0,8},{4,12},{8,0},{12,4},{1,9},{5,13},{9,1},{13,5},{2,10},{6,14},... | collective-permute-start | bytes 196616 | tf_op jit(solution)/shard_map/ppermute | solution.py:22
  218.0 5.6 %collective-permute-start.27 = (bf16[16,16,128]{2,1,0:T(8,128)(2,1)S(1)}, bf16[16,16,128]{2,1,0:T(8,128)(2,1)S(1)}, u32[]{:S(2)}, u32[]{:S(2)}) collective-permute-start(bf16[16,16,128]{2,1,0:T(8,128)(2,1)S(1)} %get-tuple-element.42), channel_id=1, source_target_pairs={{0,12},{4,0},{8,4},{12,8},{1,13},{5,1},{9,5},{13,9},{2,14},{6,2},{... | collective-permute-start | bytes 196616 | tf_op jit(solution)/shard_map/ppermute | solution.py:22
  223.6 5.0 %collective-permute-start.28 = (f32[16,16,128]{2,1,0:T(8,128)S(1)}, f32[16,16,128]{2,1,0:T(8,128)S(1)}, u32[]{:S(2)}, u32[]{:S(2)}) collective-permute-start(f32[16,16,128]{2,1,0:T(8,128)S(1)} %bitcast_add_fusion.2), channel_id=1, source_target_pairs={{0,2},{2,0},{1,3},{3,1},{4,6},{6,4},{5,7},{7,5},{8,10},{10,8},{9,1... | collective-permute-start | bytes 393224 | tf_op jit(solution)/shard_map/ppermute | solution.py:22
  (27 other events, 366.2 us)

commit v10 on v8

--- a/solution.py
+++ b/solution.py
@@ -75,18 +75,26 @@
     )(core.reshape(1), valence, valence_head[..., None], selector)
 
 
+def single(pairs_below, pairs_above):
+    pairs = pairs_below + pairs_above
+    return len({pair[0] for pair in pairs}) == len(pairs) and len({pair[1] for pair in pairs}) == len(pairs)
+
+
+def chosen(below, above, pairs_below, pairs_above, name):
+    if above is below or not single(pairs_below, pairs_above):
+        return below, above
+    sends_below = jnp.isin(lax.axis_index(name), jnp.array([pair[0] for pair in pairs_below]))
+    sent = jnp.where(sends_below, below, above)
+    return sent, sent
+
+
 def one_way(below, above, pairs_below, pairs_above, name, gates=()):
-    senders = [pair[0] for pair in pairs_below + pairs_above]
-    takers = [pair[1] for pair in pairs_below + pairs_above]
-    if len(set(senders)) < len(senders) or len(set(takers)) < len(takers):
-        below, above = after((below, above), gates)
-        return lax.ppermute(below, name, pairs_below), lax.ppermute(above, name, pairs_above)
-    sent = below
-    if above is not below:
-        sends_below = jnp.isin(lax.axis_index(name), jnp.array([pair[0] for pair in pairs_below]))
-        sent = jnp.where(sends_below, below, above)
-    moved = lax.ppermute(after(sent, gates), name, pairs_below + pairs_above)
-    return moved, moved
+    below, above = chosen(below, above, pairs_below, pairs_above, name)
+    if above is below and single(pairs_below, pairs_above):
+        moved = lax.ppermute(after(below, gates), name, pairs_below + pairs_above)
+        return moved, moved
+    below, above = after((below, above), gates)
+    return lax.ppermute(below, name, pairs_below), lax.ppermute(above, name, pairs_above)
 
 
 def line_pairs(count, step):
@@ -263,7 +271,7 @@
     ]
 
     halves = jnp.moveaxis(conduction.reshape(2, pw_count, per_index, half, columns), 1, 0)
-    dealt = deal(halves, "pw")
+    dealt = deal(after(halves, own_valence), "pw")
 
     plane = jnp.arange(deep)
     is_head = (plane >= block) & (plane < block + HEAD_PARTS)
@@ -279,9 +287,13 @@
             )
             by_block.append(jnp.where(is_head, heads[..., None], cut).reshape(2, rows, deep))
     by_block = jnp.stack(by_block)
-    arrived = deal(by_block, "kpt")
-    own_block = arrived[0]
     middle = kpt_count // 2 + 1
+    own_block = lax.dynamic_index_in_dim(by_block, kpt, 0, keepdims=False)
+    own_across = share(own_block[None], "pw")
+    arrived = [own_block]
+    for shift in range(1, kpt_count):
+        piece = lax.dynamic_index_in_dim(by_block, (kpt + shift) % kpt_count, 0, keepdims=False)
+        arrived.append(shifted(piece if shift < middle else after(piece, own_across), "kpt", shift))
 
     screen = jnp.pad(screened, ((0, 0), (0, deep - block), (0, band_count * width - columns)))
     screen = lax.dynamic_slice_in_dim(screen, band * width, width, 2)
@@ -305,6 +317,7 @@
     screen = jnp.where(
         (jnp.arange(width)[None, None, :] == head_at) & has_column, column_part[:, :, None], screen
     )
+    screen = after(screen, step_one)
     right = jnp.stack(
         [
             jnp.concatenate([screen[0], screen[1]], axis=0),
@@ -326,8 +339,8 @@
         jnp.where(partner[None, :] == jnp.arange(all_points)[:, None], jnp.arange(all_points)[None, :], 0), axis=1
     ).astype(jnp.int32)
 
-    def spread(group):
-        return [own for across in share(group, "pw") for own in share(across, "band")]
+    def spread(across):
+        return [own for value in across for own in share(value, "band")]
 
     def product(shifts, pieces, right, store):
         sources = jnp.stack([((kpt - shift) % kpt_count).astype(jnp.int32) for shift in shifts])
@@ -336,18 +349,19 @@
 
     near, far = list(range(1, middle)), list(range(middle, kpt_count))
     distant = [arrived[shift] for shift in far]
-    store = product([0], spread(own_block[None]), right, None)
-    near_group = jnp.stack(after([arrived[shift] for shift in near], [store, step_one, distant]))
-    near_pieces = spread(near_group)
+    store = product([0], spread(own_across), right, None)
+    to_ends, to_others = line_pairs(kpt_count, 2)
+    onward = chosen(*step_one, *to_others, "kpt") if kpt_count > 3 else ()
+    near_group = jnp.stack(after([arrived[shift] for shift in near], [store, step_one, distant, onward]))
+    near_pieces = spread(share(near_group, "pw"))
     far_across = share(jnp.stack(distant), "pw")
-    to_ends, to_others = line_pairs(kpt_count, 2)
     early_rows = max(points // 4, 1)
     first_part = one_way(*[value[:, :early_rows] for value in step_one], *to_ends, "kpt")
     gates = [near_group, distant, first_part]
     ends = {2: [first_part, one_way(*[value[:, early_rows:] for value in step_one], *to_ends, "kpt", gates)]}
     others = {}
     if kpt_count > 3:
-        others[2] = [one_way(*step_one, *to_others, "kpt", gates)]
+        others[2] = [one_way(*onward, *to_others, "kpt", gates)]
     store = product(near, near_pieces, right, store)
     for step in range(3, kpt_count):
         below, above = others[step - 1][0]

time: 228 us -> 240 us (1.053)
  waiting for transfers between devices: 83.5 us -> 100 us
  other arithmetic: 31.6 us -> 28.1 us
    ppermute x1, waiting for transfers between devices: 1.74 us -> 13.9 us  [on_device(): lax.ppermute(own_valence, 'kpt', [(s, s - 1) for s in range(1, kpt_count)])]
    ppermute x21, waiting for transfers between devices: 66.9 us -> 57.7 us  [shifted(): return lax.ppermute(x, name, pairs)]
    ppermute x4, waiting for transfers between devices: 14.9 us -> 22.7 us  [one_way(): moved = lax.ppermute(after(below, gates), name, pairs_below + pairs_above)]
    ppermute x1, waiting for transfers between devices: 0.01 us -> 5.89 us  [on_device(): lax.ppermute(own_valence, 'kpt', [(s, s + 1) for s in range(kpt_count - 1)])]
    ppermute x21, starting transfers between devices: 21.1 us -> 24.1 us  [shifted(): return lax.ppermute(x, name, pairs)]
  transfers between devices with their start and end apart: 27 -> 27, of which waited for: 15 -> 16; matrix products, arithmetic and copies ran while one was open for 19% -> 14% of each run, Pallas kernels for 25% -> 23%
where the time goes in v10:
time: 240 us; the launch traced here: 239 us
  waiting for transfers between devices  100 us (42%)
  Pallas kernels  57.5 us (24%)
  starting transfers between devices  36.3 us (15%)
  other arithmetic  28.1 us (12%)
  local copies, waits for them, and re-layouts  14.9 us (6%)
    ppermute x21, waiting for transfers between devices, shifted(): return lax.ppermute(x, name, pairs)  57.7 us
    pallas_call x3, Pallas kernels, screen_product(): pl.pallas_call(kernel, out_shape=jax.ShapeDtypeStruct((blocks * points, b...  33.8 us
    ppermute x21, starting transfers between devices, shifted(): return lax.ppermute(x, name, pairs)  24.1 us
    ppermute x4, waiting for transfers between devices, one_way(): moved = lax.ppermute(after(below, gates), name, pairs_below + pairs_above)  22.7 us
    pallas_call x4, Pallas kernels, contract(): pl.pallas_call(kernel, out_shape=jax.ShapeDtypeStruct((blocks * points, b...  21.4 us
    ppermute x1, waiting for transfers between devices, on_device(): lax.ppermute(own_valence, 'kpt', [(s, s - 1) for s in range(1, kpt_count)])  13.9 us
    another operation x2, other arithmetic, on_device(): jnp.stack([jnp.concatenate([screen[0], screen[1]], axis=0), jnp.concatena...  11.4 us
    select_n x3, other arithmetic, chosen(): sent = jnp.where(sends_below, below, above)  8.4 us
  transfers between devices with their start and end apart: 27, of which 16 were waited for; matrix products, arithmetic and copies ran while one was open for 14% of the time, Pallas kernels for 23%

profile of v10, /device:TPU:0, one launch (start us, length us, event | category | flops | bytes accessed | tf_op | source)
XLA Modules:
  0.0 239.1 jit_solution(13661475430265854934)
XLA Ops:
  4.0 3.1 %dynamic-slice_bitcast_fusion = bf16[2,4,32,2000]{3,2,1,0:T(8,128)(2,1)} fusion(bf16[2,2,4,32,2000]{4,3,2,0,1:T(8,128)(2,1)} %bitcast.121, s32[]{:T(128)S(6)} %select_n.353), kind=kLoop, calls=%fused_computation.20 | loop fusion | bytes 2048004 | tf_op jit(solution)/shard_map/jit(dynamic_index_in_dim)/squeeze | solution.py:38
  7.1 2.9 %collective-permute-start = (bf16[2,4,32,2000]{3,2,1,0:T(8,128)(2,1)}, bf16[2,4,32,2000]{3,2,1,0:T(8,128)(2,1)S(1)}, u32[]{:S(2)}, u32[]{:S(2)}) collective-permute-start(bf16[2,4,32,2000]{3,2,1,0:T(8,128)(2,1)} %dynamic-slice_bitcast_fusion), channel_id=1, source_target_pairs={{0,2},{2,0},{1,3},{3,1},{4,6},{6,4},{5,7},{7,5},{8,10},{10,8},{9,1... | collective-permute-start | bytes 3072008 | tf_op jit(solution)/shard_map/ppermute | solution.py:22
  10.0 4.8 %collective-permute-start.8 = (bf16[2,8,64,1024]{3,2,1,0:T(8,128)(2,1)S(1)}, bf16[2,8,64,1024]{3,2,1,0:T(8,128)(2,1)}, u32[]{:S(2)}, u32[]{:S(2)}) collective-permute-start(bf16[2,8,64,1024]{3,2,1,0:T(8,128)(2,1)S(1)} %valence_columns.1.refs_2_.refs_4_.refs_5_.refs_3_), channel_id=1, source_target_pairs={{0,4},{4,8},{8,12},{1,5},{5,9},{9,13},{2,6},{6,10},{10,14},{3,7},{... | collective-permute-start | bytes 6291464 | tf_op jit(solution)/shard_map/ppermute | solution.py:269
  16.9 16.4 %collective-permute-done = bf16[2,4,32,2000]{3,2,1,0:T(8,128)(2,1)S(1)} collective-permute-done((bf16[2,4,32,2000]{3,2,1,0:T(8,128)(2,1)}, bf16[2,4,32,2000]{3,2,1,0:T(8,128)(2,1)S(1)}, u32[]{:S(2)}, u32[]{:S(2)}) %collective-permute-start) | collective-permute-done | bytes 1024032 | tf_op jit(solution)/shard_map/ppermute | solution.py:22
  43.1 8.0 %collective-permute-done.1.refs_2_ = bf16[1,2,128,1024]{3,2,1,0:T(8,128)(2,1)S(1)} collective-permute-done((bf16[1,2,128,1024]{3,2,1,0:T(8,128)(2,1)S(1)}, bf16[1,2,128,1024]{3,2,1,0:T(8,128)(2,1)S(1)}, u32[]{:S(2)}, u32[]{:S(2)}) %collective-permute-start.1) | collective-permute-done | bytes 524320 | tf_op jit(solution)/shard_map/ppermute | solution.py:22
  51.1 2.5 %collective-permute-start.5 = (bf16[2,128,1024]{2,1,0:T(8,128)(2,1)}, bf16[2,128,1024]{2,1,0:T(8,128)(2,1)S(1)}, u32[]{:S(2)}, u32[]{:S(2)}) collective-permute-start(bf16[2,128,1024]{2,1,0:T(8,128)(2,1)} %get-tuple-element.35), channel_id=1, source_target_pairs={{0,8},{4,12},{8,0},{12,4},{1,9},{5,13},{9,1},{13,5},{2,10},{6,14},... | collective-permute-start | bytes 1572872 | tf_op jit(solution)/shard_map/ppermute | solution.py:22
  53.6 5.9 %collective-permute-done.8.refs_2_ = bf16[2,8,64,1024]{3,2,1,0:T(8,128)(2,1)} collective-permute-done((bf16[2,8,64,1024]{3,2,1,0:T(8,128)(2,1)S(1)}, bf16[2,8,64,1024]{3,2,1,0:T(8,128)(2,1)}, u32[]{:S(2)}, u32[]{:S(2)}) %collective-permute-start.8) | collective-permute-done | bytes 2097184 | tf_op jit(solution)/shard_map/ppermute | solution.py:269
  59.5 4.6 %collective-permute-start.2 = (bf16[2,128,1024]{2,1,0:T(8,128)(2,1)}, bf16[2,128,1024]{2,1,0:T(8,128)(2,1)S(1)}, u32[]{:S(2)}, u32[]{:S(2)}) collective-permute-start(bf16[2,128,1024]{2,1,0:T(8,128)(2,1)} %get-tuple-element.17), channel_id=1, source_target_pairs={{0,12},{4,0},{8,4},{12,8},{1,13},{5,1},{9,5},{13,9},{2,14},{6,2},{... | collective-permute-start | bytes 1572872 | tf_op jit(solution)/shard_map/ppermute | solution.py:22
  64.2 13.9 %collective-permute-done.9.refs_3_ = bf16[2,8,64,1024]{3,2,1,0:T(8,128)(2,1)} collective-permute-done((bf16[2,8,64,1024]{3,2,1,0:T(8,128)(2,1)S(1)}, bf16[2,8,64,1024]{3,2,1,0:T(8,128)(2,1)}, u32[]{:S(2)}, u32[]{:S(2)}) %collective-permute-start.9) | collective-permute-done | bytes 2097184 | tf_op jit(solution)/shard_map/ppermute | solution.py:270
  78.7 3.8 %maximum_bitcast_fusion = (bf16[1,2048,1024]{2,1,0:T(8,128)(2,1)}, bf16[1,2048,1024]{2,1,0:T(8,128)(2,1)}) fusion(bf16[1024,1024]{1,0:T(8,128)(2,1)S(1)} %get-tuple-element.30, bf16[1024,1024]{1,0:T(8,128)(2,1)S(1)} %get-tuple-element.29, bf16[1024,1024]{1,0:T(8,128)(2,1)S(1)} %fusion.30), kind=kLoop, calls=%fused_computation.8 | loop fusion | flops 16777216 | bytes 14680064 | tf_op jit(solution)/shard_map/stack | solution.py:321
  85.8 7.5 %pad_maximum_fusion.refs_4_ = bf16[2,2048,1024]{2,1,0:T(8,128)(2,1)} fusion(bf16[1,2048,1024]{2,1,0:T(8,128)(2,1)} %get-tuple-element.34, bf16[1,2048,1024]{2,1,0:T(8,128)(2,1)} %get-tuple-element.33), kind=kLoop, calls=%fused_computation.4 | loop fusion | flops 4194304 | bytes 16777216 | tf_op jit(solution)/shard_map/stack | solution.py:321
  93.4 8.9 %screen_product.3.refs_5_ = bf16[32,2,2,32,1024]{4,3,2,1,0:T(8,128)(2,1)} custom-call(s32[5]{0:T(128)S(1)} %concatenate.33.place_ref, bf16[1,2,128,1024]{3,2,1,0:T(8,128)(2,1)S(1)} %get-tuple-element.37.refs_0_, bf16[1,2,128,1024]{3,2,1,0:T(8,128)(2,1)S(1)} %collective-permute-done.6.refs_1_, bf16[1,2,128,1024]{3,2,1,0:T(8,128)(2,1)S(1)} %collective-permute-done.1.refs_2_, ...), custom_call_target="tpu_custom_call" | custom-call | flops 1 | bytes 1 | tf_op jit(solution)/shard_map/screen_product/pallas_call | solution.py:138
  102.3 3.1 %broadcast_select_fusion = bf16[2,8,64,1024]{3,2,1,0:T(8,128)(2,1)} fusion(bf16[2,8,64,1024]{3,2,1,0:T(8,128)(2,1)} %collective-permute-done.8.refs_2_, bf16[2,8,64,1024]{3,2,1,0:T(8,128)(2,1)} %collective-permute-done.9.refs_3_, pred[]{:T(512)S(6)} %eq.158), kind=kLoop, calls=%fused_computation.14 | loop fusion | flops 1048576 | bytes 6291457 | tf_op jit(solution)/shard_map/jit(_where)/select_n | solution.py:87
  110.8 3.2 %slice_select_fusion = bf16[2,6,64,1024]{3,2,1,0:T(8,128)(2,1)} fusion(bf16[2,8,64,1024]{3,2,1,0:T(8,128)(2,1)} %collective-permute-done.9.refs_3_, bf16[2,8,64,1024]{3,2,1,0:T(8,128)(2,1)} %collective-permute-done.8.refs_2_, pred[]{:T(512)S(6)} %eq.159), kind=kLoop, calls=%fused_computation.15 | loop fusion | flops 786432 | bytes 4718593 | tf_op jit(solution)/shard_map/jit(_where)/select_n | solution.py:87
  115.4 18.0 %collective-permute-done.11.refs_2_ = bf16[2,2,128,1024]{3,2,1,0:T(8,128)(2,1)} collective-permute-done((bf16[2,2,128,1024]{3,2,1,0:T(8,128)(2,1)S(1)}, bf16[2,2,128,1024]{3,2,1,0:T(8,128)(2,1)}, u32[]{:S(2)}, u32[]{:S(2)}) %collective-permute-start.11) | collective-permute-done | bytes 1048608 | tf_op jit(solution)/shard_map/ppermute | solution.py:22
  136.5 16.1 %screen_product.4.refs_5_ = bf16[32,2,2,32,1024]{4,3,2,1,0:T(8,128)(2,1)} custom-call(s32[6]{0:T(128)S(1)} %concatenate.32.place_ref, bf16[2,2,128,1024]{3,2,1,0:T(8,128)(2,1)S(1)} %pad_maximum_fusion.2.refs_0_, bf16[2,2,128,1024]{3,2,1,0:T(8,128)(2,1)} %collective-permute-done.10.refs_1_, ...), custom_call_target="tpu_custom_call", output_to_operand_aliasing={{}: (6, {})} | custom-call | flops 1 | bytes 1 | tf_op jit(solution)/shard_map/screen_product/pallas_call | solution.py:138
  152.5 6.2 %collective-permute-done.17.refs_3_ = bf16[2,6,64,1024]{3,2,1,0:T(8,128)(2,1)} collective-permute-done((bf16[2,6,64,1024]{3,2,1,0:T(8,128)(2,1)}, bf16[2,6,64,1024]{3,2,1,0:T(8,128)(2,1)}, u32[]{:S(2)}, u32[]{:S(2)}) %collective-permute-start.17) | collective-permute-done | bytes 1572896 | tf_op jit(solution)/shard_map/ppermute | solution.py:94
  164.6 8.9 %screen_product.5.refs_0_.refs_1_ = bf16[32,2,2,32,1024]{4,3,2,1,0:T(8,128)(2,1)} custom-call(s32[5]{0:T(128)S(1)} %concatenate.31.place_ref, bf16[1,2,128,1024]{3,2,1,0:T(8,128)(2,1)S(1)} %bitcast.116, bf16[1,2,128,1024]{3,2,1,0:T(8,128)(2,1)S(1)} %collective-permute-done.13.refs_1_, ...), custom_call_target="tpu_custom_call", output_to_operand_aliasing={{}: (6, {})} | custom-call | flops 1 | bytes 1 | tf_op jit(solution)/shard_map/screen_product/pallas_call | solution.py:138
  173.5 3.9 %contract.4.refs_5_ = f32[32,64,128]{2,1,0:T(8,128)S(1)} custom-call(s32[8]{0:T(128)S(1)} %gather_fusion.2, s32[1]{0:T(128)} %constant.230.clone.1.side_ref.owner_ref, s32[1]{0:T(128)} %bitcast.39.owner_ref, bf16[32,2,2,32,1024]{4,3,2,1,0:T(8,128)(2,1)} %screen_product.5.refs_0_.refs_1_, bf16[32,2,2,32,1024]{4,3,2,1,0:T(8,128)(2,1)} %screen_product.5.refs_0_.refs_1_, ...), custom_call_target="tpu_custom_call" | custom-call | flops 1 | bytes 1 | tf_op jit(solution)/shard_map/contract/pallas_call | solution.py:216
  177.5 8.2 %contract.5.refs_6_ = f32[32,64,128]{2,1,0:T(8,128)S(1)} custom-call(s32[16]{0:T(128)S(1)} %gather_fusion.1, s32[2]{0:T(128)S(1)} %pad_add_fusion.1.side_ref, s32[2]{0:T(128)S(1)} %get-tuple-element.28.owner_ref, bf16[32,2,2,32,1024]{4,3,2,1,0:T(8,128)(2,1)} %screen_product.5.refs_0_.refs_1_, ...), custom_call_target="tpu_custom_call", output_to_operand_aliasing={{}: (8, {})} | custom-call | flops 1 | bytes 1 | tf_op jit(solution)/shard_map/contract/pallas_call | solution.py:216
  185.8 4.8 %contract.6 = f32[32,64,128]{2,1,0:T(8,128)S(1)} custom-call(s32[8]{0:T(128)S(1)} %gather_fusion, s32[1]{0:T(128)} %bitcast.1.side_ref, s32[1]{0:T(128)} %bitcast.2.owner_ref, bf16[32,2,2,32,1024]{4,3,2,1,0:T(8,128)(2,1)} %screen_product.5.refs_0_.refs_1_, ...), custom_call_target="tpu_custom_call", output_to_operand_aliasing={{}: (9, {})} | custom-call | flops 1 | bytes 1 | tf_op jit(solution)/shard_map/contract/pallas_call | solution.py:216
  198.0 16.0 %collective-permute-done.20.refs_2_ = bf16[2,8,64,1024]{3,2,1,0:T(8,128)(2,1)} collective-permute-done((bf16[2,8,64,1024]{3,2,1,0:T(8,128)(2,1)}, bf16[2,8,64,1024]{3,2,1,0:T(8,128)(2,1)}, u32[]{:S(2)}, u32[]{:S(2)}) %collective-permute-start.20) | collective-permute-done | bytes 2097184 | tf_op jit(solution)/shard_map/ppermute | solution.py:94
  214.0 4.4 %contract.7 = f32[8,64,128]{2,1,0:T(8,128)S(1)} custom-call(s32[8]{0:T(128)S(1)} %gather_fusion.3, s32[1]{0:T(128)} %bitcast.47.side_ref, s32[1]{0:T(128)} %constant.230.clone.1.side_ref.owner_ref, bf16[32,2,2,32,1024]{4,3,2,1,0:T(8,128)(2,1)} %screen_product.5.refs_0_.refs_1_, bf16[32,2,2,32,1024]{4,3,2,1,0:T(8,128)(2,1)} %screen_product.5.refs_0_.refs_1_, ...), custom_call_target="tpu_custom_call" | custom-call | flops 1 | bytes 1 | tf_op jit(solution)/shard_map/contract/pallas_call | solution.py:216
  234.2 3.5 %collective-permute-done.26 = f32[16,16,128]{2,1,0:T(8,128)S(1)} collective-permute-done((f32[16,16,128]{2,1,0:T(8,128)S(1)}, f32[16,16,128]{2,1,0:T(8,128)S(1)}, u32[]{:S(2)}, u32[]{:S(2)}) %collective-permute-start.26) | collective-permute-done | bytes 131104 | tf_op jit(solution)/shard_map/ppermute | solution.py:22
  (152 shorter events, 59.3 us)
Async XLA Ops:
  7.1 26.3 %collective-permute-start = (bf16[2,4,32,2000]{3,2,1,0:T(8,128)(2,1)}, bf16[2,4,32,2000]{3,2,1,0:T(8,128)(2,1)S(1)}, u32[]{:S(2)}, u32[]{:S(2)}) collective-permute-start(bf16[2,4,32,2000]{3,2,1,0:T(8,128)(2,1)} %dynamic-slice_bitcast_fusion), channel_id=1, source_target_pairs={{0,2},{2,0},{1,3},{3,1},{4,6},{6,4},{5,7},{7,5},{8,10},{10,8},{9,1... | collective-permute-start | bytes 3072008 | tf_op jit(solution)/shard_map/ppermute | solution.py:22
  10.0 49.5 %collective-permute-start.8 = (bf16[2,8,64,1024]{3,2,1,0:T(8,128)(2,1)S(1)}, bf16[2,8,64,1024]{3,2,1,0:T(8,128)(2,1)}, u32[]{:S(2)}, u32[]{:S(2)}) collective-permute-start(bf16[2,8,64,1024]{3,2,1,0:T(8,128)(2,1)S(1)} %valence_columns.1.refs_2_.refs_4_.refs_5_.refs_3_), channel_id=1, source_target_pairs={{0,4},{4,8},{8,12},{1,5},{5,9},{9,13},{2,6},{6,10},{10,14},{3,7},{... | collective-permute-start | bytes 6291464 | tf_op jit(solution)/shard_map/ppermute | solution.py:269
  14.9 63.2 %collective-permute-start.9 = (bf16[2,8,64,1024]{3,2,1,0:T(8,128)(2,1)S(1)}, bf16[2,8,64,1024]{3,2,1,0:T(8,128)(2,1)}, u32[]{:S(2)}, u32[]{:S(2)}) collective-permute-start(bf16[2,8,64,1024]{3,2,1,0:T(8,128)(2,1)S(1)} %valence_columns.1.refs_2_.refs_4_.refs_5_.refs_3_), channel_id=1, source_target_pairs={{4,0},{8,4},{12,8},{5,1},{9,5},{13,9},{6,2},{10,6},{14,10},{7,3},{... | collective-permute-start | bytes 6291464 | tf_op jit(solution)/shard_map/ppermute | solution.py:270
  37.9 13.2 %collective-permute-start.1 = (bf16[1,2,128,1024]{3,2,1,0:T(8,128)(2,1)S(1)}, bf16[1,2,128,1024]{3,2,1,0:T(8,128)(2,1)S(1)}, u32[]{:S(2)}, u32[]{:S(2)}) collective-permute-start(bf16[1,2,128,1024]{3,2,1,0:T(8,128)(2,1)S(1)} %get-tuple-element.37.refs_0_), channel_id=1, source_target_pairs={{0,2},{2,0},{1,3},{3,1},{4,6},{6,4},{5,7},{7,5},{8,10},{10,8},{9,1... | collective-permute-start | bytes 1572872 | tf_op jit(solution)/shard_map/ppermute | solution.py:22
  41.4 43.2 %collective-permute-start.6 = (bf16[1,2,128,1024]{3,2,1,0:T(8,128)(2,1)S(1)}, bf16[1,2,128,1024]{3,2,1,0:T(8,128)(2,1)S(1)}, u32[]{:S(2)}, u32[]{:S(2)}) collective-permute-start(bf16[1,2,128,1024]{3,2,1,0:T(8,128)(2,1)S(1)} %get-tuple-element.37.refs_0_), channel_id=1, source_target_pairs={{0,1},{1,0},{2,3},{3,2},{4,5},{5,4},{6,7},{7,6},{8,9},{9,8},{10,11... | collective-permute-start | bytes 1572872 | tf_op jit(solution)/shard_map/ppermute | solution.py:22
  41.5 63.9 %collective-permute-start.4 = (bf16[2,128,1024]{2,1,0:T(8,128)(2,1)}, bf16[2,128,1024]{2,1,0:T(8,128)(2,1)S(1)}, u32[]{:S(2)}, u32[]{:S(2)}) collective-permute-start(bf16[2,128,1024]{2,1,0:T(8,128)(2,1)} %get-tuple-element.36), channel_id=1, source_target_pairs={{0,4},{4,8},{8,12},{12,0},{1,5},{5,9},{9,13},{13,1},{2,6},{6,10},{... | collective-permute-start | bytes 1572872 | tf_op jit(solution)/shard_map/ppermute | solution.py:22
  51.1 54.3 %collective-permute-start.5 = (bf16[2,128,1024]{2,1,0:T(8,128)(2,1)}, bf16[2,128,1024]{2,1,0:T(8,128)(2,1)S(1)}, u32[]{:S(2)}, u32[]{:S(2)}) collective-permute-start(bf16[2,128,1024]{2,1,0:T(8,128)(2,1)} %get-tuple-element.35), channel_id=1, source_target_pairs={{0,8},{4,12},{8,0},{12,4},{1,9},{5,13},{9,1},{13,5},{2,10},{6,14},... | collective-permute-start | bytes 1572872 | tf_op jit(solution)/shard_map/ppermute | solution.py:22
  59.5 45.9 %collective-permute-start.2 = (bf16[2,128,1024]{2,1,0:T(8,128)(2,1)}, bf16[2,128,1024]{2,1,0:T(8,128)(2,1)S(1)}, u32[]{:S(2)}, u32[]{:S(2)}) collective-permute-start(bf16[2,128,1024]{2,1,0:T(8,128)(2,1)} %get-tuple-element.17), channel_id=1, source_target_pairs={{0,12},{4,0},{8,4},{12,8},{1,13},{5,1},{9,5},{13,9},{2,14},{6,2},{... | collective-permute-start | bytes 1572872 | tf_op jit(solution)/shard_map/ppermute | solution.py:22
  78.1 15.3 %collective-permute-start.7 = (bf16[1,2,128,1024]{3,2,1,0:T(8,128)(2,1)S(1)}, bf16[1,2,128,1024]{3,2,1,0:T(8,128)(2,1)S(1)}, u32[]{:S(2)}, u32[]{:S(2)}) collective-permute-start(bf16[1,2,128,1024]{3,2,1,0:T(8,128)(2,1)S(1)} %collective-permute-done.1.refs_2_), channel_id=1, source_target_pairs={{0,1},{1,0},{2,3},{3,2},{4,5},{5,4},{6,7},{7,6},{8,9},{9,8},{10,11... | collective-permute-start | bytes 1572872 | tf_op jit(solution)/shard_map/ppermute | solution.py:22
  84.6 24.2 %collective-permute-start.15 = (bf16[2,2,64,1024]{3,2,1,0:T(8,128)(2,1)}, bf16[2,2,64,1024]{3,2,1,0:T(8,128)(2,1)S(1)}, u32[]{:S(2)}, u32[]{:S(2)}) collective-permute-start(bf16[2,2,64,1024]{3,2,1,0:T(8,128)(2,1)} %slice_select_fusion.1), channel_id=1, source_target_pairs={{8,12},{4,0},{9,13},{5,1},{10,14},{6,2},{11,15},{7,3},{24,28},{20,... | collective-permute-start | bytes 1572872 | tf_op jit(solution)/shard_map/ppermute | solution.py:94
  107.7 25.7 %collective-permute-start.11 = (bf16[2,2,128,1024]{3,2,1,0:T(8,128)(2,1)S(1)}, bf16[2,2,128,1024]{3,2,1,0:T(8,128)(2,1)}, u32[]{:S(2)}, u32[]{:S(2)}) collective-permute-start(bf16[2,2,128,1024]{3,2,1,0:T(8,128)(2,1)S(1)} %pad_maximum_fusion.2.refs_0_), channel_id=1, source_target_pairs={{0,2},{2,0},{1,3},{3,1},{4,6},{6,4},{5,7},{7,5},{8,10},{10,8},{9,1... | collective-permute-start | bytes 3145736 | tf_op jit(solution)/shard_map/ppermute | solution.py:22
  108.8 50.0 %collective-permute-start.16 = (bf16[2,8,64,1024]{3,2,1,0:T(8,128)(2,1)}, bf16[2,8,64,1024]{3,2,1,0:T(8,128)(2,1)}, u32[]{:S(2)}, u32[]{:S(2)}) collective-permute-start(bf16[2,8,64,1024]{3,2,1,0:T(8,128)(2,1)} %broadcast_select_fusion), channel_id=1, source_target_pairs={{4,8},{8,4},{5,9},{9,5},{6,10},{10,6},{7,11},{11,7},{20,24},{24,20... | collective-permute-start | bytes 6291464 | tf_op jit(solution)/shard_map/ppermute | solution.py:94
  114.0 44.8 %collective-permute-start.17 = (bf16[2,6,64,1024]{3,2,1,0:T(8,128)(2,1)}, bf16[2,6,64,1024]{3,2,1,0:T(8,128)(2,1)}, u32[]{:S(2)}, u32[]{:S(2)}) collective-permute-start(bf16[2,6,64,1024]{3,2,1,0:T(8,128)(2,1)} %slice_select_fusion), channel_id=1, source_target_pairs={{8,12},{4,0},{9,13},{5,1},{10,14},{6,2},{11,15},{7,3},{24,28},{20,... | collective-permute-start | bytes 4718600 | tf_op jit(solution)/shard_map/ppermute | solution.py:94
  115.3 18.8 %collective-permute-start.10 = (bf16[2,2,128,1024]{3,2,1,0:T(8,128)(2,1)S(1)}, bf16[2,2,128,1024]{3,2,1,0:T(8,128)(2,1)}, u32[]{:S(2)}, u32[]{:S(2)}) collective-permute-start(bf16[2,2,128,1024]{3,2,1,0:T(8,128)(2,1)S(1)} %pad_maximum_fusion.2.refs_0_), channel_id=1, source_target_pairs={{0,1},{1,0},{2,3},{3,2},{4,5},{5,4},{6,7},{7,6},{8,9},{9,8},{10,11... | collective-permute-start | bytes 3145736 | tf_op jit(solution)/shard_map/ppermute | solution.py:22
  133.5 3.0 %collective-permute-start.12 = (bf16[2,2,128,1024]{3,2,1,0:T(8,128)(2,1)}, bf16[2,2,128,1024]{3,2,1,0:T(8,128)(2,1)}, u32[]{:S(2)}, u32[]{:S(2)}) collective-permute-start(bf16[2,2,128,1024]{3,2,1,0:T(8,128)(2,1)} %collective-permute-done.11.refs_2_), channel_id=1, source_target_pairs={{0,1},{1,0},{2,3},{3,2},{4,5},{5,4},{6,7},{7,6},{8,9},{9,8},{10,11... | collective-permute-start | bytes 3145736 | tf_op jit(solution)/shard_map/ppermute | solution.py:22
  133.5 27.1 %collective-permute-start.3 = (bf16[1,2,128,1024]{3,2,1,0:T(8,128)(2,1)}, bf16[1,2,128,1024]{3,2,1,0:T(8,128)(2,1)}, u32[]{:S(2)}, u32[]{:S(2)}) collective-permute-start(bf16[1,2,128,1024]{3,2,1,0:T(8,128)(2,1)} %bitcast.114), channel_id=1, source_target_pairs={{0,2},{2,0},{1,3},{3,1},{4,6},{6,4},{5,7},{7,5},{8,10},{10,8},{9,1... | collective-permute-start | bytes 1572872 | tf_op jit(solution)/shard_map/ppermute | solution.py:22
  158.8 55.2 %collective-permute-start.20 = (bf16[2,8,64,1024]{3,2,1,0:T(8,128)(2,1)}, bf16[2,8,64,1024]{3,2,1,0:T(8,128)(2,1)}, u32[]{:S(2)}, u32[]{:S(2)}) collective-permute-start(bf16[2,8,64,1024]{3,2,1,0:T(8,128)(2,1)} %collective-permute-done.16.refs_4_), channel_id=1, source_target_pairs={{8,12},{4,0},{9,13},{5,1},{10,14},{6,2},{11,15},{7,3},{24,28},{20,... | collective-permute-start | bytes 6291464 | tf_op jit(solution)/shard_map/ppermute | solution.py:94
  160.7 2.9 %collective-permute-start.14 = (bf16[1,2,128,1024]{3,2,1,0:T(8,128)(2,1)}, bf16[1,2,128,1024]{3,2,1,0:T(8,128)(2,1)S(1)}, u32[]{:S(2)}, u32[]{:S(2)}) collective-permute-start(bf16[1,2,128,1024]{3,2,1,0:T(8,128)(2,1)} %collective-permute-done.3.refs_2_), channel_id=1, source_target_pairs={{0,1},{1,0},{2,3},{3,2},{4,5},{5,4},{6,7},{7,6},{8,9},{9,8},{10,11... | collective-permute-start | bytes 1572872 | tf_op jit(solution)/shard_map/ppermute | solution.py:22
  195.7 22.8 %collective-permute-start.19 = (f32[32,16,128]{2,1,0:T(8,128)S(1)}, f32[32,16,128]{2,1,0:T(8,128)S(1)}, u32[]{:S(2)}, u32[]{:S(2)}) collective-permute-start(f32[32,16,128]{2,1,0:T(8,128)S(1)} %dynamic-slice_bitcast_fusion.5), channel_id=1, source_target_pairs={{0,2},{2,0},{1,3},{3,1},{4,6},{6,4},{5,7},{7,5},{8,10},{10,8},{9,1... | collective-permute-start | bytes 786440 | tf_op jit(solution)/shard_map/ppermute | solution.py:22
  219.9 4.3 %collective-permute-start.22 = (f32[8,16,128]{2,1,0:T(8,128)S(1)}, f32[8,16,128]{2,1,0:T(8,128)S(1)}, u32[]{:S(2)}, u32[]{:S(2)}) collective-permute-start(f32[8,16,128]{2,1,0:T(8,128)S(1)} %dynamic-slice_bitcast_fusion.10), channel_id=1, source_target_pairs={{0,2},{2,0},{1,3},{3,1},{4,6},{6,4},{5,7},{7,5},{8,10},{10,8},{9,1... | collective-permute-start | bytes 196616 | tf_op jit(solution)/shard_map/ppermute | solution.py:22
  225.1 6.4 %collective-permute-start.23 = (bf16[16,16,128]{2,1,0:T(8,128)(2,1)S(1)}, bf16[16,16,128]{2,1,0:T(8,128)(2,1)S(1)}, u32[]{:S(2)}, u32[]{:S(2)}) collective-permute-start(bf16[16,16,128]{2,1,0:T(8,128)(2,1)S(1)} %get-tuple-element.41), channel_id=1, source_target_pairs={{0,4},{4,8},{8,12},{12,0},{1,5},{5,9},{9,13},{13,1},{2,6},{6,10},{... | collective-permute-start | bytes 196616 | tf_op jit(solution)/shard_map/ppermute | solution.py:22
  225.1 7.5 %collective-permute-start.24 = (bf16[16,16,128]{2,1,0:T(8,128)(2,1)S(1)}, bf16[16,16,128]{2,1,0:T(8,128)(2,1)S(1)}, u32[]{:S(2)}, u32[]{:S(2)}) collective-permute-start(bf16[16,16,128]{2,1,0:T(8,128)(2,1)S(1)} %get-tuple-element.43), channel_id=1, source_target_pairs={{0,8},{4,12},{8,0},{12,4},{1,9},{5,13},{9,1},{13,5},{2,10},{6,14},... | collective-permute-start | bytes 196616 | tf_op jit(solution)/shard_map/ppermute | solution.py:22
  227.2 5.5 %collective-permute-start.25 = (bf16[16,16,128]{2,1,0:T(8,128)(2,1)S(1)}, bf16[16,16,128]{2,1,0:T(8,128)(2,1)S(1)}, u32[]{:S(2)}, u32[]{:S(2)}) collective-permute-start(bf16[16,16,128]{2,1,0:T(8,128)(2,1)S(1)} %get-tuple-element.42), channel_id=1, source_target_pairs={{0,12},{4,0},{8,4},{12,8},{1,13},{5,1},{9,5},{13,9},{2,14},{6,2},{... | collective-permute-start | bytes 196616 | tf_op jit(solution)/shard_map/ppermute | solution.py:22
  232.7 5.0 %collective-permute-start.26 = (f32[16,16,128]{2,1,0:T(8,128)S(1)}, f32[16,16,128]{2,1,0:T(8,128)S(1)}, u32[]{:S(2)}, u32[]{:S(2)}) collective-permute-start(f32[16,16,128]{2,1,0:T(8,128)S(1)} %bitcast_add_fusion.2), channel_id=1, source_target_pairs={{0,2},{2,0},{1,3},{3,1},{4,6},{6,4},{5,7},{7,5},{8,10},{10,8},{9,1... | collective-permute-start | bytes 393224 | tf_op jit(solution)/shard_map/ppermute | solution.py:22
  (25 other events, 354.1 us)

commit v11 on v10

--- a/solution.py
+++ b/solution.py
@@ -271,7 +271,7 @@
     ]
 
     halves = jnp.moveaxis(conduction.reshape(2, pw_count, per_index, half, columns), 1, 0)
-    dealt = deal(after(halves, own_valence), "pw")
+    dealt = deal(halves, "pw")
 
     plane = jnp.arange(deep)
     is_head = (plane >= block) & (plane < block + HEAD_PARTS)
@@ -287,13 +287,9 @@
             )
             by_block.append(jnp.where(is_head, heads[..., None], cut).reshape(2, rows, deep))
     by_block = jnp.stack(by_block)
+    arrived = deal(by_block, "kpt")
+    own_block = arrived[0]
     middle = kpt_count // 2 + 1
-    own_block = lax.dynamic_index_in_dim(by_block, kpt, 0, keepdims=False)
-    own_across = share(own_block[None], "pw")
-    arrived = [own_block]
-    for shift in range(1, kpt_count):
-        piece = lax.dynamic_index_in_dim(by_block, (kpt + shift) % kpt_count, 0, keepdims=False)
-        arrived.append(shifted(piece if shift < middle else after(piece, own_across), "kpt", shift))
 
     screen = jnp.pad(screened, ((0, 0), (0, deep - block), (0, band_count * width - columns)))
     screen = lax.dynamic_slice_in_dim(screen, band * width, width, 2)
@@ -317,7 +313,6 @@
     screen = jnp.where(
         (jnp.arange(width)[None, None, :] == head_at) & has_column, column_part[:, :, None], screen
     )
-    screen = after(screen, step_one)
     right = jnp.stack(
         [
             jnp.concatenate([screen[0], screen[1]], axis=0),
@@ -339,8 +334,8 @@
         jnp.where(partner[None, :] == jnp.arange(all_points)[:, None], jnp.arange(all_points)[None, :], 0), axis=1
     ).astype(jnp.int32)
 
-    def spread(across):
-        return [own for value in across for own in share(value, "band")]
+    def spread(group):
+        return [own for across in share(group, "pw") for own in share(across, "band")]
 
     def product(shifts, pieces, right, store):
         sources = jnp.stack([((kpt - shift) % kpt_count).astype(jnp.int32) for shift in shifts])
@@ -349,11 +344,11 @@
 
     near, far = list(range(1, middle)), list(range(middle, kpt_count))
     distant = [arrived[shift] for shift in far]
-    store = product([0], spread(own_across), right, None)
+    store = product([0], spread(own_block[None]), right, None)
     to_ends, to_others = line_pairs(kpt_count, 2)
     onward = chosen(*step_one, *to_others, "kpt") if kpt_count > 3 else ()
     near_group = jnp.stack(after([arrived[shift] for shift in near], [store, step_one, distant, onward]))
-    near_pieces = spread(share(near_group, "pw"))
+    near_pieces = spread(near_group)
     far_across = share(jnp.stack(distant), "pw")
     early_rows = max(points // 4, 1)
     first_part = one_way(*[value[:, :early_rows] for value in step_one], *to_ends, "kpt")

time: 240 us -> 235 us (0.979)
  waiting for transfers between devices: 100 us -> 94.6 us
  starting transfers between devices: 36.3 us -> 31.2 us
  other arithmetic: 28.1 us -> 31.6 us
    ppermute x21, waiting for transfers between devices: 57.7 us -> 81.5 us  [shifted(): return lax.ppermute(x, name, pairs)]
    ppermute x1, waiting for transfers between devices: 13.9 us -> 0.01 us  [on_device(): lax.ppermute(own_valence, 'kpt', [(s, s - 1) for s in range(1, kpt_count)])]
    ppermute x4, waiting for transfers between devices: 22.7 us -> 13.1 us  [one_way(): moved = lax.ppermute(after(below, gates), name, pairs_below + pairs_above)]
    ppermute x21, starting transfers between devices: 24.1 us -> 17.4 us  [shifted(): return lax.ppermute(x, name, pairs)]
    ppermute x1, waiting for transfers between devices: 5.89 us -> 0.01 us  [on_device(): lax.ppermute(own_valence, 'kpt', [(s, s + 1) for s in range(kpt_count - 1)])]
  transfers between devices with their start and end apart: 27 -> 27, of which waited for: 16 -> 15; matrix products, arithmetic and copies ran while one was open for 14% -> 18% of each run, Pallas kernels for 23% -> 24%
where the time goes in v11:
time: 235 us; the launch traced here: 234 us
  waiting for transfers between devices  94.6 us (40%)
  Pallas kernels  57.9 us (25%)
  other arithmetic  31.6 us (13%)
  starting transfers between devices  31.2 us (13%)
  local copies, waits for them, and re-layouts  16.9 us (7%)
    ppermute x21, waiting for transfers between devices, shifted(): return lax.ppermute(x, name, pairs)  81.5 us
    pallas_call x3, Pallas kernels, screen_product(): pl.pallas_call(kernel, out_shape=jax.ShapeDtypeStruct((blocks * points, b...  34.1 us
    pallas_call x4, Pallas kernels, contract(): pl.pallas_call(kernel, out_shape=jax.ShapeDtypeStruct((blocks * points, b...  21.6 us
    ppermute x21, starting transfers between devices, shifted(): return lax.ppermute(x, name, pairs)  17.4 us
    another operation x2, other arithmetic, on_device(): jnp.stack([jnp.concatenate([screen[0], screen[1]], axis=0), jnp.concatena...  13.3 us
    ppermute x4, waiting for transfers between devices, one_way(): moved = lax.ppermute(after(below, gates), name, pairs_below + pairs_above)  13.1 us
    select_n x3, other arithmetic, chosen(): sent = jnp.where(sends_below, below, above)  8.44 us
    ppermute x1, starting transfers between devices, on_device(): lax.ppermute(own_valence, 'kpt', [(s, s + 1) for s in range(kpt_count - 1)])  6.42 us
  transfers between devices with their start and end apart: 27, of which 15 were waited for; matrix products, arithmetic and copies ran while one was open for 18% of the time, Pallas kernels for 24%

profile of v11, /device:TPU:0, one launch (start us, length us, event | category | flops | bytes accessed | tf_op | source)
XLA Modules:
  0.0 234.2 jit_solution(15542050624784312571)
XLA Ops:
  4.0 6.4 %collective-permute-start.8 = (bf16[2,8,64,1024]{3,2,1,0:T(8,128)(2,1)S(1)}, bf16[2,8,64,1024]{3,2,1,0:T(8,128)(2,1)}, u32[]{:S(2)}, u32[]{:S(2)}) collective-permute-start(bf16[2,8,64,1024]{3,2,1,0:T(8,128)(2,1)S(1)} %valence_columns.1.refs_2_.refs_4_.refs_5_.refs_3_), channel_id=1, source_target_pairs={{0,4},{4,8},{8,12},{1,5},{5,9},{9,13},{2,6},{6,10},{10,14},{3,7},{... | collective-permute-start | bytes 6291464 | tf_op jit(solution)/shard_map/ppermute | solution.py:269
  16.1 3.3 %fusion.1 = bf16[2,1024,1024]{2,1,0:T(8,128)(2,1)S(1)} fusion(s32[]{:T(128)S(6)} %select_n.382, bf16[2,1000,2000]{2,1,0:T(8,128)(2,1)} %param.20, pred[1024]{0:T(1024)(128)(4,1)S(1)} %get-tuple-element.45, pred[1024]{0:T(1024)(128)(4,1)S(1)} %get-tuple-element.46, bf16[2,1024]{1,0:T(2,128)(2,1)S(1)} %broadcast_select_fusion.3, bf16[2,1024]{1,0:T(2,128)(2,1)S(1)} %fusion.19), kind=kLoop, calls=%fused_computation.7 | loop fusion | flops 4194304 | bytes 12204548 | tf_op jit(solution)/shard_map/jit(_where)/select_n | solution.py:313
  19.5 2.4 %slice_bitcast_fusion.1 = (bf16[1024,1024]{1,0:T(8,128)(2,1)}, bf16[1024,1024]{1,0:T(8,128)(2,1)}) fusion(bf16[2,1024,1024]{2,1,0:T(8,128)(2,1)S(1)} %fusion.1), kind=kLoop, calls=%fused_computation.12 | loop fusion | bytes 8388608 | tf_op jit(solution)/shard_map/squeeze | solution.py:318
  21.9 17.0 %collective-permute-done = bf16[2,4,32,2000]{3,2,1,0:T(8,128)(2,1)S(1)} collective-permute-done((bf16[2,4,32,2000]{3,2,1,0:T(8,128)(2,1)}, bf16[2,4,32,2000]{3,2,1,0:T(8,128)(2,1)S(1)}, u32[]{:S(2)}, u32[]{:S(2)}) %collective-permute-start) | collective-permute-done | bytes 1024032 | tf_op jit(solution)/shard_map/ppermute | solution.py:22
  44.9 5.8 %maximum_bitcast_fusion = (bf16[1,2048,1024]{2,1,0:T(8,128)(2,1)}, bf16[1,2048,1024]{2,1,0:T(8,128)(2,1)}) fusion(bf16[1024,1024]{1,0:T(8,128)(2,1)} %get-tuple-element.24, bf16[1024,1024]{1,0:T(8,128)(2,1)} %get-tuple-element.23, bf16[1024,1024]{1,0:T(8,128)(2,1)} %fusion.30), kind=kLoop, calls=%fused_computation.8 | loop fusion | flops 16777216 | bytes 14680064 | tf_op jit(solution)/shard_map/stack | solution.py:316
  50.7 3.9 %collective-permute-done.6.refs_2_ = bf16[1,2,128,1024]{3,2,1,0:T(8,128)(2,1)} collective-permute-done((bf16[1,2,128,1024]{3,2,1,0:T(8,128)(2,1)S(1)}, bf16[1,2,128,1024]{3,2,1,0:T(8,128)(2,1)}, u32[]{:S(2)}, u32[]{:S(2)}) %collective-permute-start.6) | collective-permute-done | bytes 524320 | tf_op jit(solution)/shard_map/ppermute | solution.py:22
  54.6 7.5 %pad_maximum_fusion.refs_4_ = bf16[2,2048,1024]{2,1,0:T(8,128)(2,1)} fusion(bf16[1,2048,1024]{2,1,0:T(8,128)(2,1)} %get-tuple-element.28, bf16[1,2048,1024]{2,1,0:T(8,128)(2,1)} %get-tuple-element.27), kind=kLoop, calls=%fused_computation.4 | loop fusion | flops 4194304 | bytes 16777216 | tf_op jit(solution)/shard_map/stack | solution.py:316
  62.1 4.1 %collective-permute-start.1 = (bf16[2,128,1024]{2,1,0:T(8,128)(2,1)}, bf16[2,128,1024]{2,1,0:T(8,128)(2,1)S(1)}, u32[]{:S(2)}, u32[]{:S(2)}) collective-permute-start(bf16[2,128,1024]{2,1,0:T(8,128)(2,1)} %get-tuple-element.32), channel_id=1, source_target_pairs={{0,12},{4,0},{8,4},{12,8},{1,13},{5,1},{9,5},{13,9},{2,14},{6,2},{... | collective-permute-start | bytes 1572872 | tf_op jit(solution)/shard_map/ppermute | solution.py:22
  72.1 9.1 %screen_product.3.refs_5_ = bf16[32,2,2,32,1024]{4,3,2,1,0:T(8,128)(2,1)} custom-call(s32[5]{0:T(128)S(1)} %concatenate.33.place_ref, bf16[1,2,128,1024]{3,2,1,0:T(8,128)(2,1)S(1)} %get-tuple-element.29.refs_0_, bf16[1,2,128,1024]{3,2,1,0:T(8,128)(2,1)S(1)} %copy-done.7, bf16[1,2,128,1024]{3,2,1,0:T(8,128)(2,1)} %collective-permute-done.6.refs_2_, ...), custom_call_target="tpu_custom_call" | custom-call | flops 1 | bytes 1 | tf_op jit(solution)/shard_map/screen_product/pallas_call | solution.py:138
  81.2 3.1 %broadcast_select_fusion = bf16[2,8,64,1024]{3,2,1,0:T(8,128)(2,1)} fusion(bf16[2,8,64,1024]{3,2,1,0:T(8,128)(2,1)} %collective-permute-done.8.refs_2_, bf16[2,8,64,1024]{3,2,1,0:T(8,128)(2,1)} %collective-permute-done.9.refs_3_, pred[]{:T(512)S(6)} %eq.159), kind=kLoop, calls=%fused_computation.14 | loop fusion | flops 1048576 | bytes 6291457 | tf_op jit(solution)/shard_map/jit(_where)/select_n | solution.py:87
  84.3 6.3 %collective-permute-done.3 = bf16[2,128,1024]{2,1,0:T(8,128)(2,1)} collective-permute-done((bf16[2,128,1024]{2,1,0:T(8,128)(2,1)}, bf16[2,128,1024]{2,1,0:T(8,128)(2,1)}, u32[]{:S(2)}, u32[]{:S(2)}) %collective-permute-start.3) | collective-permute-done | bytes 524320 | tf_op jit(solution)/shard_map/ppermute | solution.py:22
  90.6 21.4 %collective-permute-done.4 = bf16[2,128,1024]{2,1,0:T(8,128)(2,1)} collective-permute-done((bf16[2,128,1024]{2,1,0:T(8,128)(2,1)}, bf16[2,128,1024]{2,1,0:T(8,128)(2,1)}, u32[]{:S(2)}, u32[]{:S(2)}) %collective-permute-start.4) | collective-permute-done | bytes 524320 | tf_op jit(solution)/shard_map/ppermute | solution.py:22
  116.9 3.2 %slice_select_fusion = bf16[2,6,64,1024]{3,2,1,0:T(8,128)(2,1)} fusion(bf16[2,8,64,1024]{3,2,1,0:T(8,128)(2,1)} %collective-permute-done.9.refs_3_, bf16[2,8,64,1024]{3,2,1,0:T(8,128)(2,1)} %collective-permute-done.8.refs_2_, pred[]{:T(512)S(6)} %eq.160), kind=kLoop, calls=%fused_computation.15 | loop fusion | flops 786432 | bytes 4718593 | tf_op jit(solution)/shard_map/jit(_where)/select_n | solution.py:87
  121.5 16.8 %collective-permute-done.11.refs_2_ = bf16[2,2,128,1024]{3,2,1,0:T(8,128)(2,1)} collective-permute-done((bf16[2,2,128,1024]{3,2,1,0:T(8,128)(2,1)S(1)}, bf16[2,2,128,1024]{3,2,1,0:T(8,128)(2,1)}, u32[]{:S(2)}, u32[]{:S(2)}) %collective-permute-start.11) | collective-permute-done | bytes 1048608 | tf_op jit(solution)/shard_map/ppermute | solution.py:22
  141.3 16.1 %screen_product.4.refs_5_ = bf16[32,2,2,32,1024]{4,3,2,1,0:T(8,128)(2,1)} custom-call(s32[6]{0:T(128)S(1)} %concatenate.32.place_ref, bf16[2,2,128,1024]{3,2,1,0:T(8,128)(2,1)S(1)} %pad_maximum_fusion.2.refs_0_, bf16[2,2,128,1024]{3,2,1,0:T(8,128)(2,1)} %collective-permute-done.10.refs_1_, ...), custom_call_target="tpu_custom_call", output_to_operand_aliasing={{}: (6, {})} | custom-call | flops 1 | bytes 1 | tf_op jit(solution)/shard_map/screen_product/pallas_call | solution.py:138
  163.9 8.9 %screen_product.5.refs_0_.refs_1_ = bf16[32,2,2,32,1024]{4,3,2,1,0:T(8,128)(2,1)} custom-call(s32[5]{0:T(128)S(1)} %concatenate.31.place_ref, bf16[1,2,128,1024]{3,2,1,0:T(8,128)(2,1)S(1)} %bitcast.114, bf16[1,2,128,1024]{3,2,1,0:T(8,128)(2,1)S(1)} %collective-permute-done.13.refs_1_, ...), custom_call_target="tpu_custom_call", output_to_operand_aliasing={{}: (6, {})} | custom-call | flops 1 | bytes 1 | tf_op jit(solution)/shard_map/screen_product/pallas_call | solution.py:138
  172.8 3.9 %contract.4.refs_5_ = f32[32,64,128]{2,1,0:T(8,128)S(1)} custom-call(s32[8]{0:T(128)S(1)} %gather_fusion.2, s32[1]{0:T(128)} %constant.232.clone.1.side_ref.owner_ref, s32[1]{0:T(128)} %bitcast.38.owner_ref, bf16[32,2,2,32,1024]{4,3,2,1,0:T(8,128)(2,1)} %screen_product.5.refs_0_.refs_1_, bf16[32,2,2,32,1024]{4,3,2,1,0:T(8,128)(2,1)} %screen_product.5.refs_0_.refs_1_, ...), custom_call_target="tpu_custom_call" | custom-call | flops 1 | bytes 1 | tf_op jit(solution)/shard_map/contract/pallas_call | solution.py:216
  176.8 8.2 %contract.5.refs_6_ = f32[32,64,128]{2,1,0:T(8,128)S(1)} custom-call(s32[16]{0:T(128)S(1)} %gather_fusion.1, s32[2]{0:T(128)S(1)} %pad_add_fusion.1.side_ref, s32[2]{0:T(128)S(1)} %get-tuple-element.22.owner_ref, bf16[32,2,2,32,1024]{4,3,2,1,0:T(8,128)(2,1)} %screen_product.5.refs_0_.refs_1_, ...), custom_call_target="tpu_custom_call", output_to_operand_aliasing={{}: (8, {})} | custom-call | flops 1 | bytes 1 | tf_op jit(solution)/shard_map/contract/pallas_call | solution.py:216
  185.1 5.0 %contract.6 = f32[32,64,128]{2,1,0:T(8,128)S(1)} custom-call(s32[8]{0:T(128)S(1)} %gather_fusion, s32[1]{0:T(128)} %bitcast.1.side_ref, s32[1]{0:T(128)} %bitcast.2.owner_ref, bf16[32,2,2,32,1024]{4,3,2,1,0:T(8,128)(2,1)} %screen_product.5.refs_0_.refs_1_, ...), custom_call_target="tpu_custom_call", output_to_operand_aliasing={{}: (9, {})} | custom-call | flops 1 | bytes 1 | tf_op jit(solution)/shard_map/contract/pallas_call | solution.py:216
  196.8 12.3 %collective-permute-done.20.refs_2_ = bf16[2,8,64,1024]{3,2,1,0:T(8,128)(2,1)} collective-permute-done((bf16[2,8,64,1024]{3,2,1,0:T(8,128)(2,1)}, bf16[2,8,64,1024]{3,2,1,0:T(8,128)(2,1)}, u32[]{:S(2)}, u32[]{:S(2)}) %collective-permute-start.20) | collective-permute-done | bytes 2097184 | tf_op jit(solution)/shard_map/ppermute | solution.py:94
  209.1 4.4 %contract.7 = f32[8,64,128]{2,1,0:T(8,128)S(1)} custom-call(s32[8]{0:T(128)S(1)} %gather_fusion.3, s32[1]{0:T(128)} %bitcast.46.side_ref, s32[1]{0:T(128)} %constant.232.clone.1.side_ref.owner_ref, bf16[32,2,2,32,1024]{4,3,2,1,0:T(8,128)(2,1)} %screen_product.5.refs_0_.refs_1_, bf16[32,2,2,32,1024]{4,3,2,1,0:T(8,128)(2,1)} %screen_product.5.refs_0_.refs_1_, ...), custom_call_target="tpu_custom_call" | custom-call | flops 1 | bytes 1 | tf_op jit(solution)/shard_map/contract/pallas_call | solution.py:216
  216.3 3.0 %collective-permute-done.22 = f32[8,16,128]{2,1,0:T(8,128)S(1)} collective-permute-done((f32[8,16,128]{2,1,0:T(8,128)S(1)}, f32[8,16,128]{2,1,0:T(8,128)S(1)}, u32[]{:S(2)}, u32[]{:S(2)}) %collective-permute-start.22) | collective-permute-done | bytes 65568 | tf_op jit(solution)/shard_map/ppermute | solution.py:22
  224.0 2.5 %collective-permute-done.23 = bf16[16,16,128]{2,1,0:T(8,128)(2,1)S(1)} collective-permute-done((bf16[16,16,128]{2,1,0:T(8,128)(2,1)S(1)}, bf16[16,16,128]{2,1,0:T(8,128)(2,1)S(1)}, u32[]{:S(2)}, u32[]{:S(2)}) %collective-permute-start.23) | collective-permute-done | bytes 65568 | tf_op jit(solution)/shard_map/ppermute | solution.py:22
  228.4 4.4 %collective-permute-done.26 = f32[16,16,128]{2,1,0:T(8,128)S(1)} collective-permute-done((f32[16,16,128]{2,1,0:T(8,128)S(1)}, f32[16,16,128]{2,1,0:T(8,128)S(1)}, u32[]{:S(2)}, u32[]{:S(2)}) %collective-permute-start.26) | collective-permute-done | bytes 131104 | tf_op jit(solution)/shard_map/ppermute | solution.py:22
  (145 shorter events, 54.3 us)
Async XLA Ops:
  4.0 62.2 %collective-permute-start.8 = (bf16[2,8,64,1024]{3,2,1,0:T(8,128)(2,1)S(1)}, bf16[2,8,64,1024]{3,2,1,0:T(8,128)(2,1)}, u32[]{:S(2)}, u32[]{:S(2)}) collective-permute-start(bf16[2,8,64,1024]{3,2,1,0:T(8,128)(2,1)S(1)} %valence_columns.1.refs_2_.refs_4_.refs_5_.refs_3_), channel_id=1, source_target_pairs={{0,4},{4,8},{8,12},{1,5},{5,9},{9,13},{2,6},{6,10},{10,14},{3,7},{... | collective-permute-start | bytes 6291464 | tf_op jit(solution)/shard_map/ppermute | solution.py:269
  10.4 55.8 %collective-permute-start.9 = (bf16[2,8,64,1024]{3,2,1,0:T(8,128)(2,1)S(1)}, bf16[2,8,64,1024]{3,2,1,0:T(8,128)(2,1)}, u32[]{:S(2)}, u32[]{:S(2)}) collective-permute-start(bf16[2,8,64,1024]{3,2,1,0:T(8,128)(2,1)S(1)} %valence_columns.1.refs_2_.refs_4_.refs_5_.refs_3_), channel_id=1, source_target_pairs={{4,0},{8,4},{12,8},{5,1},{9,5},{13,9},{6,2},{10,6},{14,10},{7,3},{... | collective-permute-start | bytes 6291464 | tf_op jit(solution)/shard_map/ppermute | solution.py:270
  14.0 24.8 %collective-permute-start = (bf16[2,4,32,2000]{3,2,1,0:T(8,128)(2,1)}, bf16[2,4,32,2000]{3,2,1,0:T(8,128)(2,1)S(1)}, u32[]{:S(2)}, u32[]{:S(2)}) collective-permute-start(bf16[2,4,32,2000]{3,2,1,0:T(8,128)(2,1)} %dynamic-slice_bitcast_fusion), channel_id=1, source_target_pairs={{0,2},{2,0},{1,3},{3,1},{4,6},{6,4},{5,7},{7,5},{8,10},{10,8},{9,1... | collective-permute-start | bytes 3072008 | tf_op jit(solution)/shard_map/ppermute | solution.py:22
  41.9 12.7 %collective-permute-start.6 = (bf16[1,2,128,1024]{3,2,1,0:T(8,128)(2,1)S(1)}, bf16[1,2,128,1024]{3,2,1,0:T(8,128)(2,1)}, u32[]{:S(2)}, u32[]{:S(2)}) collective-permute-start(bf16[1,2,128,1024]{3,2,1,0:T(8,128)(2,1)S(1)} %get-tuple-element.29.refs_0_), channel_id=1, source_target_pairs={{0,2},{2,0},{1,3},{3,1},{4,6},{6,4},{5,7},{7,5},{8,10},{10,8},{9,1... | collective-permute-start | bytes 1572872 | tf_op jit(solution)/shard_map/ppermute | solution.py:22
  50.7 18.2 %collective-permute-start.5 = (bf16[1,2,128,1024]{3,2,1,0:T(8,128)(2,1)S(1)}, bf16[1,2,128,1024]{3,2,1,0:T(8,128)(2,1)S(1)}, u32[]{:S(2)}, u32[]{:S(2)}) collective-permute-start(bf16[1,2,128,1024]{3,2,1,0:T(8,128)(2,1)S(1)} %get-tuple-element.29.refs_0_), channel_id=1, source_target_pairs={{0,1},{1,0},{2,3},{3,2},{4,5},{5,4},{6,7},{7,6},{8,9},{9,8},{10,11... | collective-permute-start | bytes 1572872 | tf_op jit(solution)/shard_map/ppermute | solution.py:22
  54.6 16.5 %collective-permute-start.7 = (bf16[1,2,128,1024]{3,2,1,0:T(8,128)(2,1)}, bf16[1,2,128,1024]{3,2,1,0:T(8,128)(2,1)}, u32[]{:S(2)}, u32[]{:S(2)}) collective-permute-start(bf16[1,2,128,1024]{3,2,1,0:T(8,128)(2,1)} %collective-permute-done.6.refs_2_), channel_id=1, source_target_pairs={{0,1},{1,0},{2,3},{3,2},{4,5},{5,4},{6,7},{7,6},{8,9},{9,8},{10,11... | collective-permute-start | bytes 1572872 | tf_op jit(solution)/shard_map/ppermute | solution.py:22
  62.1 22.2 %collective-permute-start.1 = (bf16[2,128,1024]{2,1,0:T(8,128)(2,1)}, bf16[2,128,1024]{2,1,0:T(8,128)(2,1)S(1)}, u32[]{:S(2)}, u32[]{:S(2)}) collective-permute-start(bf16[2,128,1024]{2,1,0:T(8,128)(2,1)} %get-tuple-element.32), channel_id=1, source_target_pairs={{0,12},{4,0},{8,4},{12,8},{1,13},{5,1},{9,5},{13,9},{2,14},{6,2},{... | collective-permute-start | bytes 1572872 | tf_op jit(solution)/shard_map/ppermute | solution.py:22
  66.2 24.5 %collective-permute-start.3 = (bf16[2,128,1024]{2,1,0:T(8,128)(2,1)}, bf16[2,128,1024]{2,1,0:T(8,128)(2,1)}, u32[]{:S(2)}, u32[]{:S(2)}) collective-permute-start(bf16[2,128,1024]{2,1,0:T(8,128)(2,1)} %get-tuple-element.31), channel_id=1, source_target_pairs={{0,4},{4,8},{8,12},{12,0},{1,5},{5,9},{9,13},{13,1},{2,6},{6,10},{... | collective-permute-start | bytes 1572872 | tf_op jit(solution)/shard_map/ppermute | solution.py:22
  66.2 45.8 %collective-permute-start.4 = (bf16[2,128,1024]{2,1,0:T(8,128)(2,1)}, bf16[2,128,1024]{2,1,0:T(8,128)(2,1)}, u32[]{:S(2)}, u32[]{:S(2)}) collective-permute-start(bf16[2,128,1024]{2,1,0:T(8,128)(2,1)} %get-tuple-element.30), channel_id=1, source_target_pairs={{0,8},{4,12},{8,0},{12,4},{1,9},{5,13},{9,1},{13,5},{2,10},{6,14},... | collective-permute-start | bytes 1572872 | tf_op jit(solution)/shard_map/ppermute | solution.py:22
  69.6 45.2 %collective-permute-start.15 = (bf16[2,2,64,1024]{3,2,1,0:T(8,128)(2,1)}, bf16[2,2,64,1024]{3,2,1,0:T(8,128)(2,1)}, u32[]{:S(2)}, u32[]{:S(2)}) collective-permute-start(bf16[2,2,64,1024]{3,2,1,0:T(8,128)(2,1)} %slice_select_fusion.1), channel_id=1, source_target_pairs={{8,12},{4,0},{9,13},{5,1},{10,14},{6,2},{11,15},{7,3},{24,28},{20,... | collective-permute-start | bytes 1572872 | tf_op jit(solution)/shard_map/ppermute | solution.py:94
  113.3 25.0 %collective-permute-start.11 = (bf16[2,2,128,1024]{3,2,1,0:T(8,128)(2,1)S(1)}, bf16[2,2,128,1024]{3,2,1,0:T(8,128)(2,1)}, u32[]{:S(2)}, u32[]{:S(2)}) collective-permute-start(bf16[2,2,128,1024]{3,2,1,0:T(8,128)(2,1)S(1)} %pad_maximum_fusion.2.refs_0_), channel_id=1, source_target_pairs={{0,2},{2,0},{1,3},{3,1},{4,6},{6,4},{5,7},{7,5},{8,10},{10,8},{9,1... | collective-permute-start | bytes 3145736 | tf_op jit(solution)/shard_map/ppermute | solution.py:22
  114.9 43.2 %collective-permute-start.16 = (bf16[2,8,64,1024]{3,2,1,0:T(8,128)(2,1)}, bf16[2,8,64,1024]{3,2,1,0:T(8,128)(2,1)}, u32[]{:S(2)}, u32[]{:S(2)}) collective-permute-start(bf16[2,8,64,1024]{3,2,1,0:T(8,128)(2,1)} %broadcast_select_fusion), channel_id=1, source_target_pairs={{4,8},{8,4},{5,9},{9,5},{6,10},{10,6},{7,11},{11,7},{20,24},{24,20... | collective-permute-start | bytes 6291464 | tf_op jit(solution)/shard_map/ppermute | solution.py:94
  120.2 37.9 %collective-permute-start.17 = (bf16[2,6,64,1024]{3,2,1,0:T(8,128)(2,1)}, bf16[2,6,64,1024]{3,2,1,0:T(8,128)(2,1)}, u32[]{:S(2)}, u32[]{:S(2)}) collective-permute-start(bf16[2,6,64,1024]{3,2,1,0:T(8,128)(2,1)} %slice_select_fusion), channel_id=1, source_target_pairs={{8,12},{4,0},{9,13},{5,1},{10,14},{6,2},{11,15},{7,3},{24,28},{20,... | collective-permute-start | bytes 4718600 | tf_op jit(solution)/shard_map/ppermute | solution.py:94
  121.4 18.5 %collective-permute-start.10 = (bf16[2,2,128,1024]{3,2,1,0:T(8,128)(2,1)S(1)}, bf16[2,2,128,1024]{3,2,1,0:T(8,128)(2,1)}, u32[]{:S(2)}, u32[]{:S(2)}) collective-permute-start(bf16[2,2,128,1024]{3,2,1,0:T(8,128)(2,1)S(1)} %pad_maximum_fusion.2.refs_0_), channel_id=1, source_target_pairs={{0,1},{1,0},{2,3},{3,2},{4,5},{5,4},{6,7},{7,6},{8,9},{9,8},{10,11... | collective-permute-start | bytes 3145736 | tf_op jit(solution)/shard_map/ppermute | solution.py:22
  138.3 3.0 %collective-permute-start.12 = (bf16[2,2,128,1024]{3,2,1,0:T(8,128)(2,1)}, bf16[2,2,128,1024]{3,2,1,0:T(8,128)(2,1)}, u32[]{:S(2)}, u32[]{:S(2)}) collective-permute-start(bf16[2,2,128,1024]{3,2,1,0:T(8,128)(2,1)} %collective-permute-done.11.refs_2_), channel_id=1, source_target_pairs={{0,1},{1,0},{2,3},{3,2},{4,5},{5,4},{6,7},{7,6},{8,9},{9,8},{10,11... | collective-permute-start | bytes 3145736 | tf_op jit(solution)/shard_map/ppermute | solution.py:22
  138.4 21.6 %collective-permute-start.2 = (bf16[1,2,128,1024]{3,2,1,0:T(8,128)(2,1)}, bf16[1,2,128,1024]{3,2,1,0:T(8,128)(2,1)}, u32[]{:S(2)}, u32[]{:S(2)}) collective-permute-start(bf16[1,2,128,1024]{3,2,1,0:T(8,128)(2,1)} %bitcast.112), channel_id=1, source_target_pairs={{0,2},{2,0},{1,3},{3,1},{4,6},{6,4},{5,7},{7,5},{8,10},{10,8},{9,1... | collective-permute-start | bytes 1572872 | tf_op jit(solution)/shard_map/ppermute | solution.py:22
  158.1 51.0 %collective-permute-start.20 = (bf16[2,8,64,1024]{3,2,1,0:T(8,128)(2,1)}, bf16[2,8,64,1024]{3,2,1,0:T(8,128)(2,1)}, u32[]{:S(2)}, u32[]{:S(2)}) collective-permute-start(bf16[2,8,64,1024]{3,2,1,0:T(8,128)(2,1)} %collective-permute-done.16.refs_4_), channel_id=1, source_target_pairs={{8,12},{4,0},{9,13},{5,1},{10,14},{6,2},{11,15},{7,3},{24,28},{20,... | collective-permute-start | bytes 6291464 | tf_op jit(solution)/shard_map/ppermute | solution.py:94
  160.0 2.9 %collective-permute-start.14 = (bf16[1,2,128,1024]{3,2,1,0:T(8,128)(2,1)}, bf16[1,2,128,1024]{3,2,1,0:T(8,128)(2,1)S(1)}, u32[]{:S(2)}, u32[]{:S(2)}) collective-permute-start(bf16[1,2,128,1024]{3,2,1,0:T(8,128)(2,1)} %collective-permute-done.2.refs_2_), channel_id=1, source_target_pairs={{0,1},{1,0},{2,3},{3,2},{4,5},{5,4},{6,7},{7,6},{8,9},{9,8},{10,11... | collective-permute-start | bytes 1572872 | tf_op jit(solution)/shard_map/ppermute | solution.py:22
  195.2 18.4 %collective-permute-start.19 = (f32[32,16,128]{2,1,0:T(8,128)S(1)}, f32[32,16,128]{2,1,0:T(8,128)S(1)}, u32[]{:S(2)}, u32[]{:S(2)}) collective-permute-start(f32[32,16,128]{2,1,0:T(8,128)S(1)} %dynamic-slice_bitcast_fusion.5), channel_id=1, source_target_pairs={{0,2},{2,0},{1,3},{3,1},{4,6},{6,4},{5,7},{7,5},{8,10},{10,8},{9,1... | collective-permute-start | bytes 786440 | tf_op jit(solution)/shard_map/ppermute | solution.py:22
  215.0 4.3 %collective-permute-start.22 = (f32[8,16,128]{2,1,0:T(8,128)S(1)}, f32[8,16,128]{2,1,0:T(8,128)S(1)}, u32[]{:S(2)}, u32[]{:S(2)}) collective-permute-start(f32[8,16,128]{2,1,0:T(8,128)S(1)} %dynamic-slice_bitcast_fusion.10), channel_id=1, source_target_pairs={{0,2},{2,0},{1,3},{3,1},{4,6},{6,4},{5,7},{7,5},{8,10},{10,8},{9,1... | collective-permute-start | bytes 196616 | tf_op jit(solution)/shard_map/ppermute | solution.py:22
  220.2 6.4 %collective-permute-start.23 = (bf16[16,16,128]{2,1,0:T(8,128)(2,1)S(1)}, bf16[16,16,128]{2,1,0:T(8,128)(2,1)S(1)}, u32[]{:S(2)}, u32[]{:S(2)}) collective-permute-start(bf16[16,16,128]{2,1,0:T(8,128)(2,1)S(1)} %get-tuple-element.35), channel_id=1, source_target_pairs={{0,4},{4,8},{8,12},{12,0},{1,5},{5,9},{9,13},{13,1},{2,6},{6,10},{... | collective-permute-start | bytes 196616 | tf_op jit(solution)/shard_map/ppermute | solution.py:22
  220.2 7.5 %collective-permute-start.24 = (bf16[16,16,128]{2,1,0:T(8,128)(2,1)S(1)}, bf16[16,16,128]{2,1,0:T(8,128)(2,1)S(1)}, u32[]{:S(2)}, u32[]{:S(2)}) collective-permute-start(bf16[16,16,128]{2,1,0:T(8,128)(2,1)S(1)} %get-tuple-element.37), channel_id=1, source_target_pairs={{0,8},{4,12},{8,0},{12,4},{1,9},{5,13},{9,1},{13,5},{2,10},{6,14},... | collective-permute-start | bytes 196616 | tf_op jit(solution)/shard_map/ppermute | solution.py:22
  222.6 5.1 %collective-permute-start.25 = (bf16[16,16,128]{2,1,0:T(8,128)(2,1)S(1)}, bf16[16,16,128]{2,1,0:T(8,128)(2,1)S(1)}, u32[]{:S(2)}, u32[]{:S(2)}) collective-permute-start(bf16[16,16,128]{2,1,0:T(8,128)(2,1)S(1)} %get-tuple-element.36), channel_id=1, source_target_pairs={{0,12},{4,0},{8,4},{12,8},{1,13},{5,1},{9,5},{13,9},{2,14},{6,2},{... | collective-permute-start | bytes 196616 | tf_op jit(solution)/shard_map/ppermute | solution.py:22
  227.8 5.0 %collective-permute-start.26 = (f32[16,16,128]{2,1,0:T(8,128)S(1)}, f32[16,16,128]{2,1,0:T(8,128)S(1)}, u32[]{:S(2)}, u32[]{:S(2)}) collective-permute-start(f32[16,16,128]{2,1,0:T(8,128)S(1)} %bitcast_add_fusion.2), channel_id=1, source_target_pairs={{0,2},{2,0},{1,3},{3,1},{4,6},{6,4},{5,7},{7,5},{8,10},{10,8},{9,1... | collective-permute-start | bytes 393224 | tf_op jit(solution)/shard_map/ppermute | solution.py:22
  (22 other events, 354.4 us)

commit v12 on v8

--- a/solution.py
+++ b/solution.py
@@ -153,7 +153,7 @@
     _, _, pairs, _ = valences[0][0].shape
     points = sum(part.shape[1] for part in valences[0])
     slots = sides.shape[0]
-    group = 2 if points % 2 == 0 else 1
+    group = max(size for size in (1, 2, 4) if all(part.shape[1] % size == 0 for parts in valences for part in parts))
     steps = points // group
     given, places = [], []
     for side, parts in enumerate(valences):

time: 228 us -> 227 us (level)
  Pallas kernels: 57.9 us -> 54.1 us
  waiting for transfers between devices: 83.5 us -> 86.4 us
    pallas_call x4, Pallas kernels: 21.6 us -> 17.8 us  [contract(): pl.pallas_call(kernel, out_shape=jax.ShapeDtypeStruct((blocks * points, b...]
    ppermute x4, waiting for transfers between devices: 14.9 us -> 17.7 us  [one_way(): moved = lax.ppermute(after(sent, gates), name, pairs_below + pairs_above)]
  transfers between devices with their start and end apart: 27 -> 27, of which waited for: 15 -> 15; matrix products, arithmetic and copies ran while one was open for 19% -> 19% of each run, Pallas kernels for 25% -> 23%
where the time goes in v12:
time: 227 us; the launch traced here: 226 us
  waiting for transfers between devices  86.4 us (38%)
  Pallas kernels  54.1 us (24%)
  starting transfers between devices  34.8 us (15%)
  other arithmetic  31.6 us (14%)
  local copies, waits for them, and re-layouts  16.9 us (7%)
    ppermute x21, waiting for transfers between devices, shifted(): return lax.ppermute(x, name, pairs)  66.9 us
    pallas_call x3, Pallas kernels, screen_product(): pl.pallas_call(kernel, out_shape=jax.ShapeDtypeStruct((blocks * points, b...  34.1 us
    ppermute x21, starting transfers between devices, shifted(): return lax.ppermute(x, name, pairs)  21.1 us
    pallas_call x4, Pallas kernels, contract(): pl.pallas_call(kernel, out_shape=jax.ShapeDtypeStruct((blocks * points, b...  17.8 us
    ppermute x4, waiting for transfers between devices, one_way(): moved = lax.ppermute(after(sent, gates), name, pairs_below + pairs_above)  17.7 us
    another operation x2, other arithmetic, on_device(): jnp.stack([jnp.concatenate([screen[0], screen[1]], axis=0), jnp.concatena...  13.3 us
    select_n x3, other arithmetic, one_way(): sent = jnp.where(sends_below, below, above)  8.44 us
    ppermute x1, starting transfers between devices, on_device(): lax.ppermute(own_valence, 'kpt', [(s, s + 1) for s in range(kpt_count - 1)])  6.42 us
  transfers between devices with their start and end apart: 27, of which 15 were waited for; matrix products, arithmetic and copies ran while one was open for 19% of the time, Pallas kernels for 23%

profile of v12, /device:TPU:0, one launch (start us, length us, event | category | flops | bytes accessed | tf_op | source)
XLA Modules:
  0.0 225.8 jit_solution(1288512000423040423)
XLA Ops:
  4.0 6.4 %collective-permute-start.8 = (bf16[2,8,64,1024]{3,2,1,0:T(8,128)(2,1)S(1)}, bf16[2,8,64,1024]{3,2,1,0:T(8,128)(2,1)}, u32[]{:S(2)}, u32[]{:S(2)}) collective-permute-start(bf16[2,8,64,1024]{3,2,1,0:T(8,128)(2,1)S(1)} %valence_columns.1.refs_4_.refs_6_.refs_5_), channel_id=1, source_target_pairs={{0,4},{4,8},{8,12},{1,5},{5,9},{9,13},{2,6},{6,10},{10,14},{3,7},{... | collective-permute-start | bytes 6291464 | tf_op jit(solution)/shard_map/ppermute | solution.py:261
  16.1 3.3 %fusion.1 = bf16[2,1024,1024]{2,1,0:T(8,128)(2,1)S(1)} fusion(s32[]{:T(128)S(6)} %select_n.382, bf16[2,1000,2000]{2,1,0:T(8,128)(2,1)} %param.20, pred[1024]{0:T(1024)(128)(4,1)S(1)} %get-tuple-element.45, pred[1024]{0:T(1024)(128)(4,1)S(1)} %get-tuple-element.46, bf16[2,1024]{1,0:T(2,128)(2,1)S(1)} %broadcast_select_fusion.3, bf16[2,1024]{1,0:T(2,128)(2,1)S(1)} %fusion.19), kind=kLoop, calls=%fused_computation.7 | loop fusion | flops 4194304 | bytes 12204548 | tf_op jit(solution)/shard_map/jit(_where)/select_n | solution.py:305
  21.9 17.0 %collective-permute-done = bf16[2,4,32,2000]{3,2,1,0:T(8,128)(2,1)S(1)} collective-permute-done((bf16[2,4,32,2000]{3,2,1,0:T(8,128)(2,1)}, bf16[2,4,32,2000]{3,2,1,0:T(8,128)(2,1)S(1)}, u32[]{:S(2)}, u32[]{:S(2)}) %collective-permute-start) | collective-permute-done | bytes 1024032 | tf_op jit(solution)/shard_map/ppermute | solution.py:22
  44.9 5.8 %maximum_bitcast_fusion = (bf16[1,2048,1024]{2,1,0:T(8,128)(2,1)}, bf16[1,2048,1024]{2,1,0:T(8,128)(2,1)}) fusion(bf16[1024,1024]{1,0:T(8,128)(2,1)} %get-tuple-element.24, bf16[1024,1024]{1,0:T(8,128)(2,1)} %get-tuple-element.23, bf16[1024,1024]{1,0:T(8,128)(2,1)} %fusion.30), kind=kLoop, calls=%fused_computation.8 | loop fusion | flops 16777216 | bytes 14680064 | tf_op jit(solution)/shard_map/stack | solution.py:308
  50.7 4.4 %collective-permute-start.1 = (bf16[2,128,1024]{2,1,0:T(8,128)(2,1)}, bf16[2,128,1024]{2,1,0:T(8,128)(2,1)S(1)}, u32[]{:S(2)}, u32[]{:S(2)}) collective-permute-start(bf16[2,128,1024]{2,1,0:T(8,128)(2,1)} %get-tuple-element.32), channel_id=1, source_target_pairs={{0,12},{4,0},{8,4},{12,8},{1,13},{5,1},{9,5},{13,9},{2,14},{6,2},{... | collective-permute-start | bytes 1572872 | tf_op jit(solution)/shard_map/ppermute | solution.py:22
  56.6 2.6 %collective-permute-start.4 = (bf16[2,128,1024]{2,1,0:T(8,128)(2,1)}, bf16[2,128,1024]{2,1,0:T(8,128)(2,1)}, u32[]{:S(2)}, u32[]{:S(2)}) collective-permute-start(bf16[2,128,1024]{2,1,0:T(8,128)(2,1)} %get-tuple-element.30), channel_id=1, source_target_pairs={{0,8},{4,12},{8,0},{12,4},{1,9},{5,13},{9,1},{13,5},{2,10},{6,14},... | collective-permute-start | bytes 1572872 | tf_op jit(solution)/shard_map/ppermute | solution.py:22
  60.9 7.5 %pad_maximum_fusion.refs_4_ = bf16[2,2048,1024]{2,1,0:T(8,128)(2,1)} fusion(bf16[1,2048,1024]{2,1,0:T(8,128)(2,1)} %get-tuple-element.28, bf16[1,2048,1024]{2,1,0:T(8,128)(2,1)} %get-tuple-element.27), kind=kLoop, calls=%fused_computation.4 | loop fusion | flops 4194304 | bytes 16777216 | tf_op jit(solution)/shard_map/stack | solution.py:308
  73.9 9.1 %screen_product.3.refs_5_ = bf16[32,2,2,32,1024]{4,3,2,1,0:T(8,128)(2,1)} custom-call(s32[5]{0:T(128)S(1)} %concatenate.33.place_ref, bf16[1,2,128,1024]{3,2,1,0:T(8,128)(2,1)S(1)} %get-tuple-element.29.refs_0_, bf16[1,2,128,1024]{3,2,1,0:T(8,128)(2,1)S(1)} %copy-done.7, bf16[1,2,128,1024]{3,2,1,0:T(8,128)(2,1)} %collective-permute-done.6.refs_2_, ...), custom_call_target="tpu_custom_call" | custom-call | flops 1 | bytes 1 | tf_op jit(solution)/shard_map/screen_product/pallas_call | solution.py:130
  84.2 20.0 %collective-permute-done.4 = bf16[2,128,1024]{2,1,0:T(8,128)(2,1)} collective-permute-done((bf16[2,128,1024]{2,1,0:T(8,128)(2,1)}, bf16[2,128,1024]{2,1,0:T(8,128)(2,1)}, u32[]{:S(2)}, u32[]{:S(2)}) %collective-permute-start.4) | collective-permute-done | bytes 524320 | tf_op jit(solution)/shard_map/ppermute | solution.py:22
  107.1 3.1 %broadcast_select_fusion = bf16[2,8,64,1024]{3,2,1,0:T(8,128)(2,1)} fusion(bf16[2,8,64,1024]{3,2,1,0:T(8,128)(2,1)} %collective-permute-done.8.refs_4_, bf16[2,8,64,1024]{3,2,1,0:T(8,128)(2,1)} %collective-permute-done.9.refs_5_, pred[]{:T(512)S(6)} %eq.159), kind=kLoop, calls=%fused_computation.14 | loop fusion | flops 1048576 | bytes 6291457 | tf_op jit(solution)/shard_map/jit(_where)/select_n | solution.py:87
  112.2 3.2 %slice_select_fusion = bf16[2,6,64,1024]{3,2,1,0:T(8,128)(2,1)} fusion(bf16[2,8,64,1024]{3,2,1,0:T(8,128)(2,1)} %collective-permute-done.9.refs_5_, bf16[2,8,64,1024]{3,2,1,0:T(8,128)(2,1)} %collective-permute-done.8.refs_4_, pred[]{:T(512)S(6)} %eq.160), kind=kLoop, calls=%fused_computation.15 | loop fusion | flops 786432 | bytes 4718593 | tf_op jit(solution)/shard_map/jit(_where)/select_n | solution.py:87
  116.8 12.5 %collective-permute-done.11.refs_2_ = bf16[2,2,128,1024]{3,2,1,0:T(8,128)(2,1)} collective-permute-done((bf16[2,2,128,1024]{3,2,1,0:T(8,128)(2,1)S(1)}, bf16[2,2,128,1024]{3,2,1,0:T(8,128)(2,1)}, u32[]{:S(2)}, u32[]{:S(2)}) %collective-permute-start.11) | collective-permute-done | bytes 1048608 | tf_op jit(solution)/shard_map/ppermute | solution.py:22
  132.3 16.1 %screen_product.4.refs_5_ = bf16[32,2,2,32,1024]{4,3,2,1,0:T(8,128)(2,1)} custom-call(s32[6]{0:T(128)S(1)} %concatenate.32.place_ref, bf16[2,2,128,1024]{3,2,1,0:T(8,128)(2,1)S(1)} %pad_maximum_fusion.2.refs_0_, bf16[2,2,128,1024]{3,2,1,0:T(8,128)(2,1)} %collective-permute-done.10.refs_1_, ...), custom_call_target="tpu_custom_call", output_to_operand_aliasing={{}: (6, {})} | custom-call | flops 1 | bytes 1 | tf_op jit(solution)/shard_map/screen_product/pallas_call | solution.py:130
  148.4 3.9 %collective-permute-done.17.refs_3_ = bf16[2,6,64,1024]{3,2,1,0:T(8,128)(2,1)} collective-permute-done((bf16[2,6,64,1024]{3,2,1,0:T(8,128)(2,1)}, bf16[2,6,64,1024]{3,2,1,0:T(8,128)(2,1)}, u32[]{:S(2)}, u32[]{:S(2)}) %collective-permute-start.17) | collective-permute-done | bytes 1572896 | tf_op jit(solution)/shard_map/ppermute | solution.py:88
  158.1 8.9 %screen_product.5.refs_0_.refs_1_.refs_2_.refs_3_ = bf16[32,2,2,32,1024]{4,3,2,1,0:T(8,128)(2,1)} custom-call(s32[5]{0:T(128)S(1)} %concatenate.31.place_ref, bf16[1,2,128,1024]{3,2,1,0:T(8,128)(2,1)S(1)} %bitcast.114, bf16[1,2,128,1024]{3,2,1,0:T(8,128)(2,1)S(1)} %collective-permute-done.13.refs_1_, ...), custom_call_target="tpu_custom_call", output_to_operand_aliasing={{}: (6, {})} | custom-call | flops 1 | bytes 1 | tf_op jit(solution)/shard_map/screen_product/pallas_call | solution.py:130
  167.0 2.9 %contract.4.refs_7_ = f32[32,64,128]{2,1,0:T(8,128)S(1)} custom-call(s32[8]{0:T(128)S(1)} %gather_fusion.2, s32[1]{0:T(128)} %constant.232.clone.1.side_ref.owner_ref, s32[1]{0:T(128)} %bitcast.38.owner_ref, bf16[32,2,2,32,1024]{4,3,2,1,0:T(8,128)(2,1)} %screen_product.5.refs_0_.refs_1_.refs_2_.refs_3_, ...), custom_call_target="tpu_custom_call" | custom-call | flops 1 | bytes 1 | tf_op jit(solution)/shard_map/contract/pallas_call | solution.py:208
  169.9 6.4 %contract.5.refs_6_ = f32[32,64,128]{2,1,0:T(8,128)S(1)} custom-call(s32[16]{0:T(128)S(1)} %gather_fusion.1, s32[2]{0:T(128)S(1)} %pad_add_fusion.1.side_ref, s32[2]{0:T(128)S(1)} %get-tuple-element.22.owner_ref, bf16[32,2,2,32,1024]{4,3,2,1,0:T(8,128)(2,1)} %screen_product.5.refs_0_.refs_1_.refs_2_.refs_3_, ...), custom_call_target="tpu_custom_call", output_to_operand_aliasing={{}: (10, {})} | custom-call | flops 1 | bytes 1 | tf_op jit(solution)/shard_map/contract/pallas_call | solution.py:208
  176.4 5.0 %contract.6 = f32[32,64,128]{2,1,0:T(8,128)S(1)} custom-call(s32[8]{0:T(128)S(1)} %gather_fusion, s32[1]{0:T(128)} %bitcast.1.side_ref, s32[1]{0:T(128)} %bitcast.2.owner_ref, bf16[32,2,2,32,1024]{4,3,2,1,0:T(8,128)(2,1)} %screen_product.5.refs_0_.refs_1_.refs_2_.refs_3_, ...), custom_call_target="tpu_custom_call", output_to_operand_aliasing={{}: (9, {})} | custom-call | flops 1 | bytes 1 | tf_op jit(solution)/shard_map/contract/pallas_call | solution.py:208
  187.8 13.9 %collective-permute-done.20.refs_4_ = bf16[2,8,64,1024]{3,2,1,0:T(8,128)(2,1)} collective-permute-done((bf16[2,8,64,1024]{3,2,1,0:T(8,128)(2,1)}, bf16[2,8,64,1024]{3,2,1,0:T(8,128)(2,1)}, u32[]{:S(2)}, u32[]{:S(2)}) %collective-permute-start.20) | collective-permute-done | bytes 2097184 | tf_op jit(solution)/shard_map/ppermute | solution.py:88
  201.7 3.4 %contract.7 = f32[8,64,128]{2,1,0:T(8,128)S(1)} custom-call(s32[8]{0:T(128)S(1)} %gather_fusion.3, s32[1]{0:T(128)} %bitcast.46.side_ref, s32[1]{0:T(128)} %constant.232.clone.1.side_ref.owner_ref, bf16[32,2,2,32,1024]{4,3,2,1,0:T(8,128)(2,1)} %screen_product.5.refs_0_.refs_1_.refs_2_.refs_3_, ...), custom_call_target="tpu_custom_call" | custom-call | flops 1 | bytes 1 | tf_op jit(solution)/shard_map/contract/pallas_call | solution.py:208
  207.9 3.0 %collective-permute-done.22 = f32[8,16,128]{2,1,0:T(8,128)S(1)} collective-permute-done((f32[8,16,128]{2,1,0:T(8,128)S(1)}, f32[8,16,128]{2,1,0:T(8,128)S(1)}, u32[]{:S(2)}, u32[]{:S(2)}) %collective-permute-start.22) | collective-permute-done | bytes 65568 | tf_op jit(solution)/shard_map/ppermute | solution.py:22
  211.8 2.9 %collective-permute-start.24 = (bf16[16,16,128]{2,1,0:T(8,128)(2,1)S(1)}, bf16[16,16,128]{2,1,0:T(8,128)(2,1)S(1)}, u32[]{:S(2)}, u32[]{:S(2)}) collective-permute-start(bf16[16,16,128]{2,1,0:T(8,128)(2,1)S(1)} %get-tuple-element.37), channel_id=1, source_target_pairs={{0,8},{4,12},{8,0},{12,4},{1,9},{5,13},{9,1},{13,5},{2,10},{6,14},... | collective-permute-start | bytes 196616 | tf_op jit(solution)/shard_map/ppermute | solution.py:22
  215.7 2.5 %collective-permute-done.23 = bf16[16,16,128]{2,1,0:T(8,128)(2,1)S(1)} collective-permute-done((bf16[16,16,128]{2,1,0:T(8,128)(2,1)S(1)}, bf16[16,16,128]{2,1,0:T(8,128)(2,1)S(1)}, u32[]{:S(2)}, u32[]{:S(2)}) %collective-permute-start.23) | collective-permute-done | bytes 65568 | tf_op jit(solution)/shard_map/ppermute | solution.py:22
  220.0 4.4 %collective-permute-done.26 = f32[16,16,128]{2,1,0:T(8,128)S(1)} collective-permute-done((f32[16,16,128]{2,1,0:T(8,128)S(1)}, f32[16,16,128]{2,1,0:T(8,128)S(1)}, u32[]{:S(2)}, u32[]{:S(2)}) %collective-permute-start.26) | collective-permute-done | bytes 131104 | tf_op jit(solution)/shard_map/ppermute | solution.py:22
  (145 shorter events, 56.8 us)
Async XLA Ops:
  4.0 52.7 %collective-permute-start.8 = (bf16[2,8,64,1024]{3,2,1,0:T(8,128)(2,1)S(1)}, bf16[2,8,64,1024]{3,2,1,0:T(8,128)(2,1)}, u32[]{:S(2)}, u32[]{:S(2)}) collective-permute-start(bf16[2,8,64,1024]{3,2,1,0:T(8,128)(2,1)S(1)} %valence_columns.1.refs_4_.refs_6_.refs_5_), channel_id=1, source_target_pairs={{0,4},{4,8},{8,12},{1,5},{5,9},{9,13},{2,6},{6,10},{10,14},{3,7},{... | collective-permute-start | bytes 6291464 | tf_op jit(solution)/shard_map/ppermute | solution.py:261
  10.4 50.5 %collective-permute-start.9 = (bf16[2,8,64,1024]{3,2,1,0:T(8,128)(2,1)S(1)}, bf16[2,8,64,1024]{3,2,1,0:T(8,128)(2,1)}, u32[]{:S(2)}, u32[]{:S(2)}) collective-permute-start(bf16[2,8,64,1024]{3,2,1,0:T(8,128)(2,1)S(1)} %valence_columns.1.refs_4_.refs_6_.refs_5_), channel_id=1, source_target_pairs={{4,0},{8,4},{12,8},{5,1},{9,5},{13,9},{6,2},{10,6},{14,10},{7,3},{... | collective-permute-start | bytes 6291464 | tf_op jit(solution)/shard_map/ppermute | solution.py:262
  14.0 24.8 %collective-permute-start = (bf16[2,4,32,2000]{3,2,1,0:T(8,128)(2,1)}, bf16[2,4,32,2000]{3,2,1,0:T(8,128)(2,1)S(1)}, u32[]{:S(2)}, u32[]{:S(2)}) collective-permute-start(bf16[2,4,32,2000]{3,2,1,0:T(8,128)(2,1)} %dynamic-slice_bitcast_fusion), channel_id=1, source_target_pairs={{0,2},{2,0},{1,3},{3,1},{4,6},{6,4},{5,7},{7,5},{8,10},{10,8},{9,1... | collective-permute-start | bytes 3072008 | tf_op jit(solution)/shard_map/ppermute | solution.py:22
  41.9 13.2 %collective-permute-start.6 = (bf16[1,2,128,1024]{3,2,1,0:T(8,128)(2,1)S(1)}, bf16[1,2,128,1024]{3,2,1,0:T(8,128)(2,1)}, u32[]{:S(2)}, u32[]{:S(2)}) collective-permute-start(bf16[1,2,128,1024]{3,2,1,0:T(8,128)(2,1)S(1)} %get-tuple-element.29.refs_0_), channel_id=1, source_target_pairs={{0,2},{2,0},{1,3},{3,1},{4,6},{6,4},{5,7},{7,5},{8,10},{10,8},{9,1... | collective-permute-start | bytes 1572872 | tf_op jit(solution)/shard_map/ppermute | solution.py:22
  50.7 19.9 %collective-permute-start.5 = (bf16[1,2,128,1024]{3,2,1,0:T(8,128)(2,1)S(1)}, bf16[1,2,128,1024]{3,2,1,0:T(8,128)(2,1)S(1)}, u32[]{:S(2)}, u32[]{:S(2)}) collective-permute-start(bf16[1,2,128,1024]{3,2,1,0:T(8,128)(2,1)S(1)} %get-tuple-element.29.refs_0_), channel_id=1, source_target_pairs={{0,1},{1,0},{2,3},{3,2},{4,5},{5,4},{6,7},{7,6},{8,9},{9,8},{10,11... | collective-permute-start | bytes 1572872 | tf_op jit(solution)/shard_map/ppermute | solution.py:22
  50.7 32.3 %collective-permute-start.1 = (bf16[2,128,1024]{2,1,0:T(8,128)(2,1)}, bf16[2,128,1024]{2,1,0:T(8,128)(2,1)S(1)}, u32[]{:S(2)}, u32[]{:S(2)}) collective-permute-start(bf16[2,128,1024]{2,1,0:T(8,128)(2,1)} %get-tuple-element.32), channel_id=1, source_target_pairs={{0,12},{4,0},{8,4},{12,8},{1,13},{5,1},{9,5},{13,9},{2,14},{6,2},{... | collective-permute-start | bytes 1572872 | tf_op jit(solution)/shard_map/ppermute | solution.py:22
  55.1 29.1 %collective-permute-start.3 = (bf16[2,128,1024]{2,1,0:T(8,128)(2,1)}, bf16[2,128,1024]{2,1,0:T(8,128)(2,1)}, u32[]{:S(2)}, u32[]{:S(2)}) collective-permute-start(bf16[2,128,1024]{2,1,0:T(8,128)(2,1)} %get-tuple-element.31), channel_id=1, source_target_pairs={{0,4},{4,8},{8,12},{12,0},{1,5},{5,9},{9,13},{13,1},{2,6},{6,10},{... | collective-permute-start | bytes 1572872 | tf_op jit(solution)/shard_map/ppermute | solution.py:22
  56.6 47.6 %collective-permute-start.4 = (bf16[2,128,1024]{2,1,0:T(8,128)(2,1)}, bf16[2,128,1024]{2,1,0:T(8,128)(2,1)}, u32[]{:S(2)}, u32[]{:S(2)}) collective-permute-start(bf16[2,128,1024]{2,1,0:T(8,128)(2,1)} %get-tuple-element.30), channel_id=1, source_target_pairs={{0,8},{4,12},{8,0},{12,4},{1,9},{5,13},{9,1},{13,5},{2,10},{6,14},... | collective-permute-start | bytes 1572872 | tf_op jit(solution)/shard_map/ppermute | solution.py:22
  60.9 11.9 %collective-permute-start.7 = (bf16[1,2,128,1024]{3,2,1,0:T(8,128)(2,1)}, bf16[1,2,128,1024]{3,2,1,0:T(8,128)(2,1)}, u32[]{:S(2)}, u32[]{:S(2)}) collective-permute-start(bf16[1,2,128,1024]{3,2,1,0:T(8,128)(2,1)} %collective-permute-done.6.refs_2_), channel_id=1, source_target_pairs={{0,1},{1,0},{2,3},{3,2},{4,5},{5,4},{6,7},{7,6},{8,9},{9,8},{10,11... | collective-permute-start | bytes 1572872 | tf_op jit(solution)/shard_map/ppermute | solution.py:22
  71.4 38.8 %collective-permute-start.15 = (bf16[2,2,64,1024]{3,2,1,0:T(8,128)(2,1)}, bf16[2,2,64,1024]{3,2,1,0:T(8,128)(2,1)}, u32[]{:S(2)}, u32[]{:S(2)}) collective-permute-start(bf16[2,2,64,1024]{3,2,1,0:T(8,128)(2,1)} %slice_select_fusion.1), channel_id=1, source_target_pairs={{8,12},{4,0},{9,13},{5,1},{10,14},{6,2},{11,15},{7,3},{24,28},{20,... | collective-permute-start | bytes 1572872 | tf_op jit(solution)/shard_map/ppermute | solution.py:88
  105.5 23.8 %collective-permute-start.11 = (bf16[2,2,128,1024]{3,2,1,0:T(8,128)(2,1)S(1)}, bf16[2,2,128,1024]{3,2,1,0:T(8,128)(2,1)}, u32[]{:S(2)}, u32[]{:S(2)}) collective-permute-start(bf16[2,2,128,1024]{3,2,1,0:T(8,128)(2,1)S(1)} %pad_maximum_fusion.2.refs_0_), channel_id=1, source_target_pairs={{0,2},{2,0},{1,3},{3,1},{4,6},{6,4},{5,7},{7,5},{8,10},{10,8},{9,1... | collective-permute-start | bytes 3145736 | tf_op jit(solution)/shard_map/ppermute | solution.py:22
  110.2 42.1 %collective-permute-start.16 = (bf16[2,8,64,1024]{3,2,1,0:T(8,128)(2,1)}, bf16[2,8,64,1024]{3,2,1,0:T(8,128)(2,1)}, u32[]{:S(2)}, u32[]{:S(2)}) collective-permute-start(bf16[2,8,64,1024]{3,2,1,0:T(8,128)(2,1)} %broadcast_select_fusion), channel_id=1, source_target_pairs={{4,8},{8,4},{5,9},{9,5},{6,10},{10,6},{7,11},{11,7},{20,24},{24,20... | collective-permute-start | bytes 6291464 | tf_op jit(solution)/shard_map/ppermute | solution.py:88
  115.5 36.8 %collective-permute-start.17 = (bf16[2,6,64,1024]{3,2,1,0:T(8,128)(2,1)}, bf16[2,6,64,1024]{3,2,1,0:T(8,128)(2,1)}, u32[]{:S(2)}, u32[]{:S(2)}) collective-permute-start(bf16[2,6,64,1024]{3,2,1,0:T(8,128)(2,1)} %slice_select_fusion), channel_id=1, source_target_pairs={{8,12},{4,0},{9,13},{5,1},{10,14},{6,2},{11,15},{7,3},{24,28},{20,... | collective-permute-start | bytes 4718600 | tf_op jit(solution)/shard_map/ppermute | solution.py:88
  116.8 14.2 %collective-permute-start.10 = (bf16[2,2,128,1024]{3,2,1,0:T(8,128)(2,1)S(1)}, bf16[2,2,128,1024]{3,2,1,0:T(8,128)(2,1)}, u32[]{:S(2)}, u32[]{:S(2)}) collective-permute-start(bf16[2,2,128,1024]{3,2,1,0:T(8,128)(2,1)S(1)} %pad_maximum_fusion.2.refs_0_), channel_id=1, source_target_pairs={{0,1},{1,0},{2,3},{3,2},{4,5},{5,4},{6,7},{7,6},{8,9},{9,8},{10,11... | collective-permute-start | bytes 3145736 | tf_op jit(solution)/shard_map/ppermute | solution.py:22
  129.3 3.0 %collective-permute-start.12 = (bf16[2,2,128,1024]{3,2,1,0:T(8,128)(2,1)}, bf16[2,2,128,1024]{3,2,1,0:T(8,128)(2,1)}, u32[]{:S(2)}, u32[]{:S(2)}) collective-permute-start(bf16[2,2,128,1024]{3,2,1,0:T(8,128)(2,1)} %collective-permute-done.11.refs_2_), channel_id=1, source_target_pairs={{0,1},{1,0},{2,3},{3,2},{4,5},{5,4},{6,7},{7,6},{8,9},{9,8},{10,11... | collective-permute-start | bytes 3145736 | tf_op jit(solution)/shard_map/ppermute | solution.py:22
  129.4 24.7 %collective-permute-start.2 = (bf16[1,2,128,1024]{3,2,1,0:T(8,128)(2,1)}, bf16[1,2,128,1024]{3,2,1,0:T(8,128)(2,1)}, u32[]{:S(2)}, u32[]{:S(2)}) collective-permute-start(bf16[1,2,128,1024]{3,2,1,0:T(8,128)(2,1)} %bitcast.112), channel_id=1, source_target_pairs={{0,2},{2,0},{1,3},{3,1},{4,6},{6,4},{5,7},{7,5},{8,10},{10,8},{9,1... | collective-permute-start | bytes 1572872 | tf_op jit(solution)/shard_map/ppermute | solution.py:22
  152.3 49.4 %collective-permute-start.20 = (bf16[2,8,64,1024]{3,2,1,0:T(8,128)(2,1)}, bf16[2,8,64,1024]{3,2,1,0:T(8,128)(2,1)}, u32[]{:S(2)}, u32[]{:S(2)}) collective-permute-start(bf16[2,8,64,1024]{3,2,1,0:T(8,128)(2,1)} %collective-permute-done.16.refs_4_), channel_id=1, source_target_pairs={{8,12},{4,0},{9,13},{5,1},{10,14},{6,2},{11,15},{7,3},{24,28},{20,... | collective-permute-start | bytes 6291464 | tf_op jit(solution)/shard_map/ppermute | solution.py:88
  154.2 2.9 %collective-permute-start.14 = (bf16[1,2,128,1024]{3,2,1,0:T(8,128)(2,1)}, bf16[1,2,128,1024]{3,2,1,0:T(8,128)(2,1)S(1)}, u32[]{:S(2)}, u32[]{:S(2)}) collective-permute-start(bf16[1,2,128,1024]{3,2,1,0:T(8,128)(2,1)} %collective-permute-done.2.refs_2_), channel_id=1, source_target_pairs={{0,1},{1,0},{2,3},{3,2},{4,5},{5,4},{6,7},{7,6},{8,9},{9,8},{10,11... | collective-permute-start | bytes 1572872 | tf_op jit(solution)/shard_map/ppermute | solution.py:22
  186.5 18.7 %collective-permute-start.19 = (f32[32,16,128]{2,1,0:T(8,128)S(1)}, f32[32,16,128]{2,1,0:T(8,128)S(1)}, u32[]{:S(2)}, u32[]{:S(2)}) collective-permute-start(f32[32,16,128]{2,1,0:T(8,128)S(1)} %dynamic-slice_bitcast_fusion.5), channel_id=1, source_target_pairs={{0,2},{2,0},{1,3},{3,1},{4,6},{6,4},{5,7},{7,5},{8,10},{10,8},{9,1... | collective-permute-start | bytes 786440 | tf_op jit(solution)/shard_map/ppermute | solution.py:22
  206.6 4.3 %collective-permute-start.22 = (f32[8,16,128]{2,1,0:T(8,128)S(1)}, f32[8,16,128]{2,1,0:T(8,128)S(1)}, u32[]{:S(2)}, u32[]{:S(2)}) collective-permute-start(f32[8,16,128]{2,1,0:T(8,128)S(1)} %dynamic-slice_bitcast_fusion.10), channel_id=1, source_target_pairs={{0,2},{2,0},{1,3},{3,1},{4,6},{6,4},{5,7},{7,5},{8,10},{10,8},{9,1... | collective-permute-start | bytes 196616 | tf_op jit(solution)/shard_map/ppermute | solution.py:22
  211.8 6.3 %collective-permute-start.23 = (bf16[16,16,128]{2,1,0:T(8,128)(2,1)S(1)}, bf16[16,16,128]{2,1,0:T(8,128)(2,1)S(1)}, u32[]{:S(2)}, u32[]{:S(2)}) collective-permute-start(bf16[16,16,128]{2,1,0:T(8,128)(2,1)S(1)} %get-tuple-element.35), channel_id=1, source_target_pairs={{0,4},{4,8},{8,12},{12,0},{1,5},{5,9},{9,13},{13,1},{2,6},{6,10},{... | collective-permute-start | bytes 196616 | tf_op jit(solution)/shard_map/ppermute | solution.py:22
  211.8 7.5 %collective-permute-start.24 = (bf16[16,16,128]{2,1,0:T(8,128)(2,1)S(1)}, bf16[16,16,128]{2,1,0:T(8,128)(2,1)S(1)}, u32[]{:S(2)}, u32[]{:S(2)}) collective-permute-start(bf16[16,16,128]{2,1,0:T(8,128)(2,1)S(1)} %get-tuple-element.37), channel_id=1, source_target_pairs={{0,8},{4,12},{8,0},{12,4},{1,9},{5,13},{9,1},{13,5},{2,10},{6,14},... | collective-permute-start | bytes 196616 | tf_op jit(solution)/shard_map/ppermute | solution.py:22
  214.7 4.6 %collective-permute-start.25 = (bf16[16,16,128]{2,1,0:T(8,128)(2,1)S(1)}, bf16[16,16,128]{2,1,0:T(8,128)(2,1)S(1)}, u32[]{:S(2)}, u32[]{:S(2)}) collective-permute-start(bf16[16,16,128]{2,1,0:T(8,128)(2,1)S(1)} %get-tuple-element.36), channel_id=1, source_target_pairs={{0,12},{4,0},{8,4},{12,8},{1,13},{5,1},{9,5},{13,9},{2,14},{6,2},{... | collective-permute-start | bytes 196616 | tf_op jit(solution)/shard_map/ppermute | solution.py:22
  219.4 5.0 %collective-permute-start.26 = (f32[16,16,128]{2,1,0:T(8,128)S(1)}, f32[16,16,128]{2,1,0:T(8,128)S(1)}, u32[]{:S(2)}, u32[]{:S(2)}) collective-permute-start(f32[16,16,128]{2,1,0:T(8,128)S(1)} %bitcast_add_fusion.2), channel_id=1, source_target_pairs={{0,2},{2,0},{1,3},{3,1},{4,6},{6,4},{5,7},{7,5},{8,10},{10,8},{9,1... | collective-permute-start | bytes 393224 | tf_op jit(solution)/shard_map/ppermute | solution.py:22
  (22 other events, 335.8 us)
